TPU v7x, 32 devices: a whole 2x2x4 slice. The times are simulated.
32 devices in a mesh: row: 4 (over z), col: 8 (over y, x, core).
Axes of the slice: x: 2, y: 2, z: 4, core: 2. Of those that a mesh axis runs over, the one named last changes fastest.
Arguments:
- tokens: bfloat16 [512, 4096], P('row', 'col'), may hold values from -6 to 6
- upstream: bfloat16 [512, 4096], P('row', 'col'), may hold values from -6 to 6
- w_in: bfloat16 [8, 64, 256, 256], P('col', 'row'), may hold values from -0.1875 to 0.1875
- in_codes: int32 [8, 64], P('col'), may hold values from -1 to 127, as said below
- w_out: bfloat16 [8, 64, 256, 256], P('col', 'row'), may hold values from -0.09375 to 0.09375
- out_codes: int32 [8, 64], P('col'), may hold values from -1 to 127, as said below
Outputs:
- layer_out: bfloat16 [512, 4096], P('row', 'col')
- grad_tokens: bfloat16 [512, 4096], P('row', 'col')
- grad_w_in: bfloat16 [8, 64, 256, 256], P('col', 'row')
- grad_w_out: bfloat16 [8, 64, 256, 256], P('col', 'row')
Inputs may be any that keep to these rules, and one draw needn't show every extreme that they name: `in_codes`: row c describes panel c's 64 slots: a code k names input tile row k // 8 and local hidden tile column k % 8; -1 marks an empty slot. Codes of a row are distinct, every row has one filled slot or more, and some row has all 64 slots filled. `out_codes`: row c describes panel c's 64 slots: a code k names output tile column k // 8 and local hidden tile row k % 8; -1 marks an empty slot. Codes of a row are distinct, every row has one filled slot or more, and some row has all 64 slots filled.
All inputs are finite; a program needn't handle non-finite values.
Results may differ from a plain program's by a relative error of at most 0.015.
Values may be sent and summed in bfloat16 or wider, within the bound.
No kernel may reach another device: no remote copies, remote signals or barrier semaphores. Data moves between devices by JAX's collectives and lax.ppermute only.
A program may use at most 128 MiB of HBM per device.

v0:
```python
import jax
import jax.numpy as jnp
from jax import lax
from jax.sharding import PartitionSpec as P

D = 4096
FF = 16384


def silu_slope(hidden):
    sigmoid_value = jax.nn.sigmoid(hidden)
    return sigmoid_value * (1.0 + hidden * (1.0 - sigmoid_value))


def split_codes(slot_codes, tile_cols):
    filled = slot_codes >= 0
    clipped = jnp.maximum(slot_codes, 0)
    return (clipped // tile_cols, clipped % tile_cols, filled)


def selector(position, filled, classes):
    matches = position[:, None] == jnp.arange(classes, dtype=jnp.int32)[None, :]
    return (matches & filled[:, None]).astype(jnp.float32)


def slices_at(row_codes, col_codes, filled):
    return (row_codes, col_codes, filled)


def per_device(tokens, upstream, w_in, in_codes, w_out, out_codes):
    tile_size = w_in.shape[3]
    row_count = tokens.shape[0]
    tile_rows = D // tile_size
    tile_cols = FF // (tile_size * lax.axis_size("col"))
    own_slots = w_in.shape[1]
    highest = lax.Precision.HIGHEST
    in_row, in_col, in_filled = split_codes(in_codes[0], tile_cols)
    out_row, out_col, out_filled = split_codes(out_codes[0], tile_cols)
    first_slot = lax.axis_index("row") * own_slots
    whole_tokens, whole_upstream = (
        lax.all_gather(tokens, "col", axis=1, tiled=True),
        lax.all_gather(upstream, "col", axis=1, tiled=True),
    )
    token_tiles = whole_tokens.reshape(row_count, tile_rows, tile_size)
    up_tiles = whole_upstream.reshape(row_count, tile_rows, tile_size)
    slot_major_tokens = jnp.swapaxes(token_tiles, 0, 1)
    rows_at, cols_at, filled_at = slices_at(in_row, in_col, in_filled)
    picked = jnp.take(token_tiles, rows_at, axis=1)
    partial_sum = jnp.einsum(
        "tkd,kdn->tkn",
        picked,
        lax.all_gather(w_in, "row", axis=1, tiled=True)[0],
        preferred_element_type=jnp.float32,
    )
    hidden = jnp.einsum(
        "tkn,kj->tjn", partial_sum, selector(cols_at, filled_at, tile_cols), precision=highest
    )
    activ = jax.nn.silu(hidden).astype(jnp.bfloat16)
    rows_at, cols_at, filled_at = slices_at(out_row, out_col, out_filled)
    picked = jnp.take(activ, cols_at, axis=1)
    partial_sum = jnp.einsum(
        "tkf,kfd->tkd",
        picked,
        lax.all_gather(w_out, "row", axis=1, tiled=True)[0],
        preferred_element_type=jnp.float32,
    )
    layer_part = jnp.einsum(
        "tkd,ki->tid", partial_sum, selector(rows_at, filled_at, tile_rows), precision=highest
    )
    layer_out = lax.psum_scatter(
        layer_part.reshape(row_count, D).astype(jnp.bfloat16),
        "col",
        scatter_dimension=1,
        tiled=True,
    )
    rows_at, cols_at, filled_at = slices_at(out_row, out_col, out_filled)
    picked = jnp.take(up_tiles, rows_at, axis=1)
    partial_sum = jnp.einsum(
        "tkd,kfd->tkf",
        picked,
        lax.all_gather(w_out, "row", axis=1, tiled=True)[0],
        preferred_element_type=jnp.float32,
    )
    grad_activ = jnp.einsum(
        "tkf,kj->tjf", partial_sum, selector(cols_at, filled_at, tile_cols), precision=highest
    )
    grad_hidden = (grad_activ * silu_slope(hidden)).astype(jnp.bfloat16)
    grad_sends = jnp.take(jnp.swapaxes(grad_hidden, 0, 1), in_col, axis=0)
    activ_sends = jnp.take(jnp.swapaxes(activ, 0, 1), out_col, axis=0)
    upstream_sends = jnp.take(jnp.swapaxes(up_tiles, 0, 1), out_row, axis=0)
    token_sends = jnp.take(slot_major_tokens, in_row, axis=0)
    token_slots, grad_slots, activ_slots, upstream_slots = (
        lax.all_to_all(token_sends, "row", split_axis=0, concat_axis=1, tiled=True),
        lax.all_to_all(grad_sends, "row", split_axis=0, concat_axis=1, tiled=True),
        lax.all_to_all(activ_sends, "row", split_axis=0, concat_axis=1, tiled=True),
        lax.all_to_all(upstream_sends, "row", split_axis=0, concat_axis=1, tiled=True),
    )
    rows_at, cols_at, filled_at = slices_at(in_row, in_col, in_filled)
    picked = jnp.take(grad_hidden, cols_at, axis=1)
    partial_sum = jnp.einsum(
        "tkf,kdf->tkd",
        picked,
        lax.all_gather(w_in, "row", axis=1, tiled=True)[0],
        preferred_element_type=jnp.float32,
    )
    input_part = jnp.einsum(
        "tkd,ki->tid", partial_sum, selector(rows_at, filled_at, tile_rows), precision=highest
    )
    grad_tokens = lax.psum_scatter(
        input_part.reshape(row_count, D).astype(jnp.bfloat16),
        "col",
        scatter_dimension=1,
        tiled=True,
    )
    mine_in = lax.dynamic_slice_in_dim(in_filled, first_slot, own_slots)
    mine_out = lax.dynamic_slice_in_dim(out_filled, first_slot, own_slots)
    grad_w_in = jnp.einsum(
        "ktd,ktn->kdn", token_slots, grad_slots, preferred_element_type=jnp.float32
    )
    grad_w_in = jnp.where(mine_in[:, None, None], grad_w_in, 0.0).astype(jnp.bfloat16)[None]
    grad_w_out = jnp.einsum(
        "ktf,ktd->kfd", activ_slots, upstream_slots, preferred_element_type=jnp.float32
    )
    grad_w_out = jnp.where(mine_out[:, None, None], grad_w_out, 0.0).astype(jnp.bfloat16)[None]
    return (layer_out, grad_tokens, grad_w_in, grad_w_out)


def solution(mesh):
    placed = (
        P("row", "col"),
        P("row", "col"),
        P("col", "row", None, None),
        P("col", None),
        P("col", "row", None, None),
        P("col", None),
    )
    return jax.shard_map(
        per_device,
        mesh=mesh,
        in_specs=placed,
        out_specs=(
            P("row", "col"),
            P("row", "col"),
            P("col", "row", None, None),
            P("col", "row", None, None),
        ),
        check_vma=False,
    )
```

profile of v0, /device:TPU:0, one launch (start us, length us, event | category | flops | bytes accessed | tf_op | source)
XLA Modules:
  0.0 756.5 jit_solution(16098698966518231134)
XLA Ops:
  12.0 24.7 %all-gather.5.cloned.1.call-done = bf16[128,4096]{0,1:T(8,128)(2,1)} async-done(((bf16[128,512]{0,1:T(8,128)(2,1)}), bf16[128,4096]{0,1:T(8,128)(2,1)}) %all-gather.5.cloned.1.call-update) | async-done | bytes 1048592 | tf_op jit(solution)/shard_map/all_gather | solution.py:41
  45.7 5.0 all-to-all-start
  50.7 12.0 %all-gather.11.cloned.1.call-done = bf16[128,4096]{0,1:T(8,128)(2,1)} async-done(((bf16[128,512]{0,1:T(8,128)(2,1)}), bf16[128,4096]{0,1:T(8,128)(2,1)}) %all-gather.11.cloned.1.call-update) | async-done | bytes 1048592 | tf_op jit(solution)/shard_map/all_gather | solution.py:42
  71.7 173.1 %all-to-all-done = bf16[64,128,256]{2,1,0:T(8,128)(2,1)} async-done(((bf16[64,128,256]{2,1,0:T(8,128)(2,1)}), bf16[64,128,256]{2,1,0:T(8,128)(2,1)}, u32[]{:S(2)}, u32[]{:S(2)}) %all-to-all-start) | async-done | bytes 4194336 | tf_op jit(solution)/shard_map/all_to_all | solution.py:93
  244.9 5.4 all-to-all-start.3
  255.9 90.1 %all-gather.7.cloned.1.call-done = bf16[1,64,256,256]{3,2,0,1:T(8,128)(2,1)} async-done(((bf16[1,16,256,256]{3,2,0,1:T(8,128)(2,1)}), bf16[1,64,256,256]{3,2,0,1:T(8,128)(2,1)}) %all-gather.7.cloned.1.call-update) | async-done | bytes 8388624 | tf_op jit(solution)/shard_map/all_gather | solution.py:52
  346.0 6.0 fusion.28
  352.0 7.5 fusion.14
  359.5 145.5 %all-gather.9.cloned.1.call-done = bf16[1,64,256,256]{3,2,0,1:T(8,128)(2,1)} async-done(((bf16[1,16,256,256]{3,2,0,1:T(8,128)(2,1)}), bf16[1,64,256,256]{3,2,0,1:T(8,128)(2,1)}) %all-gather.9.cloned.1.call-update) | async-done | bytes 8388624 | tf_op jit(solution)/shard_map/all_gather | solution.py:64
  505.0 7.5 fusion.43
  512.5 8.9 %fusion.60 = (bf16[128,8,256]{2,1,0:T(8,128)(2,1)}, bf16[128,8,256]{2,1,0:T(8,128)(2,1)}, f32[8,128,256]{2,0,1:T(8,128)S(1)}) fusion(f32[8,128,256]{2,0,1:T(8,128)S(1)} %fusion.14, f32[128,64,256]{2,0,1:T(8,128)S(1)} %fusion.43, s32[64]{0:T(128)S(1)} %get-tuple-element.25, pred[64]{0:T(512)(128)(4,1)S(1)} %get-tuple-element.21), kind=kOutput, calls=%fused_computation.55 | convolution fusion | flops 204211200 | bytes 11534656 | tf_op jit(solution)/shard_map/tkf,kj->tjf/dot_general | solution.py:84
  529.5 4.9 all-to-all-start.1
  541.9 86.1 %all-to-all-done.1 = bf16[64,128,256]{2,1,0:T(8,128)(2,1)} async-done(((bf16[64,128,256]{2,1,0:T(8,128)(2,1)}), bf16[64,128,256]{2,1,0:T(8,128)(2,1)}, u32[]{:S(2)}, u32[]{:S(2)}) %all-to-all-start.1) | async-done | bytes 4194336 | tf_op jit(solution)/shard_map/all_to_all | solution.py:94
  628.1 4.9 all-to-all-start.2
  636.2 7.5 fusion.33
  643.7 7.5 fusion.57
  655.9 6.1 fusion.38
  662.1 7.5 fusion.54
  671.1 7.8 %copy.51 = bf16[16,4,128,256]{2,1,3,0:T(4,128)(2,1)} copy(bf16[16,4,128,256]{3,2,0,1:T(8,128)(2,1)} %bitcast.33) | data formatting | bytes 8388608 | tf_op jit(solution)/shard_map/all_to_all | solution.py:93
  678.9 7.2 all_to_all.55
  695.6 30.2 %all-to-all-done.2 = bf16[64,128,256]{2,1,0:T(8,128)(2,1)} async-done(((bf16[64,128,256]{2,1,0:T(8,128)(2,1)}), bf16[64,128,256]{2,1,0:T(8,128)(2,1)}, u32[]{:S(2)}, u32[]{:S(2)}) %all-to-all-start.2) | async-done | bytes 4194336 | tf_op jit(solution)/shard_map/all_to_all | solution.py:95
  725.8 7.4 copy.55
  733.2 7.2 all_to_all.63
  740.4 6.2 fusion.52
  (66 shorter events, 65.3 us)
Async XLA Ops:
  7.2 4.8 copy-start.4
  7.2 29.5 %all-gather.5.cloned.1.call-start = ((), (), s32[]{:S(2)}) async-start(), calls=%async_computation.6 | async-start | bytes 1179648 | tf_op jit(solution)/shard_map/all_gather | solution.py:41
  8.9 53.8 %all-gather.11.cloned.1.call-start = ((), (), s32[]{:S(2)}) async-start(), calls=%async_computation.10 | async-start | bytes 1179648 | tf_op jit(solution)/shard_map/all_gather | solution.py:42
  10.6 335.4 %all-gather.7.cloned.1.call-start = ((), (), s32[]{:S(2)}) async-start(), calls=%async_computation.7 | async-start | bytes 10485760 | tf_op jit(solution)/shard_map/all_gather | solution.py:52
  11.4 493.6 %all-gather.9.cloned.1.call-start = ((), (), s32[]{:S(2)}) async-start(), calls=%async_computation.8 | async-start | bytes 10485760 | tf_op jit(solution)/shard_map/all_gather | solution.py:64
  45.7 5.0 copy-start.5
  45.7 199.2 %all-to-all-start = ((bf16[64,128,256]{2,1,0:T(8,128)(2,1)}), bf16[64,128,256]{2,1,0:T(8,128)(2,1)}, u32[]{:S(2)}, u32[]{:S(2)}) async-start(bf16[64,128,256]{2,1,0:T(8,128)(2,1)} %broadcast_select_fusion.3), calls=%async_computation.2 | async-start | bytes 8388608 | tf_op jit(solution)/shard_map/all_to_all | solution.py:93
  244.9 284.6 %all-to-all-start.3 = ((bf16[64,128,256]{2,1,0:T(8,128)(2,1)}), bf16[64,128,256]{2,1,0:T(8,128)(2,1)}, u32[]{:S(2)}, u32[]{:S(2)}) async-start(bf16[64,128,256]{2,1,0:T(8,128)(2,1)} %broadcast_select_fusion.1), calls=%async_computation.5 | async-start | bytes 8388608 | tf_op jit(solution)/shard_map/all_to_all | solution.py:96
  529.5 98.6 %all-to-all-start.1 = ((bf16[64,128,256]{2,1,0:T(8,128)(2,1)}), bf16[64,128,256]{2,1,0:T(8,128)(2,1)}, u32[]{:S(2)}, u32[]{:S(2)}) async-start(bf16[64,128,256]{2,1,0:T(8,128)(2,1)} %broadcast_select_fusion), calls=%async_computation.3 | async-start | bytes 8388608 | tf_op jit(solution)/shard_map/all_to_all | solution.py:94
  541.9 91.3 %copy-start.3 = (bf16[128,8,256]{2,1,0:T(8,128)(2,1)S(1)}, bf16[128,8,256]{2,1,0:T(8,128)(2,1)}, u32[]{:S(2)}) copy-start(bf16[128,8,256]{2,1,0:T(8,128)(2,1)} %get-tuple-element.18) | copy-start | bytes 1572868
  628.1 97.7 %all-to-all-start.2 = ((bf16[64,128,256]{2,1,0:T(8,128)(2,1)}), bf16[64,128,256]{2,1,0:T(8,128)(2,1)}, u32[]{:S(2)}, u32[]{:S(2)}) async-start(bf16[64,128,256]{2,1,0:T(8,128)(2,1)} %broadcast_select_fusion.2), calls=%async_computation.4 | async-start | bytes 8388608 | tf_op jit(solution)/shard_map/all_to_all | solution.py:95
  632.9 116.3 %reduce-scatter.5.cloned.1.call-start = ((), (), s32[]{:S(2)}) async-start(), calls=%async_computation.11 | async-start | bytes 1179648 | tf_op jit(solution)/shard_map/reduce_scatter | solution.py:109
  643.7 9.3 %copy-start.2 = (bf16[128,8,256]{2,1,0:T(8,128)(2,1)S(1)}, bf16[128,8,256]{2,1,0:T(8,128)(2,1)}, u32[]{:S(2)}) copy-start(bf16[128,8,256]{2,1,0:T(8,128)(2,1)} %get-tuple-element.19) | copy-start | bytes 1572868
  652.7 96.5 %reduce-scatter.3.cloned.1.call-start = ((), (), s32[]{:S(2)}) async-start(), calls=%async_computation.9 | async-start | bytes 1179648 | tf_op jit(solution)/shard_map/reduce_scatter | solution.py:70
  740.4 6.2 copy-start
  740.4 6.2 copy-start.1
Sparse Core Ops, SparseCore 0:
  10.5 26.1 all-gather.4
  39.2 23.4 all-gather.10
  64.3 281.7 all-gather.6
  347.4 157.5 all-gather.8
  652.8 36.4 reduce-scatter.4
  692.9 35.9 reduce-scatter.2
where the time goes:
time: 760 us; the launch traced here: 757 us
  waiting for transfers between devices  563 us (74%)
  local copies, waits for them, and re-layouts  71.3 us (9%)
  matrix products  67.4 us (9%)
  starting transfers between devices  20.9 us (3%)
  other arithmetic  19.1 us (3%)
  between operations  14.9 us (2%)
    all_to_all x1, waiting for transfers between devices, per_device(): lax.all_to_all(token_sends, 'row', split_axis=0, concat_axis=1, tiled=True)  173 us
    all_gather x1, waiting for transfers between devices, per_device(): lax.all_gather(w_out, 'row', axis=1, tiled=True)[0]  146 us
    all_gather x1, waiting for transfers between devices, per_device(): lax.all_gather(w_in, 'row', axis=1, tiled=True)[0]  90.1 us
    all_to_all x1, waiting for transfers between devices, per_device(): lax.all_to_all(grad_sends, 'row', split_axis=0, concat_axis=1, tiled=True)  86.1 us
    all_to_all x1, waiting for transfers between devices, per_device(): lax.all_to_all(activ_sends, 'row', split_axis=0, concat_axis=1, tiled=True)  30.2 us
    all_gather x1, waiting for transfers between devices, per_device(): lax.all_gather(tokens, 'col', axis=1, tiled=True)  24.7 us
  transfers between devices with their start and end apart: 10, of which 7 were waited for; matrix products, arithmetic and copies ran while one was open for 19% of the time, Pallas kernels for 0%

commit v1 on v0

v1 whole, which is shorter than its diff:
```python
import functools

import jax
import jax.numpy as jnp
from jax import lax
from jax.experimental import pallas as pl
from jax.experimental.pallas import tpu as pltpu
from jax.sharding import PartitionSpec as P

D = 4096
FF = 16384
VMEM = 56 * 1024 * 1024


def params():
    return pltpu.CompilerParams(
        dimension_semantics=("arbitrary",), vmem_limit_bytes=VMEM
    )


def matmul(a, b, a_dim, b_dim):
    return lax.dot_general(
        a, b, (((a_dim,), (b_dim,)), ((), ())), preferred_element_type=jnp.float32
    )


def rows_of(ref, at):
    block = ref[:, at]
    return block.reshape(block.shape[0] * block.shape[1], block.shape[2])


def place(code, cols, forward):
    wide, hidden = code // cols, code % cols
    return (wide, hidden) if forward else (hidden, wide)


def to_hidden_kernel(cols, flip, codes, x_ref, w_ref, o_ref, acc):
    group, _, rows, tile = x_ref.shape
    acc[...] = jnp.zeros_like(acc)

    def slot(s, carry):
        code = codes[s]

        @pl.when(code >= 0)
        def _():
            source, target = place(code, cols, True)
            acc[target] += matmul(rows_of(x_ref, source), w_ref[s], 1, 1 if flip else 0)

        return carry

    lax.fori_loop(0, w_ref.shape[0], slot, 0)
    for part in range(group):
        o_ref[part] = acc[:, part * rows:(part + 1) * rows].astype(o_ref.dtype)


def to_hidden(x, w, codes, cols, flip):
    blocks, wide, rows, tile = x.shape
    group = min(blocks, 4)
    slots = w.shape[0]
    return pl.pallas_call(
        functools.partial(to_hidden_kernel, cols, flip),
        grid_spec=pltpu.PrefetchScalarGridSpec(
            num_scalar_prefetch=1,
            grid=(blocks // group,),
            in_specs=[
                pl.BlockSpec((group, wide, rows, tile), lambda b, codes: (b, 0, 0, 0)),
                pl.BlockSpec((slots, tile, tile), lambda b, codes: (0, 0, 0)),
            ],
            out_specs=pl.BlockSpec((group, cols, rows, tile), lambda b, codes: (b, 0, 0, 0)),
            scratch_shapes=[pltpu.VMEM((cols, group * rows, tile), jnp.float32)],
        ),
        out_shape=jax.ShapeDtypeStruct((blocks, cols, rows, tile), jnp.bfloat16),
        compiler_params=params(),
    )(codes, x, w)


def from_hidden_kernel(cols, flip, codes, h_ref, x_ref, w_ref, o_ref, g_ref, acc, grad):
    group, _, rows, tile = x_ref.shape
    acc[...] = jnp.zeros_like(acc)

    @pl.when(pl.program_id(0) == 0)
    def _():
        grad[...] = jnp.zeros_like(grad)

    def slot(s, carry):
        code = codes[s]

        @pl.when(code >= 0)
        def _():
            source, target = place(code, cols, False)
            h, x = rows_of(h_ref, source), rows_of(x_ref, target)
            acc[target] += matmul(h, w_ref[s], 1, 1 if flip else 0)
            grad[s] += matmul(x, h, 0, 0) if flip else matmul(h, x, 0, 0)

        return carry

    lax.fori_loop(0, w_ref.shape[0], slot, 0)
    for part in range(group):
        o_ref[part] = acc[:, part * rows:(part + 1) * rows].astype(o_ref.dtype)

    @pl.when(pl.program_id(0) == pl.num_programs(0) - 1)
    def _():
        g_ref[...] = grad[...].astype(g_ref.dtype)


def from_hidden(h, x, w, codes, flip, held):
    blocks, cols, rows, tile = h.shape
    wide = x.shape[1]
    group = min(blocks, 4)
    slots = w.shape[0]
    return pl.pallas_call(
        functools.partial(from_hidden_kernel, cols, flip),
        grid_spec=pltpu.PrefetchScalarGridSpec(
            num_scalar_prefetch=1,
            grid=(blocks // group,),
            in_specs=[
                pl.BlockSpec((group, cols, rows, tile), lambda b, codes: (b, 0, 0, 0)),
                pl.BlockSpec((group, wide, rows, tile), lambda b, codes: (b, 0, 0, 0)),
                pl.BlockSpec((slots, tile, tile), lambda b, codes: (0, 0, 0)),
            ],
            out_specs=[
                pl.BlockSpec((group, wide, rows, tile), lambda b, codes: (b, 0, 0, 0)),
                pl.BlockSpec((slots, tile, tile), lambda b, codes: (0, 0, 0)),
            ],
            scratch_shapes=[
                pltpu.VMEM((wide, group * rows, tile), jnp.float32),
                pltpu.VMEM((slots, tile, tile), jnp.float32),
            ],
        ),
        out_shape=[
            jax.ShapeDtypeStruct((blocks, wide, rows, tile), jnp.bfloat16),
            jax.ShapeDtypeStruct((slots, tile, tile), held),
        ],
        compiler_params=params(),
    )(codes, h, x, w)


def to_pieces(x, tile):
    rows, width = x.shape
    unit = min(width, tile)
    return jnp.swapaxes(x.reshape(rows, width // unit, unit), 0, 1)


def join_pieces(x, tile):
    blocks, devices, pieces, rows, unit = x.shape
    parts = tile // unit
    x = x.reshape(blocks, devices * pieces // parts, parts, rows, unit)
    return jnp.swapaxes(x, 2, 3).reshape(blocks, -1, rows, tile)


def cut_pieces(x, devices):
    blocks, tiles, rows, tile = x.shape
    unit = min(tile, tiles * tile // devices)
    x = jnp.swapaxes(x.reshape(blocks, tiles, rows, tile // unit, unit), 2, 3)
    x = x.reshape(blocks, devices, -1, rows, unit)
    return jnp.swapaxes(x, 0, 1)


def finish(hidden_side, x, w, codes, flip, devices):
    blocks = x.shape[0]
    group = min(blocks, 4)
    held = jnp.bfloat16 if group == blocks else jnp.float32
    sums, grad = [], None
    for at in range(0, blocks, group):
        h, wide = hidden_side[at:at + group], x[at:at + group]
        if sums:
            h, wide, _ = lax.optimization_barrier((h, wide, sums[-1]))
        part, slots_grad = from_hidden(h, wide, w, codes, flip, held)
        grad = slots_grad if grad is None else grad + slots_grad
        sums.append(lax.psum_scatter(cut_pieces(part, devices), "col", scatter_dimension=0))
    own = lax.psum_scatter(jnp.concatenate(sums), "row", scatter_dimension=0)
    return jnp.swapaxes(own, 0, 1).reshape(own.shape[1], -1), grad.astype(jnp.bfloat16)


def per_device(tokens, upstream, w_in, in_codes, w_out, out_codes):
    tile = w_in.shape[3]
    slots = w_in.shape[1]
    devices = lax.axis_size("col")
    blocks = lax.axis_size("row")
    cols = FF // (tile * devices)
    first = lax.axis_index("row") * slots
    codes_in = lax.dynamic_slice_in_dim(in_codes[0], first, slots)
    codes_out = lax.dynamic_slice_in_dim(out_codes[0], first, slots)

    def everywhere(x):
        pieces = lax.all_gather(to_pieces(x, tile), ("row", "col"))
        return join_pieces(pieces.reshape(blocks, devices, *pieces.shape[1:]), tile)

    all_tokens = everywhere(tokens)
    hidden = to_hidden(all_tokens, w_in[0], codes_in, cols, False)
    if blocks > 4:
        upstream, hidden = lax.optimization_barrier((upstream, hidden))
    all_up = everywhere(upstream)
    hidden = lax.psum_scatter(hidden, "row", scatter_dimension=0).astype(jnp.float32)
    grad_activ = to_hidden(all_up, w_out[0], codes_out, cols, True)
    grad_activ = lax.psum_scatter(grad_activ, "row", scatter_dimension=0).astype(jnp.float32)
    sigmoid = jax.nn.sigmoid(hidden)
    activ = (hidden * sigmoid).astype(jnp.bfloat16)
    grad_hidden = grad_activ * sigmoid * (1.0 + hidden * (1.0 - sigmoid))
    grad_hidden = grad_hidden.astype(jnp.bfloat16)
    all_activ = lax.all_gather(activ, "row")
    all_grad = lax.all_gather(grad_hidden, "row")
    layer_out, grad_w_out = finish(all_activ, all_up, w_out[0], codes_out, False, devices)
    if blocks > 4:
        all_grad, layer_out = lax.optimization_barrier((all_grad, layer_out))
    grad_tokens, grad_w_in = finish(all_grad, all_tokens, w_in[0], codes_in, True, devices)
    return layer_out, grad_tokens, grad_w_in[None], grad_w_out[None]


def solution(mesh):
    placed = (
        P("row", "col"),
        P("row", "col"),
        P("col", "row", None, None),
        P("col", None),
        P("col", "row", None, None),
        P("col", None),
    )
    return jax.shard_map(
        per_device,
        mesh=mesh,
        in_specs=placed,
        out_specs=(
            P("row", "col"),
            P("row", "col"),
            P("col", "row", None, None),
            P("col", "row", None, None),
        ),
        check_vma=False,
    )
```

time: 760 us -> 521 us (0.69)
  waiting for transfers between devices: 563 us -> 454 us
  matrix products: 67.4 us -> 0 us
  local copies, waits for them, and re-layouts: 71.3 us -> 13.2 us
  Pallas kernels: 0 us -> 36.7 us
  starting transfers between devices: 20.9 us -> 0.37 us
  other arithmetic: 19.1 us -> 2.66 us
    all_to_all x4 -> x0, waiting for transfers between devices: 289 us -> none  [the longest x1 173 us: per_device(): lax.all_to_all(token_sends, 'row', split_axis=0, concat_axis=1, tiled=True)]
    unnamed x6 -> x10, waiting for transfers between devices: 1.27 us -> 128 us
    reduce_scatter x2 -> x4, waiting for transfers between devices: 0.01 us -> 126 us  [the longest x1 46 us: per_device(): lax.psum_scatter(grad_activ, 'row', scatter_dimension=0).astype(jnp.float32)]
    all_gather x4, waiting for transfers between devices: 272 us -> 200 us  [the longest x2 120 us: everywhere(): pieces = lax.all_gather(to_pieces(x, tile), ('row', 'col'))]
    dot_general x10 -> x0, matrix products: 67.4 us -> none  [the longest x2 15.1 us: per_device(): jnp.einsum('tkd,ki->tid', partial_sum, selector(rows_at, filled_at, tile_...]
    all_to_all x6 -> x0, local copies, waits for them, and re-layouts: 39.1 us -> none  [the longest x2 15 us: per_device(): lax.all_to_all(token_sends, 'row', split_axis=0, concat_axis=1, tiled=True)]
    pallas_call x0 -> x4, Pallas kernels: none -> 36.7 us  [the longest x2 21.7 us: from_hidden(): pl.pallas_call(functools.partial(from_hidden_kernel, cols, flip), grid_sp...]
    gather x8 -> x0, local copies, waits for them, and re-layouts: 22.6 us -> none  [the longest x1 2.88 us: per_device(): upstream_sends = jnp.take(jnp.swapaxes(up_tiles, 0, 1), out_row, axis=0)]
  transfers between devices with their start and end apart: 10 -> 9, of which waited for: 7 -> 9; matrix products, arithmetic and copies ran while one was open for 19% -> 1% of each run, Pallas kernels for 0% -> 5%
where the time goes in v1:
time: 521 us
  waiting for transfers between devices  454 us (87%)
  Pallas kernels  36.7 us (7%)
  between operations  13.9 us (3%)
  local copies, waits for them, and re-layouts  13.2 us (3%)
    unnamed x10, waiting for transfers between devices  128 us
    all_gather x2, waiting for transfers between devices, everywhere(): pieces = lax.all_gather(to_pieces(x, tile), ('row', 'col'))  120 us
    reduce_scatter x1, waiting for transfers between devices, per_device(): lax.psum_scatter(grad_activ, 'row', scatter_dimension=0).astype(jnp.float32)  46 us
    all_gather x1, waiting for transfers between devices, per_device(): all_grad = lax.all_gather(grad_hidden, 'row')  44.8 us
    reduce_scatter x2, waiting for transfers between devices, finish(): own = lax.psum_scatter(jnp.concatenate(sums), 'row', scatter_dimension=0)  41.6 us
    reduce_scatter x1, waiting for transfers between devices, per_device(): lax.psum_scatter(hidden, 'row', scatter_dimension=0).astype(jnp.float32)  38.2 us
    all_gather x1, waiting for transfers between devices, per_device(): all_activ = lax.all_gather(activ, 'row')  35.1 us
    pallas_call x2, Pallas kernels, from_hidden(): pl.pallas_call(functools.partial(from_hidden_kernel, cols, flip), grid_sp...  21.7 us
  transfers between devices with their start and end apart: 9, of which 9 were waited for; matrix products, arithmetic and copies ran while one was open for 1% of the time, Pallas kernels for 5%

profile of v1, /device:TPU:0, one launch (start us, length us, event | category | flops | bytes accessed | tf_op | source)
XLA Modules:
  0.0 520.6 jit_solution(161938600495033104)
XLA Ops:
  7.2 1.0 copy.14
  8.3 0.8 copy.15
  9.1 1.0 copy.16
  10.1 0.8 copy.17
  11.0 0.6 dynamic-slice_bitcast_fusion.codes
  11.6 64.6 %all-gather.11.cloned.1.call-done = bf16[64,128,256]{2,1,0:T(8,128)(2,1)} async-done(((bf16[2,128,256]{2,1,0:T(8,128)(2,1)}), bf16[64,128,256]{2,1,0:T(8,128)(2,1)}) %all-gather.11.cloned.1.call-update) | async-done | bytes 4194320 | tf_op jit(solution)/shard_map/all_gather | solution.py:186
  76.2 7.9 %shard_map.93 = bf16[4,8,128,256]{3,2,1,0:T(8,128)(2,1)} custom-call(s32[16]{0:T(128)} %dynamic-slice_bitcast_fusion.codes, bf16[4,16,128,256]{3,2,1,0:T(8,128)(2,1)} %bitcast.47, bf16[16,256,256]{2,1,0:T(8,128)(2,1)} %bitcast.51), custom_call_target="tpu_custom_call" | custom-call | tf_op jit(solution)/shard_map/pallas_call | solution.py:60
  84.8 55.5 %all-gather.13.cloned.1.call-done = bf16[64,128,256]{2,1,0:T(8,128)(2,1)} async-done(((bf16[2,128,256]{2,1,0:T(8,128)(2,1)}), bf16[64,128,256]{2,1,0:T(8,128)(2,1)}) %all-gather.13.cloned.1.call-update) | async-done | bytes 4194320 | tf_op jit(solution)/shard_map/all_gather | solution.py:186
  140.3 7.1 %shard_map.95 = bf16[4,8,128,256]{3,2,1,0:T(8,128)(2,1)} custom-call(s32[16]{0:T(128)} %dynamic-slice_bitcast_fusion.1.codes, bf16[4,16,128,256]{3,2,1,0:T(8,128)(2,1)} %bitcast.49, bf16[16,256,256]{2,1,0:T(8,128)(2,1)} %bitcast.53), custom_call_target="tpu_custom_call" | custom-call | tf_op jit(solution)/shard_map/pallas_call | solution.py:60
  147.4 38.2 %reduce-scatter.11.cloned.1.call-done = bf16[1,8,128,256]{3,2,1,0:T(8,128)(2,1)} async-done(((bf16[4,8,128,256]{3,2,1,0:T(8,128)(2,1)}), bf16[1,8,128,256]{3,2,1,0:T(8,128)(2,1)}) %reduce-scatter.11.cloned.1.call-update) | async-done | bytes 524304 | tf_op jit(solution)/shard_map/reduce_scatter | solution.py:194
  185.6 46.0 %reduce-scatter.15.cloned.1.call-done = bf16[1,8,128,256]{3,2,1,0:T(8,128)(2,1)} async-done(((bf16[4,8,128,256]{3,2,1,0:T(8,128)(2,1)}), bf16[1,8,128,256]{3,2,1,0:T(8,128)(2,1)}) %reduce-scatter.15.cloned.1.call-update) | async-done | bytes 524304 | tf_op jit(solution)/shard_map/reduce_scatter | solution.py:196
  231.6 2.7 fusion.6
  235.0 44.8 %all-gather.9.cloned.1.call-done.h_ref = bf16[4,8,128,256]{3,2,1,0:T(8,128)(2,1)} async-done(((bf16[1,8,128,256]{3,2,1,0:T(8,128)(2,1)}), bf16[4,8,128,256]{3,2,1,0:T(8,128)(2,1)}) %all-gather.9.cloned.1.call-update) | async-done | bytes 2097168 | tf_op jit(solution)/shard_map/all_gather | solution.py:202
  279.8 11.6 %shard_map.96 = (bf16[4,16,128,256]{3,2,1,0:T(8,128)(2,1)}, bf16[16,256,256]{2,1,0:T(8,128)(2,1)}) custom-call(s32[16]{0:T(128)} %dynamic-slice_bitcast_fusion.codes, bf16[4,8,128,256]{3,2,1,0:T(8,128)(2,1)} %all-gather.9.cloned.1.call-done.h_ref, bf16[4,16,128,256]{3,2,1,0:T(8,128)(2,1)} %bitcast.48, bf16[16,256,256]{2,1,0:T(8,128)(2,1)} %bitcast.52), custom_call_target="tpu_custom_call" | custom-call | tf_op jit(solution)/shard_map/pallas_call | solution.py:111
  291.4 35.1 %all-gather.7.cloned.1.call-done.h_ref = bf16[4,8,128,256]{3,2,1,0:T(8,128)(2,1)} async-done(((bf16[1,8,128,256]{3,2,1,0:T(8,128)(2,1)}), bf16[4,8,128,256]{3,2,1,0:T(8,128)(2,1)}) %all-gather.7.cloned.1.call-update) | async-done | bytes 2097168 | tf_op jit(solution)/shard_map/all_gather | solution.py:201
  326.4 10.1 %shard_map.94 = (bf16[4,16,128,256]{3,2,1,0:T(8,128)(2,1)}, bf16[16,256,256]{2,1,0:T(8,128)(2,1)}) custom-call(s32[16]{0:T(128)} %dynamic-slice_bitcast_fusion.1.codes, bf16[4,8,128,256]{3,2,1,0:T(8,128)(2,1)} %all-gather.7.cloned.1.call-done.h_ref, bf16[4,16,128,256]{3,2,1,0:T(8,128)(2,1)} %bitcast.50, bf16[16,256,256]{2,1,0:T(8,128)(2,1)} %bitcast.54), custom_call_target="tpu_custom_call" | custom-call | tf_op jit(solution)/shard_map/pallas_call | solution.py:111
  337.8 127.3 %all-reduce.5.cloned.1.call-done = (bf16[8,4,2,128,256]{4,3,2,0,1:T(8,128)(2,1)}, bf16[8,4,2,128,256]{4,3,2,0,1:T(8,128)(2,1)}) async-done(((bf16[8,4,2,128,256]{4,3,2,0,1:T(8,128)(2,1)}, bf16[8,4,2,128,256]{4,3,2,0,1:T(8,128)(2,1)}), (bf16[8,4,2,128,256]{4,3,2,0,1:T(8,128)(2,1)}, bf16[8,4,2,128,256]{4,3,2,0,1:T(8,128)(2,1)})) %all-reduce.5.cloned.1.call-update) | async-done | bytes 8388624
  465.1 1.9 constant_dynamic-slice_fusion
  467.0 1.0 copy.18
  468.1 1.0 copy.19
  469.1 20.9 %reduce-scatter.13.cloned.1.call-done = bf16[1,2,128,256]{2,3,1,0:T(8,128)(2,1)} async-done(((bf16[4,2,128,256]{2,3,1,0:T(8,128)(2,1)}), bf16[1,2,128,256]{2,3,1,0:T(8,128)(2,1)}) %reduce-scatter.13.cloned.1.call-update) | async-done | bytes 131088 | tf_op jit(solution)/shard_map/reduce_scatter | solution.py:171
  490.0 1.7 copy.20
  491.7 20.7 %reduce-scatter.17.cloned.1.call-done = bf16[1,2,128,256]{2,3,1,0:T(8,128)(2,1)} async-done(((bf16[4,2,128,256]{2,3,1,0:T(8,128)(2,1)}), bf16[1,2,128,256]{2,3,1,0:T(8,128)(2,1)}) %reduce-scatter.17.cloned.1.call-update) | async-done | bytes 131088 | tf_op jit(solution)/shard_map/reduce_scatter | solution.py:171
  512.4 1.7 copy.21
  (26 shorter events, 2.8 us)
Async XLA Ops:
  7.2 3.8 copy-start
  7.2 69.0 %all-gather.11.cloned.1.call-start = ((), (), s32[]{:S(2)}) async-start(), calls=%async_computation.10 | async-start | bytes 4325376 | tf_op jit(solution)/shard_map/all_gather | solution.py:186
  9.1 131.2 %all-gather.13.cloned.1.call-start = ((), (), s32[]{:S(2)}) async-start(), calls=%async_computation.11 | async-start | bytes 4325376 | tf_op jit(solution)/shard_map/all_gather | solution.py:186
  10.9 174.7 %reduce-scatter.11.cloned.1.call-start = ((), (), s32[]{:S(2)}) async-start(), calls=%async_computation.4 | async-start | bytes 2621440 | tf_op jit(solution)/shard_map/reduce_scatter | solution.py:194
  76.2 7.9 %copy-start.1 = (s32[1,64]{1,0:T(1,128)S(1)}, s32[1,64]{1,0:T(1,128)}, u32[]{:S(2)}) copy-start(s32[1,64]{1,0:T(1,128)} %param.11) | copy-start | bytes 772
  84.1 147.5 %reduce-scatter.15.cloned.1.call-start = ((), (), s32[]{:S(2)}) async-start(), calls=%async_computation.7 | async-start | bytes 2621440 | tf_op jit(solution)/shard_map/reduce_scatter | solution.py:196
  147.4 132.4 %all-gather.9.cloned.1.call-start = ((), (), s32[]{:S(2)}) async-start(), calls=%async_computation.8 | async-start | bytes 2621440 | tf_op jit(solution)/shard_map/all_gather | solution.py:202
  234.3 92.1 %all-gather.7.cloned.1.call-start = ((), (), s32[]{:S(2)}) async-start(), calls=%async_computation.5 | async-start | bytes 2621440 | tf_op jit(solution)/shard_map/all_gather | solution.py:201
  234.9 230.2 %all-reduce.5.cloned.1.call-start = ((), (), s32[]{:S(2)}) async-start(), calls=%async_computation.12 | async-start | bytes 16777216
  336.5 0.7 copy-start.2
  336.6 153.4 %reduce-scatter.13.cloned.1.call-start = ((), (), s32[]{:S(2)}) async-start(), calls=%async_computation.6 | async-start | bytes 655360 | tf_op jit(solution)/shard_map/reduce_scatter | solution.py:171
  468.0 44.4 %reduce-scatter.17.cloned.1.call-start = ((), (), s32[]{:S(2)}) async-start(), calls=%async_computation.9 | async-start | bytes 655360 | tf_op jit(solution)/shard_map/reduce_scatter | solution.py:171
Sparse Core Ops, SparseCore 0:
  11.4 64.7 all-gather.10
  79.6 60.5 all-gather.12
  143.1 42.4 reduce-scatter.10
  188.4 43.1 reduce-scatter.14
  234.4 45.2 all-gather.8
  281.8 44.6 all-gather.6
  336.7 128.3 all-reduce.4
  468.2 21.8 reduce-scatter.12
  492.4 19.9 reduce-scatter.16

commit v2 on v1

v2 whole, which is shorter than its diff:
```python
import functools

import jax
import jax.numpy as jnp
from jax import lax
from jax.experimental import pallas as pl
from jax.experimental.pallas import tpu as pltpu
from jax.sharding import PartitionSpec as P

D = 4096
FF = 16384
VMEM = 56 * 1024 * 1024
GROUP = 4
ANY = pl.BlockSpec(memory_space=pl.ANY)


def matmul(a, b, a_dim, b_dim):
    return lax.dot_general(
        a, b, (((a_dim,), (b_dim,)), ((), ())), preferred_element_type=jnp.float32
    )


def flat(block):
    return block.reshape(block.shape[0] * block.shape[1], block.shape[2])


def chunks(blocks):
    group = min(blocks, GROUP)
    return [slice(at, at + group) for at in range(0, blocks, group)]


def wide_copies(refs, held, sems, col):
    tile = held.shape[3]
    if len(refs[0].shape) == 5:
        refs = [refs[0].at[m] for m in range(refs[0].shape[0])]
    pieces, unit = refs[0].shape[1], refs[0].shape[3]
    copies = []
    for m, ref in enumerate(refs):
        owner = lax.bitwise_xor(col, m)
        for q in range(pieces):
            if unit == tile:
                target = held.at[owner * pieces + q]
            else:
                parts = tile // unit
                lane = pl.multiple_of(lax.rem(owner, parts) * unit, unit)
                target = held.at[lax.div(owner, parts), :, :, pl.ds(lane, unit)]
            copies.append(pltpu.make_async_copy(ref.at[:, q], target, sems.at[len(copies)]))
    for copy in copies:
        copy.start()
    return copies


def hidden_copies(refs, held, sems, row, at, blocks):
    copies = []
    for g in range(held.shape[1]):
        j = at + g
        target, sem = held.at[:, g], sems.at[g]
        if j == 0:
            copy = pltpu.make_async_copy(refs[0], target, sem)
            copy.start()
        else:
            copy = pltpu.make_async_copy(refs[blocks - 1 + j], target, sem)
            other = pltpu.make_async_copy(refs[blocks - j], target, sem)

            @pl.when(row + j < blocks)
            def _():
                copy.start()

            @pl.when(row + j >= blocks)
            def _():
                other.start()

        copies.append(copy)
    return copies


def over_slots(info, slots, cols, body):
    def slot(s, carry):
        code = info[2 + s]

        @pl.when(code >= 0)
        def _():
            body(s, lax.div(code, cols), lax.rem(code, cols))

        return carry

    lax.fori_loop(0, slots, slot, 0)


def to_hidden_kernel(cols, flip, wides, info, w_ref, *refs):
    x_refs, refs = refs[:wides], refs[wides:]
    *outs, x, acc, sems = refs
    copies = wide_copies(x_refs, x, sems, info[1])
    acc[...] = jnp.zeros_like(acc)
    for copy in copies:
        copy.wait()

    def add(s, wide, hidden):
        for chunk in chunks(x.shape[1]):
            product = matmul(flat(x[wide, chunk]), w_ref[s], 1, 1 if flip else 0)
            acc[hidden, chunk] += product.reshape(-1, *acc.shape[2:])

    over_slots(info, w_ref.shape[0], cols, add)
    for part, out in enumerate(outs):
        out[...] = acc[:, part].astype(out.dtype)


def from_hidden_kernel(cols, flip, at, blocks, info, w_ref, *refs):
    h_refs, refs = refs[:2 * blocks - 1], refs[2 * blocks - 1:]
    *outs, h, acc, sems = refs
    if len(outs[0].shape) == 5:
        outs = [outs[0].at[m] for m in range(outs[0].shape[0])]
    copies = hidden_copies(h_refs, h, sems, info[0], at, blocks)
    acc[...] = jnp.zeros_like(acc)
    for copy in copies:
        copy.wait()

    def add(s, wide, hidden):
        acc[wide] += matmul(flat(h[hidden]), w_ref[s], 1, 1 if flip else 0)

    over_slots(info, w_ref.shape[0], cols, add)
    tile = w_ref.shape[2]
    group, pieces, rows, unit = outs[0].shape
    for m, out in enumerate(outs):
        owner = lax.bitwise_xor(info[1], m)
        for q in range(pieces):
            if unit == tile:
                block = acc[owner * pieces + q]
            else:
                parts = tile // unit
                lane = pl.multiple_of(lax.rem(owner, parts) * unit, unit)
                block = acc[lax.div(owner, parts), :, pl.ds(lane, unit)]
            out[:, q] = block.astype(out.dtype).reshape(group, rows, unit)


def grad_kernel(cols, flip, wides, info, *refs):
    x_refs, h_refs, refs = refs[:wides], refs[wides:-5], refs[-5:]
    out, x, h, x_sems, h_sems = refs
    copies = wide_copies(x_refs, x, x_sems, info[1])
    copies += hidden_copies(h_refs, h, h_sems, info[0], 0, x.shape[1])
    out[...] = jnp.zeros_like(out)
    for copy in copies:
        copy.wait()

    def add(s, wide, hidden):
        total = 0.0
        for chunk in chunks(x.shape[1]):
            a, b = flat(x[wide, chunk]), flat(h[hidden, chunk])
            a, b = (a, b) if flip else (b, a)
            total += matmul(a, b, 0, 0)
        out[s] = total.astype(out.dtype)

    over_slots(info, out.shape[0], cols, add)


def call(kernel, out_shape, scratch, flops, moved, *args):
    return pl.pallas_call(
        kernel,
        out_shape=out_shape,
        in_specs=[pl.BlockSpec(memory_space=pltpu.SMEM)] + args[1],
        out_specs=jax.tree.map(lambda _: pl.BlockSpec(memory_space=pltpu.VMEM), out_shape),
        scratch_shapes=scratch,
        compiler_params=pltpu.CompilerParams(vmem_limit_bytes=VMEM),
        cost_estimate=pl.CostEstimate(flops=flops, bytes_accessed=moved, transcendentals=0),
    )(args[0], *args[2])


def to_hidden(info, xs, w, cols, flip):
    blocks, pieces, rows, unit = xs[0].shape[-4:]
    slots, tile, _ = w.shape
    outs = [jax.ShapeDtypeStruct((cols, rows, tile), jnp.bfloat16)] * blocks
    scratch = [
        pltpu.VMEM((D // tile, blocks, rows, tile), jnp.bfloat16),
        pltpu.VMEM((cols, blocks, rows, tile), jnp.float32),
        pltpu.SemaphoreType.DMA((D // unit,)),
    ]
    kernel = functools.partial(to_hidden_kernel, cols, flip, len(xs))
    specs = [pl.BlockSpec(memory_space=pltpu.VMEM)] + [ANY] * len(xs)
    flops = 2 * slots * blocks * rows * tile * tile
    return call(kernel, outs, scratch, flops, 8 << 20, info, specs, [w, *xs])


def from_hidden(info, hs, w, cols, flip, at, group, devices):
    _, rows, tile = hs[0].shape
    slots = w.shape[0]
    unit = min(tile, D // devices)
    pieces = D // devices // unit
    outs = [jax.ShapeDtypeStruct((group, pieces, rows, unit), jnp.bfloat16)] * devices
    if long_row():
        outs = [jax.ShapeDtypeStruct((devices, *outs[0].shape), jnp.bfloat16)]
    scratch = [
        pltpu.VMEM((cols, group, rows, tile), jnp.bfloat16),
        pltpu.VMEM((D // tile, group * rows, tile), jnp.float32),
        pltpu.SemaphoreType.DMA((group,)),
    ]
    blocks = (len(hs) + 1) // 2
    kernel = functools.partial(from_hidden_kernel, cols, flip, at, blocks)
    specs = [pl.BlockSpec(memory_space=pltpu.VMEM)] + [ANY] * len(hs)
    flops = 2 * slots * group * rows * tile * tile
    return call(kernel, outs, scratch, flops, 8 << 20, info, specs, [w, *hs])


def slot_grads(info, xs, hs, slots, cols, flip):
    blocks, pieces, rows, unit = xs[0].shape[-4:]
    tile = hs[0].shape[2]
    out = jax.ShapeDtypeStruct((slots, tile, tile), jnp.bfloat16)
    scratch = [
        pltpu.VMEM((D // tile, blocks, rows, tile), jnp.bfloat16),
        pltpu.VMEM((cols, blocks, rows, tile), jnp.bfloat16),
        pltpu.SemaphoreType.DMA((D // unit,)),
        pltpu.SemaphoreType.DMA((blocks,)),
    ]
    kernel = functools.partial(grad_kernel, cols, flip, len(xs))
    specs = [ANY] * (len(xs) + len(hs))
    flops = 2 * slots * blocks * rows * tile * tile
    return call(kernel, out, scratch, flops, 8 << 20, info, specs, [*xs, *hs])


def long_row():
    return lax.axis_size("row") > GROUP


def swap_col(x, m):
    count = lax.axis_size("col")
    return lax.ppermute(x, "col", [(s, s ^ m) for s in range(count)])


def shift_row(x, step):
    count = lax.axis_size("row")
    return lax.ppermute(x, "row", [(s, (s + step) % count) for s in range(count)])


def step_row(x, step, first, last):
    return lax.ppermute(x, "row", [(s, s + step) for s in range(first, last + 1)])


def spread(x, tile):
    rows, width = x.shape
    unit = min(width, tile)
    own = jnp.swapaxes(x.reshape(rows, width // unit, unit), 0, 1)
    if long_row():
        everything = lax.all_gather(lax.all_gather(own, "row"), "col")
        return [everything]
    mine = jnp.stack([own] + [shift_row(own, -j) for j in range(1, lax.axis_size("row"))])
    held = []
    for m in range(0, lax.axis_size("col"), 2):
        held.append(swap_col(mine, m) if m else mine)
        held.append(swap_col(held[m], 1))
    return held


def add(*terms):
    total = sum(term.astype(jnp.float32) for term in terms)
    return total


def line_reduce(parts):
    if long_row():
        return lax.psum_scatter(jnp.stack(parts), "row", scatter_dimension=0).astype(jnp.float32)
    count = len(parts)
    right = left = None
    for k in range(1, count):
        out_right, out_left = parts[count - k], parts[k]
        if k > 1:
            out_right = add(out_right, right).astype(jnp.bfloat16)
            out_left = add(out_left, left).astype(jnp.bfloat16)
        right = step_row(out_right, 1, 0, k - 1)
        left = step_row(out_left, -1, count - k, count - 1)
    return add(parts[0], right, left)


def line_gather(x):
    count = lax.axis_size("row")
    if long_row():
        everything = lax.all_gather(x, "row")
        return [everything[0]] * count + [everything[j] for j in range(1, count)]
    right, left = [x], [x]
    for k in range(1, count):
        right.append(step_row(right[-1], 1, k - 1, count - 2))
        left.append(step_row(left[-1], -1, 1, count - k))
    return right + left[1:]


def finish_col(parts):
    if long_row():
        return lax.psum_scatter(parts[0], "col", scatter_dimension=0)
    sums = []
    for m in range(0, len(parts), 2):
        pair = add(parts[m], swap_col(parts[m + 1], 1)).astype(jnp.bfloat16)
        sums.append(swap_col(pair, m) if m else pair)
    return add(*sums).astype(jnp.bfloat16)


def finish_row(blocks):
    if long_row():
        total = lax.psum_scatter(jnp.stack(blocks), "row", scatter_dimension=0)
        return jnp.swapaxes(total, 0, 1).reshape(total.shape[1], -1)
    total = add(blocks[0], *[shift_row(blocks[j], j) for j in range(1, len(blocks))])
    _, rows, _ = total.shape
    return jnp.swapaxes(total, 0, 1).reshape(rows, -1).astype(jnp.bfloat16)


def per_device(tokens, upstream, w_in, in_codes, w_out, out_codes):
    tile = w_in.shape[3]
    slots = w_in.shape[1]
    devices = lax.axis_size("col")
    blocks = lax.axis_size("row")
    cols = FF // (tile * devices)
    group = min(blocks, GROUP)
    starts = range(0, blocks, group)
    row, col = lax.axis_index("row"), lax.axis_index("col")

    def slot_info(codes):
        own = lax.dynamic_slice_in_dim(codes[0], row * slots, slots)
        place = jnp.stack([row, col]).astype(jnp.int32)
        if long_row():
            place = jnp.zeros_like(place)
        return jnp.concatenate([place, own])

    info_in, info_out = slot_info(in_codes), slot_info(out_codes)
    w_in, w_out = w_in[0], w_out[0]

    def hidden_side(info, xs, w, flip):
        return line_reduce(to_hidden(info, xs, w, cols, flip))

    def wide_side(info, hs, w, flip):
        sums = []
        for at in starts:
            if sums:
                hs, _ = lax.optimization_barrier((hs, sums[-1]))
            parts = from_hidden(info, hs, w, cols, flip, at, group, devices)
            sums.append(finish_col(parts))
        return finish_row([part[g] for part in sums for g in range(group)])

    all_tokens = spread(tokens, tile)
    hidden = hidden_side(info_in, all_tokens, w_in, False)
    if len(starts) > 1:
        upstream, hidden = lax.optimization_barrier((upstream, hidden))
    all_up = spread(upstream, tile)
    grad_activ = hidden_side(info_out, all_up, w_out, True)
    sigmoid = jax.nn.sigmoid(hidden)
    activ = (hidden * sigmoid).astype(jnp.bfloat16)
    grad_hidden = grad_activ * sigmoid * (1.0 + hidden * (1.0 - sigmoid))
    grad_hidden = grad_hidden.astype(jnp.bfloat16)
    all_activ, all_grad = line_gather(activ), line_gather(grad_hidden)
    layer_out = wide_side(info_out, all_activ, w_out, False)
    grad_w_out = slot_grads(info_out, all_up, all_activ, slots, cols, False)
    if len(starts) > 1:
        held = (all_grad, tokens, layer_out, grad_w_out)
        all_grad, tokens, layer_out, grad_w_out = lax.optimization_barrier(held)
        all_tokens = spread(tokens, tile)
    grad_tokens = wide_side(info_in, all_grad, w_in, True)
    grad_w_in = slot_grads(info_in, all_tokens, all_grad, slots, cols, True)
    return layer_out, grad_tokens, grad_w_in[None], grad_w_out[None]


def solution(mesh):
    placed = (
        P("row", "col"),
        P("row", "col"),
        P("col", "row", None, None),
        P("col", None),
        P("col", "row", None, None),
        P("col", None),
    )
    return jax.shard_map(
        per_device,
        mesh=mesh,
        in_specs=placed,
        out_specs=(
            P("row", "col"),
            P("row", "col"),
            P("col", "row", None, None),
            P("col", "row", None, None),
        ),
        check_vma=False,
    )
```

time: 521 us -> 324 us (0.62)
  waiting for transfers between devices: 454 us -> 158 us
  starting transfers between devices: 0.37 us -> 105 us
  between operations: 13.9 us -> 1.6 us
  Pallas kernels: 36.7 us -> 42.1 us
    all_gather x4 -> x0, waiting for transfers between devices: 200 us -> none  [the longest x2 120 us: everywhere(): pieces = lax.all_gather(to_pieces(x, tile), ('row', 'col'))]
    ppermute x0 -> x64, waiting for transfers between devices: none -> 158 us  [the longest x24 74.5 us: step_row(): lax.ppermute(x, 'row', [(s, s + step) for s in range(first, last + 1)])]
    unnamed x10 -> x0, waiting for transfers between devices: 128 us -> none
    reduce_scatter x4 -> x0, waiting for transfers between devices: 126 us -> none  [the longest x1 46 us: per_device(): lax.psum_scatter(grad_activ, 'row', scatter_dimension=0).astype(jnp.float32)]
    ppermute x0 -> x64, starting transfers between devices: none -> 105 us  [the longest x24 49.4 us: step_row(): lax.ppermute(x, 'row', [(s, s + step) for s in range(first, last + 1)])]
    pallas_call x4 -> x6, Pallas kernels: 36.7 us -> 42.1 us  [call(): pl.pallas_call(kernel, out_shape=out_shape, in_specs=[pl.BlockSpec(memory...]
  transfers between devices with their start and end apart: 9 -> 64, of which waited for: 9 -> 27; matrix products, arithmetic and copies ran while one was open for 1% -> 2% of each run, Pallas kernels for 5% -> 13%
where the time goes in v2:
time: 324 us; the launch traced here: 320 us
  waiting for transfers between devices  158 us (49%)
  starting transfers between devices  105 us (32%)
  Pallas kernels  42.1 us (13%)
  local copies, waits for them, and re-layouts  8.76 us (3%)
  other arithmetic  4.9 us (2%)
    ppermute x24, waiting for transfers between devices, step_row(): lax.ppermute(x, 'row', [(s, s + step) for s in range(first, last + 1)])  74.5 us
    ppermute x28, waiting for transfers between devices, swap_col(): return lax.ppermute(x, 'col', [(s, s ^ m) for s in range(count)])  57.6 us
    ppermute x24, starting transfers between devices, step_row(): lax.ppermute(x, 'row', [(s, s + step) for s in range(first, last + 1)])  49.4 us
    pallas_call x6, Pallas kernels, call(): pl.pallas_call(kernel, out_shape=out_shape, in_specs=[pl.BlockSpec(memory...  42.1 us
    ppermute x28, starting transfers between devices, swap_col(): return lax.ppermute(x, 'col', [(s, s ^ m) for s in range(count)])  30.6 us
    ppermute x12, waiting for transfers between devices, shift_row(): lax.ppermute(x, 'row', [(s, (s + step) % count) for s in range(count)])  25.9 us
    ppermute x12, starting transfers between devices, shift_row(): lax.ppermute(x, 'row', [(s, (s + step) % count) for s in range(count)])  24.6 us
    unnamed x94, local copies, waits for them, and re-layouts  8.08 us
  transfers between devices with their start and end apart: 64, of which 27 were waited for; matrix products, arithmetic and copies ran while one was open for 2% of the time, Pallas kernels for 13%

profile of v2, /device:TPU:0, one launch (start us, length us, event | category | flops | bytes accessed | tf_op | source)
XLA Modules:
  0.0 319.9 jit_solution(2301908339672557174)
XLA Ops:
  7.9 5.9 %collective-permute-done.1 = bf16[2,128,256]{2,1,0:T(8,128)(2,1)S(1)} collective-permute-done((bf16[2,128,256]{2,1,0:T(8,128)(2,1)S(1)}, bf16[2,128,256]{2,1,0:T(8,128)(2,1)S(1)}, u32[]{:S(2)}, u32[]{:S(2)}) %collective-permute-start.1) | collective-permute-done | bytes 131104 | tf_op jit(solution)/shard_map/ppermute | solution.py:230
  26.9 6.8 %collective-permute-done.33 = bf16[2,128,256]{2,1,0:T(8,128)(2,1)S(1)} collective-permute-done((bf16[2,128,256]{2,1,0:T(8,128)(2,1)S(1)}, bf16[2,128,256]{2,1,0:T(8,128)(2,1)S(1)}, u32[]{:S(2)}, u32[]{:S(2)}) %collective-permute-start.33) | collective-permute-done | bytes 131104 | tf_op jit(solution)/shard_map/ppermute | solution.py:230
  38.7 13.8 %collective-permute-done.6.refs_4_ = bf16[4,2,128,256]{3,2,1,0:T(8,128)(2,1)S(1)} collective-permute-done((bf16[4,2,128,256]{3,2,1,0:T(8,128)(2,1)S(1)}, bf16[4,2,128,256]{3,2,1,0:T(8,128)(2,1)S(1)}, u32[]{:S(2)}, u32[]{:S(2)}) %collective-permute-start.6) | collective-permute-done | bytes 524320 | tf_op jit(solution)/shard_map/ppermute | solution.py:225
  53.1 10.6 %collective-permute-done.38.refs_4_ = bf16[4,2,128,256]{3,2,1,0:T(8,128)(2,1)S(1)} collective-permute-done((bf16[4,2,128,256]{3,2,1,0:T(8,128)(2,1)S(1)}, bf16[4,2,128,256]{3,2,1,0:T(8,128)(2,1)S(1)}, u32[]{:S(2)}, u32[]{:S(2)}) %collective-permute-start.38) | collective-permute-done | bytes 524320 | tf_op jit(solution)/shard_map/ppermute | solution.py:225
  71.4 6.8 %shard_map.95 = (bf16[8,128,256]{2,1,0:T(8,128)(2,1)}, bf16[8,128,256]{2,1,0:T(8,128)(2,1)}, bf16[8,128,256]{2,1,0:T(8,128)(2,1)}, bf16[8,128,256]{2,1,0:T(8,128)(2,1)}) custom-call(s32[18]{0:T(128)} %pad_add_fusion.info, bf16[16,256,256]{2,1,0:T(8,128)(2,1)} %bitcast.54, bf16[4,2,128,256]{3,2,1,0:T(8,128)(2,1)} %copy-done.2, ...), custom_call_target="tpu_custom_call" | custom-call | flops 1073741824 | bytes 8388608 | tf_op jit(solution)/shard_map/pallas_call | solution.py:157
  78.9 5.6 %collective-permute-start.42 = (bf16[8,128,256]{2,1,0:T(8,128)(2,1)}, bf16[8,128,256]{2,1,0:T(8,128)(2,1)S(1)}, u32[]{:S(2)}, u32[]{:S(2)}) collective-permute-start(bf16[8,128,256]{2,1,0:T(8,128)(2,1)} %get-tuple-element.43), channel_id=1, source_target_pairs={{0,8},{1,9},{2,10},{3,11},{4,12},{5,13},{6,14},{7,15}} | collective-permute-start | bytes 1572872 | tf_op jit(solution)/shard_map/ppermute | solution.py:234
  86.4 7.1 %shard_map.93 = (bf16[8,128,256]{2,1,0:T(8,128)(2,1)}, bf16[8,128,256]{2,1,0:T(8,128)(2,1)}, bf16[8,128,256]{2,1,0:T(8,128)(2,1)}, bf16[8,128,256]{2,1,0:T(8,128)(2,1)}) custom-call(s32[18]{0:T(128)} %pad_add_fusion.2.info, bf16[16,256,256]{2,1,0:T(8,128)(2,1)} %bitcast.52, bf16[4,2,128,256]{3,2,1,0:T(8,128)(2,1)} %copy-done.1, ...), custom_call_target="tpu_custom_call" | custom-call | flops 1073741824 | bytes 8388608 | tf_op jit(solution)/shard_map/pallas_call | solution.py:157
  99.9 6.5 %collective-permute-done.10 = bf16[8,128,256]{2,1,0:T(8,128)(2,1)S(1)} collective-permute-done((bf16[8,128,256]{2,1,0:T(8,128)(2,1)}, bf16[8,128,256]{2,1,0:T(8,128)(2,1)S(1)}, u32[]{:S(2)}, u32[]{:S(2)}) %collective-permute-start.10) | collective-permute-done | bytes 524320 | tf_op jit(solution)/shard_map/ppermute | solution.py:234
  112.0 5.6 %collective-permute-done.43 = bf16[8,128,256]{2,1,0:T(8,128)(2,1)S(1)} collective-permute-done((bf16[8,128,256]{2,1,0:T(8,128)(2,1)S(1)}, bf16[8,128,256]{2,1,0:T(8,128)(2,1)S(1)}, u32[]{:S(2)}, u32[]{:S(2)}) %collective-permute-start.43) | collective-permute-done | bytes 524320 | tf_op jit(solution)/shard_map/ppermute | solution.py:234
  134.9 5.2 %collective-permute-done.44 = bf16[8,128,256]{2,1,0:T(8,128)(2,1)S(1)} collective-permute-done((bf16[8,128,256]{2,1,0:T(8,128)(2,1)S(1)}, bf16[8,128,256]{2,1,0:T(8,128)(2,1)S(1)}, u32[]{:S(2)}, u32[]{:S(2)}) %collective-permute-start.44) | collective-permute-done | bytes 524320 | tf_op jit(solution)/shard_map/ppermute | solution.py:234
  140.1 11.2 %collective-permute-done.12 = bf16[8,128,256]{2,1,0:T(8,128)(2,1)S(1)} collective-permute-done((bf16[8,128,256]{2,1,0:T(8,128)(2,1)S(1)}, bf16[8,128,256]{2,1,0:T(8,128)(2,1)S(1)}, u32[]{:S(2)}, u32[]{:S(2)}) %collective-permute-start.12) | collective-permute-done | bytes 524320 | tf_op jit(solution)/shard_map/ppermute | solution.py:234
  153.4 5.0 %collective-permute-start.48 = (bf16[8,128,256]{2,1,0:T(8,128)(2,1)S(1)}, bf16[8,128,256]{2,1,0:T(8,128)(2,1)S(1)}, u32[]{:S(2)}, u32[]{:S(2)}) collective-permute-start(bf16[8,128,256]{2,1,0:T(8,128)(2,1)S(1)} %get-tuple-element.56.refs_0_.refs_8_), channel_id=1, source_target_pairs={{0,8},{8,16},{16,24},{1,9},{9,17},{17,25},{2,10},{10,18},{18,26},{... | collective-permute-start | bytes 1572872 | tf_op jit(solution)/shard_map/ppermute | solution.py:234
  170.7 8.8 %collective-permute-done.19.refs_4_.refs_12_ = bf16[8,128,256]{2,1,0:T(8,128)(2,1)S(1)} collective-permute-done((bf16[8,128,256]{2,1,0:T(8,128)(2,1)S(1)}, bf16[8,128,256]{2,1,0:T(8,128)(2,1)S(1)}, u32[]{:S(2)}, u32[]{:S(2)}) %collective-permute-start.19) | collective-permute-done | bytes 524320 | tf_op jit(solution)/shard_map/ppermute | solution.py:234
  182.0 8.8 %collective-permute-done.52.refs_5_.refs_13_ = bf16[8,128,256]{2,1,0:T(8,128)(2,1)S(1)} collective-permute-done((bf16[8,128,256]{2,1,0:T(8,128)(2,1)S(1)}, bf16[8,128,256]{2,1,0:T(8,128)(2,1)S(1)}, u32[]{:S(2)}, u32[]{:S(2)}) %collective-permute-start.52) | collective-permute-done | bytes 524320 | tf_op jit(solution)/shard_map/ppermute | solution.py:234
  192.7 9.2 %collective-permute-done.20.refs_5_.refs_13_ = bf16[8,128,256]{2,1,0:T(8,128)(2,1)S(1)} collective-permute-done((bf16[8,128,256]{2,1,0:T(8,128)(2,1)S(1)}, bf16[8,128,256]{2,1,0:T(8,128)(2,1)S(1)}, u32[]{:S(2)}, u32[]{:S(2)}) %collective-permute-start.20) | collective-permute-done | bytes 524320 | tf_op jit(solution)/shard_map/ppermute | solution.py:234
  204.2 9.0 %collective-permute-done.53.refs_6_.refs_14_ = bf16[8,128,256]{2,1,0:T(8,128)(2,1)S(1)} collective-permute-done((bf16[8,128,256]{2,1,0:T(8,128)(2,1)S(1)}, bf16[8,128,256]{2,1,0:T(8,128)(2,1)S(1)}, u32[]{:S(2)}, u32[]{:S(2)}) %collective-permute-start.53) | collective-permute-done | bytes 524320 | tf_op jit(solution)/shard_map/ppermute | solution.py:234
  214.8 7.7 %shard_map.96 = (bf16[4,2,128,256]{3,2,1,0:T(8,128)(2,1)}, bf16[4,2,128,256]{3,2,1,0:T(8,128)(2,1)}, bf16[4,2,128,256]{3,2,1,0:T(8,128)(2,1)}, bf16[4,2,128,256]...) custom-call(s32[18]{0:T(128)} %pad_add_fusion.2.info, ...), custom_call_target="tpu_custom_call" | custom-call | flops 1073741824 | bytes 8388608 | tf_op jit(solution)/shard_map/pallas_call | solution.py:157
  226.0 6.8 %shard_map.94 = (bf16[4,2,128,256]{3,2,1,0:T(8,128)(2,1)}, bf16[4,2,128,256]{3,2,1,0:T(8,128)(2,1)}, bf16[4,2,128,256]{3,2,1,0:T(8,128)(2,1)}, bf16[4,2,128,256]...) custom-call(s32[18]{0:T(128)} %pad_add_fusion.info, ...), custom_call_target="tpu_custom_call" | custom-call | flops 1073741824 | bytes 8388608 | tf_op jit(solution)/shard_map/pallas_call | solution.py:157
  236.1 7.0 %shard_map.97 = bf16[16,256,256]{2,1,0:T(8,128)(2,1)} custom-call(s32[18]{0:T(128)} %pad_add_fusion.2.info, bf16[4,2,128,256]{3,2,1,0:T(8,128)(2,1)} %copy-done.1, bf16[4,2,128,256]{3,2,1,0:T(8,128)(2,1)} %collective-permute-done.3.refs_1_, bf16[4,2,128,256]{3,2,1,0:T(8,128)(2,1)} %copy-done.9, bf16[4,2,128,256]{3,2,1,0:T(8,128)(2,1)} %copy-done.12, ...), custom_call_target="tpu_custom_call" | custom-call | flops 1073741824 | bytes 8388608 | tf_op jit(solution)/shard_map/pallas_call | solution.py:157
  243.2 6.7 %shard_map.98 = bf16[16,256,256]{2,1,0:T(8,128)(2,1)} custom-call(s32[18]{0:T(128)} %pad_add_fusion.info, bf16[4,2,128,256]{3,2,1,0:T(8,128)(2,1)} %copy-done.2, bf16[4,2,128,256]{3,2,1,0:T(8,128)(2,1)} %collective-permute-done.35.refs_1_, bf16[4,2,128,256]{3,2,1,0:T(8,128)(2,1)} %collective-permute-done.36.refs_2_, ...), custom_call_target="tpu_custom_call" | custom-call | flops 1073741824 | bytes 8388608 | tf_op jit(solution)/shard_map/pallas_call | solution.py:157
  260.1 8.3 %collective-permute-done.56 = bf16[4,2,128,256]{3,2,1,0:T(8,128)(2,1)S(1)} collective-permute-done((bf16[4,2,128,256]{3,2,1,0:T(8,128)(2,1)S(1)}, bf16[4,2,128,256]{3,2,1,0:T(8,128)(2,1)S(1)}, u32[]{:S(2)}, u32[]{:S(2)}) %collective-permute-start.56) | collective-permute-done | bytes 524320 | tf_op jit(solution)/shard_map/ppermute | solution.py:225
  271.0 9.0 %collective-permute-done.58 = bf16[4,2,128,256]{3,2,1,0:T(8,128)(2,1)S(1)} collective-permute-done((bf16[4,2,128,256]{3,2,1,0:T(8,128)(2,1)S(1)}, bf16[4,2,128,256]{3,2,1,0:T(8,128)(2,1)S(1)}, u32[]{:S(2)}, u32[]{:S(2)}) %collective-permute-start.58) | collective-permute-done | bytes 524320 | tf_op jit(solution)/shard_map/ppermute | solution.py:225
  295.1 7.0 %collective-permute-done.26 = bf16[4,2,128,256]{3,2,1,0:T(8,128)(2,1)S(1)} collective-permute-done((bf16[4,2,128,256]{3,2,1,0:T(8,128)(2,1)S(1)}, bf16[4,2,128,256]{3,2,1,0:T(8,128)(2,1)S(1)}, u32[]{:S(2)}, u32[]{:S(2)}) %collective-permute-start.26) | collective-permute-done | bytes 524320 | tf_op jit(solution)/shard_map/ppermute | solution.py:225
  312.5 6.5 %collective-permute-done.30 = bf16[2,128,256]{2,1,0:T(8,128)(2,1)S(1)} collective-permute-done((bf16[2,128,256]{2,1,0:T(8,128)(2,1)S(1)}, bf16[2,128,256]{2,1,0:T(8,128)(2,1)S(1)}, u32[]{:S(2)}, u32[]{:S(2)}) %collective-permute-start.30) | collective-permute-done | bytes 131104 | tf_op jit(solution)/shard_map/ppermute | solution.py:230
  (233 shorter events, 133.3 us)
Async XLA Ops:
  26.4 26.2 %collective-permute-start.6 = (bf16[4,2,128,256]{3,2,1,0:T(8,128)(2,1)S(1)}, bf16[4,2,128,256]{3,2,1,0:T(8,128)(2,1)S(1)}, u32[]{:S(2)}, u32[]{:S(2)}) collective-permute-start(bf16[4,2,128,256]{3,2,1,0:T(8,128)(2,1)S(1)} %pad_maximum_fusion.refs_0_), channel_id=1, source_target_pairs={{0,4},{1,5},{2,6},{3,7},{4,0},{5,1},{6,2},{7,3},{8,12},{9,13},{10,... | collective-permute-start | bytes 1572872 | tf_op jit(solution)/shard_map/ppermute | solution.py:225
  35.2 28.5 %collective-permute-start.38 = (bf16[4,2,128,256]{3,2,1,0:T(8,128)(2,1)S(1)}, bf16[4,2,128,256]{3,2,1,0:T(8,128)(2,1)S(1)}, u32[]{:S(2)}, u32[]{:S(2)}) collective-permute-start(bf16[4,2,128,256]{3,2,1,0:T(8,128)(2,1)S(1)} %pad_maximum_fusion.1.refs_0_), channel_id=1, source_target_pairs={{0,4},{1,5},{2,6},{3,7},{4,0},{5,1},{6,2},{7,3},{8,12},{9,13},{10,... | collective-permute-start | bytes 1572872 | tf_op jit(solution)/shard_map/ppermute | solution.py:225
  36.7 27.0 %collective-permute-start.36 = (bf16[4,2,128,256]{3,2,1,0:T(8,128)(2,1)S(1)}, bf16[4,2,128,256]{3,2,1,0:T(8,128)(2,1)}, u32[]{:S(2)}, u32[]{:S(2)}) collective-permute-start(bf16[4,2,128,256]{3,2,1,0:T(8,128)(2,1)S(1)} %pad_maximum_fusion.1.refs_0_), channel_id=1, source_target_pairs={{0,2},{1,3},{2,0},{3,1},{4,6},{5,7},{6,4},{7,5},{8,10},{9,11},{10,... | collective-permute-start | bytes 1572872 | tf_op jit(solution)/shard_map/ppermute | solution.py:225
  38.2 30.7 %collective-permute-start.4 = (bf16[4,2,128,256]{3,2,1,0:T(8,128)(2,1)S(1)}, bf16[4,2,128,256]{3,2,1,0:T(8,128)(2,1)S(1)}, u32[]{:S(2)}, u32[]{:S(2)}) collective-permute-start(bf16[4,2,128,256]{3,2,1,0:T(8,128)(2,1)S(1)} %pad_maximum_fusion.refs_0_), channel_id=1, source_target_pairs={{0,2},{1,3},{2,0},{3,1},{4,6},{5,7},{6,4},{7,5},{8,10},{9,11},{10,... | collective-permute-start | bytes 1572872 | tf_op jit(solution)/shard_map/ppermute | solution.py:225
  99.2 23.1 %collective-permute-start.46 = (bf16[8,128,256]{2,1,0:T(8,128)(2,1)S(1)}, bf16[8,128,256]{2,1,0:T(8,128)(2,1)S(1)}, u32[]{:S(2)}, u32[]{:S(2)}) collective-permute-start(bf16[8,128,256]{2,1,0:T(8,128)(2,1)S(1)} %get-tuple-element.62), channel_id=1, source_target_pairs={{16,8},{24,16},{17,9},{25,17},{18,10},{26,18},{19,11},{27,19},{20,... | collective-permute-start | bytes 1572872 | tf_op jit(solution)/shard_map/ppermute | solution.py:234
  117.8 22.3 %collective-permute-start.44 = (bf16[8,128,256]{2,1,0:T(8,128)(2,1)S(1)}, bf16[8,128,256]{2,1,0:T(8,128)(2,1)S(1)}, u32[]{:S(2)}, u32[]{:S(2)}) collective-permute-start(bf16[8,128,256]{2,1,0:T(8,128)(2,1)S(1)} %add_convert_fusion.6), channel_id=1, source_target_pairs={{0,8},{8,16},{16,24},{1,9},{9,17},{17,25},{2,10},{10,18},{18,26},{... | collective-permute-start | bytes 1572872 | tf_op jit(solution)/shard_map/ppermute | solution.py:234
  129.0 22.3 %collective-permute-start.12 = (bf16[8,128,256]{2,1,0:T(8,128)(2,1)S(1)}, bf16[8,128,256]{2,1,0:T(8,128)(2,1)S(1)}, u32[]{:S(2)}, u32[]{:S(2)}) collective-permute-start(bf16[8,128,256]{2,1,0:T(8,128)(2,1)S(1)} %add_convert_fusion.13), channel_id=1, source_target_pairs={{0,8},{8,16},{16,24},{1,9},{9,17},{17,25},{2,10},{10,18},{18,26},{... | collective-permute-start | bytes 1572872 | tf_op jit(solution)/shard_map/ppermute | solution.py:234
  168.3 22.5 %collective-permute-start.52 = (bf16[8,128,256]{2,1,0:T(8,128)(2,1)S(1)}, bf16[8,128,256]{2,1,0:T(8,128)(2,1)S(1)}, u32[]{:S(2)}, u32[]{:S(2)}) collective-permute-start(bf16[8,128,256]{2,1,0:T(8,128)(2,1)S(1)} %collective-permute-done.51.refs_4_.refs_12_), channel_id=1, source_target_pairs={{8,0},{16,8},{9,1},{17,9},{10,2},{18,10},{11,3},{19,11},{12,4},{20... | collective-permute-start | bytes 1572872 | tf_op jit(solution)/shard_map/ppermute | solution.py:234
  179.5 22.5 %collective-permute-start.20 = (bf16[8,128,256]{2,1,0:T(8,128)(2,1)S(1)}, bf16[8,128,256]{2,1,0:T(8,128)(2,1)S(1)}, u32[]{:S(2)}, u32[]{:S(2)}) collective-permute-start(bf16[8,128,256]{2,1,0:T(8,128)(2,1)S(1)} %collective-permute-done.19.refs_4_.refs_12_), channel_id=1, source_target_pairs={{8,0},{16,8},{9,1},{17,9},{10,2},{18,10},{11,3},{19,11},{12,4},{20... | collective-permute-start | bytes 1572872 | tf_op jit(solution)/shard_map/ppermute | solution.py:234
  190.7 22.5 %collective-permute-start.53 = (bf16[8,128,256]{2,1,0:T(8,128)(2,1)S(1)}, bf16[8,128,256]{2,1,0:T(8,128)(2,1)S(1)}, u32[]{:S(2)}, u32[]{:S(2)}) collective-permute-start(bf16[8,128,256]{2,1,0:T(8,128)(2,1)S(1)} %collective-permute-done.52.refs_5_.refs_13_), channel_id=1, source_target_pairs={{8,0},{9,1},{10,2},{11,3},{12,4},{13,5},{14,6},{15,7}} | collective-permute-start | bytes 1572872 | tf_op jit(solution)/shard_map/ppermute | solution.py:234
  202.0 22.5 %collective-permute-start.21 = (bf16[8,128,256]{2,1,0:T(8,128)(2,1)S(1)}, bf16[8,128,256]{2,1,0:T(8,128)(2,1)S(1)}, u32[]{:S(2)}, u32[]{:S(2)}) collective-permute-start(bf16[8,128,256]{2,1,0:T(8,128)(2,1)S(1)} %collective-permute-done.20.refs_5_.refs_13_), channel_id=1, source_target_pairs={{8,0},{9,1},{10,2},{11,3},{12,4},{13,5},{14,6},{15,7}} | collective-permute-start | bytes 1572872 | tf_op jit(solution)/shard_map/ppermute | solution.py:234
  222.6 27.2 %collective-permute-start.55 = (bf16[4,2,128,256]{3,2,1,0:T(8,128)(2,1)}, bf16[4,2,128,256]{3,2,1,0:T(8,128)(2,1)S(1)}, u32[]{:S(2)}, u32[]{:S(2)}) collective-permute-start(bf16[4,2,128,256]{3,2,1,0:T(8,128)(2,1)} %get-tuple-element.47), channel_id=1, source_target_pairs={{0,1},{1,0},{2,3},{3,2},{4,5},{5,4},{6,7},{7,6},{8,9},{9,8},{10,11... | collective-permute-start | bytes 1572872 | tf_op jit(solution)/shard_map/ppermute | solution.py:225
  223.7 34.9 %collective-permute-start.54 = (bf16[4,2,128,256]{3,2,1,0:T(8,128)(2,1)}, bf16[4,2,128,256]{3,2,1,0:T(8,128)(2,1)S(1)}, u32[]{:S(2)}, u32[]{:S(2)}) collective-permute-start(bf16[4,2,128,256]{3,2,1,0:T(8,128)(2,1)} %get-tuple-element.45), channel_id=1, source_target_pairs={{0,1},{1,0},{2,3},{3,2},{4,5},{5,4},{6,7},{7,6},{8,9},{9,8},{10,11... | collective-permute-start | bytes 1572872 | tf_op jit(solution)/shard_map/ppermute | solution.py:225
  223.8 28.2 %collective-permute-start.57 = (bf16[4,2,128,256]{3,2,1,0:T(8,128)(2,1)}, bf16[4,2,128,256]{3,2,1,0:T(8,128)(2,1)S(1)}, u32[]{:S(2)}, u32[]{:S(2)}) collective-permute-start(bf16[4,2,128,256]{3,2,1,0:T(8,128)(2,1)} %get-tuple-element.49), channel_id=1, source_target_pairs={{0,1},{1,0},{2,3},{3,2},{4,5},{5,4},{6,7},{7,6},{8,9},{9,8},{10,11... | collective-permute-start | bytes 1572872 | tf_op jit(solution)/shard_map/ppermute | solution.py:225
  224.4 27.8 %collective-permute-start.59 = (bf16[4,2,128,256]{3,2,1,0:T(8,128)(2,1)}, bf16[4,2,128,256]{3,2,1,0:T(8,128)(2,1)S(1)}, u32[]{:S(2)}, u32[]{:S(2)}) collective-permute-start(bf16[4,2,128,256]{3,2,1,0:T(8,128)(2,1)} %get-tuple-element.51), channel_id=1, source_target_pairs={{0,1},{1,0},{2,3},{3,2},{4,5},{5,4},{6,7},{7,6},{8,9},{9,8},{10,11... | collective-permute-start | bytes 1572872 | tf_op jit(solution)/shard_map/ppermute | solution.py:225
  232.9 22.9 %collective-permute-start.23 = (bf16[4,2,128,256]{3,2,1,0:T(8,128)(2,1)}, bf16[4,2,128,256]{3,2,1,0:T(8,128)(2,1)S(1)}, u32[]{:S(2)}, u32[]{:S(2)}) collective-permute-start(bf16[4,2,128,256]{3,2,1,0:T(8,128)(2,1)} %get-tuple-element.35), channel_id=1, source_target_pairs={{0,1},{1,0},{2,3},{3,2},{4,5},{5,4},{6,7},{7,6},{8,9},{9,8},{10,11... | collective-permute-start | bytes 1572872 | tf_op jit(solution)/shard_map/ppermute | solution.py:225
  255.8 24.2 %collective-permute-start.58 = (bf16[4,2,128,256]{3,2,1,0:T(8,128)(2,1)S(1)}, bf16[4,2,128,256]{3,2,1,0:T(8,128)(2,1)S(1)}, u32[]{:S(2)}, u32[]{:S(2)}) collective-permute-start(bf16[4,2,128,256]{3,2,1,0:T(8,128)(2,1)S(1)} %add_convert_fusion.2), channel_id=1, source_target_pairs={{0,4},{1,5},{2,6},{3,7},{4,0},{5,1},{6,2},{7,3},{8,12},{9,13},{10,... | collective-permute-start | bytes 1572872 | tf_op jit(solution)/shard_map/ppermute | solution.py:225
  256.7 27.3 %collective-permute-start.60 = (bf16[4,2,128,256]{3,2,1,0:T(8,128)(2,1)S(1)}, bf16[4,2,128,256]{3,2,1,0:T(8,128)(2,1)S(1)}, u32[]{:S(2)}, u32[]{:S(2)}) collective-permute-start(bf16[4,2,128,256]{3,2,1,0:T(8,128)(2,1)S(1)} %add_convert_fusion.1), channel_id=1, source_target_pairs={{0,6},{1,7},{2,4},{3,5},{4,2},{5,3},{6,0},{7,1},{8,14},{9,15},{10,... | collective-permute-start | bytes 1572872 | tf_op jit(solution)/shard_map/ppermute | solution.py:225
  258.4 26.1 %collective-permute-start.22 = (bf16[4,2,128,256]{3,2,1,0:T(8,128)(2,1)S(1)}, bf16[4,2,128,256]{3,2,1,0:T(8,128)(2,1)S(1)}, u32[]{:S(2)}, u32[]{:S(2)}) collective-permute-start(bf16[4,2,128,256]{3,2,1,0:T(8,128)(2,1)S(1)} %copy-done.41), channel_id=1, source_target_pairs={{0,1},{1,0},{2,3},{3,2},{4,5},{5,4},{6,7},{7,6},{8,9},{9,8},{10,11... | collective-permute-start | bytes 1572872 | tf_op jit(solution)/shard_map/ppermute | solution.py:225
  258.7 32.2 %collective-permute-start.24 = (bf16[4,2,128,256]{3,2,1,0:T(8,128)(2,1)S(1)}, bf16[4,2,128,256]{3,2,1,0:T(8,128)(2,1)S(1)}, u32[]{:S(2)}, u32[]{:S(2)}) collective-permute-start(bf16[4,2,128,256]{3,2,1,0:T(8,128)(2,1)S(1)} %add_convert_fusion.10), channel_id=1, source_target_pairs={{0,2},{1,3},{2,0},{3,1},{4,6},{5,7},{6,4},{7,5},{8,10},{9,11},{10,... | collective-permute-start | bytes 1572872 | tf_op jit(solution)/shard_map/ppermute | solution.py:225
  268.4 33.7 %collective-permute-start.26 = (bf16[4,2,128,256]{3,2,1,0:T(8,128)(2,1)S(1)}, bf16[4,2,128,256]{3,2,1,0:T(8,128)(2,1)S(1)}, u32[]{:S(2)}, u32[]{:S(2)}) collective-permute-start(bf16[4,2,128,256]{3,2,1,0:T(8,128)(2,1)S(1)} %add_convert_fusion.9), channel_id=1, source_target_pairs={{0,4},{1,5},{2,6},{3,7},{4,0},{5,1},{6,2},{7,3},{8,12},{9,13},{10,... | collective-permute-start | bytes 1572872 | tf_op jit(solution)/shard_map/ppermute | solution.py:225
  280.0 23.7 %collective-permute-start.28 = (bf16[4,2,128,256]{3,2,1,0:T(8,128)(2,1)S(1)}, bf16[4,2,128,256]{3,2,1,0:T(8,128)(2,1)S(1)}, u32[]{:S(2)}, u32[]{:S(2)}) collective-permute-start(bf16[4,2,128,256]{3,2,1,0:T(8,128)(2,1)S(1)} %add_convert_fusion.8), channel_id=1, source_target_pairs={{0,6},{1,7},{2,4},{3,5},{4,2},{5,3},{6,0},{7,1},{8,14},{9,15},{10,... | collective-permute-start | bytes 1572872 | tf_op jit(solution)/shard_map/ppermute | solution.py:225
  284.4 23.7 %collective-permute-start.61 = (bf16[2,128,256]{2,1,0:T(8,128)(2,1)S(1)}, bf16[2,128,256]{2,1,0:T(8,128)(2,1)S(1)}, u32[]{:S(2)}, u32[]{:S(2)}) collective-permute-start(bf16[2,128,256]{2,1,0:T(8,128)(2,1)S(1)} %get-tuple-element.58), channel_id=1, source_target_pairs={{0,8},{8,16},{16,24},{24,0},{1,9},{9,17},{17,25},{25,1},{2,10},{10... | collective-permute-start | bytes 393224 | tf_op jit(solution)/shard_map/ppermute | solution.py:230
  284.5 23.6 %collective-permute-start.63 = (bf16[2,128,256]{2,1,0:T(8,128)(2,1)S(1)}, bf16[2,128,256]{2,1,0:T(8,128)(2,1)S(1)}, u32[]{:S(2)}, u32[]{:S(2)}) collective-permute-start(bf16[2,128,256]{2,1,0:T(8,128)(2,1)S(1)} %get-tuple-element.59), channel_id=1, source_target_pairs={{0,24},{8,0},{16,8},{24,16},{1,25},{9,1},{17,9},{25,17},{2,26},{10... | collective-permute-start | bytes 393224 | tf_op jit(solution)/shard_map/ppermute | solution.py:230
  (85 other events, 1563.4 us)

commit v3 on v2

v3 whole, which is shorter than its diff:
```python
import functools

import jax
import jax.numpy as jnp
from jax import lax
from jax.experimental import pallas as pl
from jax.experimental.pallas import tpu as pltpu
from jax.sharding import PartitionSpec as P

D = 4096
FF = 16384
VMEM = 56 * 1024 * 1024
GROUP = 4
REACH = {0: (0,), 1: (-1, 1), 2: (-2, 2), 3: (-3, -1, 1, 3)}
ANY = pl.BlockSpec(memory_space=pl.ANY)


def matmul(a, b, a_dim, b_dim):
    return lax.dot_general(
        a, b, (((a_dim,), (b_dim,)), ((), ())), preferred_element_type=jnp.float32
    )


def flat(block):
    return block.reshape(block.shape[0] * block.shape[1], block.shape[2])


def chunks(blocks):
    group = min(blocks, GROUP)
    return [slice(at, at + group) for at in range(0, blocks, group)]


def tile_part(held, owner, q, pieces, unit):
    tile = held.shape[-1]
    if unit == tile:
        return owner * pieces + q, slice(None)
    parts = tile // unit
    lane = pl.multiple_of(lax.rem(owner, parts) * unit, unit)
    return lax.div(owner, parts), pl.ds(lane, unit)


def wide_copies(refs, held, sems, col):
    copies = []

    def copy(source, owner, q, pieces, block):
        unit = source.shape[-1]
        at, lanes = tile_part(held, owner, q, pieces, unit)
        target = held.at[at, block, :, lanes]
        copies.append(pltpu.make_async_copy(source, target, sems.at[len(copies)]))
        copies[-1].start()

    if len(refs) == 1:
        devices, _, pieces, _, _ = refs[0].shape
        for owner in range(devices):
            for q in range(pieces):
                copy(refs[0].at[owner, :, q], owner, q, pieces, slice(None))
        return copies
    for at, ref in enumerate(refs):
        half, pieces, _, _ = ref.shape
        for m in range(half):
            owner = lax.bitwise_xor(col, 2 * m + at % 2)
            for q in range(pieces):
                copy(ref.at[m, q], owner, q, pieces, at // 2)
    return copies


def hidden_copies(refs, names, labels, held, sems, row):
    copies = []
    if names is None:
        for g, block in enumerate(labels):
            copies.append(pltpu.make_async_copy(refs[0].at[block], held.at[:, g], sems.at[g]))
            copies[-1].start()
        return copies
    for g, t in enumerate(labels):
        distance = lax.bitwise_xor(row, t) - row
        for name, ref in zip(names, refs):
            if name in REACH[t]:
                copy = pltpu.make_async_copy(ref, held.at[:, g], sems.at[g])
                pl.when(distance == name)(copy.start)
        copies.append(copy)
    return copies


def over_slots(info, slots, cols, body):
    def slot(s, carry):
        code = info[2 + s]

        @pl.when(code >= 0)
        def _():
            body(s, lax.div(code, cols), lax.rem(code, cols))

        return carry

    lax.fori_loop(0, slots, slot, 0)


def to_hidden_kernel(cols, flip, wides, info, w_ref, *refs):
    x_refs, refs = refs[:wides], refs[wides:]
    *outs, x, acc, sems = refs
    copies = wide_copies(x_refs, x, sems, info[1])
    acc[...] = jnp.zeros_like(acc)
    for copy in copies:
        copy.wait()

    def add(s, wide, hidden):
        for chunk in chunks(x.shape[1]):
            product = matmul(flat(x[wide, chunk]), w_ref[s], 1, 1 if flip else 0)
            acc[hidden, chunk] += product.reshape(-1, *acc.shape[2:])

    over_slots(info, w_ref.shape[0], cols, add)
    for part, out in enumerate(outs):
        out[...] = acc[:, part].astype(out.dtype)


def from_hidden_kernel(cols, flip, names, labels, info, w_ref, *refs):
    count = 1 if names is None else 2 * len(labels)
    h_refs, outs, (h, acc, sems) = refs[:-3 - count], refs[-3 - count:-3], refs[-3:]
    copies = hidden_copies(h_refs, names, labels, h, sems, info[0])
    acc[...] = jnp.zeros_like(acc)
    for copy in copies:
        copy.wait()

    def add(s, wide, hidden):
        for chunk in chunks(h.shape[1]):
            product = matmul(flat(h[hidden, chunk]), w_ref[s], 1, 1 if flip else 0)
            acc[wide, chunk] += product.reshape(-1, *acc.shape[2:])

    over_slots(info, w_ref.shape[0], cols, add)
    for at, out in enumerate(outs):
        pieces, unit = out.shape[-3], out.shape[-1]
        for m in range(out.shape[0]):
            for q in range(pieces):
                if names is None:
                    tile, lanes = tile_part(acc, m, q, pieces, unit)
                    out[m, :, q] = acc[tile, :, :, lanes].astype(out.dtype)
                else:
                    owner = lax.bitwise_xor(info[1], 2 * m + at % 2)
                    tile, lanes = tile_part(acc, owner, q, pieces, unit)
                    out[m, q] = acc[tile, at // 2, :, lanes].astype(out.dtype)


def grad_kernel(cols, flip, wides, names, labels, info, *refs):
    x_refs, h_refs, refs = refs[:wides], refs[wides:-5], refs[-5:]
    out, x, h, x_sems, h_sems = refs
    copies = wide_copies(x_refs, x, x_sems, info[1])
    copies += hidden_copies(h_refs, names, labels, h, h_sems, info[0])
    out[...] = jnp.zeros_like(out)
    for copy in copies:
        copy.wait()

    def add(s, wide, hidden):
        total = 0.0
        for chunk in chunks(x.shape[1]):
            a, b = flat(x[wide, chunk]), flat(h[hidden, chunk])
            a, b = (a, b) if flip else (b, a)
            total += matmul(a, b, 0, 0)
        out[s] = total.astype(out.dtype)

    over_slots(info, out.shape[0], cols, add)


def call(kernel, out_shape, scratch, flops, moved, *args):
    return pl.pallas_call(
        kernel,
        out_shape=out_shape,
        in_specs=[pl.BlockSpec(memory_space=pltpu.SMEM)] + args[1],
        out_specs=jax.tree.map(lambda _: pl.BlockSpec(memory_space=pltpu.VMEM), out_shape),
        scratch_shapes=scratch,
        compiler_params=pltpu.CompilerParams(vmem_limit_bytes=VMEM),
        cost_estimate=pl.CostEstimate(flops=flops, bytes_accessed=moved, transcendentals=0),
    )(args[0], *args[2])


def wide_scratch(blocks, rows, tile, unit):
    pieces = D // unit
    count = pieces if long_row() else pieces * blocks
    held = pltpu.VMEM((D // tile, blocks, rows, tile), jnp.bfloat16)
    return [held, pltpu.SemaphoreType.DMA((count,))]


def to_hidden(info, xs, w, cols, flip):
    rows, unit = xs[0].shape[-2:]
    slots, tile, _ = w.shape
    blocks = lax.axis_size("row")
    outs = [jax.ShapeDtypeStruct((cols, rows, tile), jnp.bfloat16)] * blocks
    held, sems = wide_scratch(blocks, rows, tile, unit)
    scratch = [held, pltpu.VMEM((cols, blocks, rows, tile), jnp.float32), sems]
    kernel = functools.partial(to_hidden_kernel, cols, flip, len(xs))
    specs = [pl.BlockSpec(memory_space=pltpu.VMEM)] + [ANY] * len(xs)
    flops = 2 * slots * blocks * rows * tile * tile
    return call(kernel, outs, scratch, flops, 8 << 20, info, specs, [w, *xs])


def sources(hs, labels):
    if not isinstance(hs, dict):
        return None, [hs]
    names = sorted({name for t in labels for name in REACH[t]})
    return names, [hs[name] for name in names]


def from_hidden(info, hs, w, cols, flip, labels, devices):
    names, hs = sources(hs, labels)
    rows, tile = hs[0].shape[-2:]
    slots, group = w.shape[0], len(labels)
    unit = min(tile, D // devices)
    pieces = D // devices // unit
    if names is None:
        outs = [jax.ShapeDtypeStruct((devices, group, pieces, rows, unit), jnp.bfloat16)]
    else:
        outs = [jax.ShapeDtypeStruct((devices // 2, pieces, rows, unit), jnp.bfloat16)] * (2 * group)
    scratch = [
        pltpu.VMEM((cols, group, rows, tile), jnp.bfloat16),
        pltpu.VMEM((D // tile, group, rows, tile), jnp.float32),
        pltpu.SemaphoreType.DMA((group,)),
    ]
    kernel = functools.partial(from_hidden_kernel, cols, flip, names, labels)
    specs = [pl.BlockSpec(memory_space=pltpu.VMEM)] + [ANY] * len(hs)
    flops = 2 * slots * group * rows * tile * tile
    return call(kernel, outs, scratch, flops, 8 << 20, info, specs, [w, *hs])


def slot_grads(info, xs, hs, slots, cols, flip):
    blocks = lax.axis_size("row")
    labels = range(blocks)
    names, hs = sources(hs, labels)
    rows, unit = xs[0].shape[-2:]
    tile = hs[0].shape[-1]
    out = jax.ShapeDtypeStruct((slots, tile, tile), jnp.bfloat16)
    held, sems = wide_scratch(blocks, rows, tile, unit)
    scratch = [
        held,
        pltpu.VMEM((cols, blocks, rows, tile), jnp.bfloat16),
        sems,
        pltpu.SemaphoreType.DMA((blocks,)),
    ]
    kernel = functools.partial(grad_kernel, cols, flip, len(xs), names, labels)
    specs = [ANY] * (len(xs) + len(hs))
    flops = 2 * slots * blocks * rows * tile * tile
    return call(kernel, out, scratch, flops, 8 << 20, info, specs, [*xs, *hs])


def long_row():
    return lax.axis_size("row") != 4


def swap_col(x, m):
    count = lax.axis_size("col")
    return lax.ppermute(x, "col", [(s, s ^ m) for s in range(count)])


def swap_row(x, t):
    return lax.ppermute(x, "row", [(s, s ^ t) for s in range(4)])


def step_row(x, step, first, last):
    return lax.ppermute(x, "row", [(s, s + step) for s in range(first, last + 1)])


def own_pieces(x, tile):
    rows, width = x.shape
    unit = min(width, tile)
    return jnp.swapaxes(x.reshape(rows, width // unit, unit), 0, 1)


def spread(blocks):
    held = []
    for own in blocks:
        even = [swap_col(own, m) if m else own for m in range(0, lax.axis_size("col"), 2)]
        held.append(jnp.stack(even))
        held.append(swap_col(held[-1], 1))
    return held


def add(*terms):
    return sum(term.astype(jnp.float32) for term in terms)


def line_reduce(parts, row):
    right = step_row(parts[3], 1, 0, 0)
    left = step_row(parts[3], -1, 3, 3)
    right = step_row(add(parts[2], right).astype(jnp.bfloat16), 1, 0, 1)
    left = step_row(add(parts[2], left).astype(jnp.bfloat16), -1, 2, 3)
    last_right = add(jnp.where(row == 1, parts[3], parts[1]), right).astype(jnp.bfloat16)
    last_left = add(jnp.where(row == 2, parts[3], parts[1]), left).astype(jnp.bfloat16)
    right = step_row(last_right, 1, 0, 2)
    left = step_row(last_left, -1, 1, 3)
    return add(parts[0], right, left), (last_right, last_left)


def line_gather(x):
    held = {0: x}
    for k in range(1, 4):
        held[-k] = step_row(held[1 - k], 1, k - 1, 2)
        held[k] = step_row(held[k - 1], -1, 1, 4 - k)
    return held


def finish_col(even, odd):
    pairs = add(even, swap_col(odd, 1)).astype(jnp.bfloat16)
    sums = [pairs[0]] + [swap_col(pairs[m], 2 * m) for m in range(1, even.shape[0])]
    return add(*sums).astype(jnp.bfloat16)


def rows_first(total):
    return jnp.swapaxes(total, 0, 1).reshape(total.shape[1], -1).astype(jnp.bfloat16)


def finish_row(sums):
    return rows_first(add(sums[0], *[swap_row(sums[t], t) for t in range(1, 4)]))


def activations(hidden, grad_activ):
    sigmoid = jax.nn.sigmoid(hidden)
    slope = sigmoid * (1.0 + hidden * (1.0 - sigmoid))
    return (grad_activ * slope).astype(jnp.bfloat16)


def silu(hidden):
    return (hidden * jax.nn.sigmoid(hidden)).astype(jnp.bfloat16)


def per_device(tokens, upstream, w_in, in_codes, w_out, out_codes):
    tile = w_in.shape[3]
    slots = w_in.shape[1]
    devices = lax.axis_size("col")
    cols = FF // (tile * devices)
    row, col = lax.axis_index("row"), lax.axis_index("col")

    def slot_info(codes):
        own = lax.dynamic_slice_in_dim(codes[0], row * slots, slots)
        place = jnp.stack([row, col]).astype(jnp.int32)
        return jnp.concatenate([place, own])

    info_in, info_out = slot_info(in_codes), slot_info(out_codes)
    w_in, w_out = w_in[0], w_out[0]
    tokens, upstream = own_pieces(tokens, tile), own_pieces(upstream, tile)
    args = (info_in, info_out, tokens, upstream, w_in, w_out, cols, devices)
    results = on_long_row(*args) if long_row() else on_line(*args)
    layer_out, grad_tokens, grad_w_in, grad_w_out = results
    return layer_out, grad_tokens, grad_w_in[None], grad_w_out[None]


def on_line(info_in, info_out, tokens, upstream, w_in, w_out, cols, devices):
    row, slots = info_in[0], w_in.shape[0]
    token_blocks = [tokens] + [swap_row(tokens, t) for t in range(1, 4)]
    up_blocks = [upstream] + [swap_row(upstream, t) for t in range(1, 4)]
    all_tokens = spread(token_blocks)
    up_blocks, all_tokens[-2] = lax.optimization_barrier((up_blocks, all_tokens[-2]))
    all_up = spread(up_blocks)
    parts = to_hidden(info_in, all_tokens, w_in, cols, False)
    hidden, last = line_reduce(parts, row)
    parts = to_hidden(info_out, all_up, w_out, cols, True)
    parts, _ = lax.optimization_barrier((parts, last))
    grad_activ, _ = line_reduce(parts, row)
    all_activ = line_gather(silu(hidden))
    all_grad = line_gather(activations(hidden, grad_activ))

    def wide_side(info, hs, w, flip, groups):
        sums = []
        for labels in groups:
            outs = from_hidden(info, hs, w, cols, flip, labels, devices)
            sums += [finish_col(*outs[2 * g:2 * g + 2]) for g in range(len(labels))]
        return finish_row(sums)

    layer_out = wide_side(info_out, all_activ, w_out, False, [(0, 1, 2, 3)])
    grad_w_out = slot_grads(info_out, all_up, all_activ, slots, cols, False)
    grad_tokens = wide_side(info_in, all_grad, w_in, True, [(0, 1), (2,), (3,)])
    grad_w_in = slot_grads(info_in, all_tokens, all_grad, slots, cols, True)
    return layer_out, grad_tokens, grad_w_in, grad_w_out


def on_long_row(info_in, info_out, tokens, upstream, w_in, w_out, cols, devices):
    slots, blocks = w_in.shape[0], lax.axis_size("row")

    def everywhere(x):
        return [lax.all_gather(lax.all_gather(x, "row"), "col")]

    def hidden_side(info, xs, w, flip):
        parts = jnp.stack(to_hidden(info, xs, w, cols, flip))
        return lax.psum_scatter(parts, "row", scatter_dimension=0).astype(jnp.float32)

    def wide_side(info, hs, w, flip):
        sums = []
        for chunk in chunks(blocks):
            if sums:
                hs, _ = lax.optimization_barrier((hs, sums[-1]))
            labels = range(blocks)[chunk]
            [parts] = from_hidden(info, hs, w, cols, flip, labels, devices)
            sums.append(lax.psum_scatter(parts, "col", scatter_dimension=0))
        total = lax.psum_scatter(jnp.concatenate(sums), "row", scatter_dimension=0)
        return rows_first(total)

    hidden = hidden_side(info_in, everywhere(tokens), w_in, False)
    upstream, hidden = lax.optimization_barrier((upstream, hidden))
    all_up = everywhere(upstream)
    grad_activ = hidden_side(info_out, all_up, w_out, True)
    all_activ = lax.all_gather(silu(hidden), "row")
    layer_out = wide_side(info_out, all_activ, w_out, False)
    grad_w_out = slot_grads(info_out, all_up, all_activ, slots, cols, False)
    held = (activations(hidden, grad_activ), tokens, layer_out, grad_w_out)
    grad_hidden, tokens, layer_out, grad_w_out = lax.optimization_barrier(held)
    all_grad = lax.all_gather(grad_hidden, "row")
    grad_tokens = wide_side(info_in, all_grad, w_in, True)
    grad_w_in = slot_grads(info_in, everywhere(tokens), all_grad, slots, cols, True)
    return layer_out, grad_tokens, grad_w_in, grad_w_out


def solution(mesh):
    placed = (
        P("row", "col"),
        P("row", "col"),
        P("col", "row", None, None),
        P("col", None),
        P("col", "row", None, None),
        P("col", None),
    )
    return jax.shard_map(
        per_device,
        mesh=mesh,
        in_specs=placed,
        out_specs=(
            P("row", "col"),
            P("row", "col"),
            P("col", "row", None, None),
            P("col", "row", None, None),
        ),
        check_vma=False,
    )
```

time: 324 us -> 339 us (1.046)
  waiting for transfers between devices: 158 us -> 108 us
  starting transfers between devices: 105 us -> 143 us
  Pallas kernels: 42.1 us -> 66.8 us
  other arithmetic: 4.9 us -> 10.6 us
    ppermute x28 -> x64, starting transfers between devices: 30.6 us -> 67.7 us  [swap_col(): return lax.ppermute(x, 'col', [(s, s ^ m) for s in range(count)])]
    pallas_call x6 -> x8, Pallas kernels: 42.1 us -> 66.8 us  [call(): pl.pallas_call(kernel, out_shape=out_shape, in_specs=[pl.BlockSpec(memory...]
    ppermute x28 -> x64, waiting for transfers between devices: 57.6 us -> 34.2 us  [swap_col(): return lax.ppermute(x, 'col', [(s, s ^ m) for s in range(count)])]
    ppermute x24, waiting for transfers between devices: 74.5 us -> 54.9 us  [step_row(): lax.ppermute(x, 'row', [(s, s + step) for s in range(first, last + 1)])]
    ppermute x12, waiting for transfers between devices: 25.9 us -> 18.9 us  [swap_row(): return lax.ppermute(x, 'row', [(s, s ^ t) for s in range(4)])]
    convert_element_type x15, other arithmetic: 2.82 us -> 6.49 us  [the longest x8 2.17 us: finish_col(): pairs = add(even, swap_col(odd, 1)).astype(jnp.bfloat16)]
    unnamed x94 -> x104, local copies, waits for them, and re-layouts: 8.08 us -> 6.89 us
  transfers between devices with their start and end apart: 64 -> 100, of which waited for: 27 -> 31; matrix products, arithmetic and copies ran while one was open for 2% -> 3% of each run, Pallas kernels for 13% -> 20%
where the time goes in v3:
time: 339 us; the launch traced here: 338 us
  starting transfers between devices  143 us (42%)
  waiting for transfers between devices  108 us (32%)
  Pallas kernels  66.8 us (20%)
  other arithmetic  10.6 us (3%)
  local copies, waits for them, and re-layouts  7.74 us (2%)
    ppermute x64, starting transfers between devices, swap_col(): return lax.ppermute(x, 'col', [(s, s ^ m) for s in range(count)])  67.7 us
    pallas_call x8, Pallas kernels, call(): pl.pallas_call(kernel, out_shape=out_shape, in_specs=[pl.BlockSpec(memory...  66.8 us
    ppermute x24, waiting for transfers between devices, step_row(): lax.ppermute(x, 'row', [(s, s + step) for s in range(first, last + 1)])  54.9 us
    ppermute x24, starting transfers between devices, step_row(): lax.ppermute(x, 'row', [(s, s + step) for s in range(first, last + 1)])  51.3 us
    ppermute x64, waiting for transfers between devices, swap_col(): return lax.ppermute(x, 'col', [(s, s ^ m) for s in range(count)])  34.2 us
    ppermute x12, starting transfers between devices, swap_row(): return lax.ppermute(x, 'row', [(s, s ^ t) for s in range(4)])  23.6 us
    ppermute x12, waiting for transfers between devices, swap_row(): return lax.ppermute(x, 'row', [(s, s ^ t) for s in range(4)])  18.9 us
    unnamed x104, local copies, waits for them, and re-layouts  6.89 us
  transfers between devices with their start and end apart: 100, of which 31 were waited for; matrix products, arithmetic and copies ran while one was open for 3% of the time, Pallas kernels for 20%

profile of v3, /device:TPU:0, one launch (start us, length us, event | category | flops | bytes accessed | tf_op | source)
XLA Modules:
  0.0 337.5 jit_solution(6580978387684927449)
XLA Ops:
  1.8 4.1 %collective-permute-start.9 = (bf16[2,128,256]{2,1,0:T(8,128)(2,1)S(1)}, bf16[2,128,256]{2,1,0:T(8,128)(2,1)S(1)}, u32[]{:S(2)}, u32[]{:S(2)}) collective-permute-start(bf16[2,128,256]{2,1,0:T(8,128)(2,1)S(1)} %bitcast.160), channel_id=1, source_target_pairs={{0,16},{8,24},{16,0},{24,8},{1,17},{9,25},{17,1},{25,9},{2,18},{10... | collective-permute-start | bytes 393224 | tf_op jit(solution)/shard_map/ppermute | solution.py:252
  38.4 4.2 %collective-permute-done.15 = bf16[2,128,256]{2,1,0:T(8,128)(2,1)S(1)} collective-permute-done((bf16[2,128,256]{2,1,0:T(8,128)(2,1)S(1)}, bf16[2,128,256]{2,1,0:T(8,128)(2,1)S(1)}, u32[]{:S(2)}, u32[]{:S(2)}) %collective-permute-start.15) | collective-permute-done | bytes 131104 | tf_op jit(solution)/shard_map/ppermute | solution.py:252
  42.6 5.1 %collective-permute-done.14 = bf16[2,128,256]{2,1,0:T(8,128)(2,1)} collective-permute-done((bf16[2,128,256]{2,1,0:T(8,128)(2,1)S(1)}, bf16[2,128,256]{2,1,0:T(8,128)(2,1)}, u32[]{:S(2)}, u32[]{:S(2)}) %collective-permute-start.14) | collective-permute-done | bytes 131104 | tf_op jit(solution)/shard_map/ppermute | solution.py:252
  68.1 8.8 %shard_map.93 = (bf16[8,128,256]{2,1,0:T(8,128)(2,1)}, bf16[8,128,256]{2,1,0:T(8,128)(2,1)}, bf16[8,128,256]{2,1,0:T(8,128)(2,1)}, bf16[8,128,256]{2,1,0:T(8,128)(2,1)}) custom-call(s32[18]{0:T(128)} %pad_add_fusion.2.info, bf16[16,256,256]{2,1,0:T(8,128)(2,1)} %bitcast.141, bf16[4,2,128,256]{3,2,1,0:T(8,128)(2,1)} %copy-done.2, ...), custom_call_target="tpu_custom_call" | custom-call | flops 1073741824 | bytes 8388608 | tf_op jit(solution)/shard_map/pallas_call | solution.py:163
  98.1 9.8 %shard_map.95 = (bf16[8,128,256]{2,1,0:T(8,128)(2,1)}, bf16[8,128,256]{2,1,0:T(8,128)(2,1)}, bf16[8,128,256]{2,1,0:T(8,128)(2,1)}, bf16[8,128,256]{2,1,0:T(8,128)(2,1)}) custom-call(s32[18]{0:T(128)} %pad_add_fusion.info, bf16[16,256,256]{2,1,0:T(8,128)(2,1)} %bitcast.145, bf16[4,2,128,256]{3,2,1,0:T(8,128)(2,1)} %copy-done.9, ...), custom_call_target="tpu_custom_call" | custom-call | flops 1073741824 | bytes 8388608 | tf_op jit(solution)/shard_map/pallas_call | solution.py:163
  110.4 5.9 %collective-permute-start.69 = (bf16[8,128,256]{2,1,0:T(8,128)(2,1)S(1)}, bf16[8,128,256]{2,1,0:T(8,128)(2,1)S(1)}, u32[]{:S(2)}, u32[]{:S(2)}) collective-permute-start(bf16[8,128,256]{2,1,0:T(8,128)(2,1)S(1)} %copy-done.42), channel_id=1, source_target_pairs={{0,8},{1,9},{2,10},{3,11},{4,12},{5,13},{6,14},{7,15}} | collective-permute-start | bytes 1572872 | tf_op jit(solution)/shard_map/ppermute | solution.py:256
  116.2 10.2 %collective-permute-done.69 = bf16[8,128,256]{2,1,0:T(8,128)(2,1)S(1)} collective-permute-done((bf16[8,128,256]{2,1,0:T(8,128)(2,1)S(1)}, bf16[8,128,256]{2,1,0:T(8,128)(2,1)S(1)}, u32[]{:S(2)}, u32[]{:S(2)}) %collective-permute-start.69) | collective-permute-done | bytes 524320 | tf_op jit(solution)/shard_map/ppermute | solution.py:256
  126.7 4.5 %collective-permute-start.70 = (bf16[8,128,256]{2,1,0:T(8,128)(2,1)S(1)}, bf16[8,128,256]{2,1,0:T(8,128)(2,1)S(1)}, u32[]{:S(2)}, u32[]{:S(2)}) collective-permute-start(bf16[8,128,256]{2,1,0:T(8,128)(2,1)S(1)} %get-tuple-element.92), channel_id=1, source_target_pairs={{0,8},{8,16},{1,9},{9,17},{2,10},{10,18},{3,11},{11,19},{4,12},{12... | collective-permute-start | bytes 1572872 | tf_op jit(solution)/shard_map/ppermute | solution.py:256
  135.8 7.7 %collective-permute-done.70 = bf16[8,128,256]{2,1,0:T(8,128)(2,1)S(1)} collective-permute-done((bf16[8,128,256]{2,1,0:T(8,128)(2,1)S(1)}, bf16[8,128,256]{2,1,0:T(8,128)(2,1)S(1)}, u32[]{:S(2)}, u32[]{:S(2)}) %collective-permute-start.70) | collective-permute-done | bytes 524320 | tf_op jit(solution)/shard_map/ppermute | solution.py:256
  143.9 6.4 %collective-permute-start.71 = (bf16[8,128,256]{2,1,0:T(8,128)(2,1)S(1)}, bf16[8,128,256]{2,1,0:T(8,128)(2,1)S(1)}, u32[]{:S(2)}, u32[]{:S(2)}) collective-permute-start(bf16[8,128,256]{2,1,0:T(8,128)(2,1)S(1)} %get-tuple-element.76), channel_id=1, source_target_pairs={{0,8},{8,16},{16,24},{1,9},{9,17},{17,25},{2,10},{10,18},{18,26},{... | collective-permute-start | bytes 1572872 | tf_op jit(solution)/shard_map/ppermute | solution.py:256
  154.8 8.1 %collective-permute-done.71 = bf16[8,128,256]{2,1,0:T(8,128)(2,1)S(1)} collective-permute-done((bf16[8,128,256]{2,1,0:T(8,128)(2,1)S(1)}, bf16[8,128,256]{2,1,0:T(8,128)(2,1)S(1)}, u32[]{:S(2)}, u32[]{:S(2)}) %collective-permute-start.71) | collective-permute-done | bytes 524320 | tf_op jit(solution)/shard_map/ppermute | solution.py:256
  165.0 7.4 %collective-permute-start.75 = (bf16[8,128,256]{2,1,0:T(8,128)(2,1)S(1)}, bf16[8,128,256]{2,1,0:T(8,128)(2,1)S(1)}, u32[]{:S(2)}, u32[]{:S(2)}) collective-permute-start(bf16[8,128,256]{2,1,0:T(8,128)(2,1)S(1)} %get-tuple-element.74.refs_1_.refs_11_), channel_id=1, source_target_pairs={{0,8},{8,16},{16,24},{1,9},{9,17},{17,25},{2,10},{10,18},{18,26},{... | collective-permute-start | bytes 1572872 | tf_op jit(solution)/shard_map/ppermute | solution.py:256
  173.7 4.6 %collective-permute-start.28 = (bf16[8,128,256]{2,1,0:T(8,128)(2,1)S(1)}, bf16[8,128,256]{2,1,0:T(8,128)(2,1)S(1)}, u32[]{:S(2)}, u32[]{:S(2)}) collective-permute-start(bf16[8,128,256]{2,1,0:T(8,128)(2,1)S(1)} %get-tuple-element.75.refs_3_.refs_11_), channel_id=1, source_target_pairs={{0,8},{8,16},{16,24},{1,9},{9,17},{17,25},{2,10},{10,18},{18,26},{... | collective-permute-start | bytes 1572872 | tf_op jit(solution)/shard_map/ppermute | solution.py:256
  178.3 5.0 %collective-permute-done.76.refs_2_.refs_12_ = bf16[8,128,256]{2,1,0:T(8,128)(2,1)S(1)} collective-permute-done((bf16[8,128,256]{2,1,0:T(8,128)(2,1)S(1)}, bf16[8,128,256]{2,1,0:T(8,128)(2,1)S(1)}, u32[]{:S(2)}, u32[]{:S(2)}) %collective-permute-start.76) | collective-permute-done | bytes 524320 | tf_op jit(solution)/shard_map/ppermute | solution.py:256
  185.5 7.3 %shard_map.96 = (bf16[4,2,128,256]{3,2,1,0:T(8,128)(2,1)}, bf16[4,2,128,256]{3,2,1,0:T(8,128)(2,1)}, bf16[4,2,128,256]{3,2,1,0:T(8,128)(2,1)}, bf16[4,2,128,256]{3,2,1,0:T(8,128)(2,1)}) custom-call(s32[18]{0:T(128)} %pad_add_fusion.2.info, bf16[16,256,256]{2,1,0:T(8,128)(2,1)} %bitcast.142, bf16[8,128,256]{2,1,0:T(8,128)(2,1)} %copy-done.11, ...), custom_call_target="tpu_custom_call" | custom-call | flops 536870912 | bytes 8388608 | tf_op jit(solution)/shard_map/pallas_call | solution.py:163
  199.0 11.0 %collective-permute-done.87.refs_1_.refs_13_ = bf16[8,128,256]{2,1,0:T(8,128)(2,1)S(1)} collective-permute-done((bf16[8,128,256]{2,1,0:T(8,128)(2,1)}, bf16[8,128,256]{2,1,0:T(8,128)(2,1)S(1)}, u32[]{:S(2)}, u32[]{:S(2)}) %collective-permute-start.87) | collective-permute-done | bytes 524320 | tf_op jit(solution)/shard_map/ppermute | solution.py:256
  213.3 6.4 %shard_map.97 = (bf16[4,2,128,256]{3,2,1,0:T(8,128)(2,1)}, bf16[4,2,128,256]{3,2,1,0:T(8,128)(2,1)}) custom-call(s32[18]{0:T(128)} %pad_add_fusion.2.info, bf16[16,256,256]{2,1,0:T(8,128)(2,1)} %bitcast.143, bf16[8,128,256]{2,1,0:T(8,128)(2,1)} %copy-done.28, bf16[8,128,256]{2,1,0:T(8,128)(2,1)} %copy-done.26), custom_call_target="tpu_custom_call" | custom-call | flops 268435456 | bytes 8388608 | tf_op jit(solution)/shard_map/pallas_call | solution.py:163
  229.3 8.2 %collective-permute-done.94.refs_3_.refs_14_ = bf16[8,128,256]{2,1,0:T(8,128)(2,1)S(1)} collective-permute-done((bf16[8,128,256]{2,1,0:T(8,128)(2,1)S(1)}, bf16[8,128,256]{2,1,0:T(8,128)(2,1)S(1)}, u32[]{:S(2)}, u32[]{:S(2)}) %collective-permute-start.94) | collective-permute-done | bytes 524320 | tf_op jit(solution)/shard_map/ppermute | solution.py:256
  239.2 6.4 %shard_map.98 = (bf16[4,2,128,256]{3,2,1,0:T(8,128)(2,1)}, bf16[4,2,128,256]{3,2,1,0:T(8,128)(2,1)}) custom-call(s32[18]{0:T(128)} %pad_add_fusion.2.info, bf16[16,256,256]{2,1,0:T(8,128)(2,1)} %bitcast.144, bf16[8,128,256]{2,1,0:T(8,128)(2,1)} %copy-done.25, bf16[8,128,256]{2,1,0:T(8,128)(2,1)} %copy-done.11, bf16[8,128,256]{2,1,0:T(8,128)(2,1)} %copy-done.10, ...), custom_call_target="tpu_custom_call" | custom-call | flops 268435456 | bytes 8388608 | tf_op jit(solution)/shard_map/pallas_call | solution.py:163
  245.7 9.2 %shard_map.99 = bf16[16,256,256]{2,1,0:T(8,128)(2,1)} custom-call(s32[18]{0:T(128)} %pad_add_fusion.2.info, bf16[4,2,128,256]{3,2,1,0:T(8,128)(2,1)} %copy-done.2, bf16[4,2,128,256]{3,2,1,0:T(8,128)(2,1)} %copy-done.14, bf16[4,2,128,256]{3,2,1,0:T(8,128)(2,1)} %copy-done.3, bf16[4,2,128,256]{3,2,1,0:T(8,128)(2,1)} %collective-permute-done.8.refs_3_, ...), custom_call_target="tpu_custom_call" | custom-call | flops 1073741824 | bytes 8388608 | tf_op jit(solution)/shard_map/pallas_call | solution.py:163
  258.2 9.7 %shard_map.100 = bf16[16,256,256]{2,1,0:T(8,128)(2,1)} custom-call(s32[18]{0:T(128)} %pad_add_fusion.info, bf16[4,2,128,256]{3,2,1,0:T(8,128)(2,1)} %copy-done.9, bf16[4,2,128,256]{3,2,1,0:T(8,128)(2,1)} %collective-permute-done.56.refs_1_, bf16[4,2,128,256]{3,2,1,0:T(8,128)(2,1)} %copy-done.6, bf16[4,2,128,256]{3,2,1,0:T(8,128)(2,1)} %collective-permute-done.60.refs_3_, ...), custom_call_target="tpu_custom_call" | custom-call | flops 1073741824 | bytes 8388608 | tf_op jit(solution)/shard_map/pallas_call | solution.py:163
  267.9 9.1 %shard_map.94 = (bf16[4,2,128,256]{3,2,1,0:T(8,128)(2,1)}, bf16[4,2,128,256]{3,2,1,0:T(8,128)(2,1)}, bf16[4,2,128,256]{3,2,1,0:T(8,128)(2,1)}, bf16[4,2,128,256]...) custom-call(s32[18]{0:T(128)} %pad_add_fusion.info, ...), custom_call_target="tpu_custom_call" | custom-call | flops 1073741824 | bytes 8388608 | tf_op jit(solution)/shard_map/pallas_call | solution.py:163
  287.8 4.5 %collective-permute-done.98 = bf16[2,128,256]{2,1,0:T(8,128)(2,1)S(1)} collective-permute-done((bf16[2,128,256]{2,1,0:T(8,128)(2,1)S(1)}, bf16[2,128,256]{2,1,0:T(8,128)(2,1)S(1)}, u32[]{:S(2)}, u32[]{:S(2)}) %collective-permute-start.98) | collective-permute-done | bytes 131104 | tf_op jit(solution)/shard_map/ppermute | solution.py:248
  311.4 6.9 %collective-permute-start.92 = (bf16[2,128,256]{2,1,0:T(8,128)(2,1)S(1)}, bf16[2,128,256]{2,1,0:T(8,128)(2,1)S(1)}, u32[]{:S(2)}, u32[]{:S(2)}) collective-permute-start(bf16[2,128,256]{2,1,0:T(8,128)(2,1)S(1)} %fusion.9), channel_id=1, source_target_pairs={{0,16},{8,24},{16,0},{24,8},{1,17},{9,25},{17,1},{25,9},{2,18},{10... | collective-permute-start | bytes 393224 | tf_op jit(solution)/shard_map/ppermute | solution.py:252
  (333 shorter events, 165.1 us)
Async XLA Ops:
  35.0 27.4 %collective-permute-start.3 = (bf16[4,2,128,256]{3,2,1,0:T(8,128)(2,1)S(1)}, bf16[4,2,128,256]{3,2,1,0:T(8,128)(2,1)S(1)}, u32[]{:S(2)}, u32[]{:S(2)}) collective-permute-start(bf16[4,2,128,256]{3,2,1,0:T(8,128)(2,1)S(1)} %pad_maximum_fusion.refs_0_), channel_id=1, source_target_pairs={{0,1},{1,0},{2,3},{3,2},{4,5},{5,4},{6,7},{7,6},{8,9},{9,8},{10,11... | collective-permute-start | bytes 1572872 | tf_op jit(solution)/shard_map/ppermute | solution.py:248
  35.1 28.6 %collective-permute-start.21 = (bf16[4,2,128,256]{3,2,1,0:T(8,128)(2,1)S(1)}, bf16[4,2,128,256]{3,2,1,0:T(8,128)(2,1)S(1)}, u32[]{:S(2)}, u32[]{:S(2)}) collective-permute-start(bf16[4,2,128,256]{3,2,1,0:T(8,128)(2,1)S(1)} %pad_maximum_fusion.3.refs_6_), channel_id=1, source_target_pairs={{0,1},{1,0},{2,3},{3,2},{4,5},{5,4},{6,7},{7,6},{8,9},{9,8},{10,11... | collective-permute-start | bytes 1572872 | tf_op jit(solution)/shard_map/ppermute | solution.py:248
  35.6 28.4 %collective-permute-start.8 = (bf16[4,2,128,256]{3,2,1,0:T(8,128)(2,1)S(1)}, bf16[4,2,128,256]{3,2,1,0:T(8,128)(2,1)}, u32[]{:S(2)}, u32[]{:S(2)}) collective-permute-start(bf16[4,2,128,256]{3,2,1,0:T(8,128)(2,1)S(1)} %pad_maximum_fusion.1.refs_2_), channel_id=1, source_target_pairs={{0,1},{1,0},{2,3},{3,2},{4,5},{5,4},{6,7},{7,6},{8,9},{9,8},{10,11... | collective-permute-start | bytes 1572872 | tf_op jit(solution)/shard_map/ppermute | solution.py:248
  38.4 27.6 %collective-permute-start.13 = (bf16[4,2,128,256]{3,2,1,0:T(8,128)(2,1)S(1)}, bf16[4,2,128,256]{3,2,1,0:T(8,128)(2,1)}, u32[]{:S(2)}, u32[]{:S(2)}) collective-permute-start(bf16[4,2,128,256]{3,2,1,0:T(8,128)(2,1)S(1)} %pad_maximum_fusion.2.refs_4_), channel_id=1, source_target_pairs={{0,1},{1,0},{2,3},{3,2},{4,5},{5,4},{6,7},{7,6},{8,9},{9,8},{10,11... | collective-permute-start | bytes 1572872 | tf_op jit(solution)/shard_map/ppermute | solution.py:248
  64.0 17.9 %collective-permute-start.62 = (bf16[2,128,256]{2,1,0:T(8,128)(2,1)S(1)}, bf16[2,128,256]{2,1,0:T(8,128)(2,1)S(1)}, u32[]{:S(2)}, u32[]{:S(2)}) collective-permute-start(bf16[2,128,256]{2,1,0:T(8,128)(2,1)S(1)} %collective-permute-done.15), channel_id=1, source_target_pairs={{0,4},{1,5},{2,6},{3,7},{4,0},{5,1},{6,2},{7,3},{8,12},{9,13},{10,... | collective-permute-start | bytes 393224 | tf_op jit(solution)/shard_map/ppermute | solution.py:248
  131.9 22.9 %collective-permute-start.24 = (bf16[8,128,256]{2,1,0:T(8,128)(2,1)S(1)}, bf16[8,128,256]{2,1,0:T(8,128)(2,1)S(1)}, u32[]{:S(2)}, u32[]{:S(2)}) collective-permute-start(bf16[8,128,256]{2,1,0:T(8,128)(2,1)S(1)} %get-tuple-element.78), channel_id=1, source_target_pairs={{0,8},{8,16},{16,24},{1,9},{9,17},{17,25},{2,10},{10,18},{18,26},{... | collective-permute-start | bytes 1572872 | tf_op jit(solution)/shard_map/ppermute | solution.py:256
  134.5 20.3 %collective-permute-start.27 = (bf16[8,128,256]{2,1,0:T(8,128)(2,1)S(1)}, bf16[8,128,256]{2,1,0:T(8,128)(2,1)S(1)}, u32[]{:S(2)}, u32[]{:S(2)}) collective-permute-start(bf16[8,128,256]{2,1,0:T(8,128)(2,1)S(1)} %get-tuple-element.79), channel_id=1, source_target_pairs={{8,0},{16,8},{24,16},{9,1},{17,9},{25,17},{10,2},{18,10},{26,18},{... | collective-permute-start | bytes 1572872 | tf_op jit(solution)/shard_map/ppermute | solution.py:256
  143.9 19.0 %collective-permute-start.71 = (bf16[8,128,256]{2,1,0:T(8,128)(2,1)S(1)}, bf16[8,128,256]{2,1,0:T(8,128)(2,1)S(1)}, u32[]{:S(2)}, u32[]{:S(2)}) collective-permute-start(bf16[8,128,256]{2,1,0:T(8,128)(2,1)S(1)} %get-tuple-element.76), channel_id=1, source_target_pairs={{0,8},{8,16},{16,24},{1,9},{9,17},{17,25},{2,10},{10,18},{18,26},{... | collective-permute-start | bytes 1572872 | tf_op jit(solution)/shard_map/ppermute | solution.py:256
  163.7 19.6 %collective-permute-start.76 = (bf16[8,128,256]{2,1,0:T(8,128)(2,1)S(1)}, bf16[8,128,256]{2,1,0:T(8,128)(2,1)S(1)}, u32[]{:S(2)}, u32[]{:S(2)}) collective-permute-start(bf16[8,128,256]{2,1,0:T(8,128)(2,1)S(1)} %get-tuple-element.74.refs_1_.refs_11_), channel_id=1, source_target_pairs={{8,0},{16,8},{24,16},{9,1},{17,9},{25,17},{10,2},{18,10},{26,18},{... | collective-permute-start | bytes 1572872 | tf_op jit(solution)/shard_map/ppermute | solution.py:256
  165.0 19.7 %collective-permute-start.75 = (bf16[8,128,256]{2,1,0:T(8,128)(2,1)S(1)}, bf16[8,128,256]{2,1,0:T(8,128)(2,1)S(1)}, u32[]{:S(2)}, u32[]{:S(2)}) collective-permute-start(bf16[8,128,256]{2,1,0:T(8,128)(2,1)S(1)} %get-tuple-element.74.refs_1_.refs_11_), channel_id=1, source_target_pairs={{0,8},{8,16},{16,24},{1,9},{9,17},{17,25},{2,10},{10,18},{18,26},{... | collective-permute-start | bytes 1572872 | tf_op jit(solution)/shard_map/ppermute | solution.py:256
  172.4 22.6 %collective-permute-start.31 = (bf16[8,128,256]{2,1,0:T(8,128)(2,1)S(1)}, bf16[8,128,256]{2,1,0:T(8,128)(2,1)S(1)}, u32[]{:S(2)}, u32[]{:S(2)}) collective-permute-start(bf16[8,128,256]{2,1,0:T(8,128)(2,1)S(1)} %get-tuple-element.75.refs_3_.refs_11_), channel_id=1, source_target_pairs={{8,0},{16,8},{24,16},{9,1},{17,9},{25,17},{10,2},{18,10},{26,18},{... | collective-permute-start | bytes 1572872 | tf_op jit(solution)/shard_map/ppermute | solution.py:256
  173.7 21.8 %collective-permute-start.28 = (bf16[8,128,256]{2,1,0:T(8,128)(2,1)S(1)}, bf16[8,128,256]{2,1,0:T(8,128)(2,1)S(1)}, u32[]{:S(2)}, u32[]{:S(2)}) collective-permute-start(bf16[8,128,256]{2,1,0:T(8,128)(2,1)S(1)} %get-tuple-element.75.refs_3_.refs_11_), channel_id=1, source_target_pairs={{0,8},{8,16},{16,24},{1,9},{9,17},{17,25},{2,10},{10,18},{18,26},{... | collective-permute-start | bytes 1572872 | tf_op jit(solution)/shard_map/ppermute | solution.py:256
  193.0 16.9 %collective-permute-start.87 = (bf16[8,128,256]{2,1,0:T(8,128)(2,1)}, bf16[8,128,256]{2,1,0:T(8,128)(2,1)S(1)}, u32[]{:S(2)}, u32[]{:S(2)}) collective-permute-start(bf16[8,128,256]{2,1,0:T(8,128)(2,1)} %copy-done.10), channel_id=1, source_target_pairs={{8,0},{16,8},{9,1},{17,9},{10,2},{18,10},{11,3},{19,11},{12,4},{20... | collective-permute-start | bytes 1572872 | tf_op jit(solution)/shard_map/ppermute | solution.py:256
  195.0 24.8 %collective-permute-start.77 = (bf16[4,2,128,256]{3,2,1,0:T(8,128)(2,1)}, bf16[4,2,128,256]{3,2,1,0:T(8,128)(2,1)S(1)}, u32[]{:S(2)}, u32[]{:S(2)}) collective-permute-start(bf16[4,2,128,256]{3,2,1,0:T(8,128)(2,1)} %get-tuple-element.63), channel_id=1, source_target_pairs={{0,1},{1,0},{2,3},{3,2},{4,5},{5,4},{6,7},{7,6},{8,9},{9,8},{10,11... | collective-permute-start | bytes 1572872 | tf_op jit(solution)/shard_map/ppermute | solution.py:248
  195.6 31.2 %collective-permute-start.32 = (bf16[8,128,256]{2,1,0:T(8,128)(2,1)S(1)}, bf16[8,128,256]{2,1,0:T(8,128)(2,1)S(1)}, u32[]{:S(2)}, u32[]{:S(2)}) collective-permute-start(bf16[8,128,256]{2,1,0:T(8,128)(2,1)S(1)} %collective-permute-done.31.refs_4_.refs_12_), channel_id=1, source_target_pairs={{8,0},{16,8},{9,1},{17,9},{10,2},{18,10},{11,3},{19,11},{12,4},{20... | collective-permute-start | bytes 1572872 | tf_op jit(solution)/shard_map/ppermute | solution.py:256
  196.9 30.3 %collective-permute-start.29 = (bf16[8,128,256]{2,1,0:T(8,128)(2,1)S(1)}, bf16[8,128,256]{2,1,0:T(8,128)(2,1)S(1)}, u32[]{:S(2)}, u32[]{:S(2)}) collective-permute-start(bf16[8,128,256]{2,1,0:T(8,128)(2,1)S(1)} %collective-permute-done.28.refs_2_.refs_10_), channel_id=1, source_target_pairs={{8,16},{16,24},{9,17},{17,25},{10,18},{18,26},{11,19},{19,27},{12,... | collective-permute-start | bytes 1572872 | tf_op jit(solution)/shard_map/ppermute | solution.py:256
  226.8 82.5 %collective-permute-start.78 = (bf16[2,128,256]{2,1,0:T(8,128)(2,1)S(1)}, bf16[2,128,256]{2,1,0:T(8,128)(2,1)S(1)}, u32[]{:S(2)}, u32[]{:S(2)}) collective-permute-start(bf16[2,128,256]{2,1,0:T(8,128)(2,1)S(1)} %get-tuple-element.80), channel_id=1, source_target_pairs={{0,2},{1,3},{2,0},{3,1},{4,6},{5,7},{6,4},{7,5},{8,10},{9,11},{10,... | collective-permute-start | bytes 393224 | tf_op jit(solution)/shard_map/ppermute | solution.py:248
  227.1 27.8 %collective-permute-start.33 = (bf16[8,128,256]{2,1,0:T(8,128)(2,1)S(1)}, bf16[8,128,256]{2,1,0:T(8,128)(2,1)S(1)}, u32[]{:S(2)}, u32[]{:S(2)}) collective-permute-start(bf16[8,128,256]{2,1,0:T(8,128)(2,1)S(1)} %collective-permute-done.32.refs_5_.refs_13_), channel_id=1, source_target_pairs={{8,0},{9,1},{10,2},{11,3},{12,4},{13,5},{14,6},{15,7}} | collective-permute-start | bytes 1572872 | tf_op jit(solution)/shard_map/ppermute | solution.py:256
  228.4 29.0 %collective-permute-start.30 = (bf16[8,128,256]{2,1,0:T(8,128)(2,1)S(1)}, bf16[8,128,256]{2,1,0:T(8,128)(2,1)S(1)}, u32[]{:S(2)}, u32[]{:S(2)}) collective-permute-start(bf16[8,128,256]{2,1,0:T(8,128)(2,1)S(1)} %collective-permute-done.29.refs_1_.refs_9_), channel_id=1, source_target_pairs={{16,24},{17,25},{18,26},{19,27},{20,28},{21,29},{22,30},{23,31}} | collective-permute-start | bytes 1572872 | tf_op jit(solution)/shard_map/ppermute | solution.py:256
  237.6 39.5 %collective-permute-start.89 = (bf16[2,128,256]{2,1,0:T(8,128)(2,1)S(1)}, bf16[2,128,256]{2,1,0:T(8,128)(2,1)S(1)}, u32[]{:S(2)}, u32[]{:S(2)}) collective-permute-start(bf16[2,128,256]{2,1,0:T(8,128)(2,1)S(1)} %get-tuple-element.86), channel_id=1, source_target_pairs={{0,2},{1,3},{2,0},{3,1},{4,6},{5,7},{6,4},{7,5},{8,10},{9,11},{10,... | collective-permute-start | bytes 393224 | tf_op jit(solution)/shard_map/ppermute | solution.py:248
  245.6 33.5 %collective-permute-start.95 = (bf16[4,2,128,256]{3,2,1,0:T(8,128)(2,1)}, bf16[4,2,128,256]{3,2,1,0:T(8,128)(2,1)S(1)}, u32[]{:S(2)}, u32[]{:S(2)}) collective-permute-start(bf16[4,2,128,256]{3,2,1,0:T(8,128)(2,1)} %get-tuple-element.69), channel_id=1, source_target_pairs={{0,1},{1,0},{2,3},{3,2},{4,5},{5,4},{6,7},{7,6},{8,9},{9,8},{10,11... | collective-permute-start | bytes 1572872 | tf_op jit(solution)/shard_map/ppermute | solution.py:248
  254.9 23.6 %collective-permute-start.91 = (bf16[2,128,256]{2,1,0:T(8,128)(2,1)S(1)}, bf16[2,128,256]{2,1,0:T(8,128)(2,1)S(1)}, u32[]{:S(2)}, u32[]{:S(2)}) collective-permute-start(bf16[2,128,256]{2,1,0:T(8,128)(2,1)S(1)} %get-tuple-element.87), channel_id=1, source_target_pairs={{0,6},{1,7},{2,4},{3,5},{4,2},{5,3},{6,0},{7,1},{8,14},{9,15},{10,... | collective-permute-start | bytes 393224 | tf_op jit(solution)/shard_map/ppermute | solution.py:248
  257.4 21.2 %collective-permute-start.90 = (bf16[2,128,256]{2,1,0:T(8,128)(2,1)S(1)}, bf16[2,128,256]{2,1,0:T(8,128)(2,1)S(1)}, u32[]{:S(2)}, u32[]{:S(2)}) collective-permute-start(bf16[2,128,256]{2,1,0:T(8,128)(2,1)S(1)} %get-tuple-element.88), channel_id=1, source_target_pairs={{0,4},{1,5},{2,6},{3,7},{4,0},{5,1},{6,2},{7,3},{8,12},{9,13},{10,... | collective-permute-start | bytes 393224 | tf_op jit(solution)/shard_map/ppermute | solution.py:248
  277.1 34.3 %collective-permute-start.80 = (bf16[2,128,256]{2,1,0:T(8,128)(2,1)S(1)}, bf16[2,128,256]{2,1,0:T(8,128)(2,1)S(1)}, u32[]{:S(2)}, u32[]{:S(2)}) collective-permute-start(bf16[2,128,256]{2,1,0:T(8,128)(2,1)S(1)} %get-tuple-element.81), channel_id=1, source_target_pairs={{0,6},{1,7},{2,4},{3,5},{4,2},{5,3},{6,0},{7,1},{8,14},{9,15},{10,... | collective-permute-start | bytes 393224 | tf_op jit(solution)/shard_map/ppermute | solution.py:248
  (126 other events, 1425.4 us)

commit v4 on v3

--- a/solution.py
+++ b/solution.py
@@ -41,26 +41,17 @@
 
 def wide_copies(refs, held, sems, col):
     copies = []
-
-    def copy(source, owner, q, pieces, block):
-        unit = source.shape[-1]
-        at, lanes = tile_part(held, owner, q, pieces, unit)
-        target = held.at[at, block, :, lanes]
-        copies.append(pltpu.make_async_copy(source, target, sems.at[len(copies)]))
-        copies[-1].start()
-
     if len(refs) == 1:
-        devices, _, pieces, _, _ = refs[0].shape
-        for owner in range(devices):
-            for q in range(pieces):
-                copy(refs[0].at[owner, :, q], owner, q, pieces, slice(None))
-        return copies
-    for at, ref in enumerate(refs):
-        half, pieces, _, _ = ref.shape
-        for m in range(half):
-            owner = lax.bitwise_xor(col, 2 * m + at % 2)
-            for q in range(pieces):
-                copy(ref.at[m, q], owner, q, pieces, at // 2)
+        pairs = [(m, refs[0].at[m]) for m in range(refs[0].shape[0])]
+    else:
+        pairs = [(lax.bitwise_xor(col, m), ref) for m, ref in enumerate(refs)]
+    for owner, ref in pairs:
+        _, pieces, _, unit = ref.shape
+        for q in range(pieces):
+            tile, lanes = tile_part(held, owner, q, pieces, unit)
+            target = held.at[tile, :, :, lanes]
+            copies.append(pltpu.make_async_copy(ref.at[:, q], target, sems.at[len(copies)]))
+            copies[-1].start()
     return copies
 
 
@@ -113,7 +104,7 @@
 
 
 def from_hidden_kernel(cols, flip, names, labels, info, w_ref, *refs):
-    count = 1 if names is None else 2 * len(labels)
+    count = 1 if names is None else 2
     h_refs, outs, (h, acc, sems) = refs[:-3 - count], refs[-3 - count:-3], refs[-3:]
     copies = hidden_copies(h_refs, names, labels, h, sems, info[0])
     acc[...] = jnp.zeros_like(acc)
@@ -129,14 +120,10 @@
     for at, out in enumerate(outs):
         pieces, unit = out.shape[-3], out.shape[-1]
         for m in range(out.shape[0]):
+            owner = m if names is None else lax.bitwise_xor(info[1], 2 * m + at)
             for q in range(pieces):
-                if names is None:
-                    tile, lanes = tile_part(acc, m, q, pieces, unit)
-                    out[m, :, q] = acc[tile, :, :, lanes].astype(out.dtype)
-                else:
-                    owner = lax.bitwise_xor(info[1], 2 * m + at % 2)
-                    tile, lanes = tile_part(acc, owner, q, pieces, unit)
-                    out[m, q] = acc[tile, at // 2, :, lanes].astype(out.dtype)
+                tile, lanes = tile_part(acc, owner, q, pieces, unit)
+                out[m, :, q] = acc[tile, :, :, lanes].astype(out.dtype)
 
 
 def grad_kernel(cols, flip, wides, names, labels, info, *refs):
@@ -172,10 +159,8 @@
 
 
 def wide_scratch(blocks, rows, tile, unit):
-    pieces = D // unit
-    count = pieces if long_row() else pieces * blocks
     held = pltpu.VMEM((D // tile, blocks, rows, tile), jnp.bfloat16)
-    return [held, pltpu.SemaphoreType.DMA((count,))]
+    return [held, pltpu.SemaphoreType.DMA((D // unit,))]
 
 
 def to_hidden(info, xs, w, cols, flip):
@@ -204,10 +189,11 @@
     slots, group = w.shape[0], len(labels)
     unit = min(tile, D // devices)
     pieces = D // devices // unit
+    shape = (group, pieces, rows, unit)
     if names is None:
-        outs = [jax.ShapeDtypeStruct((devices, group, pieces, rows, unit), jnp.bfloat16)]
+        outs = [jax.ShapeDtypeStruct((devices, *shape), jnp.bfloat16)]
     else:
-        outs = [jax.ShapeDtypeStruct((devices // 2, pieces, rows, unit), jnp.bfloat16)] * (2 * group)
+        outs = [jax.ShapeDtypeStruct((devices // 2, *shape), jnp.bfloat16)] * 2
     scratch = [
         pltpu.VMEM((cols, group, rows, tile), jnp.bfloat16),
         pltpu.VMEM((D // tile, group, rows, tile), jnp.float32),
@@ -262,12 +248,14 @@
     return jnp.swapaxes(x.reshape(rows, width // unit, unit), 0, 1)
 
 
-def spread(blocks):
+def spread(mine, after):
+    mine = jnp.stack(mine)
+    if after is not None:
+        mine, _ = lax.optimization_barrier((mine, after))
     held = []
-    for own in blocks:
-        even = [swap_col(own, m) if m else own for m in range(0, lax.axis_size("col"), 2)]
-        held.append(jnp.stack(even))
-        held.append(swap_col(held[-1], 1))
+    for m in range(0, lax.axis_size("col"), 2):
+        held.append(swap_col(mine, m) if m else mine)
+        held.append(swap_col(held[m], 1))
     return held
 
 
@@ -284,7 +272,7 @@
     last_left = add(jnp.where(row == 2, parts[3], parts[1]), left).astype(jnp.bfloat16)
     right = step_row(last_right, 1, 0, 2)
     left = step_row(last_left, -1, 1, 3)
-    return add(parts[0], right, left), (last_right, last_left)
+    return add(parts[0], right, left)
 
 
 def line_gather(x):
@@ -344,27 +332,25 @@
     row, slots = info_in[0], w_in.shape[0]
     token_blocks = [tokens] + [swap_row(tokens, t) for t in range(1, 4)]
     up_blocks = [upstream] + [swap_row(upstream, t) for t in range(1, 4)]
-    all_tokens = spread(token_blocks)
-    up_blocks, all_tokens[-2] = lax.optimization_barrier((up_blocks, all_tokens[-2]))
-    all_up = spread(up_blocks)
+    all_tokens = spread(token_blocks, None)
+    all_up = spread(up_blocks, tuple(all_tokens[2::2]))
     parts = to_hidden(info_in, all_tokens, w_in, cols, False)
-    hidden, last = line_reduce(parts, row)
+    hidden = line_reduce(parts, row)
     parts = to_hidden(info_out, all_up, w_out, cols, True)
-    parts, _ = lax.optimization_barrier((parts, last))
-    grad_activ, _ = line_reduce(parts, row)
+    grad_activ = line_reduce(parts, row)
     all_activ = line_gather(silu(hidden))
     all_grad = line_gather(activations(hidden, grad_activ))
 
     def wide_side(info, hs, w, flip, groups):
         sums = []
         for labels in groups:
-            outs = from_hidden(info, hs, w, cols, flip, labels, devices)
-            sums += [finish_col(*outs[2 * g:2 * g + 2]) for g in range(len(labels))]
+            total = finish_col(*from_hidden(info, hs, w, cols, flip, labels, devices))
+            sums += [total[g] for g in range(len(labels))]
         return finish_row(sums)
 
     layer_out = wide_side(info_out, all_activ, w_out, False, [(0, 1, 2, 3)])
     grad_w_out = slot_grads(info_out, all_up, all_activ, slots, cols, False)
-    grad_tokens = wide_side(info_in, all_grad, w_in, True, [(0, 1), (2,), (3,)])
+    grad_tokens = wide_side(info_in, all_grad, w_in, True, [(0, 1, 2, 3)])
     grad_w_in = slot_grads(info_in, all_tokens, all_grad, slots, cols, True)
     return layer_out, grad_tokens, grad_w_in, grad_w_out
 

time: 339 us -> 330 us (0.973)
  waiting for transfers between devices: 108 us -> 180 us
  starting transfers between devices: 143 us -> 88.7 us
  Pallas kernels: 66.8 us -> 42 us
    ppermute x64 -> x22, starting transfers between devices: 67.7 us -> 22 us  [swap_col(): return lax.ppermute(x, 'col', [(s, s ^ m) for s in range(count)])]
    ppermute x24, waiting for transfers between devices: 54.9 us -> 89.1 us  [step_row(): lax.ppermute(x, 'row', [(s, s + step) for s in range(first, last + 1)])]
    ppermute x64 -> x22, waiting for transfers between devices: 34.2 us -> 60.5 us  [swap_col(): return lax.ppermute(x, 'col', [(s, s ^ m) for s in range(count)])]
    pallas_call x8 -> x6, Pallas kernels: 66.8 us -> 42 us  [call(): pl.pallas_call(kernel, out_shape=out_shape, in_specs=[pl.BlockSpec(memory...]
    ppermute x12, waiting for transfers between devices: 18.9 us -> 30.8 us  [swap_row(): return lax.ppermute(x, 'row', [(s, s ^ t) for s in range(4)])]
    ppermute x12, starting transfers between devices: 23.6 us -> 18.7 us  [swap_row(): return lax.ppermute(x, 'row', [(s, s ^ t) for s in range(4)])]
    unnamed x104 -> x76, local copies, waits for them, and re-layouts: 6.89 us -> 8.12 us
  transfers between devices with their start and end apart: 100 -> 58, of which waited for: 31 -> 29; matrix products, arithmetic and copies ran while one was open for 3% -> 3% of each run, Pallas kernels for 20% -> 13%
where the time goes in v4:
time: 330 us
  waiting for transfers between devices  180 us (55%)
  starting transfers between devices  88.7 us (27%)
  Pallas kernels  42 us (13%)
  local copies, waits for them, and re-layouts  9.05 us (3%)
  other arithmetic  8.08 us (2%)
    ppermute x24, waiting for transfers between devices, step_row(): lax.ppermute(x, 'row', [(s, s + step) for s in range(first, last + 1)])  89.1 us
    ppermute x22, waiting for transfers between devices, swap_col(): return lax.ppermute(x, 'col', [(s, s ^ m) for s in range(count)])  60.5 us
    ppermute x24, starting transfers between devices, step_row(): lax.ppermute(x, 'row', [(s, s + step) for s in range(first, last + 1)])  47.9 us
    pallas_call x6, Pallas kernels, call(): pl.pallas_call(kernel, out_shape=out_shape, in_specs=[pl.BlockSpec(memory...  42 us
    ppermute x12, waiting for transfers between devices, swap_row(): return lax.ppermute(x, 'row', [(s, s ^ t) for s in range(4)])  30.8 us
    ppermute x22, starting transfers between devices, swap_col(): return lax.ppermute(x, 'col', [(s, s ^ m) for s in range(count)])  22 us
    ppermute x12, starting transfers between devices, swap_row(): return lax.ppermute(x, 'row', [(s, s ^ t) for s in range(4)])  18.7 us
    unnamed x76, local copies, waits for them, and re-layouts  8.12 us
  transfers between devices with their start and end apart: 58, of which 29 were waited for; matrix products, arithmetic and copies ran while one was open for 3% of the time, Pallas kernels for 13%

profile of v4, /device:TPU:0, one launch (start us, length us, event | category | flops | bytes accessed | tf_op | source)
XLA Modules:
  0.0 329.6 jit_solution(400251231689322)
XLA Ops:
  7.5 8.4 %collective-permute-done.1 = bf16[2,128,256]{2,1,0:T(8,128)(2,1)S(1)} collective-permute-done((bf16[2,128,256]{2,1,0:T(8,128)(2,1)S(1)}, bf16[2,128,256]{2,1,0:T(8,128)(2,1)S(1)}, u32[]{:S(2)}, u32[]{:S(2)}) %collective-permute-start.1) | collective-permute-done | bytes 131104 | tf_op jit(solution)/shard_map/ppermute | solution.py:238
  31.4 6.1 %collective-permute-done.30 = bf16[2,128,256]{2,1,0:T(8,128)(2,1)S(1)} collective-permute-done((bf16[2,128,256]{2,1,0:T(8,128)(2,1)S(1)}, bf16[2,128,256]{2,1,0:T(8,128)(2,1)S(1)}, u32[]{:S(2)}, u32[]{:S(2)}) %collective-permute-start.30) | collective-permute-done | bytes 131104 | tf_op jit(solution)/shard_map/ppermute | solution.py:238
  49.8 9.8 %collective-permute-done.33.refs_2_ = bf16[4,2,128,256]{3,2,1,0:T(8,128)(2,1)} collective-permute-done((bf16[4,2,128,256]{3,2,1,0:T(8,128)(2,1)S(1)}, bf16[4,2,128,256]{3,2,1,0:T(8,128)(2,1)}, u32[]{:S(2)}, u32[]{:S(2)}) %collective-permute-start.33) | collective-permute-done | bytes 524320 | tf_op jit(solution)/shard_map/ppermute | solution.py:234
  59.7 10.4 %collective-permute-done.35.refs_4_ = bf16[4,2,128,256]{3,2,1,0:T(8,128)(2,1)} collective-permute-done((bf16[4,2,128,256]{3,2,1,0:T(8,128)(2,1)S(1)}, bf16[4,2,128,256]{3,2,1,0:T(8,128)(2,1)}, u32[]{:S(2)}, u32[]{:S(2)}) %collective-permute-start.35) | collective-permute-done | bytes 524320 | tf_op jit(solution)/shard_map/ppermute | solution.py:234
  71.4 5.3 %shard_map.93 = (bf16[8,128,256]{2,1,0:T(8,128)(2,1)}, bf16[8,128,256]{2,1,0:T(8,128)(2,1)}, bf16[8,128,256]{2,1,0:T(8,128)(2,1)}, bf16[8,128,256]{2,1,0:T(8,128)(2,1)}) custom-call(s32[18]{0:T(128)} %pad_add_fusion.2.info, bf16[16,256,256]{2,1,0:T(8,128)(2,1)} %bitcast.74, bf16[4,2,128,256]{3,2,1,0:T(8,128)(2,1)} %copy-done.1, ...), custom_call_target="tpu_custom_call" | custom-call | flops 1073741824 | bytes 8388608 | tf_op jit(solution)/shard_map/pallas_call | solution.py:150
  83.2 8.8 %shard_map.95 = (bf16[8,128,256]{2,1,0:T(8,128)(2,1)}, bf16[8,128,256]{2,1,0:T(8,128)(2,1)}, bf16[8,128,256]{2,1,0:T(8,128)(2,1)}, bf16[8,128,256]{2,1,0:T(8,128)(2,1)}) custom-call(s32[18]{0:T(128)} %pad_add_fusion.info, bf16[16,256,256]{2,1,0:T(8,128)(2,1)} %bitcast.76, bf16[4,2,128,256]{3,2,1,0:T(8,128)(2,1)} %copy-done.2, ...), custom_call_target="tpu_custom_call" | custom-call | flops 1073741824 | bytes 8388608 | tf_op jit(solution)/shard_map/pallas_call | solution.py:150
  98.4 7.7 %collective-permute-done.39 = bf16[8,128,256]{2,1,0:T(8,128)(2,1)S(1)} collective-permute-done((bf16[8,128,256]{2,1,0:T(8,128)(2,1)}, bf16[8,128,256]{2,1,0:T(8,128)(2,1)S(1)}, u32[]{:S(2)}, u32[]{:S(2)}) %collective-permute-start.39) | collective-permute-done | bytes 524320 | tf_op jit(solution)/shard_map/ppermute | solution.py:242
  106.4 5.1 %collective-permute-start.40 = (bf16[8,128,256]{2,1,0:T(8,128)(2,1)S(1)}, bf16[8,128,256]{2,1,0:T(8,128)(2,1)}, u32[]{:S(2)}, u32[]{:S(2)}) collective-permute-start(bf16[8,128,256]{2,1,0:T(8,128)(2,1)S(1)} %get-tuple-element.49), channel_id=1, source_target_pairs={{0,8},{8,16},{1,9},{9,17},{2,10},{10,18},{3,11},{11,19},{4,12},{12... | collective-permute-start | bytes 1572872 | tf_op jit(solution)/shard_map/ppermute | solution.py:242
  141.2 9.7 %collective-permute-done.41 = bf16[8,128,256]{2,1,0:T(8,128)(2,1)S(1)} collective-permute-done((bf16[8,128,256]{2,1,0:T(8,128)(2,1)S(1)}, bf16[8,128,256]{2,1,0:T(8,128)(2,1)S(1)}, u32[]{:S(2)}, u32[]{:S(2)}) %collective-permute-start.41) | collective-permute-done | bytes 524320 | tf_op jit(solution)/shard_map/ppermute | solution.py:242
  158.1 9.8 %collective-permute-done.45.refs_2_.refs_10_ = bf16[8,128,256]{2,1,0:T(8,128)(2,1)S(1)} collective-permute-done((bf16[8,128,256]{2,1,0:T(8,128)(2,1)S(1)}, bf16[8,128,256]{2,1,0:T(8,128)(2,1)S(1)}, u32[]{:S(2)}, u32[]{:S(2)}) %collective-permute-start.45) | collective-permute-done | bytes 524320 | tf_op jit(solution)/shard_map/ppermute | solution.py:242
  181.1 8.8 %collective-permute-done.49.refs_5_.refs_13_ = bf16[8,128,256]{2,1,0:T(8,128)(2,1)S(1)} collective-permute-done((bf16[8,128,256]{2,1,0:T(8,128)(2,1)S(1)}, bf16[8,128,256]{2,1,0:T(8,128)(2,1)S(1)}, u32[]{:S(2)}, u32[]{:S(2)}) %collective-permute-start.49) | collective-permute-done | bytes 524320 | tf_op jit(solution)/shard_map/ppermute | solution.py:242
  191.9 9.2 %collective-permute-done.19.refs_4_.refs_12_ = bf16[8,128,256]{2,1,0:T(8,128)(2,1)S(1)} collective-permute-done((bf16[8,128,256]{2,1,0:T(8,128)(2,1)S(1)}, bf16[8,128,256]{2,1,0:T(8,128)(2,1)S(1)}, u32[]{:S(2)}, u32[]{:S(2)}) %collective-permute-start.19) | collective-permute-done | bytes 524320 | tf_op jit(solution)/shard_map/ppermute | solution.py:242
  202.4 9.9 %collective-permute-done.50.refs_6_.refs_14_ = bf16[8,128,256]{2,1,0:T(8,128)(2,1)S(1)} collective-permute-done((bf16[8,128,256]{2,1,0:T(8,128)(2,1)S(1)}, bf16[8,128,256]{2,1,0:T(8,128)(2,1)S(1)}, u32[]{:S(2)}, u32[]{:S(2)}) %collective-permute-start.50) | collective-permute-done | bytes 524320 | tf_op jit(solution)/shard_map/ppermute | solution.py:242
  213.2 5.6 %shard_map.96 = (bf16[4,4,2,128,256]{4,3,2,1,0:T(8,128)(2,1)}, bf16[4,4,2,128,256]{4,3,2,1,0:T(8,128)(2,1)}) custom-call(s32[18]{0:T(128)} %pad_add_fusion.2.info, bf16[16,256,256]{2,1,0:T(8,128)(2,1)} %bitcast.75, bf16[8,128,256]{2,1,0:T(8,128)(2,1)} %copy-done.20, bf16[8,128,256]{2,1,0:T(8,128)(2,1)} %copy-done.18, bf16[8,128,256]{2,1,0:T(8,128)(2,1)} %copy-done.16, ...), custom_call_target="tpu_custom_call" | custom-call | flops 1073741824 | bytes 8388608 | tf_op jit(solution)/shard_map/pallas_call | solution.py:150
  223.5 12.8 %collective-permute-done.21.refs_6_.refs_14_ = bf16[8,128,256]{2,1,0:T(8,128)(2,1)S(1)} collective-permute-done((bf16[8,128,256]{2,1,0:T(8,128)(2,1)}, bf16[8,128,256]{2,1,0:T(8,128)(2,1)S(1)}, u32[]{:S(2)}, u32[]{:S(2)}) %collective-permute-start.21) | collective-permute-done | bytes 524320 | tf_op jit(solution)/shard_map/ppermute | solution.py:242
  237.2 8.6 %shard_map.94 = (bf16[4,4,2,128,256]{4,3,2,1,0:T(8,128)(2,1)}, bf16[4,4,2,128,256]{4,3,2,1,0:T(8,128)(2,1)}) custom-call(s32[18]{0:T(128)} %pad_add_fusion.info, bf16[16,256,256]{2,1,0:T(8,128)(2,1)} %bitcast.77, bf16[8,128,256]{2,1,0:T(8,128)(2,1)} %copy-done.25, bf16[8,128,256]{2,1,0:T(8,128)(2,1)} %copy-done.24, bf16[8,128,256]{2,1,0:T(8,128)(2,1)} %copy-done.22, ...), custom_call_target="tpu_custom_call" | custom-call | flops 1073741824 | bytes 8388608 | tf_op jit(solution)/shard_map/pallas_call | solution.py:150
  245.9 8.7 %shard_map.98 = bf16[16,256,256]{2,1,0:T(8,128)(2,1)} custom-call(s32[18]{0:T(128)} %pad_add_fusion.info, bf16[4,2,128,256]{3,2,1,0:T(8,128)(2,1)} %copy-done.2, bf16[4,2,128,256]{3,2,1,0:T(8,128)(2,1)} %collective-permute-done.32.refs_1_, bf16[4,2,128,256]{3,2,1,0:T(8,128)(2,1)} %collective-permute-done.33.refs_2_, bf16[4,2,128,256]{3,2,1,0:T(8,128)(2,1)} %copy-done.13, ...), custom_call_target="tpu_custom_call" | custom-call | flops 1073741824 | bytes 8388608 | tf_op jit(solution)/shard_map/pallas_call | solution.py:150
  254.6 5.1 %shard_map.97 = bf16[16,256,256]{2,1,0:T(8,128)(2,1)} custom-call(s32[18]{0:T(128)} %pad_add_fusion.2.info, bf16[4,2,128,256]{3,2,1,0:T(8,128)(2,1)} %copy-done.1, bf16[4,2,128,256]{3,2,1,0:T(8,128)(2,1)} %copy-done.10, bf16[4,2,128,256]{3,2,1,0:T(8,128)(2,1)} %copy-done.7, bf16[4,2,128,256]{3,2,1,0:T(8,128)(2,1)} %copy-done.11, ...), custom_call_target="tpu_custom_call" | custom-call | flops 1073741824 | bytes 8388608 | tf_op jit(solution)/shard_map/pallas_call | solution.py:150
  260.7 6.1 %collective-permute-start.52 = (bf16[4,2,128,256]{3,2,1,0:T(8,128)(2,1)S(1)}, bf16[4,2,128,256]{3,2,1,0:T(8,128)(2,1)S(1)}, u32[]{:S(2)}, u32[]{:S(2)}) collective-permute-start(bf16[4,2,128,256]{3,2,1,0:T(8,128)(2,1)S(1)} %get-tuple-element.34), channel_id=1, source_target_pairs={{0,2},{1,3},{2,0},{3,1},{4,6},{5,7},{6,4},{7,5},{8,10},{9,11},{10,... | collective-permute-start | bytes 1572872 | tf_op jit(solution)/shard_map/ppermute | solution.py:234
  272.1 6.9 %collective-permute-done.52 = bf16[4,2,128,256]{3,2,1,0:T(8,128)(2,1)S(1)} collective-permute-done((bf16[4,2,128,256]{3,2,1,0:T(8,128)(2,1)S(1)}, bf16[4,2,128,256]{3,2,1,0:T(8,128)(2,1)S(1)}, u32[]{:S(2)}, u32[]{:S(2)}) %collective-permute-start.52) | collective-permute-done | bytes 524320 | tf_op jit(solution)/shard_map/ppermute | solution.py:234
  282.0 10.8 %collective-permute-done.53 = bf16[4,2,128,256]{3,2,1,0:T(8,128)(2,1)S(1)} collective-permute-done((bf16[4,2,128,256]{3,2,1,0:T(8,128)(2,1)S(1)}, bf16[4,2,128,256]{3,2,1,0:T(8,128)(2,1)S(1)}, u32[]{:S(2)}, u32[]{:S(2)}) %collective-permute-start.53) | collective-permute-done | bytes 524320 | tf_op jit(solution)/shard_map/ppermute | solution.py:234
  293.3 8.3 %collective-permute-done.23 = bf16[4,2,128,256]{3,2,1,0:T(8,128)(2,1)S(1)} collective-permute-done((bf16[4,2,128,256]{3,2,1,0:T(8,128)(2,1)S(1)}, bf16[4,2,128,256]{3,2,1,0:T(8,128)(2,1)S(1)}, u32[]{:S(2)}, u32[]{:S(2)}) %collective-permute-start.23) | collective-permute-done | bytes 524320 | tf_op jit(solution)/shard_map/ppermute | solution.py:234
  301.6 13.7 %collective-permute-done.24 = bf16[4,2,128,256]{3,2,1,0:T(8,128)(2,1)S(1)} collective-permute-done((bf16[4,2,128,256]{3,2,1,0:T(8,128)(2,1)S(1)}, bf16[4,2,128,256]{3,2,1,0:T(8,128)(2,1)S(1)}, u32[]{:S(2)}, u32[]{:S(2)}) %collective-permute-start.24) | collective-permute-done | bytes 524320 | tf_op jit(solution)/shard_map/ppermute | solution.py:234
  322.4 6.2 %collective-permute-done.27 = bf16[2,128,256]{2,1,0:T(8,128)(2,1)S(1)} collective-permute-done((bf16[2,128,256]{2,1,0:T(8,128)(2,1)S(1)}, bf16[2,128,256]{2,1,0:T(8,128)(2,1)S(1)}, u32[]{:S(2)}, u32[]{:S(2)}) %collective-permute-start.27) | collective-permute-done | bytes 131104 | tf_op jit(solution)/shard_map/ppermute | solution.py:238
  (199 shorter events, 126.3 us)
Async XLA Ops:
  18.1 22.4 %collective-permute-start.6 = (bf16[4,2,128,256]{3,2,1,0:T(8,128)(2,1)S(1)}, bf16[4,2,128,256]{3,2,1,0:T(8,128)(2,1)S(1)}, u32[]{:S(2)}, u32[]{:S(2)}) collective-permute-start(bf16[4,2,128,256]{3,2,1,0:T(8,128)(2,1)S(1)} %pad_maximum_fusion.refs_0_), channel_id=1, source_target_pairs={{0,4},{1,5},{2,6},{3,7},{4,0},{5,1},{6,2},{7,3},{8,12},{9,13},{10,... | collective-permute-start | bytes 1572872 | tf_op jit(solution)/shard_map/ppermute | solution.py:234
  19.6 25.0 %collective-permute-start.8 = (bf16[4,2,128,256]{3,2,1,0:T(8,128)(2,1)S(1)}, bf16[4,2,128,256]{3,2,1,0:T(8,128)(2,1)S(1)}, u32[]{:S(2)}, u32[]{:S(2)}) collective-permute-start(bf16[4,2,128,256]{3,2,1,0:T(8,128)(2,1)S(1)} %pad_maximum_fusion.refs_0_), channel_id=1, source_target_pairs={{0,6},{1,7},{2,4},{3,5},{4,2},{5,3},{6,0},{7,1},{8,14},{9,15},{10,... | collective-permute-start | bytes 1572872 | tf_op jit(solution)/shard_map/ppermute | solution.py:234
  20.0 27.7 %collective-permute-start.3 = (bf16[4,2,128,256]{3,2,1,0:T(8,128)(2,1)S(1)}, bf16[4,2,128,256]{3,2,1,0:T(8,128)(2,1)S(1)}, u32[]{:S(2)}, u32[]{:S(2)}) collective-permute-start(bf16[4,2,128,256]{3,2,1,0:T(8,128)(2,1)S(1)} %pad_maximum_fusion.refs_0_), channel_id=1, source_target_pairs={{0,1},{1,0},{2,3},{3,2},{4,5},{5,4},{6,7},{7,6},{8,9},{9,8},{10,11... | collective-permute-start | bytes 1572872 | tf_op jit(solution)/shard_map/ppermute | solution.py:234
  46.2 23.9 %collective-permute-start.35 = (bf16[4,2,128,256]{3,2,1,0:T(8,128)(2,1)S(1)}, bf16[4,2,128,256]{3,2,1,0:T(8,128)(2,1)}, u32[]{:S(2)}, u32[]{:S(2)}) collective-permute-start(bf16[4,2,128,256]{3,2,1,0:T(8,128)(2,1)S(1)} %pad_maximum_fusion.1.refs_0_), channel_id=1, source_target_pairs={{0,4},{1,5},{2,6},{3,7},{4,0},{5,1},{6,2},{7,3},{8,12},{9,13},{10,... | collective-permute-start | bytes 1572872 | tf_op jit(solution)/shard_map/ppermute | solution.py:234
  47.7 22.4 %collective-permute-start.37 = (bf16[4,2,128,256]{3,2,1,0:T(8,128)(2,1)S(1)}, bf16[4,2,128,256]{3,2,1,0:T(8,128)(2,1)}, u32[]{:S(2)}, u32[]{:S(2)}) collective-permute-start(bf16[4,2,128,256]{3,2,1,0:T(8,128)(2,1)S(1)} %pad_maximum_fusion.1.refs_0_), channel_id=1, source_target_pairs={{0,6},{1,7},{2,4},{3,5},{4,2},{5,3},{6,0},{7,1},{8,14},{9,15},{10,... | collective-permute-start | bytes 1572872 | tf_op jit(solution)/shard_map/ppermute | solution.py:234
  48.2 23.1 %collective-permute-start.9 = (bf16[4,2,128,256]{3,2,1,0:T(8,128)(2,1)S(1)}, bf16[4,2,128,256]{3,2,1,0:T(8,128)(2,1)}, u32[]{:S(2)}, u32[]{:S(2)}) collective-permute-start(bf16[4,2,128,256]{3,2,1,0:T(8,128)(2,1)S(1)} %collective-permute-done.8.refs_6_), channel_id=1, source_target_pairs={{0,1},{1,0},{2,3},{3,2},{4,5},{5,4},{6,7},{7,6},{8,9},{9,8},{10,11... | collective-permute-start | bytes 1572872 | tf_op jit(solution)/shard_map/ppermute | solution.py:234
  49.0 31.5 %collective-permute-start.32 = (bf16[4,2,128,256]{3,2,1,0:T(8,128)(2,1)S(1)}, bf16[4,2,128,256]{3,2,1,0:T(8,128)(2,1)}, u32[]{:S(2)}, u32[]{:S(2)}) collective-permute-start(bf16[4,2,128,256]{3,2,1,0:T(8,128)(2,1)S(1)} %pad_maximum_fusion.1.refs_0_), channel_id=1, source_target_pairs={{0,1},{1,0},{2,3},{3,2},{4,5},{5,4},{6,7},{7,6},{8,9},{9,8},{10,11... | collective-permute-start | bytes 1572872 | tf_op jit(solution)/shard_map/ppermute | solution.py:234
  59.7 22.3 %collective-permute-start.34 = (bf16[4,2,128,256]{3,2,1,0:T(8,128)(2,1)}, bf16[4,2,128,256]{3,2,1,0:T(8,128)(2,1)S(1)}, u32[]{:S(2)}, u32[]{:S(2)}) collective-permute-start(bf16[4,2,128,256]{3,2,1,0:T(8,128)(2,1)} %collective-permute-done.33.refs_2_), channel_id=1, source_target_pairs={{0,1},{1,0},{2,3},{3,2},{4,5},{5,4},{6,7},{7,6},{8,9},{9,8},{10,11... | collective-permute-start | bytes 1572872 | tf_op jit(solution)/shard_map/ppermute | solution.py:234
  94.7 22.6 %collective-permute-start.11 = (bf16[8,128,256]{2,1,0:T(8,128)(2,1)S(1)}, bf16[8,128,256]{2,1,0:T(8,128)(2,1)}, u32[]{:S(2)}, u32[]{:S(2)}) collective-permute-start(bf16[8,128,256]{2,1,0:T(8,128)(2,1)S(1)} %get-tuple-element.54), channel_id=1, source_target_pairs={{0,8},{8,16},{1,9},{9,17},{2,10},{10,18},{3,11},{11,19},{4,12},{12... | collective-permute-start | bytes 1572872 | tf_op jit(solution)/shard_map/ppermute | solution.py:242
  106.4 22.1 %collective-permute-start.40 = (bf16[8,128,256]{2,1,0:T(8,128)(2,1)S(1)}, bf16[8,128,256]{2,1,0:T(8,128)(2,1)}, u32[]{:S(2)}, u32[]{:S(2)}) collective-permute-start(bf16[8,128,256]{2,1,0:T(8,128)(2,1)S(1)} %get-tuple-element.49), channel_id=1, source_target_pairs={{0,8},{8,16},{1,9},{9,17},{2,10},{10,18},{3,11},{11,19},{4,12},{12... | collective-permute-start | bytes 1572872 | tf_op jit(solution)/shard_map/ppermute | solution.py:242
  130.0 20.9 %collective-permute-start.41 = (bf16[8,128,256]{2,1,0:T(8,128)(2,1)S(1)}, bf16[8,128,256]{2,1,0:T(8,128)(2,1)S(1)}, u32[]{:S(2)}, u32[]{:S(2)}) collective-permute-start(bf16[8,128,256]{2,1,0:T(8,128)(2,1)S(1)} %get-tuple-element.42), channel_id=1, source_target_pairs={{0,8},{8,16},{16,24},{1,9},{9,17},{17,25},{2,10},{10,18},{18,26},{... | collective-permute-start | bytes 1572872 | tf_op jit(solution)/shard_map/ppermute | solution.py:242
  179.0 22.1 %collective-permute-start.19 = (bf16[8,128,256]{2,1,0:T(8,128)(2,1)S(1)}, bf16[8,128,256]{2,1,0:T(8,128)(2,1)S(1)}, u32[]{:S(2)}, u32[]{:S(2)}) collective-permute-start(bf16[8,128,256]{2,1,0:T(8,128)(2,1)S(1)} %get-tuple-element.41.refs_3_.refs_11_), channel_id=1, source_target_pairs={{8,0},{16,8},{24,16},{9,1},{17,9},{25,17},{10,2},{18,10},{26,18},{... | collective-permute-start | bytes 1572872 | tf_op jit(solution)/shard_map/ppermute | solution.py:242
  180.4 22.1 %collective-permute-start.47 = (bf16[8,128,256]{2,1,0:T(8,128)(2,1)S(1)}, bf16[8,128,256]{2,1,0:T(8,128)(2,1)S(1)}, u32[]{:S(2)}, u32[]{:S(2)}) collective-permute-start(bf16[8,128,256]{2,1,0:T(8,128)(2,1)S(1)} %collective-permute-done.46.refs_1_.refs_9_), channel_id=1, source_target_pairs={{16,24},{17,25},{18,26},{19,27},{20,28},{21,29},{22,30},{23,31}} | collective-permute-start | bytes 1572872 | tf_op jit(solution)/shard_map/ppermute | solution.py:242
  189.9 22.5 %collective-permute-start.50 = (bf16[8,128,256]{2,1,0:T(8,128)(2,1)S(1)}, bf16[8,128,256]{2,1,0:T(8,128)(2,1)S(1)}, u32[]{:S(2)}, u32[]{:S(2)}) collective-permute-start(bf16[8,128,256]{2,1,0:T(8,128)(2,1)S(1)} %collective-permute-done.49.refs_5_.refs_13_), channel_id=1, source_target_pairs={{8,0},{9,1},{10,2},{11,3},{12,4},{13,5},{14,6},{15,7}} | collective-permute-start | bytes 1572872 | tf_op jit(solution)/shard_map/ppermute | solution.py:242
  191.2 28.4 %collective-permute-start.17 = (bf16[8,128,256]{2,1,0:T(8,128)(2,1)S(1)}, bf16[8,128,256]{2,1,0:T(8,128)(2,1)S(1)}, u32[]{:S(2)}, u32[]{:S(2)}) collective-permute-start(bf16[8,128,256]{2,1,0:T(8,128)(2,1)S(1)} %collective-permute-done.16.refs_2_.refs_10_), channel_id=1, source_target_pairs={{8,16},{16,24},{9,17},{17,25},{10,18},{18,26},{11,19},{19,27},{12,... | collective-permute-start | bytes 1572872 | tf_op jit(solution)/shard_map/ppermute | solution.py:242
  218.8 40.9 %collective-permute-start.51 = (bf16[4,4,2,128,256]{4,3,2,1,0:T(8,128)(2,1)}, bf16[4,4,2,128,256]{4,3,2,1,0:T(8,128)(2,1)S(1)}, u32[]{:S(2)}, u32[]{:S(2)}) collective-permute-start(bf16[4,4,2,128,256]{4,3,2,1,0:T(8,128)(2,1)} %get-tuple-element.29), channel_id=1, source_target_pairs={{0,1},{1,0},{2,3},{3,2},{4,5},{5,4},{6,7},{7,6},{8,9},{9,8},{10,11... | collective-permute-start | bytes 6291464 | tf_op jit(solution)/shard_map/ppermute | solution.py:234
  245.8 22.5 %collective-permute-start.22 = (bf16[4,4,2,128,256]{4,3,2,1,0:T(8,128)(2,1)}, bf16[4,4,2,128,256]{4,3,2,1,0:T(8,128)(2,1)S(1)}, u32[]{:S(2)}, u32[]{:S(2)}) collective-permute-start(bf16[4,4,2,128,256]{4,3,2,1,0:T(8,128)(2,1)} %get-tuple-element.22), channel_id=1, source_target_pairs={{0,1},{1,0},{2,3},{3,2},{4,5},{5,4},{6,7},{7,6},{8,9},{9,8},{10,11... | collective-permute-start | bytes 6291464 | tf_op jit(solution)/shard_map/ppermute | solution.py:234
  266.8 26.0 %collective-permute-start.53 = (bf16[4,2,128,256]{3,2,1,0:T(8,128)(2,1)S(1)}, bf16[4,2,128,256]{3,2,1,0:T(8,128)(2,1)S(1)}, u32[]{:S(2)}, u32[]{:S(2)}) collective-permute-start(bf16[4,2,128,256]{3,2,1,0:T(8,128)(2,1)S(1)} %get-tuple-element.36), channel_id=1, source_target_pairs={{0,4},{1,5},{2,6},{3,7},{4,0},{5,1},{6,2},{7,3},{8,12},{9,13},{10,... | collective-permute-start | bytes 1572872 | tf_op jit(solution)/shard_map/ppermute | solution.py:234
  267.7 25.1 %collective-permute-start.54 = (bf16[4,2,128,256]{3,2,1,0:T(8,128)(2,1)S(1)}, bf16[4,2,128,256]{3,2,1,0:T(8,128)(2,1)S(1)}, u32[]{:S(2)}, u32[]{:S(2)}) collective-permute-start(bf16[4,2,128,256]{3,2,1,0:T(8,128)(2,1)S(1)} %get-tuple-element.35), channel_id=1, source_target_pairs={{0,6},{1,7},{2,4},{3,5},{4,2},{5,3},{6,0},{7,1},{8,14},{9,15},{10,... | collective-permute-start | bytes 1572872 | tf_op jit(solution)/shard_map/ppermute | solution.py:234
  269.2 32.4 %collective-permute-start.23 = (bf16[4,2,128,256]{3,2,1,0:T(8,128)(2,1)S(1)}, bf16[4,2,128,256]{3,2,1,0:T(8,128)(2,1)S(1)}, u32[]{:S(2)}, u32[]{:S(2)}) collective-permute-start(bf16[4,2,128,256]{3,2,1,0:T(8,128)(2,1)S(1)} %get-tuple-element.37), channel_id=1, source_target_pairs={{0,2},{1,3},{2,0},{3,1},{4,6},{5,7},{6,4},{7,5},{8,10},{9,11},{10,... | collective-permute-start | bytes 1572872 | tf_op jit(solution)/shard_map/ppermute | solution.py:234
  271.2 44.1 %collective-permute-start.24 = (bf16[4,2,128,256]{3,2,1,0:T(8,128)(2,1)S(1)}, bf16[4,2,128,256]{3,2,1,0:T(8,128)(2,1)S(1)}, u32[]{:S(2)}, u32[]{:S(2)}) collective-permute-start(bf16[4,2,128,256]{3,2,1,0:T(8,128)(2,1)S(1)} %get-tuple-element.39), channel_id=1, source_target_pairs={{0,4},{1,5},{2,6},{3,7},{4,0},{5,1},{6,2},{7,3},{8,12},{9,13},{10,... | collective-permute-start | bytes 1572872 | tf_op jit(solution)/shard_map/ppermute | solution.py:234
  279.1 36.2 %collective-permute-start.25 = (bf16[4,2,128,256]{3,2,1,0:T(8,128)(2,1)S(1)}, bf16[4,2,128,256]{3,2,1,0:T(8,128)(2,1)S(1)}, u32[]{:S(2)}, u32[]{:S(2)}) collective-permute-start(bf16[4,2,128,256]{3,2,1,0:T(8,128)(2,1)S(1)} %get-tuple-element.38), channel_id=1, source_target_pairs={{0,6},{1,7},{2,4},{3,5},{4,2},{5,3},{6,0},{7,1},{8,14},{9,15},{10,... | collective-permute-start | bytes 1572872 | tf_op jit(solution)/shard_map/ppermute | solution.py:234
  293.1 22.6 %collective-permute-start.55 = (bf16[2,128,256]{2,1,0:T(8,128)(2,1)S(1)}, bf16[2,128,256]{2,1,0:T(8,128)(2,1)S(1)}, u32[]{:S(2)}, u32[]{:S(2)}) collective-permute-start(bf16[2,128,256]{2,1,0:T(8,128)(2,1)S(1)} %get-tuple-element.46), channel_id=1, source_target_pairs={{0,8},{8,0},{16,24},{24,16},{1,9},{9,1},{17,25},{25,17},{2,10},{10... | collective-permute-start | bytes 393224 | tf_op jit(solution)/shard_map/ppermute | solution.py:238
  293.2 26.8 %collective-permute-start.56 = (bf16[2,128,256]{2,1,0:T(8,128)(2,1)S(1)}, bf16[2,128,256]{2,1,0:T(8,128)(2,1)S(1)}, u32[]{:S(2)}, u32[]{:S(2)}) collective-permute-start(bf16[2,128,256]{2,1,0:T(8,128)(2,1)S(1)} %get-tuple-element.48), channel_id=1, source_target_pairs={{0,16},{8,24},{16,0},{24,8},{1,17},{9,25},{17,1},{25,9},{2,18},{10... | collective-permute-start | bytes 393224 | tf_op jit(solution)/shard_map/ppermute | solution.py:238
  (70 other events, 1332.2 us)

commit v5 on v4

--- a/solution.py
+++ b/solution.py
@@ -248,38 +248,43 @@
     return jnp.swapaxes(x.reshape(rows, width // unit, unit), 0, 1)
 
 
-def spread(mine, after):
-    mine = jnp.stack(mine)
-    if after is not None:
-        mine, _ = lax.optimization_barrier((mine, after))
-    held = []
-    for m in range(0, lax.axis_size("col"), 2):
-        held.append(swap_col(mine, m) if m else mine)
-        held.append(swap_col(held[m], 1))
-    return held
+def after(values, *others):
+    return lax.optimization_barrier((values, others))[0]
+
+
+def across(mine):
+    return [swap_col(mine, m) if m else mine for m in range(0, lax.axis_size("col"), 2)]
+
+
+def with_odd(even):
+    return [x for own in even for x in (own, swap_col(own, 1))]
 
 
 def add(*terms):
     return sum(term.astype(jnp.float32) for term in terms)
 
 
-def line_reduce(parts, row):
+def line_reduce(parts, row, second=(), third=()):
     right = step_row(parts[3], 1, 0, 0)
     left = step_row(parts[3], -1, 3, 3)
+    right, left = first = after((right, left), second)
     right = step_row(add(parts[2], right).astype(jnp.bfloat16), 1, 0, 1)
     left = step_row(add(parts[2], left).astype(jnp.bfloat16), -1, 2, 3)
+    right, left = again = after((right, left), third)
     last_right = add(jnp.where(row == 1, parts[3], parts[1]), right).astype(jnp.bfloat16)
     last_left = add(jnp.where(row == 2, parts[3], parts[1]), left).astype(jnp.bfloat16)
     right = step_row(last_right, 1, 0, 2)
     left = step_row(last_left, -1, 1, 3)
-    return add(parts[0], right, left)
-
-
-def line_gather(x):
+    return (parts[0], right, left), (first, again), (last_right, last_left)
+
+
+def line_gather(x, waits=()):
     held = {0: x}
     for k in range(1, 4):
         held[-k] = step_row(held[1 - k], 1, k - 1, 2)
         held[k] = step_row(held[k - 1], -1, 1, 4 - k)
+        if k <= len(waits):
+            held[-k], held[k] = after((held[-k], held[k]), waits[k - 1])
     return held
 
 
@@ -332,26 +337,30 @@
     row, slots = info_in[0], w_in.shape[0]
     token_blocks = [tokens] + [swap_row(tokens, t) for t in range(1, 4)]
     up_blocks = [upstream] + [swap_row(upstream, t) for t in range(1, 4)]
-    all_tokens = spread(token_blocks, None)
-    all_up = spread(up_blocks, tuple(all_tokens[2::2]))
+    token_even = across(jnp.stack(token_blocks))
+    up_mine = jnp.stack(up_blocks)
+    all_tokens = with_odd(after(token_even, up_mine))
+    up_even = across(after(up_mine, token_even[1:]))
     parts = to_hidden(info_in, all_tokens, w_in, cols, False)
-    hidden = line_reduce(parts, row)
-    parts = to_hidden(info_out, all_up, w_out, cols, True)
-    grad_activ = line_reduce(parts, row)
-    all_activ = line_gather(silu(hidden))
-    all_grad = line_gather(activations(hidden, grad_activ))
-
-    def wide_side(info, hs, w, flip, groups):
-        sums = []
-        for labels in groups:
-            total = finish_col(*from_hidden(info, hs, w, cols, flip, labels, devices))
-            sums += [total[g] for g in range(len(labels))]
-        return finish_row(sums)
-
-    layer_out = wide_side(info_out, all_activ, w_out, False, [(0, 1, 2, 3)])
+    all_up = with_odd(after(up_even, parts))
+    terms, _, last = line_reduce(parts, row, up_even, all_up)
+    parts = to_hidden(info_out, after(all_up, last), w_out, cols, True)
+    hidden = add(*after(terms, parts))
+    activ = silu(hidden)
+    terms, steps, _ = line_reduce(after(parts, activ), row)
+    all_activ = line_gather(activ, steps)
+    all_grad = line_gather(activations(hidden, add(*terms)))
+    labels = range(4)
+
+    def column_sums(info, hs, w, flip):
+        return finish_col(*from_hidden(info, hs, w, cols, flip, labels, devices))
+
+    layer_sums = column_sums(info_out, all_activ, w_out, False)
     grad_w_out = slot_grads(info_out, all_up, all_activ, slots, cols, False)
-    grad_tokens = wide_side(info_in, all_grad, w_in, True, [(0, 1, 2, 3)])
+    all_grad, layer_sums, grad_w_out = lax.optimization_barrier((all_grad, layer_sums, grad_w_out))
+    input_sums = column_sums(info_in, all_grad, w_in, True)
     grad_w_in = slot_grads(info_in, all_tokens, all_grad, slots, cols, True)
+    layer_out, grad_tokens = finish_row(layer_sums), finish_row(input_sums)
     return layer_out, grad_tokens, grad_w_in, grad_w_out
 
 

time: 330 us -> 305 us (0.924)
  waiting for transfers between devices: 180 us -> 141 us
  starting transfers between devices: 88.7 us -> 96.8 us
  Pallas kernels: 42 us -> 46.9 us
    ppermute x22, waiting for transfers between devices: 60.5 us -> 31.4 us  [swap_col(): return lax.ppermute(x, 'col', [(s, s ^ m) for s in range(count)])]
    ppermute x24, waiting for transfers between devices: 89.1 us -> 79.2 us  [step_row(): lax.ppermute(x, 'row', [(s, s + step) for s in range(first, last + 1)])]
    ppermute x12, starting transfers between devices: 18.7 us -> 25.5 us  [swap_row(): return lax.ppermute(x, 'row', [(s, s ^ t) for s in range(4)])]
    ppermute x24, starting transfers between devices: 47.9 us -> 53.3 us  [step_row(): lax.ppermute(x, 'row', [(s, s + step) for s in range(first, last + 1)])]
    pallas_call x6, Pallas kernels: 42 us -> 46.9 us  [call(): pl.pallas_call(kernel, out_shape=out_shape, in_specs=[pl.BlockSpec(memory...]
    ppermute x22, starting transfers between devices: 22 us -> 18 us  [swap_col(): return lax.ppermute(x, 'col', [(s, s ^ m) for s in range(count)])]
    convert_element_type x2 -> x4, other arithmetic: 0.52 us -> 4.47 us  [the longest x2 2.39 us: line_reduce(): left = step_row(add(parts[2], left).astype(jnp.bfloat16), -1, 2, 3)]
    unnamed x76 -> x70, local copies, waits for them, and re-layouts: 8.12 us -> 6.13 us
  transfers between devices with their start and end apart: 58 -> 58, of which waited for: 29 -> 29; matrix products, arithmetic and copies ran while one was open for 3% -> 3% of each run, Pallas kernels for 13% -> 10%
where the time goes in v5:
time: 305 us; the launch traced here: 304 us
  waiting for transfers between devices  141 us (46%)
  starting transfers between devices  96.8 us (32%)
  Pallas kernels  46.9 us (15%)
  other arithmetic  10.7 us (4%)
  local copies, waits for them, and re-layouts  7.09 us (2%)
    ppermute x24, waiting for transfers between devices, step_row(): lax.ppermute(x, 'row', [(s, s + step) for s in range(first, last + 1)])  79.2 us
    ppermute x24, starting transfers between devices, step_row(): lax.ppermute(x, 'row', [(s, s + step) for s in range(first, last + 1)])  53.3 us
    pallas_call x6, Pallas kernels, call(): pl.pallas_call(kernel, out_shape=out_shape, in_specs=[pl.BlockSpec(memory...  46.9 us
    ppermute x22, waiting for transfers between devices, swap_col(): return lax.ppermute(x, 'col', [(s, s ^ m) for s in range(count)])  31.4 us
    ppermute x12, waiting for transfers between devices, swap_row(): return lax.ppermute(x, 'row', [(s, s ^ t) for s in range(4)])  30.7 us
    ppermute x12, starting transfers between devices, swap_row(): return lax.ppermute(x, 'row', [(s, s ^ t) for s in range(4)])  25.5 us
    ppermute x22, starting transfers between devices, swap_col(): return lax.ppermute(x, 'col', [(s, s ^ m) for s in range(count)])  18 us
    unnamed x70, local copies, waits for them, and re-layouts  6.13 us
  transfers between devices with their start and end apart: 58, of which 29 were waited for; matrix products, arithmetic and copies ran while one was open for 3% of the time, Pallas kernels for 10%

profile of v5, /device:TPU:0, one launch (start us, length us, event | category | flops | bytes accessed | tf_op | source)
XLA Modules:
  0.0 304.3 jit_solution(3506211825567870143)
XLA Ops:
  7.5 6.4 %collective-permute-done.4 = bf16[2,128,256]{2,1,0:T(8,128)(2,1)S(1)} collective-permute-done((bf16[2,128,256]{2,1,0:T(8,128)(2,1)S(1)}, bf16[2,128,256]{2,1,0:T(8,128)(2,1)S(1)}, u32[]{:S(2)}, u32[]{:S(2)}) %collective-permute-start.4) | collective-permute-done | bytes 131104 | tf_op jit(solution)/shard_map/ppermute | solution.py:238
  25.3 5.7 %collective-permute-done.1 = bf16[2,128,256]{2,1,0:T(8,128)(2,1)S(1)} collective-permute-done((bf16[2,128,256]{2,1,0:T(8,128)(2,1)S(1)}, bf16[2,128,256]{2,1,0:T(8,128)(2,1)S(1)}, u32[]{:S(2)}, u32[]{:S(2)}) %collective-permute-start.1) | collective-permute-done | bytes 131104 | tf_op jit(solution)/shard_map/ppermute | solution.py:238
  32.2 5.9 %collective-permute-done.2 = bf16[2,128,256]{2,1,0:T(8,128)(2,1)S(1)} collective-permute-done((bf16[2,128,256]{2,1,0:T(8,128)(2,1)S(1)}, bf16[2,128,256]{2,1,0:T(8,128)(2,1)S(1)}, u32[]{:S(2)}, u32[]{:S(2)}) %collective-permute-start.2) | collective-permute-done | bytes 131104 | tf_op jit(solution)/shard_map/ppermute | solution.py:238
  46.6 6.6 %shard_map.93 = (bf16[8,128,256]{2,1,0:T(8,128)(2,1)}, bf16[8,128,256]{2,1,0:T(8,128)(2,1)}, bf16[8,128,256]{2,1,0:T(8,128)(2,1)}, bf16[8,128,256]{2,1,0:T(8,128)(2,1)}) custom-call(s32[18]{0:T(128)} %pad_add_fusion.2.info, bf16[16,256,256]{2,1,0:T(8,128)(2,1)} %bitcast.74, bf16[4,2,128,256]{3,2,1,0:T(8,128)(2,1)} %copy-done.2, ...), custom_call_target="tpu_custom_call" | custom-call | flops 1073741824 | bytes 8388608 | tf_op jit(solution)/shard_map/pallas_call | solution.py:150
  58.8 9.7 %collective-permute-done.10.refs_4_ = bf16[4,2,128,256]{3,2,1,0:T(8,128)(2,1)} collective-permute-done((bf16[4,2,128,256]{3,2,1,0:T(8,128)(2,1)S(1)}, bf16[4,2,128,256]{3,2,1,0:T(8,128)(2,1)}, u32[]{:S(2)}, u32[]{:S(2)}) %collective-permute-start.10) | collective-permute-done | bytes 524320 | tf_op jit(solution)/shard_map/ppermute | solution.py:234
  73.5 5.0 %collective-permute-start.22 = (bf16[8,128,256]{2,1,0:T(8,128)(2,1)S(1)}, bf16[8,128,256]{2,1,0:T(8,128)(2,1)S(1)}, u32[]{:S(2)}, u32[]{:S(2)}) collective-permute-start(bf16[8,128,256]{2,1,0:T(8,128)(2,1)S(1)} %get-tuple-element.141), channel_id=1, source_target_pairs={{0,8},{8,16},{1,9},{9,17},{2,10},{10,18},{3,11},{11,19},{4,12},{12... | collective-permute-start | bytes 1572872 | tf_op jit(solution)/shard_map/ppermute | solution.py:242
  78.6 11.7 %collective-permute-done.22 = bf16[8,128,256]{2,1,0:T(8,128)(2,1)S(1)} collective-permute-done((bf16[8,128,256]{2,1,0:T(8,128)(2,1)S(1)}, bf16[8,128,256]{2,1,0:T(8,128)(2,1)S(1)}, u32[]{:S(2)}, u32[]{:S(2)}) %collective-permute-start.22) | collective-permute-done | bytes 524320 | tf_op jit(solution)/shard_map/ppermute | solution.py:242
  93.4 5.4 %collective-permute-start.24 = (bf16[8,128,256]{2,1,0:T(8,128)(2,1)S(1)}, bf16[8,128,256]{2,1,0:T(8,128)(2,1)S(1)}, u32[]{:S(2)}, u32[]{:S(2)}) collective-permute-start(bf16[8,128,256]{2,1,0:T(8,128)(2,1)S(1)} %get-tuple-element.131), channel_id=1, source_target_pairs={{0,8},{8,16},{16,24},{1,9},{9,17},{17,25},{2,10},{10,18},{18,26},{... | collective-permute-start | bytes 1572872 | tf_op jit(solution)/shard_map/ppermute | solution.py:242
  99.6 9.1 %shard_map.94 = (bf16[8,128,256]{2,1,0:T(8,128)(2,1)}, bf16[8,128,256]{2,1,0:T(8,128)(2,1)}, bf16[8,128,256]{2,1,0:T(8,128)(2,1)}, bf16[8,128,256]{2,1,0:T(8,128)(2,1)}) custom-call(s32[18]{0:T(128)} %pad_add_fusion.info, bf16[16,256,256]{2,1,0:T(8,128)(2,1)} %bitcast.72, bf16[4,2,128,256]{3,2,1,0:T(8,128)(2,1)} %copy-done.3, ...), custom_call_target="tpu_custom_call" | custom-call | flops 1073741824 | bytes 8388608 | tf_op jit(solution)/shard_map/pallas_call | solution.py:150
  121.0 6.4 %collective-permute-done.26 = bf16[8,128,256]{2,1,0:T(8,128)(2,1)S(1)} collective-permute-done((bf16[8,128,256]{2,1,0:T(8,128)(2,1)S(1)}, bf16[8,128,256]{2,1,0:T(8,128)(2,1)S(1)}, u32[]{:S(2)}, u32[]{:S(2)}) %collective-permute-start.26) | collective-permute-done | bytes 524320 | tf_op jit(solution)/shard_map/ppermute | solution.py:242
  128.4 5.1 %collective-permute-start.28 = (bf16[8,128,256]{2,1,0:T(8,128)(2,1)S(1)}, bf16[8,128,256]{2,1,0:T(8,128)(2,1)S(1)}, u32[]{:S(2)}, u32[]{:S(2)}) collective-permute-start(bf16[8,128,256]{2,1,0:T(8,128)(2,1)S(1)} %get-tuple-element.139), channel_id=1, source_target_pairs={{0,8},{8,16},{1,9},{9,17},{2,10},{10,18},{3,11},{11,19},{4,12},{12... | collective-permute-start | bytes 1572872 | tf_op jit(solution)/shard_map/ppermute | solution.py:242
  133.6 5.1 %collective-permute-done.38.refs_2_.refs_10_ = bf16[8,128,256]{2,1,0:T(8,128)(2,1)S(1)} collective-permute-done((bf16[8,128,256]{2,1,0:T(8,128)(2,1)S(1)}, bf16[8,128,256]{2,1,0:T(8,128)(2,1)S(1)}, u32[]{:S(2)}, u32[]{:S(2)}) %collective-permute-start.38) | collective-permute-done | bytes 524320 | tf_op jit(solution)/shard_map/ppermute | solution.py:242
  140.6 6.7 %collective-permute-done.28 = bf16[8,128,256]{2,1,0:T(8,128)(2,1)S(1)} collective-permute-done((bf16[8,128,256]{2,1,0:T(8,128)(2,1)S(1)}, bf16[8,128,256]{2,1,0:T(8,128)(2,1)S(1)}, u32[]{:S(2)}, u32[]{:S(2)}) %collective-permute-start.28) | collective-permute-done | bytes 524320 | tf_op jit(solution)/shard_map/ppermute | solution.py:242
  147.3 6.5 %collective-permute-done.41.refs_5_.refs_13_ = bf16[8,128,256]{2,1,0:T(8,128)(2,1)S(1)} collective-permute-done((bf16[8,128,256]{2,1,0:T(8,128)(2,1)S(1)}, bf16[8,128,256]{2,1,0:T(8,128)(2,1)S(1)}, u32[]{:S(2)}, u32[]{:S(2)}) %collective-permute-start.41) | collective-permute-done | bytes 524320 | tf_op jit(solution)/shard_map/ppermute | solution.py:242
  155.8 9.8 %collective-permute-done.43.refs_6_.refs_14_ = bf16[8,128,256]{2,1,0:T(8,128)(2,1)S(1)} collective-permute-done((bf16[8,128,256]{2,1,0:T(8,128)(2,1)S(1)}, bf16[8,128,256]{2,1,0:T(8,128)(2,1)S(1)}, u32[]{:S(2)}, u32[]{:S(2)}) %collective-permute-start.43) | collective-permute-done | bytes 524320 | tf_op jit(solution)/shard_map/ppermute | solution.py:242
  166.4 8.8 %shard_map.95 = (bf16[4,4,2,128,256]{4,3,2,1,0:T(8,128)(2,1)}, bf16[4,4,2,128,256]{4,3,2,1,0:T(8,128)(2,1)}) custom-call(s32[18]{0:T(128)} %pad_add_fusion.info, bf16[16,256,256]{2,1,0:T(8,128)(2,1)} %bitcast.73, bf16[8,128,256]{2,1,0:T(8,128)(2,1)} %copy-done.22, bf16[8,128,256]{2,1,0:T(8,128)(2,1)} %copy-done.18, bf16[8,128,256]{2,1,0:T(8,128)(2,1)} %copy-done.15, ...), custom_call_target="tpu_custom_call" | custom-call | flops 1073741824 | bytes 8388608 | tf_op jit(solution)/shard_map/pallas_call | solution.py:150
  178.9 10.5 %collective-permute-done.30 = bf16[8,128,256]{2,1,0:T(8,128)(2,1)S(1)} collective-permute-done((bf16[8,128,256]{2,1,0:T(8,128)(2,1)S(1)}, bf16[8,128,256]{2,1,0:T(8,128)(2,1)S(1)}, u32[]{:S(2)}, u32[]{:S(2)}) %collective-permute-start.30) | collective-permute-done | bytes 524320 | tf_op jit(solution)/shard_map/ppermute | solution.py:242
  195.5 5.1 %collective-permute-start.32 = (bf16[8,128,256]{2,1,0:T(8,128)(2,1)S(1)}, bf16[8,128,256]{2,1,0:T(8,128)(2,1)S(1)}, u32[]{:S(2)}, u32[]{:S(2)}) collective-permute-start(bf16[8,128,256]{2,1,0:T(8,128)(2,1)S(1)} %multiply_convert_fusion.refs_3_.refs_11_), channel_id=1, source_target_pairs={{0,8},{8,16},{16,24},{1,9},{9,17},{17,25},{2,10},{10,18},{18,26},{... | collective-permute-start | bytes 1572872 | tf_op jit(solution)/shard_map/ppermute | solution.py:242
  200.6 9.8 %collective-permute-done.35.refs_4_.refs_12_ = bf16[8,128,256]{2,1,0:T(8,128)(2,1)S(1)} collective-permute-done((bf16[8,128,256]{2,1,0:T(8,128)(2,1)S(1)}, bf16[8,128,256]{2,1,0:T(8,128)(2,1)S(1)}, u32[]{:S(2)}, u32[]{:S(2)}) %collective-permute-start.35) | collective-permute-done | bytes 524320 | tf_op jit(solution)/shard_map/ppermute | solution.py:242
  217.6 7.6 %collective-permute-done.36.refs_5_.refs_13_ = bf16[8,128,256]{2,1,0:T(8,128)(2,1)S(1)} collective-permute-done((bf16[8,128,256]{2,1,0:T(8,128)(2,1)S(1)}, bf16[8,128,256]{2,1,0:T(8,128)(2,1)S(1)}, u32[]{:S(2)}, u32[]{:S(2)}) %collective-permute-start.36) | collective-permute-done | bytes 524320 | tf_op jit(solution)/shard_map/ppermute | solution.py:242
  227.4 8.9 %shard_map.96 = bf16[16,256,256]{2,1,0:T(8,128)(2,1)} custom-call(s32[18]{0:T(128)} %pad_add_fusion.info, bf16[4,2,128,256]{3,2,1,0:T(8,128)(2,1)} %copy-done.3, bf16[4,2,128,256]{3,2,1,0:T(8,128)(2,1)} %copy-done.10, bf16[4,2,128,256]{3,2,1,0:T(8,128)(2,1)} %collective-permute-done.9.refs_2_, bf16[4,2,128,256]{3,2,1,0:T(8,128)(2,1)} %copy-done.11, ...), custom_call_target="tpu_custom_call" | custom-call | flops 1073741824 | bytes 8388608 | tf_op jit(solution)/shard_map/pallas_call | solution.py:150
  243.2 7.0 %shard_map.97 = (bf16[4,4,2,128,256]{4,3,2,1,0:T(8,128)(2,1)}, bf16[4,4,2,128,256]{4,3,2,1,0:T(8,128)(2,1)}) custom-call(s32[18]{0:T(128)} %pad_add_fusion.2.info, bf16[16,256,256]{2,1,0:T(8,128)(2,1)} %bitcast.75, bf16[8,128,256]{2,1,0:T(8,128)(2,1)} %copy-done.25, bf16[8,128,256]{2,1,0:T(8,128)(2,1)} %copy-done.21, bf16[8,128,256]{2,1,0:T(8,128)(2,1)} %copy-done.17, ...), custom_call_target="tpu_custom_call" | custom-call | flops 1073741824 | bytes 8388608 | tf_op jit(solution)/shard_map/pallas_call | solution.py:150
  268.2 6.5 %shard_map.98 = bf16[16,256,256]{2,1,0:T(8,128)(2,1)} custom-call(s32[18]{0:T(128)} %pad_add_fusion.2.info, bf16[4,2,128,256]{3,2,1,0:T(8,128)(2,1)} %copy-done.2, bf16[4,2,128,256]{3,2,1,0:T(8,128)(2,1)} %copy-done.9, bf16[4,2,128,256]{3,2,1,0:T(8,128)(2,1)} %copy-done.8, bf16[4,2,128,256]{3,2,1,0:T(8,128)(2,1)} %collective-permute-done.13.refs_3_, ...), custom_call_target="tpu_custom_call" | custom-call | flops 1073741824 | bytes 8388608 | tf_op jit(solution)/shard_map/pallas_call | solution.py:150
  277.2 7.8 %collective-permute-done.54 = bf16[4,2,128,256]{3,2,1,0:T(8,128)(2,1)S(1)} collective-permute-done((bf16[4,2,128,256]{3,2,1,0:T(8,128)(2,1)S(1)}, bf16[4,2,128,256]{3,2,1,0:T(8,128)(2,1)S(1)}, u32[]{:S(2)}, u32[]{:S(2)}) %collective-permute-start.54) | collective-permute-done | bytes 524320 | tf_op jit(solution)/shard_map/ppermute | solution.py:234
  (194 shorter events, 125.8 us)
Async XLA Ops:
  16.3 21.8 %collective-permute-start.8 = (bf16[4,2,128,256]{3,2,1,0:T(8,128)(2,1)S(1)}, bf16[4,2,128,256]{3,2,1,0:T(8,128)(2,1)S(1)}, u32[]{:S(2)}, u32[]{:S(2)}) collective-permute-start(bf16[4,2,128,256]{3,2,1,0:T(8,128)(2,1)S(1)} %pad_maximum_fusion.1.refs_0_), channel_id=1, source_target_pairs={{0,6},{1,7},{2,4},{3,5},{4,2},{5,3},{6,0},{7,1},{8,14},{9,15},{10,... | collective-permute-start | bytes 1572872 | tf_op jit(solution)/shard_map/ppermute | solution.py:234
  18.8 22.4 %collective-permute-start.7 = (bf16[4,2,128,256]{3,2,1,0:T(8,128)(2,1)S(1)}, bf16[4,2,128,256]{3,2,1,0:T(8,128)(2,1)S(1)}, u32[]{:S(2)}, u32[]{:S(2)}) collective-permute-start(bf16[4,2,128,256]{3,2,1,0:T(8,128)(2,1)S(1)} %pad_maximum_fusion.1.refs_0_), channel_id=1, source_target_pairs={{0,4},{1,5},{2,6},{3,7},{4,0},{5,1},{6,2},{7,3},{8,12},{9,13},{10,... | collective-permute-start | bytes 1572872 | tf_op jit(solution)/shard_map/ppermute | solution.py:234
  19.3 22.0 %collective-permute-start.6 = (bf16[4,2,128,256]{3,2,1,0:T(8,128)(2,1)S(1)}, bf16[4,2,128,256]{3,2,1,0:T(8,128)(2,1)S(1)}, u32[]{:S(2)}, u32[]{:S(2)}) collective-permute-start(bf16[4,2,128,256]{3,2,1,0:T(8,128)(2,1)S(1)} %pad_maximum_fusion.1.refs_0_), channel_id=1, source_target_pairs={{0,2},{1,3},{2,0},{3,1},{4,6},{5,7},{6,4},{7,5},{8,10},{9,11},{10,... | collective-permute-start | bytes 1572872 | tf_op jit(solution)/shard_map/ppermute | solution.py:234
  42.4 16.4 %collective-permute-start.11 = (bf16[4,2,128,256]{3,2,1,0:T(8,128)(2,1)S(1)}, bf16[4,2,128,256]{3,2,1,0:T(8,128)(2,1)}, u32[]{:S(2)}, u32[]{:S(2)}) collective-permute-start(bf16[4,2,128,256]{3,2,1,0:T(8,128)(2,1)S(1)} %pad_maximum_fusion.refs_0_), channel_id=1, source_target_pairs={{0,6},{1,7},{2,4},{3,5},{4,2},{5,3},{6,0},{7,1},{8,14},{9,15},{10,... | collective-permute-start | bytes 1572872 | tf_op jit(solution)/shard_map/ppermute | solution.py:234
  44.1 24.4 %collective-permute-start.10 = (bf16[4,2,128,256]{3,2,1,0:T(8,128)(2,1)S(1)}, bf16[4,2,128,256]{3,2,1,0:T(8,128)(2,1)}, u32[]{:S(2)}, u32[]{:S(2)}) collective-permute-start(bf16[4,2,128,256]{3,2,1,0:T(8,128)(2,1)S(1)} %pad_maximum_fusion.refs_0_), channel_id=1, source_target_pairs={{0,4},{1,5},{2,6},{3,7},{4,0},{5,1},{6,2},{7,3},{8,12},{9,13},{10,... | collective-permute-start | bytes 1572872 | tf_op jit(solution)/shard_map/ppermute | solution.py:234
  45.3 23.2 %collective-permute-start.9 = (bf16[4,2,128,256]{3,2,1,0:T(8,128)(2,1)S(1)}, bf16[4,2,128,256]{3,2,1,0:T(8,128)(2,1)}, u32[]{:S(2)}, u32[]{:S(2)}) collective-permute-start(bf16[4,2,128,256]{3,2,1,0:T(8,128)(2,1)S(1)} %pad_maximum_fusion.refs_0_), channel_id=1, source_target_pairs={{0,2},{1,3},{2,0},{3,1},{4,6},{5,7},{6,4},{7,5},{8,10},{9,11},{10,... | collective-permute-start | bytes 1572872 | tf_op jit(solution)/shard_map/ppermute | solution.py:234
  73.5 16.8 %collective-permute-start.22 = (bf16[8,128,256]{2,1,0:T(8,128)(2,1)S(1)}, bf16[8,128,256]{2,1,0:T(8,128)(2,1)S(1)}, u32[]{:S(2)}, u32[]{:S(2)}) collective-permute-start(bf16[8,128,256]{2,1,0:T(8,128)(2,1)S(1)} %get-tuple-element.141), channel_id=1, source_target_pairs={{0,8},{8,16},{1,9},{9,17},{2,10},{10,18},{3,11},{11,19},{4,12},{12... | collective-permute-start | bytes 1572872 | tf_op jit(solution)/shard_map/ppermute | solution.py:242
  92.1 16.6 %collective-permute-start.25 = (bf16[8,128,256]{2,1,0:T(8,128)(2,1)S(1)}, bf16[8,128,256]{2,1,0:T(8,128)(2,1)S(1)}, u32[]{:S(2)}, u32[]{:S(2)}) collective-permute-start(bf16[8,128,256]{2,1,0:T(8,128)(2,1)S(1)} %get-tuple-element.130), channel_id=1, source_target_pairs={{8,0},{16,8},{24,16},{9,1},{17,9},{25,17},{10,2},{18,10},{26,18},{... | collective-permute-start | bytes 1572872 | tf_op jit(solution)/shard_map/ppermute | solution.py:242
  110.6 16.8 %collective-permute-start.26 = (bf16[8,128,256]{2,1,0:T(8,128)(2,1)S(1)}, bf16[8,128,256]{2,1,0:T(8,128)(2,1)S(1)}, u32[]{:S(2)}, u32[]{:S(2)}) collective-permute-start(bf16[8,128,256]{2,1,0:T(8,128)(2,1)S(1)} %copy-done.30), channel_id=1, source_target_pairs={{0,8},{1,9},{2,10},{3,11},{4,12},{5,13},{6,14},{7,15}} | collective-permute-start | bytes 1572872 | tf_op jit(solution)/shard_map/ppermute | solution.py:242
  115.1 18.5 %collective-permute-start.39 = (bf16[8,128,256]{2,1,0:T(8,128)(2,1)S(1)}, bf16[8,128,256]{2,1,0:T(8,128)(2,1)S(1)}, u32[]{:S(2)}, u32[]{:S(2)}) collective-permute-start(bf16[8,128,256]{2,1,0:T(8,128)(2,1)S(1)} %multiply_convert_fusion.1.refs_3_.refs_11_), channel_id=1, source_target_pairs={{8,0},{16,8},{24,16},{9,1},{17,9},{25,17},{10,2},{18,10},{26,18},{... | collective-permute-start | bytes 1572872 | tf_op jit(solution)/shard_map/ppermute | solution.py:242
  116.4 22.3 %collective-permute-start.38 = (bf16[8,128,256]{2,1,0:T(8,128)(2,1)S(1)}, bf16[8,128,256]{2,1,0:T(8,128)(2,1)S(1)}, u32[]{:S(2)}, u32[]{:S(2)}) collective-permute-start(bf16[8,128,256]{2,1,0:T(8,128)(2,1)S(1)} %multiply_convert_fusion.1.refs_3_.refs_11_), channel_id=1, source_target_pairs={{0,8},{8,16},{16,24},{1,9},{9,17},{17,25},{2,10},{10,18},{18,26},{... | collective-permute-start | bytes 1572872 | tf_op jit(solution)/shard_map/ppermute | solution.py:242
  128.4 18.9 %collective-permute-start.28 = (bf16[8,128,256]{2,1,0:T(8,128)(2,1)S(1)}, bf16[8,128,256]{2,1,0:T(8,128)(2,1)S(1)}, u32[]{:S(2)}, u32[]{:S(2)}) collective-permute-start(bf16[8,128,256]{2,1,0:T(8,128)(2,1)S(1)} %get-tuple-element.139), channel_id=1, source_target_pairs={{0,8},{8,16},{1,9},{9,17},{2,10},{10,18},{3,11},{11,19},{4,12},{12... | collective-permute-start | bytes 1572872 | tf_op jit(solution)/shard_map/ppermute | solution.py:242
  175.3 37.1 %collective-permute-start.44 = (bf16[4,4,2,128,256]{4,3,2,1,0:T(8,128)(2,1)}, bf16[4,4,2,128,256]{4,3,2,1,0:T(8,128)(2,1)S(1)}, u32[]{:S(2)}, u32[]{:S(2)}) collective-permute-start(bf16[4,4,2,128,256]{4,3,2,1,0:T(8,128)(2,1)} %get-tuple-element.106), channel_id=1, source_target_pairs={{0,1},{1,0},{2,3},{3,2},{4,5},{5,4},{6,7},{7,6},{8,9},{9,8},{10,11... | collective-permute-start | bytes 6291464 | tf_op jit(solution)/shard_map/ppermute | solution.py:234
  194.2 16.2 %collective-permute-start.35 = (bf16[8,128,256]{2,1,0:T(8,128)(2,1)S(1)}, bf16[8,128,256]{2,1,0:T(8,128)(2,1)S(1)}, u32[]{:S(2)}, u32[]{:S(2)}) collective-permute-start(bf16[8,128,256]{2,1,0:T(8,128)(2,1)S(1)} %multiply_convert_fusion.refs_3_.refs_11_), channel_id=1, source_target_pairs={{8,0},{16,8},{24,16},{9,1},{17,9},{25,17},{10,2},{18,10},{26,18},{... | collective-permute-start | bytes 1572872 | tf_op jit(solution)/shard_map/ppermute | solution.py:242
  213.4 23.0 %collective-permute-start.45 = (bf16[4,2,128,256]{3,2,1,0:T(8,128)(2,1)S(1)}, bf16[4,2,128,256]{3,2,1,0:T(8,128)(2,1)S(1)}, u32[]{:S(2)}, u32[]{:S(2)}) collective-permute-start(bf16[4,2,128,256]{3,2,1,0:T(8,128)(2,1)S(1)} %get-tuple-element.125), channel_id=1, source_target_pairs={{0,2},{1,3},{2,0},{3,1},{4,6},{5,7},{6,4},{7,5},{8,10},{9,11},{10,... | collective-permute-start | bytes 1572872 | tf_op jit(solution)/shard_map/ppermute | solution.py:234
  213.5 26.4 %collective-permute-start.47 = (bf16[4,2,128,256]{3,2,1,0:T(8,128)(2,1)S(1)}, bf16[4,2,128,256]{3,2,1,0:T(8,128)(2,1)S(1)}, u32[]{:S(2)}, u32[]{:S(2)}) collective-permute-start(bf16[4,2,128,256]{3,2,1,0:T(8,128)(2,1)S(1)} %get-tuple-element.126), channel_id=1, source_target_pairs={{0,6},{1,7},{2,4},{3,5},{4,2},{5,3},{6,0},{7,1},{8,14},{9,15},{10,... | collective-permute-start | bytes 1572872 | tf_op jit(solution)/shard_map/ppermute | solution.py:234
  217.6 23.6 %collective-permute-start.46 = (bf16[4,2,128,256]{3,2,1,0:T(8,128)(2,1)S(1)}, bf16[4,2,128,256]{3,2,1,0:T(8,128)(2,1)S(1)}, u32[]{:S(2)}, u32[]{:S(2)}) collective-permute-start(bf16[4,2,128,256]{3,2,1,0:T(8,128)(2,1)S(1)} %get-tuple-element.127), channel_id=1, source_target_pairs={{0,4},{1,5},{2,6},{3,7},{4,0},{5,1},{6,2},{7,3},{8,12},{9,13},{10,... | collective-permute-start | bytes 1572872 | tf_op jit(solution)/shard_map/ppermute | solution.py:234
  225.2 16.3 %collective-permute-start.37 = (bf16[8,128,256]{2,1,0:T(8,128)(2,1)S(1)}, bf16[8,128,256]{2,1,0:T(8,128)(2,1)S(1)}, u32[]{:S(2)}, u32[]{:S(2)}) collective-permute-start(bf16[8,128,256]{2,1,0:T(8,128)(2,1)S(1)} %collective-permute-done.36.refs_5_.refs_13_), channel_id=1, source_target_pairs={{8,0},{9,1},{10,2},{11,3},{12,4},{13,5},{14,6},{15,7}} | collective-permute-start | bytes 1572872 | tf_op jit(solution)/shard_map/ppermute | solution.py:242
  257.1 17.6 %collective-permute-start.52 = (bf16[4,2,128,256]{3,2,1,0:T(8,128)(2,1)S(1)}, bf16[4,2,128,256]{3,2,1,0:T(8,128)(2,1)S(1)}, u32[]{:S(2)}, u32[]{:S(2)}) collective-permute-start(bf16[4,2,128,256]{3,2,1,0:T(8,128)(2,1)S(1)} %get-tuple-element.122), channel_id=1, source_target_pairs={{0,2},{1,3},{2,0},{3,1},{4,6},{5,7},{6,4},{7,5},{8,10},{9,11},{10,... | collective-permute-start | bytes 1572872 | tf_op jit(solution)/shard_map/ppermute | solution.py:234
  259.6 25.4 %collective-permute-start.54 = (bf16[4,2,128,256]{3,2,1,0:T(8,128)(2,1)S(1)}, bf16[4,2,128,256]{3,2,1,0:T(8,128)(2,1)S(1)}, u32[]{:S(2)}, u32[]{:S(2)}) collective-permute-start(bf16[4,2,128,256]{3,2,1,0:T(8,128)(2,1)S(1)} %get-tuple-element.123), channel_id=1, source_target_pairs={{0,6},{1,7},{2,4},{3,5},{4,2},{5,3},{6,0},{7,1},{8,14},{9,15},{10,... | collective-permute-start | bytes 1572872 | tf_op jit(solution)/shard_map/ppermute | solution.py:234
  261.7 24.6 %collective-permute-start.53 = (bf16[4,2,128,256]{3,2,1,0:T(8,128)(2,1)S(1)}, bf16[4,2,128,256]{3,2,1,0:T(8,128)(2,1)S(1)}, u32[]{:S(2)}, u32[]{:S(2)}) collective-permute-start(bf16[4,2,128,256]{3,2,1,0:T(8,128)(2,1)S(1)} %get-tuple-element.124), channel_id=1, source_target_pairs={{0,4},{1,5},{2,6},{3,7},{4,0},{5,1},{6,2},{7,3},{8,12},{9,13},{10,... | collective-permute-start | bytes 1572872 | tf_op jit(solution)/shard_map/ppermute | solution.py:234
  261.7 31.4 %collective-permute-start.48 = (bf16[2,128,256]{2,1,0:T(8,128)(2,1)S(1)}, bf16[2,128,256]{2,1,0:T(8,128)(2,1)S(1)}, u32[]{:S(2)}, u32[]{:S(2)}) collective-permute-start(bf16[2,128,256]{2,1,0:T(8,128)(2,1)S(1)} %get-tuple-element.135), channel_id=1, source_target_pairs={{0,8},{8,0},{16,24},{24,16},{1,9},{9,1},{17,25},{25,17},{2,10},{10... | collective-permute-start | bytes 393224 | tf_op jit(solution)/shard_map/ppermute | solution.py:238
  266.6 26.6 %collective-permute-start.50 = (bf16[2,128,256]{2,1,0:T(8,128)(2,1)S(1)}, bf16[2,128,256]{2,1,0:T(8,128)(2,1)S(1)}, u32[]{:S(2)}, u32[]{:S(2)}) collective-permute-start(bf16[2,128,256]{2,1,0:T(8,128)(2,1)S(1)} %get-tuple-element.136), channel_id=1, source_target_pairs={{0,24},{8,16},{16,8},{24,0},{1,25},{9,17},{17,9},{25,1},{2,26},{10... | collective-permute-start | bytes 393224 | tf_op jit(solution)/shard_map/ppermute | solution.py:238
  274.7 18.5 %collective-permute-start.49 = (bf16[2,128,256]{2,1,0:T(8,128)(2,1)S(1)}, bf16[2,128,256]{2,1,0:T(8,128)(2,1)S(1)}, u32[]{:S(2)}, u32[]{:S(2)}) collective-permute-start(bf16[2,128,256]{2,1,0:T(8,128)(2,1)S(1)} %get-tuple-element.137), channel_id=1, source_target_pairs={{0,16},{8,24},{16,0},{24,8},{1,17},{9,25},{17,1},{25,9},{2,18},{10... | collective-permute-start | bytes 393224 | tf_op jit(solution)/shard_map/ppermute | solution.py:238
  (67 other events, 962.9 us)

commit v6 on v5

--- a/solution.py
+++ b/solution.py
@@ -11,7 +11,6 @@
 FF = 16384
 VMEM = 56 * 1024 * 1024
 GROUP = 4
-REACH = {0: (0,), 1: (-1, 1), 2: (-2, 2), 3: (-3, -1, 1, 3)}
 ANY = pl.BlockSpec(memory_space=pl.ANY)
 
 
@@ -55,20 +54,12 @@
     return copies
 
 
-def hidden_copies(refs, names, labels, held, sems, row):
+def hidden_copies(ref, labels, held, sems, row):
     copies = []
-    if names is None:
-        for g, block in enumerate(labels):
-            copies.append(pltpu.make_async_copy(refs[0].at[block], held.at[:, g], sems.at[g]))
-            copies[-1].start()
-        return copies
     for g, t in enumerate(labels):
-        distance = lax.bitwise_xor(row, t) - row
-        for name, ref in zip(names, refs):
-            if name in REACH[t]:
-                copy = pltpu.make_async_copy(ref, held.at[:, g], sems.at[g])
-                pl.when(distance == name)(copy.start)
-        copies.append(copy)
+        source = ref.at[lax.bitwise_xor(row, t)]
+        copies.append(pltpu.make_async_copy(source, held.at[:, g], sems.at[g]))
+        copies[-1].start()
     return copies
 
 
@@ -103,10 +94,9 @@
         out[...] = acc[:, part].astype(out.dtype)
 
 
-def from_hidden_kernel(cols, flip, names, labels, info, w_ref, *refs):
-    count = 1 if names is None else 2
-    h_refs, outs, (h, acc, sems) = refs[:-3 - count], refs[-3 - count:-3], refs[-3:]
-    copies = hidden_copies(h_refs, names, labels, h, sems, info[0])
+def from_hidden_kernel(cols, flip, labels, info, w_ref, *refs):
+    h_ref, *outs, h, acc, sems = refs
+    copies = hidden_copies(h_ref, labels, h, sems, info[0])
     acc[...] = jnp.zeros_like(acc)
     for copy in copies:
         copy.wait()
@@ -120,17 +110,16 @@
     for at, out in enumerate(outs):
         pieces, unit = out.shape[-3], out.shape[-1]
         for m in range(out.shape[0]):
-            owner = m if names is None else lax.bitwise_xor(info[1], 2 * m + at)
+            owner = m if len(outs) == 1 else lax.bitwise_xor(info[1], 2 * m + at)
             for q in range(pieces):
                 tile, lanes = tile_part(acc, owner, q, pieces, unit)
                 out[m, :, q] = acc[tile, :, :, lanes].astype(out.dtype)
 
 
-def grad_kernel(cols, flip, wides, names, labels, info, *refs):
-    x_refs, h_refs, refs = refs[:wides], refs[wides:-5], refs[-5:]
-    out, x, h, x_sems, h_sems = refs
+def grad_kernel(cols, flip, wides, labels, info, *refs):
+    x_refs, (h_ref, out, x, h, x_sems, h_sems) = refs[:wides], refs[wides:]
     copies = wide_copies(x_refs, x, x_sems, info[1])
-    copies += hidden_copies(h_refs, names, labels, h, h_sems, info[0])
+    copies += hidden_copies(h_ref, labels, h, h_sems, info[0])
     out[...] = jnp.zeros_like(out)
     for copy in copies:
         copy.wait()
@@ -176,21 +165,13 @@
     return call(kernel, outs, scratch, flops, 8 << 20, info, specs, [w, *xs])
 
 
-def sources(hs, labels):
-    if not isinstance(hs, dict):
-        return None, [hs]
-    names = sorted({name for t in labels for name in REACH[t]})
-    return names, [hs[name] for name in names]
-
-
-def from_hidden(info, hs, w, cols, flip, labels, devices):
-    names, hs = sources(hs, labels)
-    rows, tile = hs[0].shape[-2:]
+def from_hidden(info, h, w, cols, flip, labels, devices):
+    rows, tile = h.shape[-2:]
     slots, group = w.shape[0], len(labels)
     unit = min(tile, D // devices)
     pieces = D // devices // unit
     shape = (group, pieces, rows, unit)
-    if names is None:
+    if long_row():
         outs = [jax.ShapeDtypeStruct((devices, *shape), jnp.bfloat16)]
     else:
         outs = [jax.ShapeDtypeStruct((devices // 2, *shape), jnp.bfloat16)] * 2
@@ -199,18 +180,17 @@
         pltpu.VMEM((D // tile, group, rows, tile), jnp.float32),
         pltpu.SemaphoreType.DMA((group,)),
     ]
-    kernel = functools.partial(from_hidden_kernel, cols, flip, names, labels)
-    specs = [pl.BlockSpec(memory_space=pltpu.VMEM)] + [ANY] * len(hs)
+    kernel = functools.partial(from_hidden_kernel, cols, flip, labels)
+    specs = [pl.BlockSpec(memory_space=pltpu.VMEM), ANY]
     flops = 2 * slots * group * rows * tile * tile
-    return call(kernel, outs, scratch, flops, 8 << 20, info, specs, [w, *hs])
-
-
-def slot_grads(info, xs, hs, slots, cols, flip):
+    return call(kernel, outs, scratch, flops, 8 << 20, info, specs, [w, h])
+
+
+def slot_grads(info, xs, h, slots, cols, flip):
     blocks = lax.axis_size("row")
     labels = range(blocks)
-    names, hs = sources(hs, labels)
     rows, unit = xs[0].shape[-2:]
-    tile = hs[0].shape[-1]
+    tile = h.shape[-1]
     out = jax.ShapeDtypeStruct((slots, tile, tile), jnp.bfloat16)
     held, sems = wide_scratch(blocks, rows, tile, unit)
     scratch = [
@@ -219,10 +199,10 @@
         sems,
         pltpu.SemaphoreType.DMA((blocks,)),
     ]
-    kernel = functools.partial(grad_kernel, cols, flip, len(xs), names, labels)
-    specs = [ANY] * (len(xs) + len(hs))
+    kernel = functools.partial(grad_kernel, cols, flip, len(xs), labels)
+    specs = [ANY] * (len(xs) + 1)
     flops = 2 * slots * blocks * rows * tile * tile
-    return call(kernel, out, scratch, flops, 8 << 20, info, specs, [*xs, *hs])
+    return call(kernel, out, scratch, flops, 8 << 20, info, specs, [*xs, h])
 
 
 def long_row():
@@ -238,8 +218,8 @@
     return lax.ppermute(x, "row", [(s, s ^ t) for s in range(4)])
 
 
-def step_row(x, step, first, last):
-    return lax.ppermute(x, "row", [(s, s + step) for s in range(first, last + 1)])
+def send_row(x, *pairs):
+    return lax.ppermute(x, "row", pairs)
 
 
 def own_pieces(x, tile):
@@ -264,28 +244,21 @@
     return sum(term.astype(jnp.float32) for term in terms)
 
 
-def line_reduce(parts, row, second=(), third=()):
-    right = step_row(parts[3], 1, 0, 0)
-    left = step_row(parts[3], -1, 3, 3)
-    right, left = first = after((right, left), second)
-    right = step_row(add(parts[2], right).astype(jnp.bfloat16), 1, 0, 1)
-    left = step_row(add(parts[2], left).astype(jnp.bfloat16), -1, 2, 3)
-    right, left = again = after((right, left), third)
-    last_right = add(jnp.where(row == 1, parts[3], parts[1]), right).astype(jnp.bfloat16)
-    last_left = add(jnp.where(row == 2, parts[3], parts[1]), left).astype(jnp.bfloat16)
-    right = step_row(last_right, 1, 0, 2)
-    left = step_row(last_left, -1, 1, 3)
-    return (parts[0], right, left), (first, again), (last_right, last_left)
-
-
-def line_gather(x, waits=()):
-    held = {0: x}
-    for k in range(1, 4):
-        held[-k] = step_row(held[1 - k], 1, k - 1, 2)
-        held[k] = step_row(held[k - 1], -1, 1, 4 - k)
-        if k <= len(waits):
-            held[-k], held[k] = after((held[-k], held[k]), waits[k - 1])
-    return held
+def line_reduce(parts, row, wait=()):
+    right = send_row(parts[2], (0, 1), (1, 2))
+    left = send_row(parts[2], (3, 2), (2, 1))
+    far = send_row(parts[3], (0, 2), (3, 1))
+    right, left, far = first = after((right, left, far), wait)
+    none = jnp.zeros_like(far)
+    right = add(jnp.where(row == 1, parts[3], parts[1]), right, jnp.where(row == 2, far, none))
+    left = add(jnp.where(row == 2, parts[3], parts[1]), left, jnp.where(row == 1, far, none))
+    right = send_row(right.astype(jnp.bfloat16), (0, 1), (1, 2), (2, 3))
+    left = send_row(left.astype(jnp.bfloat16), (3, 2), (2, 1), (1, 0))
+    return (parts[0], right, left), first
+
+
+def line_gather(x):
+    return [x] + [swap_row(x, t) for t in range(1, 4)]
 
 
 def finish_col(even, odd):
@@ -335,30 +308,32 @@
 
 def on_line(info_in, info_out, tokens, upstream, w_in, w_out, cols, devices):
     row, slots = info_in[0], w_in.shape[0]
-    token_blocks = [tokens] + [swap_row(tokens, t) for t in range(1, 4)]
-    up_blocks = [upstream] + [swap_row(upstream, t) for t in range(1, 4)]
+    token_blocks, up_blocks = line_gather(tokens), line_gather(upstream)
     token_even = across(jnp.stack(token_blocks))
     up_mine = jnp.stack(up_blocks)
     all_tokens = with_odd(after(token_even, up_mine))
     up_even = across(after(up_mine, token_even[1:]))
     parts = to_hidden(info_in, all_tokens, w_in, cols, False)
     all_up = with_odd(after(up_even, parts))
-    terms, _, last = line_reduce(parts, row, up_even, all_up)
-    parts = to_hidden(info_out, after(all_up, last), w_out, cols, True)
+    terms, first = line_reduce(parts, row, up_even)
+    parts = to_hidden(info_out, after(all_up, first), w_out, cols, True)
     hidden = add(*after(terms, parts))
     activ = silu(hidden)
-    terms, steps, _ = line_reduce(after(parts, activ), row)
-    all_activ = line_gather(activ, steps)
-    all_grad = line_gather(activations(hidden, add(*terms)))
-    labels = range(4)
-
-    def column_sums(info, hs, w, flip):
-        return finish_col(*from_hidden(info, hs, w, cols, flip, labels, devices))
-
-    layer_sums = column_sums(info_out, all_activ, w_out, False)
+    terms, _ = line_reduce(after(parts, activ), row)
+    all_activ = lax.all_gather(activ, "row")
+    grad_hidden = activations(hidden, add(*terms))
+    all_grad = lax.all_gather(grad_hidden, "row")
+
+    def column_sums(info, hs, w, flip, labels):
+        total = finish_col(*from_hidden(info, hs, w, cols, flip, labels, devices))
+        return [total[g] for g in range(len(labels))]
+
+    all_activ = after(all_activ, grad_hidden)
+    layer_sums = column_sums(info_out, all_activ, w_out, False, (0, 1, 2, 3))
     grad_w_out = slot_grads(info_out, all_up, all_activ, slots, cols, False)
-    all_grad, layer_sums, grad_w_out = lax.optimization_barrier((all_grad, layer_sums, grad_w_out))
-    input_sums = column_sums(info_in, all_grad, w_in, True)
+    held = (all_grad, layer_sums, grad_w_out)
+    all_grad, layer_sums, grad_w_out = lax.optimization_barrier(held)
+    input_sums = column_sums(info_in, all_grad, w_in, True, (0, 1, 2, 3))
     grad_w_in = slot_grads(info_in, all_tokens, all_grad, slots, cols, True)
     layer_out, grad_tokens = finish_row(layer_sums), finish_row(input_sums)
     return layer_out, grad_tokens, grad_w_in, grad_w_out

time: 305 us -> 308 us (level)
  starting transfers between devices: 96.8 us -> 72.7 us
  between operations: 1.54 us -> 14.6 us
  waiting for transfers between devices: 141 us -> 151 us
    ppermute x24 -> x10, starting transfers between devices: 53.3 us -> 34.9 us  [send_row(): return lax.ppermute(x, 'row', pairs)]
    ppermute x22, waiting for transfers between devices: 31.4 us -> 48.1 us  [swap_col(): return lax.ppermute(x, 'col', [(s, s ^ m) for s in range(count)])]
    ppermute x24 -> x10, waiting for transfers between devices: 79.2 us -> 64.6 us  [send_row(): return lax.ppermute(x, 'row', pairs)]
    all_gather x0 -> x2, waiting for transfers between devices: none -> 13.7 us  [the longest x1 13.7 us: on_line(): all_grad = lax.all_gather(grad_hidden, 'row')]
    ppermute x12, waiting for transfers between devices: 30.7 us -> 24.5 us  [swap_row(): return lax.ppermute(x, 'row', [(s, s ^ t) for s in range(4)])]
    ppermute x12, starting transfers between devices: 25.5 us -> 19.4 us  [swap_row(): return lax.ppermute(x, 'row', [(s, s ^ t) for s in range(4)])]
    unnamed x70 -> x44, local copies, waits for them, and re-layouts: 6.13 us -> 6.62 us
  transfers between devices with their start and end apart: 58 -> 46, of which waited for: 29 -> 20; matrix products, arithmetic and copies ran while one was open for 3% -> 3% of each run, Pallas kernels for 10% -> 11%
where the time goes in v6:
time: 308 us; the launch traced here: 307 us
  waiting for transfers between devices  151 us (49%)
  starting transfers between devices  72.7 us (24%)
  Pallas kernels  49.2 us (16%)
  between operations  14.6 us (5%)
  other arithmetic  11.7 us (4%)
  local copies, waits for them, and re-layouts  7.61 us (2%)
    ppermute x10, waiting for transfers between devices, send_row(): return lax.ppermute(x, 'row', pairs)  64.6 us
    pallas_call x6, Pallas kernels, call(): pl.pallas_call(kernel, out_shape=out_shape, in_specs=[pl.BlockSpec(memory...  49.2 us
    ppermute x22, waiting for transfers between devices, swap_col(): return lax.ppermute(x, 'col', [(s, s ^ m) for s in range(count)])  48.1 us
    ppermute x10, starting transfers between devices, send_row(): return lax.ppermute(x, 'row', pairs)  34.9 us
    ppermute x12, waiting for transfers between devices, swap_row(): return lax.ppermute(x, 'row', [(s, s ^ t) for s in range(4)])  24.5 us
    ppermute x12, starting transfers between devices, swap_row(): return lax.ppermute(x, 'row', [(s, s ^ t) for s in range(4)])  19.4 us
    ppermute x22, starting transfers between devices, swap_col(): return lax.ppermute(x, 'col', [(s, s ^ m) for s in range(count)])  18.3 us
    all_gather x1, waiting for transfers between devices, on_line(): all_grad = lax.all_gather(grad_hidden, 'row')  13.7 us
  transfers between devices with their start and end apart: 46, of which 20 were waited for; matrix products, arithmetic and copies ran while one was open for 3% of the time, Pallas kernels for 11%

profile of v6, /device:TPU:0, one launch (start us, length us, event | category | flops | bytes accessed | tf_op | source)
XLA Modules:
  0.0 306.6 jit_solution(11739890597508166201)
XLA Ops:
  16.5 7.9 %collective-permute-done.4 = bf16[2,128,256]{2,1,0:T(8,128)(2,1)S(1)} collective-permute-done((bf16[2,128,256]{2,1,0:T(8,128)(2,1)S(1)}, bf16[2,128,256]{2,1,0:T(8,128)(2,1)S(1)}, u32[]{:S(2)}, u32[]{:S(2)}) %collective-permute-start.4) | collective-permute-done | bytes 131104 | tf_op jit(solution)/shard_map/ppermute | solution.py:218
  38.0 4.2 %collective-permute-done.1 = bf16[2,128,256]{2,1,0:T(8,128)(2,1)S(1)} collective-permute-done((bf16[2,128,256]{2,1,0:T(8,128)(2,1)S(1)}, bf16[2,128,256]{2,1,0:T(8,128)(2,1)S(1)}, u32[]{:S(2)}, u32[]{:S(2)}) %collective-permute-start.1) | collective-permute-done | bytes 131104 | tf_op jit(solution)/shard_map/ppermute | solution.py:218
  42.4 5.8 %collective-permute-done.7.refs_4_ = bf16[4,2,128,256]{3,2,1,0:T(8,128)(2,1)S(1)} collective-permute-done((bf16[4,2,128,256]{3,2,1,0:T(8,128)(2,1)S(1)}, bf16[4,2,128,256]{3,2,1,0:T(8,128)(2,1)S(1)}, u32[]{:S(2)}, u32[]{:S(2)}) %collective-permute-start.7) | collective-permute-done | bytes 524320 | tf_op jit(solution)/shard_map/ppermute | solution.py:214
  53.9 7.4 %shard_map.93 = (bf16[8,128,256]{2,1,0:T(8,128)(2,1)}, bf16[8,128,256]{2,1,0:T(8,128)(2,1)}, bf16[8,128,256]{2,1,0:T(8,128)(2,1)}, bf16[8,128,256]{2,1,0:T(8,128)(2,1)}) custom-call(s32[18]{0:T(128)} %pad_add_fusion.2.info, bf16[16,256,256]{2,1,0:T(8,128)(2,1)} %bitcast.75, bf16[4,2,128,256]{3,2,1,0:T(8,128)(2,1)} %copy-done.1, ...), custom_call_target="tpu_custom_call" | custom-call | flops 1073741824 | bytes 8388608 | tf_op jit(solution)/shard_map/pallas_call | solution.py:139
  61.3 4.4 %collective-permute-start.20 = (bf16[8,128,256]{2,1,0:T(8,128)(2,1)}, bf16[8,128,256]{2,1,0:T(8,128)(2,1)S(1)}, u32[]{:S(2)}, u32[]{:S(2)}) collective-permute-start(bf16[8,128,256]{2,1,0:T(8,128)(2,1)} %get-tuple-element.60), channel_id=1, source_target_pairs={{0,8},{8,16},{1,9},{9,17},{2,10},{10,18},{3,11},{11,19},{4,12},{12... | collective-permute-start | bytes 1572872 | tf_op jit(solution)/shard_map/ppermute | solution.py:222
  66.4 8.1 %collective-permute-done.10.refs_4_ = bf16[4,2,128,256]{3,2,1,0:T(8,128)(2,1)} collective-permute-done((bf16[4,2,128,256]{3,2,1,0:T(8,128)(2,1)S(1)}, bf16[4,2,128,256]{3,2,1,0:T(8,128)(2,1)}, u32[]{:S(2)}, u32[]{:S(2)}) %collective-permute-start.10) | collective-permute-done | bytes 524320 | tf_op jit(solution)/shard_map/ppermute | solution.py:214
  74.5 6.4 %collective-permute-start.22 = (bf16[8,128,256]{2,1,0:T(8,128)(2,1)}, bf16[8,128,256]{2,1,0:T(8,128)(2,1)S(1)}, u32[]{:S(2)}, u32[]{:S(2)}) collective-permute-start(bf16[8,128,256]{2,1,0:T(8,128)(2,1)} %get-tuple-element.61), channel_id=1, source_target_pairs={{0,16},{24,8},{1,17},{25,9},{2,18},{26,10},{3,19},{27,11},{4,20},{... | collective-permute-start | bytes 1572872 | tf_op jit(solution)/shard_map/ppermute | solution.py:222
  83.0 8.8 %collective-permute-done.22 = bf16[8,128,256]{2,1,0:T(8,128)(2,1)S(1)} collective-permute-done((bf16[8,128,256]{2,1,0:T(8,128)(2,1)}, bf16[8,128,256]{2,1,0:T(8,128)(2,1)S(1)}, u32[]{:S(2)}, u32[]{:S(2)}) %collective-permute-start.22) | collective-permute-done | bytes 524320 | tf_op jit(solution)/shard_map/ppermute | solution.py:222
  93.5 5.4 %collective-permute-start.23 = (bf16[8,128,256]{2,1,0:T(8,128)(2,1)S(1)}, bf16[8,128,256]{2,1,0:T(8,128)(2,1)S(1)}, u32[]{:S(2)}, u32[]{:S(2)}) collective-permute-start(bf16[8,128,256]{2,1,0:T(8,128)(2,1)S(1)} %get-tuple-element.119), channel_id=1, source_target_pairs={{0,8},{8,16},{16,24},{1,9},{9,17},{17,25},{2,10},{10,18},{18,26},{... | collective-permute-start | bytes 1572872 | tf_op jit(solution)/shard_map/ppermute | solution.py:222
  102.2 8.8 %shard_map.94 = (bf16[8,128,256]{2,1,0:T(8,128)(2,1)}, bf16[8,128,256]{2,1,0:T(8,128)(2,1)}, bf16[8,128,256]{2,1,0:T(8,128)(2,1)}, bf16[8,128,256]{2,1,0:T(8,128)(2,1)}) custom-call(s32[18]{0:T(128)} %pad_add_fusion.info, bf16[16,256,256]{2,1,0:T(8,128)(2,1)} %bitcast.73, bf16[4,2,128,256]{3,2,1,0:T(8,128)(2,1)} %copy-done.2, ...), custom_call_target="tpu_custom_call" | custom-call | flops 1073741824 | bytes 8388608 | tf_op jit(solution)/shard_map/pallas_call | solution.py:139
  120.0 4.6 %collective-permute-start.27 = (bf16[8,128,256]{2,1,0:T(8,128)(2,1)S(1)}, bf16[8,128,256]{2,1,0:T(8,128)(2,1)S(1)}, u32[]{:S(2)}, u32[]{:S(2)}) collective-permute-start(bf16[8,128,256]{2,1,0:T(8,128)(2,1)S(1)} %copy-done.18), channel_id=1, source_target_pairs={{0,16},{24,8},{1,17},{25,9},{2,18},{26,10},{3,19},{27,11},{4,20},{... | collective-permute-start | bytes 1572872 | tf_op jit(solution)/shard_map/ppermute | solution.py:222
  124.6 17.8 %collective-permute-done.25 = bf16[8,128,256]{2,1,0:T(8,128)(2,1)S(1)} collective-permute-done((bf16[8,128,256]{2,1,0:T(8,128)(2,1)}, bf16[8,128,256]{2,1,0:T(8,128)(2,1)S(1)}, u32[]{:S(2)}, u32[]{:S(2)}) %collective-permute-start.25) | collective-permute-done | bytes 524320 | tf_op jit(solution)/shard_map/ppermute | solution.py:222
  142.4 21.3 %collective-permute-done.27 = bf16[8,128,256]{2,1,0:T(8,128)(2,1)S(1)} collective-permute-done((bf16[8,128,256]{2,1,0:T(8,128)(2,1)S(1)}, bf16[8,128,256]{2,1,0:T(8,128)(2,1)S(1)}, u32[]{:S(2)}, u32[]{:S(2)}) %collective-permute-start.27) | collective-permute-done | bytes 524320 | tf_op jit(solution)/shard_map/ppermute | solution.py:222
  164.2 7.7 %collective-permute-start.28 = (bf16[8,128,256]{2,1,0:T(8,128)(2,1)S(1)}, bf16[8,128,256]{2,1,0:T(8,128)(2,1)S(1)}, u32[]{:S(2)}, u32[]{:S(2)}) collective-permute-start(bf16[8,128,256]{2,1,0:T(8,128)(2,1)S(1)} %get-tuple-element.116), channel_id=1, source_target_pairs={{0,8},{8,16},{16,24},{1,9},{9,17},{17,25},{2,10},{10,18},{18,26},{... | collective-permute-start | bytes 1572872 | tf_op jit(solution)/shard_map/ppermute | solution.py:222
  173.4 12.9 %collective-permute-done.28 = bf16[8,128,256]{2,1,0:T(8,128)(2,1)S(1)} collective-permute-done((bf16[8,128,256]{2,1,0:T(8,128)(2,1)S(1)}, bf16[8,128,256]{2,1,0:T(8,128)(2,1)S(1)}, u32[]{:S(2)}, u32[]{:S(2)}) %collective-permute-start.28) | collective-permute-done | bytes 524320 | tf_op jit(solution)/shard_map/ppermute | solution.py:222
  187.7 8.6 %shard_map.95 = (bf16[4,4,2,128,256]{4,3,2,1,0:T(8,128)(2,1)}, bf16[4,4,2,128,256]{4,3,2,1,0:T(8,128)(2,1)}) custom-call(s32[18]{0:T(128)} %pad_add_fusion.info, bf16[16,256,256]{2,1,0:T(8,128)(2,1)} %bitcast.74, bf16[4,8,128,256]{3,2,1,0:T(8,128)(2,1)} %bitcast.79), custom_call_target="tpu_custom_call" | custom-call | flops 1073741824 | bytes 8388608 | tf_op jit(solution)/shard_map/pallas_call | solution.py:139
  196.5 4.3 %collective-permute-done.30 = bf16[4,4,2,128,256]{4,3,2,1,0:T(8,128)(2,1)S(1)} collective-permute-done((bf16[4,4,2,128,256]{4,3,2,1,0:T(8,128)(2,1)}, bf16[4,4,2,128,256]{4,3,2,1,0:T(8,128)(2,1)S(1)}, u32[]{:S(2)}, u32[]{:S(2)}) %collective-permute-start.30) | collective-permute-done | bytes 2097184 | tf_op jit(solution)/shard_map/ppermute | solution.py:214
  206.8 8.6 %shard_map.96 = bf16[16,256,256]{2,1,0:T(8,128)(2,1)} custom-call(s32[18]{0:T(128)} %pad_add_fusion.info, bf16[4,2,128,256]{3,2,1,0:T(8,128)(2,1)} %copy-done.2, bf16[4,2,128,256]{3,2,1,0:T(8,128)(2,1)} %copy-done.9, bf16[4,2,128,256]{3,2,1,0:T(8,128)(2,1)} %copy-done.8, bf16[4,2,128,256]{3,2,1,0:T(8,128)(2,1)} %copy-done.10, ...), custom_call_target="tpu_custom_call" | custom-call | flops 1073741824 | bytes 8388608 | tf_op jit(solution)/shard_map/pallas_call | solution.py:139
  218.1 10.5 %collective-permute-done.32 = bf16[4,2,128,256]{3,2,1,0:T(8,128)(2,1)S(1)} collective-permute-done((bf16[4,2,128,256]{3,2,1,0:T(8,128)(2,1)S(1)}, bf16[4,2,128,256]{3,2,1,0:T(8,128)(2,1)S(1)}, u32[]{:S(2)}, u32[]{:S(2)}) %collective-permute-start.32) | collective-permute-done | bytes 524320 | tf_op jit(solution)/shard_map/ppermute | solution.py:214
  229.0 13.7 %all-gather.5.cloned.1.call-done = bf16[32,128,256]{2,1,0:T(8,128)(2,1)} async-done(((bf16[8,128,256]{2,1,0:T(8,128)(2,1)}), bf16[32,128,256]{2,1,0:T(8,128)(2,1)}) %all-gather.5.cloned.1.call-update) | async-done | bytes 2097168 | tf_op jit(solution)/shard_map/all_gather | solution.py:325
  242.7 8.1 %shard_map.97 = (bf16[4,4,2,128,256]{4,3,2,1,0:T(8,128)(2,1)}, bf16[4,4,2,128,256]{4,3,2,1,0:T(8,128)(2,1)}) custom-call(s32[18]{0:T(128)} %pad_add_fusion.2.info, bf16[16,256,256]{2,1,0:T(8,128)(2,1)} %bitcast.76, bf16[4,8,128,256]{3,2,1,0:T(8,128)(2,1)} %bitcast.77), custom_call_target="tpu_custom_call" | custom-call | flops 1073741824 | bytes 8388608 | tf_op jit(solution)/shard_map/pallas_call | solution.py:139
  264.1 7.6 %shard_map.98 = bf16[16,256,256]{2,1,0:T(8,128)(2,1)} custom-call(s32[18]{0:T(128)} %pad_add_fusion.2.info, bf16[4,2,128,256]{3,2,1,0:T(8,128)(2,1)} %copy-done.1, bf16[4,2,128,256]{3,2,1,0:T(8,128)(2,1)} %copy-done.6, bf16[4,2,128,256]{3,2,1,0:T(8,128)(2,1)} %copy-done.3, bf16[4,2,128,256]{3,2,1,0:T(8,128)(2,1)} %collective-permute-done.13.refs_3_, ...), custom_call_target="tpu_custom_call" | custom-call | flops 1073741824 | bytes 8388608 | tf_op jit(solution)/shard_map/pallas_call | solution.py:139
  274.4 11.2 %collective-permute-done.39 = bf16[4,2,128,256]{3,2,1,0:T(8,128)(2,1)S(1)} collective-permute-done((bf16[4,2,128,256]{3,2,1,0:T(8,128)(2,1)S(1)}, bf16[4,2,128,256]{3,2,1,0:T(8,128)(2,1)S(1)}, u32[]{:S(2)}, u32[]{:S(2)}) %collective-permute-start.39) | collective-permute-done | bytes 524320 | tf_op jit(solution)/shard_map/ppermute | solution.py:214
  292.7 6.1 %collective-permute-done.42 = bf16[2,128,256]{2,1,0:T(8,128)(2,1)S(1)} collective-permute-done((bf16[2,128,256]{2,1,0:T(8,128)(2,1)S(1)}, bf16[2,128,256]{2,1,0:T(8,128)(2,1)S(1)}, u32[]{:S(2)}, u32[]{:S(2)}) %collective-permute-start.42) | collective-permute-done | bytes 131104 | tf_op jit(solution)/shard_map/ppermute | solution.py:218
  (144 shorter events, 81.8 us)
Async XLA Ops:
  7.2 180.5 %all-gather.7.cloned.1.call-start = ((), (), s32[]{:S(2)}) async-start(), calls=%async_computation.1 | async-start | bytes 2621440 | tf_op jit(solution)/shard_map/all_gather | solution.py:323
  24.5 17.9 %collective-permute-start.6 = (bf16[4,2,128,256]{3,2,1,0:T(8,128)(2,1)S(1)}, bf16[4,2,128,256]{3,2,1,0:T(8,128)(2,1)S(1)}, u32[]{:S(2)}, u32[]{:S(2)}) collective-permute-start(bf16[4,2,128,256]{3,2,1,0:T(8,128)(2,1)S(1)} %pad_maximum_fusion.1.refs_0_), channel_id=1, source_target_pairs={{0,2},{1,3},{2,0},{3,1},{4,6},{5,7},{6,4},{7,5},{8,10},{9,11},{10,... | collective-permute-start | bytes 1572872 | tf_op jit(solution)/shard_map/ppermute | solution.py:214
  26.0 22.2 %collective-permute-start.7 = (bf16[4,2,128,256]{3,2,1,0:T(8,128)(2,1)S(1)}, bf16[4,2,128,256]{3,2,1,0:T(8,128)(2,1)S(1)}, u32[]{:S(2)}, u32[]{:S(2)}) collective-permute-start(bf16[4,2,128,256]{3,2,1,0:T(8,128)(2,1)S(1)} %pad_maximum_fusion.1.refs_0_), channel_id=1, source_target_pairs={{0,4},{1,5},{2,6},{3,7},{4,0},{5,1},{6,2},{7,3},{8,12},{9,13},{10,... | collective-permute-start | bytes 1572872 | tf_op jit(solution)/shard_map/ppermute | solution.py:214
  27.6 20.7 %collective-permute-start.8 = (bf16[4,2,128,256]{3,2,1,0:T(8,128)(2,1)S(1)}, bf16[4,2,128,256]{3,2,1,0:T(8,128)(2,1)S(1)}, u32[]{:S(2)}, u32[]{:S(2)}) collective-permute-start(bf16[4,2,128,256]{3,2,1,0:T(8,128)(2,1)S(1)} %pad_maximum_fusion.1.refs_0_), channel_id=1, source_target_pairs={{0,6},{1,7},{2,4},{3,5},{4,2},{5,3},{6,0},{7,1},{8,14},{9,15},{10,... | collective-permute-start | bytes 1572872 | tf_op jit(solution)/shard_map/ppermute | solution.py:214
  49.3 25.2 %collective-permute-start.10 = (bf16[4,2,128,256]{3,2,1,0:T(8,128)(2,1)S(1)}, bf16[4,2,128,256]{3,2,1,0:T(8,128)(2,1)}, u32[]{:S(2)}, u32[]{:S(2)}) collective-permute-start(bf16[4,2,128,256]{3,2,1,0:T(8,128)(2,1)S(1)} %pad_maximum_fusion.refs_0_), channel_id=1, source_target_pairs={{0,4},{1,5},{2,6},{3,7},{4,0},{5,1},{6,2},{7,3},{8,12},{9,13},{10,... | collective-permute-start | bytes 1572872 | tf_op jit(solution)/shard_map/ppermute | solution.py:214
  50.9 30.1 %collective-permute-start.11 = (bf16[4,2,128,256]{3,2,1,0:T(8,128)(2,1)S(1)}, bf16[4,2,128,256]{3,2,1,0:T(8,128)(2,1)S(1)}, u32[]{:S(2)}, u32[]{:S(2)}) collective-permute-start(bf16[4,2,128,256]{3,2,1,0:T(8,128)(2,1)S(1)} %pad_maximum_fusion.refs_0_), channel_id=1, source_target_pairs={{0,6},{1,7},{2,4},{3,5},{4,2},{5,3},{6,0},{7,1},{8,14},{9,15},{10,... | collective-permute-start | bytes 1572872 | tf_op jit(solution)/shard_map/ppermute | solution.py:214
  52.0 28.9 %collective-permute-start.9 = (bf16[4,2,128,256]{3,2,1,0:T(8,128)(2,1)S(1)}, bf16[4,2,128,256]{3,2,1,0:T(8,128)(2,1)S(1)}, u32[]{:S(2)}, u32[]{:S(2)}) collective-permute-start(bf16[4,2,128,256]{3,2,1,0:T(8,128)(2,1)S(1)} %pad_maximum_fusion.refs_0_), channel_id=1, source_target_pairs={{0,2},{1,3},{2,0},{3,1},{4,6},{5,7},{6,4},{7,5},{8,10},{9,11},{10,... | collective-permute-start | bytes 1572872 | tf_op jit(solution)/shard_map/ppermute | solution.py:214
  61.3 21.1 %collective-permute-start.20 = (bf16[8,128,256]{2,1,0:T(8,128)(2,1)}, bf16[8,128,256]{2,1,0:T(8,128)(2,1)S(1)}, u32[]{:S(2)}, u32[]{:S(2)}) collective-permute-start(bf16[8,128,256]{2,1,0:T(8,128)(2,1)} %get-tuple-element.60), channel_id=1, source_target_pairs={{0,8},{8,16},{1,9},{9,17},{2,10},{10,18},{3,11},{11,19},{4,12},{12... | collective-permute-start | bytes 1572872 | tf_op jit(solution)/shard_map/ppermute | solution.py:222
  74.5 17.3 %collective-permute-start.22 = (bf16[8,128,256]{2,1,0:T(8,128)(2,1)}, bf16[8,128,256]{2,1,0:T(8,128)(2,1)S(1)}, u32[]{:S(2)}, u32[]{:S(2)}) collective-permute-start(bf16[8,128,256]{2,1,0:T(8,128)(2,1)} %get-tuple-element.61), channel_id=1, source_target_pairs={{0,16},{24,8},{1,17},{25,9},{2,18},{26,10},{3,19},{27,11},{4,20},{... | collective-permute-start | bytes 1572872 | tf_op jit(solution)/shard_map/ppermute | solution.py:222
  81.9 19.0 %collective-permute-start.17 = (bf16[4,2,128,256]{3,2,1,0:T(8,128)(2,1)}, bf16[4,2,128,256]{3,2,1,0:T(8,128)(2,1)S(1)}, u32[]{:S(2)}, u32[]{:S(2)}) collective-permute-start(bf16[4,2,128,256]{3,2,1,0:T(8,128)(2,1)} %copy-done.8), channel_id=1, source_target_pairs={{0,1},{1,0},{2,3},{3,2},{4,5},{5,4},{6,7},{7,6},{8,9},{9,8},{10,11... | collective-permute-start | bytes 1572872 | tf_op jit(solution)/shard_map/ppermute | solution.py:214
  82.5 18.5 %collective-permute-start.18 = (bf16[4,2,128,256]{3,2,1,0:T(8,128)(2,1)}, bf16[4,2,128,256]{3,2,1,0:T(8,128)(2,1)S(1)}, u32[]{:S(2)}, u32[]{:S(2)}) collective-permute-start(bf16[4,2,128,256]{3,2,1,0:T(8,128)(2,1)} %collective-permute-done.10.refs_4_), channel_id=1, source_target_pairs={{0,1},{1,0},{2,3},{3,2},{4,5},{5,4},{6,7},{7,6},{8,9},{9,8},{10,11... | collective-permute-start | bytes 1572872 | tf_op jit(solution)/shard_map/ppermute | solution.py:214
  82.5 18.5 %collective-permute-start.19 = (bf16[4,2,128,256]{3,2,1,0:T(8,128)(2,1)}, bf16[4,2,128,256]{3,2,1,0:T(8,128)(2,1)S(1)}, u32[]{:S(2)}, u32[]{:S(2)}) collective-permute-start(bf16[4,2,128,256]{3,2,1,0:T(8,128)(2,1)} %copy-done.7), channel_id=1, source_target_pairs={{0,1},{1,0},{2,3},{3,2},{4,5},{5,4},{6,7},{7,6},{8,9},{9,8},{10,11... | collective-permute-start | bytes 1572872 | tf_op jit(solution)/shard_map/ppermute | solution.py:214
  93.5 17.6 %collective-permute-start.23 = (bf16[8,128,256]{2,1,0:T(8,128)(2,1)S(1)}, bf16[8,128,256]{2,1,0:T(8,128)(2,1)S(1)}, u32[]{:S(2)}, u32[]{:S(2)}) collective-permute-start(bf16[8,128,256]{2,1,0:T(8,128)(2,1)S(1)} %get-tuple-element.119), channel_id=1, source_target_pairs={{0,8},{8,16},{16,24},{1,9},{9,17},{17,25},{2,10},{10,18},{18,26},{... | collective-permute-start | bytes 1572872 | tf_op jit(solution)/shard_map/ppermute | solution.py:222
  116.9 125.8 %all-gather.5.cloned.1.call-start = ((), (), s32[]{:S(2)}) async-start(), calls=%async_computation | async-start | bytes 2621440 | tf_op jit(solution)/shard_map/all_gather | solution.py:325
  116.9 25.5 %collective-permute-start.25 = (bf16[8,128,256]{2,1,0:T(8,128)(2,1)}, bf16[8,128,256]{2,1,0:T(8,128)(2,1)S(1)}, u32[]{:S(2)}, u32[]{:S(2)}) collective-permute-start(bf16[8,128,256]{2,1,0:T(8,128)(2,1)} %get-tuple-element.87), channel_id=1, source_target_pairs={{0,8},{8,16},{1,9},{9,17},{2,10},{10,18},{3,11},{11,19},{4,12},{12... | collective-permute-start | bytes 1572872 | tf_op jit(solution)/shard_map/ppermute | solution.py:222
  119.3 23.1 %collective-permute-start.26 = (bf16[8,128,256]{2,1,0:T(8,128)(2,1)}, bf16[8,128,256]{2,1,0:T(8,128)(2,1)S(1)}, u32[]{:S(2)}, u32[]{:S(2)}) collective-permute-start(bf16[8,128,256]{2,1,0:T(8,128)(2,1)} %get-tuple-element.87), channel_id=1, source_target_pairs={{24,16},{16,8},{25,17},{17,9},{26,18},{18,10},{27,19},{19,11},{28,... | collective-permute-start | bytes 1572872 | tf_op jit(solution)/shard_map/ppermute | solution.py:222
  120.0 43.7 %collective-permute-start.27 = (bf16[8,128,256]{2,1,0:T(8,128)(2,1)S(1)}, bf16[8,128,256]{2,1,0:T(8,128)(2,1)S(1)}, u32[]{:S(2)}, u32[]{:S(2)}) collective-permute-start(bf16[8,128,256]{2,1,0:T(8,128)(2,1)S(1)} %copy-done.18), channel_id=1, source_target_pairs={{0,16},{24,8},{1,17},{25,9},{2,18},{26,10},{3,19},{27,11},{4,20},{... | collective-permute-start | bytes 1572872 | tf_op jit(solution)/shard_map/ppermute | solution.py:222
  164.2 22.0 %collective-permute-start.28 = (bf16[8,128,256]{2,1,0:T(8,128)(2,1)S(1)}, bf16[8,128,256]{2,1,0:T(8,128)(2,1)S(1)}, u32[]{:S(2)}, u32[]{:S(2)}) collective-permute-start(bf16[8,128,256]{2,1,0:T(8,128)(2,1)S(1)} %get-tuple-element.116), channel_id=1, source_target_pairs={{0,8},{8,16},{16,24},{1,9},{9,17},{17,25},{2,10},{10,18},{18,26},{... | collective-permute-start | bytes 1572872 | tf_op jit(solution)/shard_map/ppermute | solution.py:222
  203.4 25.3 %collective-permute-start.32 = (bf16[4,2,128,256]{3,2,1,0:T(8,128)(2,1)S(1)}, bf16[4,2,128,256]{3,2,1,0:T(8,128)(2,1)S(1)}, u32[]{:S(2)}, u32[]{:S(2)}) collective-permute-start(bf16[4,2,128,256]{3,2,1,0:T(8,128)(2,1)S(1)} %get-tuple-element.115), channel_id=1, source_target_pairs={{0,4},{1,5},{2,6},{3,7},{4,0},{5,1},{6,2},{7,3},{8,12},{9,13},{10,... | collective-permute-start | bytes 1572872 | tf_op jit(solution)/shard_map/ppermute | solution.py:214
  203.6 25.0 %collective-permute-start.33 = (bf16[4,2,128,256]{3,2,1,0:T(8,128)(2,1)S(1)}, bf16[4,2,128,256]{3,2,1,0:T(8,128)(2,1)S(1)}, u32[]{:S(2)}, u32[]{:S(2)}) collective-permute-start(bf16[4,2,128,256]{3,2,1,0:T(8,128)(2,1)S(1)} %get-tuple-element.114), channel_id=1, source_target_pairs={{0,6},{1,7},{2,4},{3,5},{4,2},{5,3},{6,0},{7,1},{8,14},{9,15},{10,... | collective-permute-start | bytes 1572872 | tf_op jit(solution)/shard_map/ppermute | solution.py:214
  259.2 26.4 %collective-permute-start.39 = (bf16[4,2,128,256]{3,2,1,0:T(8,128)(2,1)S(1)}, bf16[4,2,128,256]{3,2,1,0:T(8,128)(2,1)S(1)}, u32[]{:S(2)}, u32[]{:S(2)}) collective-permute-start(bf16[4,2,128,256]{3,2,1,0:T(8,128)(2,1)S(1)} %get-tuple-element.112), channel_id=1, source_target_pairs={{0,4},{1,5},{2,6},{3,7},{4,0},{5,1},{6,2},{7,3},{8,12},{9,13},{10,... | collective-permute-start | bytes 1572872 | tf_op jit(solution)/shard_map/ppermute | solution.py:214
  262.4 23.2 %collective-permute-start.40 = (bf16[4,2,128,256]{3,2,1,0:T(8,128)(2,1)S(1)}, bf16[4,2,128,256]{3,2,1,0:T(8,128)(2,1)S(1)}, u32[]{:S(2)}, u32[]{:S(2)}) collective-permute-start(bf16[4,2,128,256]{3,2,1,0:T(8,128)(2,1)S(1)} %get-tuple-element.111), channel_id=1, source_target_pairs={{0,6},{1,7},{2,4},{3,5},{4,2},{5,3},{6,0},{7,1},{8,14},{9,15},{10,... | collective-permute-start | bytes 1572872 | tf_op jit(solution)/shard_map/ppermute | solution.py:214
  262.4 25.3 %collective-permute-start.34 = (bf16[2,128,256]{2,1,0:T(8,128)(2,1)S(1)}, bf16[2,128,256]{2,1,0:T(8,128)(2,1)S(1)}, u32[]{:S(2)}, u32[]{:S(2)}) collective-permute-start(bf16[2,128,256]{2,1,0:T(8,128)(2,1)S(1)} %get-tuple-element.95), channel_id=1, source_target_pairs={{0,8},{8,0},{16,24},{24,16},{1,9},{9,1},{17,25},{25,17},{2,10},{10... | collective-permute-start | bytes 393224 | tf_op jit(solution)/shard_map/ppermute | solution.py:218
  262.4 28.0 %collective-permute-start.35 = (bf16[2,128,256]{2,1,0:T(8,128)(2,1)S(1)}, bf16[2,128,256]{2,1,0:T(8,128)(2,1)S(1)}, u32[]{:S(2)}, u32[]{:S(2)}) collective-permute-start(bf16[2,128,256]{2,1,0:T(8,128)(2,1)S(1)} %get-tuple-element.96), channel_id=1, source_target_pairs={{0,16},{8,24},{16,0},{24,8},{1,17},{9,25},{17,1},{25,9},{2,18},{10... | collective-permute-start | bytes 393224 | tf_op jit(solution)/shard_map/ppermute | solution.py:218
  (42 other events, 621.5 us)
Sparse Core Ops, SparseCore 0:
  117.0 66.7 all-gather.6
  196.6 46.0 all-gather.4

commit v7 on v6

--- a/solution.py
+++ b/solution.py
@@ -38,34 +38,36 @@
     return lax.div(owner, parts), pl.ds(lane, unit)
 
 
-def wide_copies(refs, held, sems, col):
+def wide_copies(refs, labels, held, sems, col):
     copies = []
     if len(refs) == 1:
         pairs = [(m, refs[0].at[m]) for m in range(refs[0].shape[0])]
     else:
         pairs = [(lax.bitwise_xor(col, m), ref) for m, ref in enumerate(refs)]
     for owner, ref in pairs:
-        _, pieces, _, unit = ref.shape
+        blocks, pieces, _, unit = ref.shape
+        whole = len(labels) == blocks
         for q in range(pieces):
             tile, lanes = tile_part(held, owner, q, pieces, unit)
-            target = held.at[tile, :, :, lanes]
-            copies.append(pltpu.make_async_copy(ref.at[:, q], target, sems.at[len(copies)]))
-            copies[-1].start()
+            for g, t in [(slice(None), slice(None))] if whole else enumerate(labels):
+                target = held.at[tile, g, :, lanes]
+                copies.append(pltpu.make_async_copy(ref.at[t, q], target, sems.at[len(copies)]))
+                copies[-1].start()
     return copies
 
 
-def hidden_copies(ref, labels, held, sems, row):
+def hidden_copies(refs, labels, held, sems, row):
     copies = []
     for g, t in enumerate(labels):
-        source = ref.at[lax.bitwise_xor(row, t)]
+        source = refs[g] if len(refs) > 1 else refs[0].at[lax.bitwise_xor(row, t)]
         copies.append(pltpu.make_async_copy(source, held.at[:, g], sems.at[g]))
         copies[-1].start()
     return copies
 
 
-def over_slots(info, slots, cols, body):
+def over_slots(info, first, slots, cols, body):
     def slot(s, carry):
-        code = info[2 + s]
+        code = info[2 + first + s]
 
         @pl.when(code >= 0)
         def _():
@@ -76,37 +78,40 @@
     lax.fori_loop(0, slots, slot, 0)
 
 
-def to_hidden_kernel(cols, flip, wides, info, w_ref, *refs):
-    x_refs, refs = refs[:wides], refs[wides:]
+def to_hidden_kernel(cols, flip, labels, wides, weights, info, *refs):
+    w_refs, x_refs, refs = refs[:weights], refs[weights:weights + wides], refs[weights + wides:]
     *outs, x, acc, sems = refs
-    copies = wide_copies(x_refs, x, sems, info[1])
+    copies = wide_copies(x_refs, labels, x, sems, info[1])
     acc[...] = jnp.zeros_like(acc)
     for copy in copies:
         copy.wait()
 
-    def add(s, wide, hidden):
-        for chunk in chunks(x.shape[1]):
-            product = matmul(flat(x[wide, chunk]), w_ref[s], 1, 1 if flip else 0)
-            acc[hidden, chunk] += product.reshape(-1, *acc.shape[2:])
-
-    over_slots(info, w_ref.shape[0], cols, add)
+    for at, w_ref in enumerate(w_refs):
+        def add(s, wide, hidden, w_ref=w_ref):
+            for chunk in chunks(x.shape[1]):
+                product = matmul(flat(x[wide, chunk]), w_ref[s], 1, 1 if flip else 0)
+                acc[hidden, chunk] += product.reshape(-1, *acc.shape[2:])
+
+        over_slots(info, at * w_ref.shape[0], w_ref.shape[0], cols, add)
     for part, out in enumerate(outs):
         out[...] = acc[:, part].astype(out.dtype)
 
 
-def from_hidden_kernel(cols, flip, labels, info, w_ref, *refs):
-    h_ref, *outs, h, acc, sems = refs
-    copies = hidden_copies(h_ref, labels, h, sems, info[0])
+def from_hidden_kernel(cols, flip, labels, hiddens, weights, info, *refs):
+    w_refs, h_refs = refs[:weights], refs[weights:weights + hiddens]
+    *outs, h, acc, sems = refs[weights + hiddens:]
+    copies = hidden_copies(h_refs, labels, h, sems, info[0])
     acc[...] = jnp.zeros_like(acc)
     for copy in copies:
         copy.wait()
 
-    def add(s, wide, hidden):
-        for chunk in chunks(h.shape[1]):
-            product = matmul(flat(h[hidden, chunk]), w_ref[s], 1, 1 if flip else 0)
-            acc[wide, chunk] += product.reshape(-1, *acc.shape[2:])
-
-    over_slots(info, w_ref.shape[0], cols, add)
+    for at, w_ref in enumerate(w_refs):
+        def add(s, wide, hidden, w_ref=w_ref):
+            for chunk in chunks(h.shape[1]):
+                product = matmul(flat(h[hidden, chunk]), w_ref[s], 1, 1 if flip else 0)
+                acc[wide, chunk] += product.reshape(-1, *acc.shape[2:])
+
+        over_slots(info, at * w_ref.shape[0], w_ref.shape[0], cols, add)
     for at, out in enumerate(outs):
         pieces, unit = out.shape[-3], out.shape[-1]
         for m in range(out.shape[0]):
@@ -117,9 +122,10 @@
 
 
 def grad_kernel(cols, flip, wides, labels, info, *refs):
-    x_refs, (h_ref, out, x, h, x_sems, h_sems) = refs[:wides], refs[wides:]
-    copies = wide_copies(x_refs, x, x_sems, info[1])
-    copies += hidden_copies(h_ref, labels, h, h_sems, info[0])
+    x_refs, h_refs = refs[:wides], refs[wides:-5]
+    out, x, h, x_sems, h_sems = refs[-5:]
+    copies = wide_copies(x_refs, labels, x, x_sems, info[1])
+    copies += hidden_copies(h_refs, labels, h, h_sems, info[0])
     out[...] = jnp.zeros_like(out)
     for copy in copies:
         copy.wait()
@@ -132,7 +138,7 @@
             total += matmul(a, b, 0, 0)
         out[s] = total.astype(out.dtype)
 
-    over_slots(info, out.shape[0], cols, add)
+    over_slots(info, 0, out.shape[0], cols, add)
 
 
 def call(kernel, out_shape, scratch, flops, moved, *args):
@@ -147,27 +153,28 @@
     )(args[0], *args[2])
 
 
-def wide_scratch(blocks, rows, tile, unit):
-    held = pltpu.VMEM((D // tile, blocks, rows, tile), jnp.bfloat16)
-    return [held, pltpu.SemaphoreType.DMA((D // unit,))]
-
-
-def to_hidden(info, xs, w, cols, flip):
+def wide_scratch(labels, rows, tile, unit):
+    group = len(labels)
+    held = pltpu.VMEM((D // tile, group, rows, tile), jnp.bfloat16)
+    return [held, pltpu.SemaphoreType.DMA((D // unit * group,))]
+
+
+def to_hidden(info, xs, ws, cols, flip, labels):
     rows, unit = xs[0].shape[-2:]
-    slots, tile, _ = w.shape
-    blocks = lax.axis_size("row")
-    outs = [jax.ShapeDtypeStruct((cols, rows, tile), jnp.bfloat16)] * blocks
-    held, sems = wide_scratch(blocks, rows, tile, unit)
-    scratch = [held, pltpu.VMEM((cols, blocks, rows, tile), jnp.float32), sems]
-    kernel = functools.partial(to_hidden_kernel, cols, flip, len(xs))
-    specs = [pl.BlockSpec(memory_space=pltpu.VMEM)] + [ANY] * len(xs)
-    flops = 2 * slots * blocks * rows * tile * tile
-    return call(kernel, outs, scratch, flops, 8 << 20, info, specs, [w, *xs])
-
-
-def from_hidden(info, h, w, cols, flip, labels, devices):
-    rows, tile = h.shape[-2:]
-    slots, group = w.shape[0], len(labels)
+    slots, tile, _ = ws[0].shape
+    group = len(labels)
+    outs = [jax.ShapeDtypeStruct((cols, rows, tile), jnp.bfloat16)] * group
+    held, sems = wide_scratch(labels, rows, tile, unit)
+    scratch = [held, pltpu.VMEM((cols, group, rows, tile), jnp.float32), sems]
+    kernel = functools.partial(to_hidden_kernel, cols, flip, labels, len(xs), len(ws))
+    specs = [pl.BlockSpec(memory_space=pltpu.VMEM)] * len(ws) + [ANY] * len(xs)
+    flops = 2 * len(ws) * slots * group * rows * tile * tile
+    return call(kernel, outs, scratch, flops, 8 << 20, info, specs, [*ws, *xs])
+
+
+def from_hidden(info, hs, ws, cols, flip, labels, devices):
+    rows, tile = hs[0].shape[-2:]
+    slots, group = ws[0].shape[0], len(labels)
     unit = min(tile, D // devices)
     pieces = D // devices // unit
     shape = (group, pieces, rows, unit)
@@ -180,19 +187,19 @@
         pltpu.VMEM((D // tile, group, rows, tile), jnp.float32),
         pltpu.SemaphoreType.DMA((group,)),
     ]
-    kernel = functools.partial(from_hidden_kernel, cols, flip, labels)
-    specs = [pl.BlockSpec(memory_space=pltpu.VMEM), ANY]
-    flops = 2 * slots * group * rows * tile * tile
-    return call(kernel, outs, scratch, flops, 8 << 20, info, specs, [w, h])
-
-
-def slot_grads(info, xs, h, slots, cols, flip):
+    kernel = functools.partial(from_hidden_kernel, cols, flip, labels, len(hs), len(ws))
+    specs = [pl.BlockSpec(memory_space=pltpu.VMEM)] * len(ws) + [ANY] * len(hs)
+    flops = 2 * len(ws) * slots * group * rows * tile * tile
+    return call(kernel, outs, scratch, flops, 8 << 20, info, specs, [*ws, *hs])
+
+
+def slot_grads(info, xs, hs, slots, cols, flip):
     blocks = lax.axis_size("row")
     labels = range(blocks)
     rows, unit = xs[0].shape[-2:]
-    tile = h.shape[-1]
+    tile = hs[0].shape[-1]
     out = jax.ShapeDtypeStruct((slots, tile, tile), jnp.bfloat16)
-    held, sems = wide_scratch(blocks, rows, tile, unit)
+    held, sems = wide_scratch(labels, rows, tile, unit)
     scratch = [
         held,
         pltpu.VMEM((cols, blocks, rows, tile), jnp.bfloat16),
@@ -200,9 +207,9 @@
         pltpu.SemaphoreType.DMA((blocks,)),
     ]
     kernel = functools.partial(grad_kernel, cols, flip, len(xs), labels)
-    specs = [ANY] * (len(xs) + 1)
+    specs = [ANY] * (len(xs) + len(hs))
     flops = 2 * slots * blocks * rows * tile * tile
-    return call(kernel, out, scratch, flops, 8 << 20, info, specs, [*xs, h])
+    return call(kernel, out, scratch, flops, 8 << 20, info, specs, [*xs, *hs])
 
 
 def long_row():
@@ -294,8 +301,9 @@
 
     def slot_info(codes):
         own = lax.dynamic_slice_in_dim(codes[0], row * slots, slots)
+        mate = lax.dynamic_slice_in_dim(codes[0], (row ^ 1) * slots, slots)
         place = jnp.stack([row, col]).astype(jnp.int32)
-        return jnp.concatenate([place, own])
+        return jnp.concatenate([place, own, mate])
 
     info_in, info_out = slot_info(in_codes), slot_info(out_codes)
     w_in, w_out = w_in[0], w_out[0]
@@ -308,34 +316,36 @@
 
 def on_line(info_in, info_out, tokens, upstream, w_in, w_out, cols, devices):
     row, slots = info_in[0], w_in.shape[0]
-    token_blocks, up_blocks = line_gather(tokens), line_gather(upstream)
-    token_even = across(jnp.stack(token_blocks))
-    up_mine = jnp.stack(up_blocks)
-    all_tokens = with_odd(after(token_even, up_mine))
-    up_even = across(after(up_mine, token_even[1:]))
-    parts = to_hidden(info_in, all_tokens, w_in, cols, False)
-    all_up = with_odd(after(up_even, parts))
-    terms, first = line_reduce(parts, row, up_even)
-    parts = to_hidden(info_out, after(all_up, first), w_out, cols, True)
-    hidden = add(*after(terms, parts))
+    every, ends = range(4), (0, 3)
+    w_pair = [w_in, swap_row(w_in, 1)]
+    both = line_gather(jnp.stack([tokens, upstream]))
+    token_even = across(jnp.stack([block[0] for block in both]))
+    up_mine = after(jnp.stack([block[1] for block in both]), token_even[1:])
+    up_even = across(up_mine)
+    all_tokens = with_odd(token_even)
+    own, far = to_hidden(info_in, all_tokens, w_pair, cols, False, ends)
+    all_up = with_odd(after(up_even, own))
+    parts = to_hidden(info_out, all_up, [w_out], cols, True, every)
+    hidden = add(*after((own, swap_row(far, 3)), parts))
     activ = silu(hidden)
+    all_activ = [lax.all_gather(activ, "row")]
     terms, _ = line_reduce(after(parts, activ), row)
-    all_activ = lax.all_gather(activ, "row")
     grad_hidden = activations(hidden, add(*terms))
-    all_grad = lax.all_gather(grad_hidden, "row")
-
-    def column_sums(info, hs, w, flip, labels):
-        total = finish_col(*from_hidden(info, hs, w, cols, flip, labels, devices))
+    far_grad = swap_row(grad_hidden, 3)
+
+    def column_sums(info, hs, ws, flip, labels):
+        total = finish_col(*from_hidden(info, hs, ws, cols, flip, labels, devices))
         return [total[g] for g in range(len(labels))]
 
     all_activ = after(all_activ, grad_hidden)
-    layer_sums = column_sums(info_out, all_activ, w_out, False, (0, 1, 2, 3))
+    layer_sums = column_sums(info_out, all_activ, [w_out], False, every)
     grad_w_out = slot_grads(info_out, all_up, all_activ, slots, cols, False)
-    held = (all_grad, layer_sums, grad_w_out)
-    all_grad, layer_sums, grad_w_out = lax.optimization_barrier(held)
-    input_sums = column_sums(info_in, all_grad, w_in, True, (0, 1, 2, 3))
+    ends_grad = after([grad_hidden, far_grad], grad_w_out)
+    input_sums = column_sums(info_in, ends_grad, w_pair, True, ends)
+    all_grad = [grad_hidden, swap_row(grad_hidden, 1), swap_row(far_grad, 1), far_grad]
     grad_w_in = slot_grads(info_in, all_tokens, all_grad, slots, cols, True)
-    layer_out, grad_tokens = finish_row(layer_sums), finish_row(input_sums)
+    layer_out = finish_row(layer_sums)
+    grad_tokens = rows_first(add(input_sums[0], swap_row(input_sums[1], 3)))
     return layer_out, grad_tokens, grad_w_in, grad_w_out
 
 
@@ -346,7 +356,7 @@
         return [lax.all_gather(lax.all_gather(x, "row"), "col")]
 
     def hidden_side(info, xs, w, flip):
-        parts = jnp.stack(to_hidden(info, xs, w, cols, flip))
+        parts = jnp.stack(to_hidden(info, xs, [w], cols, flip, range(blocks)))
         return lax.psum_scatter(parts, "row", scatter_dimension=0).astype(jnp.float32)
 
     def wide_side(info, hs, w, flip):
@@ -355,7 +365,7 @@
             if sums:
                 hs, _ = lax.optimization_barrier((hs, sums[-1]))
             labels = range(blocks)[chunk]
-            [parts] = from_hidden(info, hs, w, cols, flip, labels, devices)
+            [parts] = from_hidden(info, [hs], [w], cols, flip, labels, devices)
             sums.append(lax.psum_scatter(parts, "col", scatter_dimension=0))
         total = lax.psum_scatter(jnp.concatenate(sums), "row", scatter_dimension=0)
         return rows_first(total)
@@ -366,12 +376,12 @@
     grad_activ = hidden_side(info_out, all_up, w_out, True)
     all_activ = lax.all_gather(silu(hidden), "row")
     layer_out = wide_side(info_out, all_activ, w_out, False)
-    grad_w_out = slot_grads(info_out, all_up, all_activ, slots, cols, False)
+    grad_w_out = slot_grads(info_out, all_up, [all_activ], slots, cols, False)
     held = (activations(hidden, grad_activ), tokens, layer_out, grad_w_out)
     grad_hidden, tokens, layer_out, grad_w_out = lax.optimization_barrier(held)
     all_grad = lax.all_gather(grad_hidden, "row")
     grad_tokens = wide_side(info_in, all_grad, w_in, True)
-    grad_w_in = slot_grads(info_in, everywhere(tokens), all_grad, slots, cols, True)
+    grad_w_in = slot_grads(info_in, everywhere(tokens), [all_grad], slots, cols, True)
     return layer_out, grad_tokens, grad_w_in, grad_w_out
 
 

time: 308 us -> 307 us (level)
  starting transfers between devices: 72.7 us -> 99.6 us
  waiting for transfers between devices: 151 us -> 128 us
  Pallas kernels: 49.2 us -> 45.8 us
    ppermute x12, waiting for transfers between devices: 24.5 us -> 50.9 us  [swap_row(): return lax.ppermute(x, 'row', [(s, s ^ t) for s in range(4)])]
    ppermute x10 -> x5, waiting for transfers between devices: 64.6 us -> 46.8 us  [send_row(): return lax.ppermute(x, 'row', pairs)]
    ppermute x22, waiting for transfers between devices: 48.1 us -> 30.6 us  [swap_col(): return lax.ppermute(x, 'col', [(s, s ^ m) for s in range(count)])]
    ppermute x12, starting transfers between devices: 19.4 us -> 35 us  [swap_row(): return lax.ppermute(x, 'row', [(s, s ^ t) for s in range(4)])]
    all_gather x2 -> x1, waiting for transfers between devices: 13.7 us -> 0.01 us  [on_line(): all_activ = [lax.all_gather(activ, 'row')]]
    ppermute x22, starting transfers between devices: 18.3 us -> 29.2 us  [swap_col(): return lax.ppermute(x, 'col', [(s, s ^ m) for s in range(count)])]
    pallas_call x6, Pallas kernels: 49.2 us -> 45.8 us  [call(): pl.pallas_call(kernel, out_shape=out_shape, in_specs=[pl.BlockSpec(memory...]
    ppermute x10 -> x5, starting transfers between devices: 34.9 us -> 35.3 us  [send_row(): return lax.ppermute(x, 'row', pairs)]
  transfers between devices with their start and end apart: 46 -> 40, of which waited for: 20 -> 14; matrix products, arithmetic and copies ran while one was open for 3% -> 3% of each run, Pallas kernels for 11% -> 15%
where the time goes in v7:
time: 307 us; the launch traced here: 306 us
  waiting for transfers between devices  128 us (42%)
  starting transfers between devices  99.6 us (32%)
  Pallas kernels  45.8 us (15%)
  between operations  14.6 us (5%)
  other arithmetic  8.87 us (3%)
  local copies, waits for them, and re-layouts  8.65 us (3%)
    ppermute x12, waiting for transfers between devices, swap_row(): return lax.ppermute(x, 'row', [(s, s ^ t) for s in range(4)])  50.9 us
    ppermute x5, waiting for transfers between devices, send_row(): return lax.ppermute(x, 'row', pairs)  46.8 us
    pallas_call x6, Pallas kernels, call(): pl.pallas_call(kernel, out_shape=out_shape, in_specs=[pl.BlockSpec(memory...  45.8 us
    ppermute x5, starting transfers between devices, send_row(): return lax.ppermute(x, 'row', pairs)  35.3 us
    ppermute x12, starting transfers between devices, swap_row(): return lax.ppermute(x, 'row', [(s, s ^ t) for s in range(4)])  35 us
    ppermute x22, waiting for transfers between devices, swap_col(): return lax.ppermute(x, 'col', [(s, s ^ m) for s in range(count)])  30.6 us
    ppermute x22, starting transfers between devices, swap_col(): return lax.ppermute(x, 'col', [(s, s ^ m) for s in range(count)])  29.2 us
    unnamed x52, local copies, waits for them, and re-layouts  7.04 us
  transfers between devices with their start and end apart: 40, of which 14 were waited for; matrix products, arithmetic and copies ran while one was open for 3% of the time, Pallas kernels for 15%

profile of v7, /device:TPU:0, one launch (start us, length us, event | category | flops | bytes accessed | tf_op | source)
XLA Modules:
  0.0 305.9 jit_solution(12091099418021365828)
XLA Ops:
  16.2 8.5 %collective-permute-done.1 = bf16[2,2,128,256]{3,2,1,0:T(8,128)(2,1)S(1)} collective-permute-done((bf16[2,2,128,256]{3,2,1,0:T(8,128)(2,1)S(1)}, bf16[2,2,128,256]{3,2,1,0:T(8,128)(2,1)S(1)}, u32[]{:S(2)}, u32[]{:S(2)}) %collective-permute-start.1) | collective-permute-done | bytes 262176 | tf_op jit(solution)/shard_map/ppermute | solution.py:225
  24.7 9.4 %collective-permute-done.2 = bf16[2,2,128,256]{3,2,1,0:T(8,128)(2,1)S(1)} collective-permute-done((bf16[2,2,128,256]{3,2,1,0:T(8,128)(2,1)S(1)}, bf16[2,2,128,256]{3,2,1,0:T(8,128)(2,1)S(1)}, u32[]{:S(2)}, u32[]{:S(2)}) %collective-permute-start.2) | collective-permute-done | bytes 262176 | tf_op jit(solution)/shard_map/ppermute | solution.py:225
  37.8 12.3 %collective-permute-done.9.refs_8_.refs_6_ = bf16[4,2,128,256]{3,2,1,0:T(8,128)(2,1)S(1)} collective-permute-done((bf16[4,2,128,256]{3,2,1,0:T(8,128)(2,1)S(1)}, bf16[4,2,128,256]{3,2,1,0:T(8,128)(2,1)S(1)}, u32[]{:S(2)}, u32[]{:S(2)}) %collective-permute-start.9) | collective-permute-done | bytes 524320 | tf_op jit(solution)/shard_map/ppermute | solution.py:221
  50.1 7.6 %collective-permute-done.5.refs_4_.refs_2_ = bf16[4,2,128,256]{3,2,1,0:T(8,128)(2,1)S(1)} collective-permute-done((bf16[4,2,128,256]{3,2,1,0:T(8,128)(2,1)S(1)}, bf16[4,2,128,256]{3,2,1,0:T(8,128)(2,1)S(1)}, u32[]{:S(2)}, u32[]{:S(2)}) %collective-permute-start.5) | collective-permute-done | bytes 524320 | tf_op jit(solution)/shard_map/ppermute | solution.py:221
  62.7 12.4 %collective-permute-done.refs_1_ = bf16[16,256,256]{2,1,0:T(8,128)(2,1)S(1)} collective-permute-done((bf16[16,256,256]{2,1,0:T(8,128)(2,1)}, bf16[16,256,256]{2,1,0:T(8,128)(2,1)S(1)}, u32[]{:S(2)}, u32[]{:S(2)}) %collective-permute-start) | collective-permute-done | bytes 2097184 | tf_op jit(solution)/shard_map/ppermute | solution.py:225
  76.5 9.2 %shard_map.93 = (bf16[8,128,256]{2,1,0:T(8,128)(2,1)}, bf16[8,128,256]{2,1,0:T(8,128)(2,1)}) custom-call(s32[34]{0:T(128)} %pad_add_fusion.2.info, bf16[16,256,256]{2,1,0:T(8,128)(2,1)} %bitcast.72, bf16[16,256,256]{2,1,0:T(8,128)(2,1)} %copy-done, bf16[4,2,128,256]{3,2,1,0:T(8,128)(2,1)} %copy-done.1, bf16[4,2,128,256]{3,2,1,0:T(8,128)(2,1)} %copy-done.8, ...), custom_call_target="tpu_custom_call" | custom-call | flops 1073741824 | bytes 8388608 | tf_op jit(solution)/shard_map/pallas_call | solution.py:145
  86.8 4.1 %collective-permute-start.11 = (bf16[8,128,256]{2,1,0:T(8,128)(2,1)}, bf16[8,128,256]{2,1,0:T(8,128)(2,1)S(1)}, u32[]{:S(2)}, u32[]{:S(2)}) collective-permute-start(bf16[8,128,256]{2,1,0:T(8,128)(2,1)} %get-tuple-element.32), channel_id=1, source_target_pairs={{0,24},{8,16},{16,8},{24,0},{1,25},{9,17},{17,9},{25,1},{2,26},{10... | collective-permute-start | bytes 1572872 | tf_op jit(solution)/shard_map/ppermute | solution.py:225
  92.9 6.5 %shard_map.94 = (bf16[8,128,256]{2,1,0:T(8,128)(2,1)}, bf16[8,128,256]{2,1,0:T(8,128)(2,1)}, bf16[8,128,256]{2,1,0:T(8,128)(2,1)}, bf16[8,128,256]{2,1,0:T(8,128)(2,1)}) custom-call(s32[34]{0:T(128)} %pad_add_fusion.info, bf16[16,256,256]{2,1,0:T(8,128)(2,1)} %bitcast.69, bf16[4,2,128,256]{3,2,1,0:T(8,128)(2,1)} %copy-done.2, ...), custom_call_target="tpu_custom_call" | custom-call | flops 1073741824 | bytes 8388608 | tf_op jit(solution)/shard_map/pallas_call | solution.py:145
  104.5 14.0 %collective-permute-start.19 = (bf16[8,128,256]{2,1,0:T(8,128)(2,1)}, bf16[8,128,256]{2,1,0:T(8,128)(2,1)S(1)}, u32[]{:S(2)}, u32[]{:S(2)}) collective-permute-start(bf16[8,128,256]{2,1,0:T(8,128)(2,1)} %get-tuple-element.47), channel_id=1, source_target_pairs={{0,8},{8,16},{1,9},{9,17},{2,10},{10,18},{3,11},{11,19},{4,12},{12... | collective-permute-start | bytes 1572872 | tf_op jit(solution)/shard_map/ppermute | solution.py:229
  120.0 7.0 %collective-permute-start.21 = (bf16[8,128,256]{2,1,0:T(8,128)(2,1)S(1)}, bf16[8,128,256]{2,1,0:T(8,128)(2,1)}, u32[]{:S(2)}, u32[]{:S(2)}) collective-permute-start(bf16[8,128,256]{2,1,0:T(8,128)(2,1)S(1)} %copy-done.21), channel_id=1, source_target_pairs={{0,16},{24,8},{1,17},{25,9},{2,18},{26,10},{3,19},{27,11},{4,20},{... | collective-permute-start | bytes 1572872 | tf_op jit(solution)/shard_map/ppermute | solution.py:229
  127.0 10.8 %collective-permute-done.19 = bf16[8,128,256]{2,1,0:T(8,128)(2,1)S(1)} collective-permute-done((bf16[8,128,256]{2,1,0:T(8,128)(2,1)}, bf16[8,128,256]{2,1,0:T(8,128)(2,1)S(1)}, u32[]{:S(2)}, u32[]{:S(2)}) %collective-permute-start.19) | collective-permute-done | bytes 524320 | tf_op jit(solution)/shard_map/ppermute | solution.py:229
  137.7 21.4 %collective-permute-done.21 = bf16[8,128,256]{2,1,0:T(8,128)(2,1)} collective-permute-done((bf16[8,128,256]{2,1,0:T(8,128)(2,1)S(1)}, bf16[8,128,256]{2,1,0:T(8,128)(2,1)}, u32[]{:S(2)}, u32[]{:S(2)}) %collective-permute-start.21) | collective-permute-done | bytes 524320 | tf_op jit(solution)/shard_map/ppermute | solution.py:229
  160.8 11.4 %collective-permute-start.22 = (bf16[8,128,256]{2,1,0:T(8,128)(2,1)S(1)}, bf16[8,128,256]{2,1,0:T(8,128)(2,1)S(1)}, u32[]{:S(2)}, u32[]{:S(2)}) collective-permute-start(bf16[8,128,256]{2,1,0:T(8,128)(2,1)S(1)} %get-tuple-element.69), channel_id=1, source_target_pairs={{0,8},{8,16},{16,24},{1,9},{9,17},{17,25},{2,10},{10,18},{18,26},{... | collective-permute-start | bytes 1572872 | tf_op jit(solution)/shard_map/ppermute | solution.py:229
  173.7 12.6 %collective-permute-done.22 = bf16[8,128,256]{2,1,0:T(8,128)(2,1)S(1)} collective-permute-done((bf16[8,128,256]{2,1,0:T(8,128)(2,1)S(1)}, bf16[8,128,256]{2,1,0:T(8,128)(2,1)S(1)}, u32[]{:S(2)}, u32[]{:S(2)}) %collective-permute-start.22) | collective-permute-done | bytes 524320 | tf_op jit(solution)/shard_map/ppermute | solution.py:229
  191.8 6.2 %shard_map.95 = (bf16[4,4,2,128,256]{4,3,2,1,0:T(8,128)(2,1)}, bf16[4,4,2,128,256]{4,3,2,1,0:T(8,128)(2,1)}) custom-call(s32[34]{0:T(128)} %pad_add_fusion.info, bf16[16,256,256]{2,1,0:T(8,128)(2,1)} %bitcast.70, bf16[4,8,128,256]{3,2,1,0:T(8,128)(2,1)} %bitcast.74), custom_call_target="tpu_custom_call" | custom-call | flops 1073741824 | bytes 8388608 | tf_op jit(solution)/shard_map/pallas_call | solution.py:145
  198.1 6.1 %shard_map.96 = bf16[16,256,256]{2,1,0:T(8,128)(2,1)} custom-call(s32[34]{0:T(128)} %pad_add_fusion.info, bf16[4,2,128,256]{3,2,1,0:T(8,128)(2,1)} %copy-done.2, bf16[4,2,128,256]{3,2,1,0:T(8,128)(2,1)} %copy-done.11, bf16[4,2,128,256]{3,2,1,0:T(8,128)(2,1)} %collective-permute-done.12.refs_3_.refs_2_, bf16[4,2,128,256]{3,2,1,0:T(8,128)(2,1)} %copy-done.12, ...), custom_call_target="tpu_custom_call" | custom-call | flops 1073741824 | bytes 8388608 | tf_op jit(solution)/shard_map/pallas_call | solution.py:145
  205.0 9.7 %shard_map.97 = (bf16[4,2,2,128,256]{4,3,2,1,0:T(8,128)(2,1)}, bf16[4,2,2,128,256]{4,3,2,1,0:T(8,128)(2,1)}) custom-call(s32[34]{0:T(128)} %pad_add_fusion.2.info, bf16[16,256,256]{2,1,0:T(8,128)(2,1)} %bitcast.73, bf16[16,256,256]{2,1,0:T(8,128)(2,1)} %copy-done, bf16[8,128,256]{2,1,0:T(8,128)(2,1)} %copy-done.3, bf16[8,128,256]{2,1,0:T(8,128)(2,1)} %copy-done.16), custom_call_target="tpu_custom_call" | custom-call | flops 1073741824 | bytes 8388608 | tf_op jit(solution)/shard_map/pallas_call | solution.py:145
  214.8 14.2 %collective-permute-start.37 = (bf16[8,128,256]{2,1,0:T(8,128)(2,1)S(1)}, bf16[8,128,256]{2,1,0:T(8,128)(2,1)S(1)}, u32[]{:S(2)}, u32[]{:S(2)}) collective-permute-start(bf16[8,128,256]{2,1,0:T(8,128)(2,1)S(1)} %copy-done.4), channel_id=1, source_target_pairs={{0,8},{8,0},{16,24},{24,16},{1,9},{9,1},{17,25},{25,17},{2,10},{10... | collective-permute-start | bytes 1572872 | tf_op jit(solution)/shard_map/ppermute | solution.py:225
  231.9 9.0 %collective-permute-start.34 = (bf16[2,2,128,256]{3,2,1,0:T(8,128)(2,1)}, bf16[2,2,128,256]{3,2,1,0:T(8,128)(2,1)}, u32[]{:S(2)}, u32[]{:S(2)}) collective-permute-start(bf16[2,2,128,256]{3,2,1,0:T(8,128)(2,1)} %get-tuple-element.73), channel_id=1, source_target_pairs={{0,4},{1,5},{2,6},{3,7},{4,0},{5,1},{6,2},{7,3},{8,12},{9,13},{10,... | collective-permute-start | bytes 786440 | tf_op jit(solution)/shard_map/ppermute | solution.py:221
  243.9 8.8 %collective-permute-done.38.refs_10_ = bf16[8,128,256]{2,1,0:T(8,128)(2,1)S(1)} collective-permute-done((bf16[8,128,256]{2,1,0:T(8,128)(2,1)}, bf16[8,128,256]{2,1,0:T(8,128)(2,1)S(1)}, u32[]{:S(2)}, u32[]{:S(2)}) %collective-permute-start.38) | collective-permute-done | bytes 524320 | tf_op jit(solution)/shard_map/ppermute | solution.py:225
  252.7 9.0 %collective-permute-start.26 = (bf16[4,2,128,256]{3,2,1,0:T(8,128)(2,1)S(1)}, bf16[4,2,128,256]{3,2,1,0:T(8,128)(2,1)S(1)}, u32[]{:S(2)}, u32[]{:S(2)}) collective-permute-start(bf16[4,2,128,256]{3,2,1,0:T(8,128)(2,1)S(1)} %get-tuple-element.68), channel_id=1, source_target_pairs={{0,4},{1,5},{2,6},{3,7},{4,0},{5,1},{6,2},{7,3},{8,12},{9,13},{10,... | collective-permute-start | bytes 1572872 | tf_op jit(solution)/shard_map/ppermute | solution.py:221
  261.7 8.3 %shard_map.98 = bf16[16,256,256]{2,1,0:T(8,128)(2,1)} custom-call(s32[34]{0:T(128)} %pad_add_fusion.2.info, bf16[4,2,128,256]{3,2,1,0:T(8,128)(2,1)} %copy-done.1, bf16[4,2,128,256]{3,2,1,0:T(8,128)(2,1)} %copy-done.8, bf16[4,2,128,256]{3,2,1,0:T(8,128)(2,1)} %copy-done.7, bf16[4,2,128,256]{3,2,1,0:T(8,128)(2,1)} %copy-done.10, ...), custom_call_target="tpu_custom_call" | custom-call | flops 1073741824 | bytes 8388608 | tf_op jit(solution)/shard_map/pallas_call | solution.py:145
  273.9 10.7 %collective-permute-done.26 = bf16[4,2,128,256]{3,2,1,0:T(8,128)(2,1)S(1)} collective-permute-done((bf16[4,2,128,256]{3,2,1,0:T(8,128)(2,1)S(1)}, bf16[4,2,128,256]{3,2,1,0:T(8,128)(2,1)S(1)}, u32[]{:S(2)}, u32[]{:S(2)}) %collective-permute-start.26) | collective-permute-done | bytes 524320 | tf_op jit(solution)/shard_map/ppermute | solution.py:221
  291.1 7.0 %collective-permute-done.29 = bf16[2,128,256]{2,1,0:T(8,128)(2,1)S(1)} collective-permute-done((bf16[2,128,256]{2,1,0:T(8,128)(2,1)S(1)}, bf16[2,128,256]{2,1,0:T(8,128)(2,1)S(1)}, u32[]{:S(2)}, u32[]{:S(2)}) %collective-permute-start.29) | collective-permute-done | bytes 131104 | tf_op jit(solution)/shard_map/ppermute | solution.py:225
  (141 shorter events, 55.3 us)
Async XLA Ops:
  7.2 184.7 %all-gather.3.cloned.1.call-start = ((), (), s32[]{:S(2)}) async-start(), calls=%async_computation | async-start | bytes 2621440 | tf_op jit(solution)/shard_map/all_gather | solution.py:331
  12.7 21.4 %collective-permute-start.2 = (bf16[2,2,128,256]{3,2,1,0:T(8,128)(2,1)S(1)}, bf16[2,2,128,256]{3,2,1,0:T(8,128)(2,1)S(1)}, u32[]{:S(2)}, u32[]{:S(2)}) collective-permute-start(bf16[2,2,128,256]{3,2,1,0:T(8,128)(2,1)S(1)} %pad_maximum_fusion.2), channel_id=1, source_target_pairs={{0,16},{8,24},{16,0},{24,8},{1,17},{9,25},{17,1},{25,9},{2,18},{10... | collective-permute-start | bytes 786440 | tf_op jit(solution)/shard_map/ppermute | solution.py:225
  15.3 18.8 %collective-permute-start.3 = (bf16[2,2,128,256]{3,2,1,0:T(8,128)(2,1)S(1)}, bf16[2,2,128,256]{3,2,1,0:T(8,128)(2,1)S(1)}, u32[]{:S(2)}, u32[]{:S(2)}) collective-permute-start(bf16[2,2,128,256]{3,2,1,0:T(8,128)(2,1)S(1)} %pad_maximum_fusion.2), channel_id=1, source_target_pairs={{0,24},{8,16},{16,8},{24,0},{1,25},{9,17},{17,9},{25,1},{2,26},{10... | collective-permute-start | bytes 786440 | tf_op jit(solution)/shard_map/ppermute | solution.py:225
  15.3 59.9 %collective-permute-start = (bf16[16,256,256]{2,1,0:T(8,128)(2,1)}, bf16[16,256,256]{2,1,0:T(8,128)(2,1)S(1)}, u32[]{:S(2)}, u32[]{:S(2)}) collective-permute-start(bf16[16,256,256]{2,1,0:T(8,128)(2,1)} %bitcast.71), channel_id=1, source_target_pairs={{0,8},{8,0},{16,24},{24,16},{1,9},{9,1},{17,25},{25,17},{2,10},{10... | collective-permute-start | bytes 6291464 | tf_op jit(solution)/shard_map/ppermute | solution.py:225
  36.7 21.0 %collective-permute-start.5 = (bf16[4,2,128,256]{3,2,1,0:T(8,128)(2,1)S(1)}, bf16[4,2,128,256]{3,2,1,0:T(8,128)(2,1)S(1)}, u32[]{:S(2)}, u32[]{:S(2)}) collective-permute-start(bf16[4,2,128,256]{3,2,1,0:T(8,128)(2,1)S(1)} %pad_maximum_fusion.refs_2_.refs_0_), channel_id=1, source_target_pairs={{0,2},{1,3},{2,0},{3,1},{4,6},{5,7},{6,4},{7,5},{8,10},{9,11},{10,... | collective-permute-start | bytes 1572872 | tf_op jit(solution)/shard_map/ppermute | solution.py:221
  37.3 20.4 %collective-permute-start.7 = (bf16[4,2,128,256]{3,2,1,0:T(8,128)(2,1)S(1)}, bf16[4,2,128,256]{3,2,1,0:T(8,128)(2,1)}, u32[]{:S(2)}, u32[]{:S(2)}) collective-permute-start(bf16[4,2,128,256]{3,2,1,0:T(8,128)(2,1)S(1)} %pad_maximum_fusion.refs_2_.refs_0_), channel_id=1, source_target_pairs={{0,4},{1,5},{2,6},{3,7},{4,0},{5,1},{6,2},{7,3},{8,12},{9,13},{10,... | collective-permute-start | bytes 1572872 | tf_op jit(solution)/shard_map/ppermute | solution.py:221
  37.8 20.5 %collective-permute-start.4 = (bf16[4,2,128,256]{3,2,1,0:T(8,128)(2,1)S(1)}, bf16[4,2,128,256]{3,2,1,0:T(8,128)(2,1)S(1)}, u32[]{:S(2)}, u32[]{:S(2)}) collective-permute-start(bf16[4,2,128,256]{3,2,1,0:T(8,128)(2,1)S(1)} %pad_maximum_fusion.refs_2_.refs_0_), channel_id=1, source_target_pairs={{0,1},{1,0},{2,3},{3,2},{4,5},{5,4},{6,7},{7,6},{8,9},{9,8},{10,11... | collective-permute-start | bytes 1572872 | tf_op jit(solution)/shard_map/ppermute | solution.py:221
  58.3 27.4 %collective-permute-start.12 = (bf16[4,2,128,256]{3,2,1,0:T(8,128)(2,1)S(1)}, bf16[4,2,128,256]{3,2,1,0:T(8,128)(2,1)}, u32[]{:S(2)}, u32[]{:S(2)}) collective-permute-start(bf16[4,2,128,256]{3,2,1,0:T(8,128)(2,1)S(1)} %pad_maximum_fusion.1.refs_1_.refs_0_), channel_id=1, source_target_pairs={{0,2},{1,3},{2,0},{3,1},{4,6},{5,7},{6,4},{7,5},{8,10},{9,11},{10,... | collective-permute-start | bytes 1572872 | tf_op jit(solution)/shard_map/ppermute | solution.py:221
  59.9 25.8 %collective-permute-start.13 = (bf16[4,2,128,256]{3,2,1,0:T(8,128)(2,1)S(1)}, bf16[4,2,128,256]{3,2,1,0:T(8,128)(2,1)}, u32[]{:S(2)}, u32[]{:S(2)}) collective-permute-start(bf16[4,2,128,256]{3,2,1,0:T(8,128)(2,1)S(1)} %pad_maximum_fusion.1.refs_1_.refs_0_), channel_id=1, source_target_pairs={{0,4},{1,5},{2,6},{3,7},{4,0},{5,1},{6,2},{7,3},{8,12},{9,13},{10,... | collective-permute-start | bytes 1572872 | tf_op jit(solution)/shard_map/ppermute | solution.py:221
  60.9 24.8 %collective-permute-start.14 = (bf16[4,2,128,256]{3,2,1,0:T(8,128)(2,1)S(1)}, bf16[4,2,128,256]{3,2,1,0:T(8,128)(2,1)}, u32[]{:S(2)}, u32[]{:S(2)}) collective-permute-start(bf16[4,2,128,256]{3,2,1,0:T(8,128)(2,1)S(1)} %pad_maximum_fusion.1.refs_1_.refs_0_), channel_id=1, source_target_pairs={{0,6},{1,7},{2,4},{3,5},{4,2},{5,3},{6,0},{7,1},{8,14},{9,15},{10,... | collective-permute-start | bytes 1572872 | tf_op jit(solution)/shard_map/ppermute | solution.py:221
  104.5 33.2 %collective-permute-start.19 = (bf16[8,128,256]{2,1,0:T(8,128)(2,1)}, bf16[8,128,256]{2,1,0:T(8,128)(2,1)S(1)}, u32[]{:S(2)}, u32[]{:S(2)}) collective-permute-start(bf16[8,128,256]{2,1,0:T(8,128)(2,1)} %get-tuple-element.47), channel_id=1, source_target_pairs={{0,8},{8,16},{1,9},{9,17},{2,10},{10,18},{3,11},{11,19},{4,12},{12... | collective-permute-start | bytes 1572872 | tf_op jit(solution)/shard_map/ppermute | solution.py:229
  118.5 19.2 %collective-permute-start.20 = (bf16[8,128,256]{2,1,0:T(8,128)(2,1)}, bf16[8,128,256]{2,1,0:T(8,128)(2,1)}, u32[]{:S(2)}, u32[]{:S(2)}) collective-permute-start(bf16[8,128,256]{2,1,0:T(8,128)(2,1)} %get-tuple-element.47), channel_id=1, source_target_pairs={{24,16},{16,8},{25,17},{17,9},{26,18},{18,10},{27,19},{19,11},{28,... | collective-permute-start | bytes 1572872 | tf_op jit(solution)/shard_map/ppermute | solution.py:229
  120.0 39.2 %collective-permute-start.21 = (bf16[8,128,256]{2,1,0:T(8,128)(2,1)S(1)}, bf16[8,128,256]{2,1,0:T(8,128)(2,1)}, u32[]{:S(2)}, u32[]{:S(2)}) collective-permute-start(bf16[8,128,256]{2,1,0:T(8,128)(2,1)S(1)} %copy-done.21), channel_id=1, source_target_pairs={{0,16},{24,8},{1,17},{25,9},{2,18},{26,10},{3,19},{27,11},{4,20},{... | collective-permute-start | bytes 1572872 | tf_op jit(solution)/shard_map/ppermute | solution.py:229
  160.8 25.5 %collective-permute-start.22 = (bf16[8,128,256]{2,1,0:T(8,128)(2,1)S(1)}, bf16[8,128,256]{2,1,0:T(8,128)(2,1)S(1)}, u32[]{:S(2)}, u32[]{:S(2)}) collective-permute-start(bf16[8,128,256]{2,1,0:T(8,128)(2,1)S(1)} %get-tuple-element.69), channel_id=1, source_target_pairs={{0,8},{8,16},{16,24},{1,9},{9,17},{17,25},{2,10},{10,18},{18,26},{... | collective-permute-start | bytes 1572872 | tf_op jit(solution)/shard_map/ppermute | solution.py:229
  198.0 42.9 %collective-permute-start.24 = (bf16[4,4,2,128,256]{4,3,2,1,0:T(8,128)(2,1)}, bf16[4,4,2,128,256]{4,3,2,1,0:T(8,128)(2,1)S(1)}, u32[]{:S(2)}, u32[]{:S(2)}) collective-permute-start(bf16[4,4,2,128,256]{4,3,2,1,0:T(8,128)(2,1)} %get-tuple-element.53), channel_id=1, source_target_pairs={{0,1},{1,0},{2,3},{3,2},{4,5},{5,4},{6,7},{7,6},{8,9},{9,8},{10,11... | collective-permute-start | bytes 6291464 | tf_op jit(solution)/shard_map/ppermute | solution.py:221
  214.8 28.5 %collective-permute-start.37 = (bf16[8,128,256]{2,1,0:T(8,128)(2,1)S(1)}, bf16[8,128,256]{2,1,0:T(8,128)(2,1)S(1)}, u32[]{:S(2)}, u32[]{:S(2)}) collective-permute-start(bf16[8,128,256]{2,1,0:T(8,128)(2,1)S(1)} %copy-done.4), channel_id=1, source_target_pairs={{0,8},{8,0},{16,24},{24,16},{1,9},{9,1},{17,25},{25,17},{2,10},{10... | collective-permute-start | bytes 1572872 | tf_op jit(solution)/shard_map/ppermute | solution.py:225
  229.0 23.7 %collective-permute-start.38 = (bf16[8,128,256]{2,1,0:T(8,128)(2,1)}, bf16[8,128,256]{2,1,0:T(8,128)(2,1)S(1)}, u32[]{:S(2)}, u32[]{:S(2)}) collective-permute-start(bf16[8,128,256]{2,1,0:T(8,128)(2,1)} %copy-done.16), channel_id=1, source_target_pairs={{0,8},{8,0},{16,24},{24,16},{1,9},{9,1},{17,25},{25,17},{2,10},{10... | collective-permute-start | bytes 1572872 | tf_op jit(solution)/shard_map/ppermute | solution.py:225
  231.6 30.1 %collective-permute-start.33 = (bf16[2,2,128,256]{3,2,1,0:T(8,128)(2,1)S(1)}, bf16[2,2,128,256]{3,2,1,0:T(8,128)(2,1)S(1)}, u32[]{:S(2)}, u32[]{:S(2)}) collective-permute-start(bf16[2,2,128,256]{3,2,1,0:T(8,128)(2,1)S(1)} %get-tuple-element.71), channel_id=1, source_target_pairs={{0,2},{1,3},{2,0},{3,1},{4,6},{5,7},{6,4},{7,5},{8,10},{9,11},{10,... | collective-permute-start | bytes 786440 | tf_op jit(solution)/shard_map/ppermute | solution.py:221
  231.9 38.1 %collective-permute-start.34 = (bf16[2,2,128,256]{3,2,1,0:T(8,128)(2,1)}, bf16[2,2,128,256]{3,2,1,0:T(8,128)(2,1)}, u32[]{:S(2)}, u32[]{:S(2)}) collective-permute-start(bf16[2,2,128,256]{3,2,1,0:T(8,128)(2,1)} %get-tuple-element.73), channel_id=1, source_target_pairs={{0,4},{1,5},{2,6},{3,7},{4,0},{5,1},{6,2},{7,3},{8,12},{9,13},{10,... | collective-permute-start | bytes 786440 | tf_op jit(solution)/shard_map/ppermute | solution.py:221
  240.9 29.1 %collective-permute-start.35 = (bf16[2,2,128,256]{3,2,1,0:T(8,128)(2,1)}, bf16[2,2,128,256]{3,2,1,0:T(8,128)(2,1)}, u32[]{:S(2)}, u32[]{:S(2)}) collective-permute-start(bf16[2,2,128,256]{3,2,1,0:T(8,128)(2,1)} %get-tuple-element.72), channel_id=1, source_target_pairs={{0,6},{1,7},{2,4},{3,5},{4,2},{5,3},{6,0},{7,1},{8,14},{9,15},{10,... | collective-permute-start | bytes 786440 | tf_op jit(solution)/shard_map/ppermute | solution.py:221
  243.2 30.7 %collective-permute-start.25 = (bf16[4,2,128,256]{3,2,1,0:T(8,128)(2,1)S(1)}, bf16[4,2,128,256]{3,2,1,0:T(8,128)(2,1)S(1)}, u32[]{:S(2)}, u32[]{:S(2)}) collective-permute-start(bf16[4,2,128,256]{3,2,1,0:T(8,128)(2,1)S(1)} %get-tuple-element.66), channel_id=1, source_target_pairs={{0,2},{1,3},{2,0},{3,1},{4,6},{5,7},{6,4},{7,5},{8,10},{9,11},{10,... | collective-permute-start | bytes 1572872 | tf_op jit(solution)/shard_map/ppermute | solution.py:221
  252.7 31.9 %collective-permute-start.26 = (bf16[4,2,128,256]{3,2,1,0:T(8,128)(2,1)S(1)}, bf16[4,2,128,256]{3,2,1,0:T(8,128)(2,1)S(1)}, u32[]{:S(2)}, u32[]{:S(2)}) collective-permute-start(bf16[4,2,128,256]{3,2,1,0:T(8,128)(2,1)S(1)} %get-tuple-element.68), channel_id=1, source_target_pairs={{0,4},{1,5},{2,6},{3,7},{4,0},{5,1},{6,2},{7,3},{8,12},{9,13},{10,... | collective-permute-start | bytes 1572872 | tf_op jit(solution)/shard_map/ppermute | solution.py:221
  261.7 22.9 %collective-permute-start.27 = (bf16[4,2,128,256]{3,2,1,0:T(8,128)(2,1)S(1)}, bf16[4,2,128,256]{3,2,1,0:T(8,128)(2,1)S(1)}, u32[]{:S(2)}, u32[]{:S(2)}) collective-permute-start(bf16[4,2,128,256]{3,2,1,0:T(8,128)(2,1)S(1)} %get-tuple-element.67), channel_id=1, source_target_pairs={{0,6},{1,7},{2,4},{3,5},{4,2},{5,3},{6,0},{7,1},{8,14},{9,15},{10,... | collective-permute-start | bytes 1572872 | tf_op jit(solution)/shard_map/ppermute | solution.py:221
  271.2 18.2 %collective-permute-start.36 = (bf16[2,128,256]{2,1,0:T(8,128)(2,1)S(1)}, bf16[2,128,256]{2,1,0:T(8,128)(2,1)S(1)}, u32[]{:S(2)}, u32[]{:S(2)}) collective-permute-start(bf16[2,128,256]{2,1,0:T(8,128)(2,1)S(1)} %slice_bitcast_fusion.8), channel_id=1, source_target_pairs={{0,24},{8,16},{16,8},{24,0},{1,25},{9,17},{17,9},{25,1},{2,26},{10... | collective-permute-start | bytes 393224 | tf_op jit(solution)/shard_map/ppermute | solution.py:225
  (40 other events, 602.5 us)
Sparse Core Ops, SparseCore 0:
  104.6 80.2 all-gather.2

commit v8 on v7

--- a/solution.py
+++ b/solution.py
@@ -225,10 +225,6 @@
     return lax.ppermute(x, "row", [(s, s ^ t) for s in range(4)])
 
 
-def send_row(x, *pairs):
-    return lax.ppermute(x, "row", pairs)
-
-
 def own_pieces(x, tile):
     rows, width = x.shape
     unit = min(width, tile)
@@ -251,26 +247,16 @@
     return sum(term.astype(jnp.float32) for term in terms)
 
 
-def line_reduce(parts, row, wait=()):
-    right = send_row(parts[2], (0, 1), (1, 2))
-    left = send_row(parts[2], (3, 2), (2, 1))
-    far = send_row(parts[3], (0, 2), (3, 1))
-    right, left, far = first = after((right, left, far), wait)
-    none = jnp.zeros_like(far)
-    right = add(jnp.where(row == 1, parts[3], parts[1]), right, jnp.where(row == 2, far, none))
-    left = add(jnp.where(row == 2, parts[3], parts[1]), left, jnp.where(row == 1, far, none))
-    right = send_row(right.astype(jnp.bfloat16), (0, 1), (1, 2), (2, 3))
-    left = send_row(left.astype(jnp.bfloat16), (3, 2), (2, 1), (1, 0))
-    return (parts[0], right, left), first
-
-
 def line_gather(x):
     return [x] + [swap_row(x, t) for t in range(1, 4)]
 
 
-def finish_col(even, odd):
-    pairs = add(even, swap_col(odd, 1)).astype(jnp.bfloat16)
-    sums = [pairs[0]] + [swap_col(pairs[m], 2 * m) for m in range(1, even.shape[0])]
+def pair_sums(even, odd):
+    return add(even, swap_col(odd, 1)).astype(jnp.bfloat16)
+
+
+def finish_col(pairs):
+    sums = [pairs[0]] + [swap_col(pairs[m], 2 * m) for m in range(1, pairs.shape[0])]
     return add(*sums).astype(jnp.bfloat16)
 
 
@@ -279,7 +265,7 @@
 
 
 def finish_row(sums):
-    return rows_first(add(sums[0], *[swap_row(sums[t], t) for t in range(1, 4)]))
+    return rows_first(add(sums[0], swap_row(sums[1], 3)))
 
 
 def activations(hidden, grad_activ):
@@ -315,37 +301,39 @@
 
 
 def on_line(info_in, info_out, tokens, upstream, w_in, w_out, cols, devices):
-    row, slots = info_in[0], w_in.shape[0]
-    every, ends = range(4), (0, 3)
-    w_pair = [w_in, swap_row(w_in, 1)]
+    slots = w_in.shape[0]
+    ends = (0, 3)
+    in_pair = [w_in, swap_row(w_in, 1)]
+    out_pair = [w_out, swap_row(after(w_out, in_pair[1]), 1)]
     both = line_gather(jnp.stack([tokens, upstream]))
     token_even = across(jnp.stack([block[0] for block in both]))
     up_mine = after(jnp.stack([block[1] for block in both]), token_even[1:])
     up_even = across(up_mine)
     all_tokens = with_odd(token_even)
-    own, far = to_hidden(info_in, all_tokens, w_pair, cols, False, ends)
+    own, far = to_hidden(info_in, all_tokens, in_pair, cols, False, ends)
+    far = swap_row(far, 3)
+    hidden = add(own, far)
+    activ = silu(hidden)
     all_up = with_odd(after(up_even, own))
-    parts = to_hidden(info_out, all_up, [w_out], cols, True, every)
-    hidden = add(*after((own, swap_row(far, 3)), parts))
-    activ = silu(hidden)
-    all_activ = [lax.all_gather(activ, "row")]
-    terms, _ = line_reduce(after(parts, activ), row)
-    grad_hidden = activations(hidden, add(*terms))
-    far_grad = swap_row(grad_hidden, 3)
-
-    def column_sums(info, hs, ws, flip, labels):
-        total = finish_col(*from_hidden(info, hs, ws, cols, flip, labels, devices))
-        return [total[g] for g in range(len(labels))]
-
-    all_activ = after(all_activ, grad_hidden)
-    layer_sums = column_sums(info_out, all_activ, [w_out], False, every)
+    activ_far = swap_row(activ, 3)
+    own, far = to_hidden(info_out, after(all_up, activ_far), out_pair, cols, True, ends)
+    far, activ_near = swap_row(far, 3), swap_row(after(activ, own), 1)
+    ends_activ = after([activ, activ_far], own)
+    layer_parts = from_hidden(info_out, ends_activ, out_pair, cols, False, ends, devices)
+    grad_hidden = activations(hidden, add(own, after(far, layer_parts, activ_near)))
+    grad_far = swap_row(grad_hidden, 3)
+    all_activ = [activ, activ_near, swap_row(after(activ_far, grad_hidden), 1), activ_far]
+    layer_sums = finish_col(pair_sums(*after(layer_parts, grad_hidden)))
+    ends_grad = after([grad_hidden, grad_far], all_activ[2], layer_sums)
+    input_parts = from_hidden(info_in, ends_grad, in_pair, cols, True, ends, devices)
+    grad_near, grad_next = swap_row(grad_hidden, 1), swap_row(grad_far, 1)
+    all_grad = [grad_hidden, grad_near, grad_next, grad_far]
+    input_pairs = pair_sums(*input_parts)
+    input_sums = finish_col(input_pairs)
+    all_activ, all_grad = after((all_activ, all_grad), input_pairs)
     grad_w_out = slot_grads(info_out, all_up, all_activ, slots, cols, False)
-    ends_grad = after([grad_hidden, far_grad], grad_w_out)
-    input_sums = column_sums(info_in, ends_grad, w_pair, True, ends)
-    all_grad = [grad_hidden, swap_row(grad_hidden, 1), swap_row(far_grad, 1), far_grad]
     grad_w_in = slot_grads(info_in, all_tokens, all_grad, slots, cols, True)
-    layer_out = finish_row(layer_sums)
-    grad_tokens = rows_first(add(input_sums[0], swap_row(input_sums[1], 3)))
+    layer_out, grad_tokens = finish_row(layer_sums), finish_row(input_sums)
     return layer_out, grad_tokens, grad_w_in, grad_w_out
 
 

time: 307 us -> 302 us (0.984)
  waiting for transfers between devices: 128 us -> 196 us
  starting transfers between devices: 99.6 us -> 41 us
  between operations: 14.6 us -> 1.13 us
  Pallas kernels: 45.8 us -> 49 us
    ppermute x12 -> x15, waiting for transfers between devices: 50.9 us -> 146 us  [swap_row(): return lax.ppermute(x, 'row', [(s, s ^ t) for s in range(4)])]
    ppermute x5 -> x0, waiting for transfers between devices: 46.8 us -> none  [send_row(): return lax.ppermute(x, 'row', pairs)]
    ppermute x5 -> x0, starting transfers between devices: 35.3 us -> none  [send_row(): return lax.ppermute(x, 'row', pairs)]
    ppermute x22, waiting for transfers between devices: 30.6 us -> 50.3 us  [swap_col(): return lax.ppermute(x, 'col', [(s, s ^ m) for s in range(count)])]
    ppermute x22, starting transfers between devices: 29.2 us -> 16.3 us  [swap_col(): return lax.ppermute(x, 'col', [(s, s ^ m) for s in range(count)])]
    ppermute x12 -> x15, starting transfers between devices: 35 us -> 24.7 us  [swap_row(): return lax.ppermute(x, 'row', [(s, s ^ t) for s in range(4)])]
    unnamed x52 -> x48, local copies, waits for them, and re-layouts: 7.04 us -> 3.69 us
    pallas_call x6, Pallas kernels: 45.8 us -> 49 us  [call(): pl.pallas_call(kernel, out_shape=out_shape, in_specs=[pl.BlockSpec(memory...]
  transfers between devices with their start and end apart: 40 -> 37, of which waited for: 14 -> 17; matrix products, arithmetic and copies ran while one was open for 3% -> 4% of each run, Pallas kernels for 15% -> 10%
where the time goes in v8:
time: 302 us; the launch traced here: 300 us
  waiting for transfers between devices  196 us (65%)
  Pallas kernels  49 us (16%)
  starting transfers between devices  41 us (14%)
  other arithmetic  6.47 us (2%)
  local copies, waits for them, and re-layouts  5.92 us (2%)
    ppermute x15, waiting for transfers between devices, swap_row(): return lax.ppermute(x, 'row', [(s, s ^ t) for s in range(4)])  146 us
    ppermute x22, waiting for transfers between devices, swap_col(): return lax.ppermute(x, 'col', [(s, s ^ m) for s in range(count)])  50.3 us
    pallas_call x6, Pallas kernels, call(): pl.pallas_call(kernel, out_shape=out_shape, in_specs=[pl.BlockSpec(memory...  49 us
    ppermute x15, starting transfers between devices, swap_row(): return lax.ppermute(x, 'row', [(s, s ^ t) for s in range(4)])  24.7 us
    ppermute x22, starting transfers between devices, swap_col(): return lax.ppermute(x, 'col', [(s, s ^ m) for s in range(count)])  16.3 us
  transfers between devices with their start and end apart: 37, of which 17 were waited for; matrix products, arithmetic and copies ran while one was open for 4% of the time, Pallas kernels for 10%

profile of v8, /device:TPU:0, one launch (start us, length us, event | category | flops | bytes accessed | tf_op | source)
XLA Modules:
  0.0 299.7 jit_solution(5379911822818823985)
XLA Ops:
  0.6 3.1 %collective-permute-start = (bf16[16,256,256]{2,1,0:T(8,128)(2,1)}, bf16[16,256,256]{2,1,0:T(8,128)(2,1)}, u32[]{:S(2)}, u32[]{:S(2)}) collective-permute-start(bf16[16,256,256]{2,1,0:T(8,128)(2,1)} %bitcast.67), channel_id=1, source_target_pairs={{0,8},{8,0},{16,24},{24,16},{1,9},{9,1},{17,25},{25,17},{2,10},{10... | collective-permute-start | bytes 6291464 | tf_op jit(solution)/shard_map/ppermute | solution.py:225
  10.6 48.0 %collective-permute-done.4 = bf16[2,2,128,256]{3,2,1,0:T(8,128)(2,1)S(1)} collective-permute-done((bf16[2,2,128,256]{3,2,1,0:T(8,128)(2,1)S(1)}, bf16[2,2,128,256]{3,2,1,0:T(8,128)(2,1)S(1)}, u32[]{:S(2)}, u32[]{:S(2)}) %collective-permute-start.4) | collective-permute-done | bytes 262176 | tf_op jit(solution)/shard_map/ppermute | solution.py:225
  61.2 5.2 %collective-permute-done.2 = bf16[2,2,128,256]{3,2,1,0:T(8,128)(2,1)S(1)} collective-permute-done((bf16[2,2,128,256]{3,2,1,0:T(8,128)(2,1)S(1)}, bf16[2,2,128,256]{3,2,1,0:T(8,128)(2,1)S(1)}, u32[]{:S(2)}, u32[]{:S(2)}) %collective-permute-start.2) | collective-permute-done | bytes 262176 | tf_op jit(solution)/shard_map/ppermute | solution.py:225
  70.7 11.5 %collective-permute-done.6.refs_4_.refs_2_ = bf16[4,2,128,256]{3,2,1,0:T(8,128)(2,1)} collective-permute-done((bf16[4,2,128,256]{3,2,1,0:T(8,128)(2,1)S(1)}, bf16[4,2,128,256]{3,2,1,0:T(8,128)(2,1)}, u32[]{:S(2)}, u32[]{:S(2)}) %collective-permute-start.6) | collective-permute-done | bytes 524320 | tf_op jit(solution)/shard_map/ppermute | solution.py:221
  82.2 10.5 %collective-permute-done.8.refs_6_.refs_4_ = bf16[4,2,128,256]{3,2,1,0:T(8,128)(2,1)} collective-permute-done((bf16[4,2,128,256]{3,2,1,0:T(8,128)(2,1)S(1)}, bf16[4,2,128,256]{3,2,1,0:T(8,128)(2,1)}, u32[]{:S(2)}, u32[]{:S(2)}) %collective-permute-start.8) | collective-permute-done | bytes 524320 | tf_op jit(solution)/shard_map/ppermute | solution.py:221
  99.8 7.9 %shard_map.93 = (bf16[8,128,256]{2,1,0:T(8,128)(2,1)}, bf16[8,128,256]{2,1,0:T(8,128)(2,1)}) custom-call(s32[34]{0:T(128)} %pad_add_fusion.2.info, bf16[16,256,256]{2,1,0:T(8,128)(2,1)} %bitcast.68, bf16[16,256,256]{2,1,0:T(8,128)(2,1)} %collective-permute-done.refs_1_, bf16[4,2,128,256]{3,2,1,0:T(8,128)(2,1)} %copy-done.1, ...), custom_call_target="tpu_custom_call" | custom-call | flops 1073741824 | bytes 8388608 | tf_op jit(solution)/shard_map/pallas_call | solution.py:145
  107.7 2.9 collective-permute-start.12
  110.6 9.7 %collective-permute-done.15.refs_6_.refs_4_ = bf16[4,2,128,256]{3,2,1,0:T(8,128)(2,1)} collective-permute-done((bf16[4,2,128,256]{3,2,1,0:T(8,128)(2,1)S(1)}, bf16[4,2,128,256]{3,2,1,0:T(8,128)(2,1)}, u32[]{:S(2)}, u32[]{:S(2)}) %collective-permute-start.15) | collective-permute-done | bytes 524320 | tf_op jit(solution)/shard_map/ppermute | solution.py:221
  122.6 31.4 %collective-permute-done.12 = bf16[8,128,256]{2,1,0:T(8,128)(2,1)S(1)} collective-permute-done((bf16[8,128,256]{2,1,0:T(8,128)(2,1)}, bf16[8,128,256]{2,1,0:T(8,128)(2,1)S(1)}, u32[]{:S(2)}, u32[]{:S(2)}) %collective-permute-start.12) | collective-permute-done | bytes 524320 | tf_op jit(solution)/shard_map/ppermute | solution.py:225
  157.7 14.1 %collective-permute-done.13.refs_3_.refs_11_ = bf16[8,128,256]{2,1,0:T(8,128)(2,1)S(1)} collective-permute-done((bf16[8,128,256]{2,1,0:T(8,128)(2,1)S(1)}, bf16[8,128,256]{2,1,0:T(8,128)(2,1)S(1)}, u32[]{:S(2)}, u32[]{:S(2)}) %collective-permute-start.13) | collective-permute-done | bytes 524320 | tf_op jit(solution)/shard_map/ppermute | solution.py:225
  171.8 9.1 %shard_map.94 = (bf16[8,128,256]{2,1,0:T(8,128)(2,1)}, bf16[8,128,256]{2,1,0:T(8,128)(2,1)}) custom-call(s32[34]{0:T(128)} %pad_add_fusion.info, bf16[16,256,256]{2,1,0:T(8,128)(2,1)} %bitcast.64, bf16[16,256,256]{2,1,0:T(8,128)(2,1)} %collective-permute-done.1.refs_1_, bf16[4,2,128,256]{3,2,1,0:T(8,128)(2,1)} %copy-done.2, ...), custom_call_target="tpu_custom_call" | custom-call | flops 1073741824 | bytes 8388608 | tf_op jit(solution)/shard_map/pallas_call | solution.py:145
  181.0 3.3 %collective-permute-start.21 = (bf16[8,128,256]{2,1,0:T(8,128)(2,1)}, bf16[8,128,256]{2,1,0:T(8,128)(2,1)S(1)}, u32[]{:S(2)}, u32[]{:S(2)}) collective-permute-start(bf16[8,128,256]{2,1,0:T(8,128)(2,1)} %get-tuple-element.64), channel_id=1, source_target_pairs={{0,24},{8,16},{16,8},{24,0},{1,25},{9,17},{17,9},{25,1},{2,26},{10... | collective-permute-start | bytes 1572872 | tf_op jit(solution)/shard_map/ppermute | solution.py:225
  184.2 8.4 %shard_map.95 = (bf16[4,2,2,128,256]{4,3,2,1,0:T(8,128)(2,1)}, bf16[4,2,2,128,256]{4,3,2,1,0:T(8,128)(2,1)}) custom-call(s32[34]{0:T(128)} %pad_add_fusion.info, bf16[16,256,256]{2,1,0:T(8,128)(2,1)} %bitcast.65, bf16[16,256,256]{2,1,0:T(8,128)(2,1)} %collective-permute-done.1.refs_1_, bf16[8,128,256]{2,1,0:T(8,128)(2,1)} %copy-done.3, ...), custom_call_target="tpu_custom_call" | custom-call | flops 1073741824 | bytes 8388608 | tf_op jit(solution)/shard_map/pallas_call | solution.py:145
  192.7 5.2 %collective-permute-done.21 = bf16[8,128,256]{2,1,0:T(8,128)(2,1)S(1)} collective-permute-done((bf16[8,128,256]{2,1,0:T(8,128)(2,1)}, bf16[8,128,256]{2,1,0:T(8,128)(2,1)S(1)}, u32[]{:S(2)}, u32[]{:S(2)}) %collective-permute-start.21) | collective-permute-done | bytes 524320 | tf_op jit(solution)/shard_map/ppermute | solution.py:225
  197.8 10.2 %collective-permute-done.22.refs_9_ = bf16[8,128,256]{2,1,0:T(8,128)(2,1)S(1)} collective-permute-done((bf16[8,128,256]{2,1,0:T(8,128)(2,1)S(1)}, bf16[8,128,256]{2,1,0:T(8,128)(2,1)S(1)}, u32[]{:S(2)}, u32[]{:S(2)}) %collective-permute-start.22) | collective-permute-done | bytes 524320 | tf_op jit(solution)/shard_map/ppermute | solution.py:225
  211.9 3.4 %collective-permute-start.24 = (bf16[2,2,128,256]{3,2,1,0:T(8,128)(2,1)S(1)}, bf16[2,2,128,256]{3,2,1,0:T(8,128)(2,1)S(1)}, u32[]{:S(2)}, u32[]{:S(2)}) collective-permute-start(bf16[2,2,128,256]{3,2,1,0:T(8,128)(2,1)S(1)} %get-tuple-element.89), channel_id=1, source_target_pairs={{0,2},{1,3},{2,0},{3,1},{4,6},{5,7},{6,4},{7,5},{8,10},{9,11},{10,... | collective-permute-start | bytes 786440 | tf_op jit(solution)/shard_map/ppermute | solution.py:221
  215.3 6.6 %collective-permute-done.26 = bf16[2,2,128,256]{3,2,1,0:T(8,128)(2,1)S(1)} collective-permute-done((bf16[2,2,128,256]{3,2,1,0:T(8,128)(2,1)S(1)}, bf16[2,2,128,256]{3,2,1,0:T(8,128)(2,1)S(1)}, u32[]{:S(2)}, u32[]{:S(2)}) %collective-permute-start.26) | collective-permute-done | bytes 262176 | tf_op jit(solution)/shard_map/ppermute | solution.py:221
  221.9 3.9 %collective-permute-done.25 = bf16[2,2,128,256]{3,2,1,0:T(8,128)(2,1)S(1)} collective-permute-done((bf16[2,2,128,256]{3,2,1,0:T(8,128)(2,1)S(1)}, bf16[2,2,128,256]{3,2,1,0:T(8,128)(2,1)S(1)}, u32[]{:S(2)}, u32[]{:S(2)}) %collective-permute-start.25) | collective-permute-done | bytes 262176 | tf_op jit(solution)/shard_map/ppermute | solution.py:221
  226.0 9.5 %collective-permute-done.29.refs_10_ = bf16[8,128,256]{2,1,0:T(8,128)(2,1)S(1)} collective-permute-done((bf16[8,128,256]{2,1,0:T(8,128)(2,1)S(1)}, bf16[8,128,256]{2,1,0:T(8,128)(2,1)S(1)}, u32[]{:S(2)}, u32[]{:S(2)}) %collective-permute-start.29) | collective-permute-done | bytes 524320 | tf_op jit(solution)/shard_map/ppermute | solution.py:225
  235.5 8.4 %shard_map.96 = (bf16[4,2,2,128,256]{4,3,2,1,0:T(8,128)(2,1)}, bf16[4,2,2,128,256]{4,3,2,1,0:T(8,128)(2,1)}) custom-call(s32[34]{0:T(128)} %pad_add_fusion.2.info, bf16[16,256,256]{2,1,0:T(8,128)(2,1)} %bitcast.69, bf16[16,256,256]{2,1,0:T(8,128)(2,1)} %collective-permute-done.refs_1_, bf16[8,128,256]{2,1,0:T(8,128)(2,1)} %copy-done.4, ...), custom_call_target="tpu_custom_call" | custom-call | flops 1073741824 | bytes 8388608 | tf_op jit(solution)/shard_map/pallas_call | solution.py:145
  254.0 19.7 %collective-permute-done.27 = bf16[2,128,256]{2,1,0:T(8,128)(2,1)S(1)} collective-permute-done((bf16[2,128,256]{2,1,0:T(8,128)(2,1)S(1)}, bf16[2,128,256]{2,1,0:T(8,128)(2,1)S(1)}, u32[]{:S(2)}, u32[]{:S(2)}) %collective-permute-start.27) | collective-permute-done | bytes 131104 | tf_op jit(solution)/shard_map/ppermute | solution.py:225
  276.8 5.3 %collective-permute-done.31 = bf16[2,2,128,256]{3,2,1,0:T(8,128)(2,1)S(1)} collective-permute-done((bf16[2,2,128,256]{3,2,1,0:T(8,128)(2,1)}, bf16[2,2,128,256]{3,2,1,0:T(8,128)(2,1)S(1)}, u32[]{:S(2)}, u32[]{:S(2)}) %collective-permute-start.31) | collective-permute-done | bytes 262176 | tf_op jit(solution)/shard_map/ppermute | solution.py:221
  283.6 7.7 %shard_map.97 = bf16[16,256,256]{2,1,0:T(8,128)(2,1)} custom-call(s32[34]{0:T(128)} %pad_add_fusion.2.info, bf16[4,2,128,256]{3,2,1,0:T(8,128)(2,1)} %copy-done.1, bf16[4,2,128,256]{3,2,1,0:T(8,128)(2,1)} %collective-permute-done.5.refs_3_.refs_1_, bf16[4,2,128,256]{3,2,1,0:T(8,128)(2,1)} %collective-permute-done.6.refs_4_.refs_2_, ...), custom_call_target="tpu_custom_call" | custom-call | flops 1073741824 | bytes 8388608 | tf_op jit(solution)/shard_map/pallas_call | solution.py:145
  291.3 7.4 %shard_map.98 = bf16[16,256,256]{2,1,0:T(8,128)(2,1)} custom-call(s32[34]{0:T(128)} %pad_add_fusion.info, bf16[4,2,128,256]{3,2,1,0:T(8,128)(2,1)} %copy-done.2, bf16[4,2,128,256]{3,2,1,0:T(8,128)(2,1)} %copy-done.5, bf16[4,2,128,256]{3,2,1,0:T(8,128)(2,1)} %collective-permute-done.14.refs_4_.refs_2_, bf16[4,2,128,256]{3,2,1,0:T(8,128)(2,1)} %copy-done.6, ...), custom_call_target="tpu_custom_call" | custom-call | flops 1073741824 | bytes 8388608 | tf_op jit(solution)/shard_map/pallas_call | solution.py:145
  (129 shorter events, 46.1 us)
Async XLA Ops:
  0.6 92.1 %collective-permute-start = (bf16[16,256,256]{2,1,0:T(8,128)(2,1)}, bf16[16,256,256]{2,1,0:T(8,128)(2,1)}, u32[]{:S(2)}, u32[]{:S(2)}) collective-permute-start(bf16[16,256,256]{2,1,0:T(8,128)(2,1)} %bitcast.67), channel_id=1, source_target_pairs={{0,8},{8,0},{16,24},{24,16},{1,9},{9,1},{17,25},{25,17},{2,10},{10... | collective-permute-start | bytes 6291464 | tf_op jit(solution)/shard_map/ppermute | solution.py:225
  6.1 52.5 %collective-permute-start.4 = (bf16[2,2,128,256]{3,2,1,0:T(8,128)(2,1)S(1)}, bf16[2,2,128,256]{3,2,1,0:T(8,128)(2,1)S(1)}, u32[]{:S(2)}, u32[]{:S(2)}) collective-permute-start(bf16[2,2,128,256]{3,2,1,0:T(8,128)(2,1)S(1)} %pad_maximum_fusion.2), channel_id=1, source_target_pairs={{0,24},{8,16},{16,8},{24,0},{1,25},{9,17},{17,9},{25,1},{2,26},{10... | collective-permute-start | bytes 786440 | tf_op jit(solution)/shard_map/ppermute | solution.py:225
  8.7 52.5 %collective-permute-start.3 = (bf16[2,2,128,256]{3,2,1,0:T(8,128)(2,1)S(1)}, bf16[2,2,128,256]{3,2,1,0:T(8,128)(2,1)S(1)}, u32[]{:S(2)}, u32[]{:S(2)}) collective-permute-start(bf16[2,2,128,256]{3,2,1,0:T(8,128)(2,1)S(1)} %pad_maximum_fusion.2), channel_id=1, source_target_pairs={{0,16},{8,24},{16,0},{24,8},{1,17},{9,25},{17,1},{25,9},{2,18},{10... | collective-permute-start | bytes 786440 | tf_op jit(solution)/shard_map/ppermute | solution.py:225
  8.8 57.6 %collective-permute-start.2 = (bf16[2,2,128,256]{3,2,1,0:T(8,128)(2,1)S(1)}, bf16[2,2,128,256]{3,2,1,0:T(8,128)(2,1)S(1)}, u32[]{:S(2)}, u32[]{:S(2)}) collective-permute-start(bf16[2,2,128,256]{3,2,1,0:T(8,128)(2,1)S(1)} %pad_maximum_fusion.2), channel_id=1, source_target_pairs={{0,8},{8,0},{16,24},{24,16},{1,9},{9,1},{17,25},{25,17},{2,10},{10... | collective-permute-start | bytes 786440 | tf_op jit(solution)/shard_map/ppermute | solution.py:225
  68.9 23.9 %collective-permute-start.8 = (bf16[4,2,128,256]{3,2,1,0:T(8,128)(2,1)S(1)}, bf16[4,2,128,256]{3,2,1,0:T(8,128)(2,1)}, u32[]{:S(2)}, u32[]{:S(2)}) collective-permute-start(bf16[4,2,128,256]{3,2,1,0:T(8,128)(2,1)S(1)} %pad_maximum_fusion.refs_2_.refs_0_), channel_id=1, source_target_pairs={{0,4},{1,5},{2,6},{3,7},{4,0},{5,1},{6,2},{7,3},{8,12},{9,13},{10,... | collective-permute-start | bytes 1572872 | tf_op jit(solution)/shard_map/ppermute | solution.py:221
  70.4 24.0 %collective-permute-start.10 = (bf16[4,2,128,256]{3,2,1,0:T(8,128)(2,1)S(1)}, bf16[4,2,128,256]{3,2,1,0:T(8,128)(2,1)}, u32[]{:S(2)}, u32[]{:S(2)}) collective-permute-start(bf16[4,2,128,256]{3,2,1,0:T(8,128)(2,1)S(1)} %pad_maximum_fusion.refs_2_.refs_0_), channel_id=1, source_target_pairs={{0,6},{1,7},{2,4},{3,5},{4,2},{5,3},{6,0},{7,1},{8,14},{9,15},{10,... | collective-permute-start | bytes 1572872 | tf_op jit(solution)/shard_map/ppermute | solution.py:221
  70.7 24.8 %collective-permute-start.5 = (bf16[4,2,128,256]{3,2,1,0:T(8,128)(2,1)S(1)}, bf16[4,2,128,256]{3,2,1,0:T(8,128)(2,1)}, u32[]{:S(2)}, u32[]{:S(2)}) collective-permute-start(bf16[4,2,128,256]{3,2,1,0:T(8,128)(2,1)S(1)} %pad_maximum_fusion.refs_2_.refs_0_), channel_id=1, source_target_pairs={{0,1},{1,0},{2,3},{3,2},{4,5},{5,4},{6,7},{7,6},{8,9},{9,8},{10,11... | collective-permute-start | bytes 1572872 | tf_op jit(solution)/shard_map/ppermute | solution.py:221
  92.8 79.0 %collective-permute-start.1 = (bf16[16,256,256]{2,1,0:T(8,128)(2,1)S(1)}, bf16[16,256,256]{2,1,0:T(8,128)(2,1)}, u32[]{:S(2)}, u32[]{:S(2)}) collective-permute-start(bf16[16,256,256]{2,1,0:T(8,128)(2,1)S(1)} %bitcast.66), channel_id=1, source_target_pairs={{0,8},{8,0},{16,24},{24,16},{1,9},{9,1},{17,25},{25,17},{2,10},{10... | collective-permute-start | bytes 6291464 | tf_op jit(solution)/shard_map/ppermute | solution.py:225
  95.7 24.7 %collective-permute-start.15 = (bf16[4,2,128,256]{3,2,1,0:T(8,128)(2,1)S(1)}, bf16[4,2,128,256]{3,2,1,0:T(8,128)(2,1)}, u32[]{:S(2)}, u32[]{:S(2)}) collective-permute-start(bf16[4,2,128,256]{3,2,1,0:T(8,128)(2,1)S(1)} %pad_maximum_fusion.1.refs_2_.refs_0_), channel_id=1, source_target_pairs={{0,4},{1,5},{2,6},{3,7},{4,0},{5,1},{6,2},{7,3},{8,12},{9,13},{10,... | collective-permute-start | bytes 1572872 | tf_op jit(solution)/shard_map/ppermute | solution.py:221
  97.7 24.4 %collective-permute-start.16 = (bf16[4,2,128,256]{3,2,1,0:T(8,128)(2,1)S(1)}, bf16[4,2,128,256]{3,2,1,0:T(8,128)(2,1)}, u32[]{:S(2)}, u32[]{:S(2)}) collective-permute-start(bf16[4,2,128,256]{3,2,1,0:T(8,128)(2,1)S(1)} %pad_maximum_fusion.1.refs_2_.refs_0_), channel_id=1, source_target_pairs={{0,6},{1,7},{2,4},{3,5},{4,2},{5,3},{6,0},{7,1},{8,14},{9,15},{10,... | collective-permute-start | bytes 1572872 | tf_op jit(solution)/shard_map/ppermute | solution.py:221
  107.7 46.4 %collective-permute-start.12 = (bf16[8,128,256]{2,1,0:T(8,128)(2,1)}, bf16[8,128,256]{2,1,0:T(8,128)(2,1)S(1)}, u32[]{:S(2)}, u32[]{:S(2)}) collective-permute-start(bf16[8,128,256]{2,1,0:T(8,128)(2,1)} %get-tuple-element.45), channel_id=1, source_target_pairs={{0,24},{8,16},{16,8},{24,0},{1,25},{9,17},{17,9},{25,1},{2,26},{10... | collective-permute-start | bytes 1572872 | tf_op jit(solution)/shard_map/ppermute | solution.py:225
  122.1 33.3 %collective-permute-start.17 = (bf16[4,2,128,256]{3,2,1,0:T(8,128)(2,1)S(1)}, bf16[4,2,128,256]{3,2,1,0:T(8,128)(2,1)S(1)}, u32[]{:S(2)}, u32[]{:S(2)}) collective-permute-start(bf16[4,2,128,256]{3,2,1,0:T(8,128)(2,1)S(1)} %pad_maximum_fusion.1.refs_2_.refs_0_), channel_id=1, source_target_pairs={{0,1},{1,0},{2,3},{3,2},{4,5},{5,4},{6,7},{7,6},{8,9},{9,8},{10,11... | collective-permute-start | bytes 1572872 | tf_op jit(solution)/shard_map/ppermute | solution.py:221
  122.1 35.5 %collective-permute-start.18 = (bf16[4,2,128,256]{3,2,1,0:T(8,128)(2,1)}, bf16[4,2,128,256]{3,2,1,0:T(8,128)(2,1)S(1)}, u32[]{:S(2)}, u32[]{:S(2)}) collective-permute-start(bf16[4,2,128,256]{3,2,1,0:T(8,128)(2,1)} %collective-permute-done.14.refs_4_.refs_2_), channel_id=1, source_target_pairs={{0,1},{1,0},{2,3},{3,2},{4,5},{5,4},{6,7},{7,6},{8,9},{9,8},{10,11... | collective-permute-start | bytes 1572872 | tf_op jit(solution)/shard_map/ppermute | solution.py:221
  122.6 35.0 %collective-permute-start.19 = (bf16[4,2,128,256]{3,2,1,0:T(8,128)(2,1)}, bf16[4,2,128,256]{3,2,1,0:T(8,128)(2,1)S(1)}, u32[]{:S(2)}, u32[]{:S(2)}) collective-permute-start(bf16[4,2,128,256]{3,2,1,0:T(8,128)(2,1)} %collective-permute-done.15.refs_6_.refs_4_), channel_id=1, source_target_pairs={{0,1},{1,0},{2,3},{3,2},{4,5},{5,4},{6,7},{7,6},{8,9},{9,8},{10,11... | collective-permute-start | bytes 1572872 | tf_op jit(solution)/shard_map/ppermute | solution.py:221
  181.0 16.9 %collective-permute-start.21 = (bf16[8,128,256]{2,1,0:T(8,128)(2,1)}, bf16[8,128,256]{2,1,0:T(8,128)(2,1)S(1)}, u32[]{:S(2)}, u32[]{:S(2)}) collective-permute-start(bf16[8,128,256]{2,1,0:T(8,128)(2,1)} %get-tuple-element.64), channel_id=1, source_target_pairs={{0,24},{8,16},{16,8},{24,0},{1,25},{9,17},{17,9},{25,1},{2,26},{10... | collective-permute-start | bytes 1572872 | tf_op jit(solution)/shard_map/ppermute | solution.py:225
  184.2 23.8 %collective-permute-start.22 = (bf16[8,128,256]{2,1,0:T(8,128)(2,1)S(1)}, bf16[8,128,256]{2,1,0:T(8,128)(2,1)S(1)}, u32[]{:S(2)}, u32[]{:S(2)}) collective-permute-start(bf16[8,128,256]{2,1,0:T(8,128)(2,1)S(1)} %multiply_convert_fusion.1.refs_2_.refs_8_), channel_id=1, source_target_pairs={{0,8},{8,0},{16,24},{24,16},{1,9},{9,1},{17,25},{25,17},{2,10},{10... | collective-permute-start | bytes 1572872 | tf_op jit(solution)/shard_map/ppermute | solution.py:225
  208.7 17.3 %collective-permute-start.28 = (bf16[8,128,256]{2,1,0:T(8,128)(2,1)S(1)}, bf16[8,128,256]{2,1,0:T(8,128)(2,1)S(1)}, u32[]{:S(2)}, u32[]{:S(2)}) collective-permute-start(bf16[8,128,256]{2,1,0:T(8,128)(2,1)S(1)} %multiply_convert_fusion.refs_2_.refs_8_), channel_id=1, source_target_pairs={{0,24},{8,16},{16,8},{24,0},{1,25},{9,17},{17,9},{25,1},{2,26},{10... | collective-permute-start | bytes 1572872 | tf_op jit(solution)/shard_map/ppermute | solution.py:225
  210.3 25.2 %collective-permute-start.29 = (bf16[8,128,256]{2,1,0:T(8,128)(2,1)S(1)}, bf16[8,128,256]{2,1,0:T(8,128)(2,1)S(1)}, u32[]{:S(2)}, u32[]{:S(2)}) collective-permute-start(bf16[8,128,256]{2,1,0:T(8,128)(2,1)S(1)} %copy-done.11), channel_id=1, source_target_pairs={{0,8},{8,0},{16,24},{24,16},{1,9},{9,1},{17,25},{25,17},{2,10},{10... | collective-permute-start | bytes 1572872 | tf_op jit(solution)/shard_map/ppermute | solution.py:225
  244.0 32.7 %collective-permute-start.35 = (bf16[8,128,256]{2,1,0:T(8,128)(2,1)}, bf16[8,128,256]{2,1,0:T(8,128)(2,1)S(1)}, u32[]{:S(2)}, u32[]{:S(2)}) collective-permute-start(bf16[8,128,256]{2,1,0:T(8,128)(2,1)} %copy-done.4), channel_id=1, source_target_pairs={{0,8},{8,0},{16,24},{24,16},{1,9},{9,1},{17,25},{25,17},{2,10},{10... | collective-permute-start | bytes 1572872 | tf_op jit(solution)/shard_map/ppermute | solution.py:225
  244.5 32.3 %collective-permute-start.36 = (bf16[8,128,256]{2,1,0:T(8,128)(2,1)}, bf16[8,128,256]{2,1,0:T(8,128)(2,1)S(1)}, u32[]{:S(2)}, u32[]{:S(2)}) collective-permute-start(bf16[8,128,256]{2,1,0:T(8,128)(2,1)} %copy-done.12), channel_id=1, source_target_pairs={{0,8},{8,0},{16,24},{24,16},{1,9},{9,1},{17,25},{25,17},{2,10},{10... | collective-permute-start | bytes 1572872 | tf_op jit(solution)/shard_map/ppermute | solution.py:225
  246.1 27.6 %collective-permute-start.27 = (bf16[2,128,256]{2,1,0:T(8,128)(2,1)S(1)}, bf16[2,128,256]{2,1,0:T(8,128)(2,1)S(1)}, u32[]{:S(2)}, u32[]{:S(2)}) collective-permute-start(bf16[2,128,256]{2,1,0:T(8,128)(2,1)S(1)} %slice_bitcast_fusion.10), channel_id=1, source_target_pairs={{0,24},{8,16},{16,8},{24,0},{1,25},{9,17},{17,9},{25,1},{2,26},{10... | collective-permute-start | bytes 393224 | tf_op jit(solution)/shard_map/ppermute | solution.py:225
  251.3 25.5 %collective-permute-start.33 = (bf16[2,2,128,256]{3,2,1,0:T(8,128)(2,1)}, bf16[2,2,128,256]{3,2,1,0:T(8,128)(2,1)S(1)}, u32[]{:S(2)}, u32[]{:S(2)}) collective-permute-start(bf16[2,2,128,256]{3,2,1,0:T(8,128)(2,1)} %get-tuple-element.87), channel_id=1, source_target_pairs={{0,6},{1,7},{2,4},{3,5},{4,2},{5,3},{6,0},{7,1},{8,14},{9,15},{10,... | collective-permute-start | bytes 786440 | tf_op jit(solution)/shard_map/ppermute | solution.py:221
  253.3 23.5 %collective-permute-start.32 = (bf16[2,2,128,256]{3,2,1,0:T(8,128)(2,1)}, bf16[2,2,128,256]{3,2,1,0:T(8,128)(2,1)S(1)}, u32[]{:S(2)}, u32[]{:S(2)}) collective-permute-start(bf16[2,2,128,256]{3,2,1,0:T(8,128)(2,1)} %get-tuple-element.88), channel_id=1, source_target_pairs={{0,4},{1,5},{2,6},{3,7},{4,0},{5,1},{6,2},{7,3},{8,12},{9,13},{10,... | collective-permute-start | bytes 786440 | tf_op jit(solution)/shard_map/ppermute | solution.py:221
  282.2 16.6 %collective-permute-start.34 = (bf16[2,128,256]{2,1,0:T(8,128)(2,1)S(1)}, bf16[2,128,256]{2,1,0:T(8,128)(2,1)S(1)}, u32[]{:S(2)}, u32[]{:S(2)}) collective-permute-start(bf16[2,128,256]{2,1,0:T(8,128)(2,1)S(1)} %slice_bitcast_fusion.8), channel_id=1, source_target_pairs={{0,24},{8,16},{16,8},{24,0},{1,25},{9,17},{17,9},{25,1},{2,26},{10... | collective-permute-start | bytes 393224 | tf_op jit(solution)/shard_map/ppermute | solution.py:225
  (35 other events, 724.1 us)

commit v9 on v8

--- a/solution.py
+++ b/solution.py
@@ -66,16 +66,16 @@
 
 
 def over_slots(info, first, slots, cols, body):
-    def slot(s, carry):
-        code = info[2 + first + s]
-
-        @pl.when(code >= 0)
-        def _():
-            body(s, lax.div(code, cols), lax.rem(code, cols))
-
+    step = 4 if slots % 4 == 0 else 1
+
+    def some(at, carry):
+        for s in [at * step + i for i in range(step)]:
+            code = info[2 + first + s]
+            tile = jnp.maximum(code, 0)
+            body(s, code >= 0, lax.div(tile, cols), lax.rem(tile, cols))
         return carry
 
-    lax.fori_loop(0, slots, slot, 0)
+    lax.fori_loop(0, slots // step, some, 0)
 
 
 def to_hidden_kernel(cols, flip, labels, wides, weights, info, *refs):
@@ -87,14 +87,15 @@
         copy.wait()
 
     for at, w_ref in enumerate(w_refs):
-        def add(s, wide, hidden, w_ref=w_ref):
+        def add(s, filled, wide, hidden, w_ref=w_ref):
+            target = jnp.where(filled, hidden, acc.shape[0] - 1)
             for chunk in chunks(x.shape[1]):
                 product = matmul(flat(x[wide, chunk]), w_ref[s], 1, 1 if flip else 0)
-                acc[hidden, chunk] += product.reshape(-1, *acc.shape[2:])
+                acc[target, chunk] += product.reshape(-1, *acc.shape[2:])
 
         over_slots(info, at * w_ref.shape[0], w_ref.shape[0], cols, add)
     for part, out in enumerate(outs):
-        out[...] = acc[:, part].astype(out.dtype)
+        out[...] = acc[:out.shape[0], part].astype(out.dtype)
 
 
 def from_hidden_kernel(cols, flip, labels, hiddens, weights, info, *refs):
@@ -106,10 +107,11 @@
         copy.wait()
 
     for at, w_ref in enumerate(w_refs):
-        def add(s, wide, hidden, w_ref=w_ref):
+        def add(s, filled, wide, hidden, w_ref=w_ref):
+            target = jnp.where(filled, wide, acc.shape[0] - 1)
             for chunk in chunks(h.shape[1]):
                 product = matmul(flat(h[hidden, chunk]), w_ref[s], 1, 1 if flip else 0)
-                acc[wide, chunk] += product.reshape(-1, *acc.shape[2:])
+                acc[target, chunk] += product.reshape(-1, *acc.shape[2:])
 
         over_slots(info, at * w_ref.shape[0], w_ref.shape[0], cols, add)
     for at, out in enumerate(outs):
@@ -126,17 +128,16 @@
     out, x, h, x_sems, h_sems = refs[-5:]
     copies = wide_copies(x_refs, labels, x, x_sems, info[1])
     copies += hidden_copies(h_refs, labels, h, h_sems, info[0])
-    out[...] = jnp.zeros_like(out)
     for copy in copies:
         copy.wait()
 
-    def add(s, wide, hidden):
+    def add(s, filled, wide, hidden):
         total = 0.0
         for chunk in chunks(x.shape[1]):
             a, b = flat(x[wide, chunk]), flat(h[hidden, chunk])
             a, b = (a, b) if flip else (b, a)
             total += matmul(a, b, 0, 0)
-        out[s] = total.astype(out.dtype)
+        out[s] = jnp.where(filled, total, 0.0).astype(out.dtype)
 
     over_slots(info, 0, out.shape[0], cols, add)
 
@@ -165,7 +166,7 @@
     group = len(labels)
     outs = [jax.ShapeDtypeStruct((cols, rows, tile), jnp.bfloat16)] * group
     held, sems = wide_scratch(labels, rows, tile, unit)
-    scratch = [held, pltpu.VMEM((cols, group, rows, tile), jnp.float32), sems]
+    scratch = [held, pltpu.VMEM((cols + 1, group, rows, tile), jnp.float32), sems]
     kernel = functools.partial(to_hidden_kernel, cols, flip, labels, len(xs), len(ws))
     specs = [pl.BlockSpec(memory_space=pltpu.VMEM)] * len(ws) + [ANY] * len(xs)
     flops = 2 * len(ws) * slots * group * rows * tile * tile
@@ -184,7 +185,7 @@
         outs = [jax.ShapeDtypeStruct((devices // 2, *shape), jnp.bfloat16)] * 2
     scratch = [
         pltpu.VMEM((cols, group, rows, tile), jnp.bfloat16),
-        pltpu.VMEM((D // tile, group, rows, tile), jnp.float32),
+        pltpu.VMEM((D // tile + 1, group, rows, tile), jnp.float32),
         pltpu.SemaphoreType.DMA((group,)),
     ]
     kernel = functools.partial(from_hidden_kernel, cols, flip, labels, len(hs), len(ws))
@@ -255,17 +256,13 @@
     return add(even, swap_col(odd, 1)).astype(jnp.bfloat16)
 
 
-def finish_col(pairs):
+def finish_col(pairs, *wait):
     sums = [pairs[0]] + [swap_col(pairs[m], 2 * m) for m in range(1, pairs.shape[0])]
-    return add(*sums).astype(jnp.bfloat16)
+    return add(*after(sums, *wait)).astype(jnp.bfloat16)
 
 
 def rows_first(total):
     return jnp.swapaxes(total, 0, 1).reshape(total.shape[1], -1).astype(jnp.bfloat16)
-
-
-def finish_row(sums):
-    return rows_first(add(sums[0], swap_row(sums[1], 3)))
 
 
 def activations(hidden, grad_activ):
@@ -303,20 +300,18 @@
 def on_line(info_in, info_out, tokens, upstream, w_in, w_out, cols, devices):
     slots = w_in.shape[0]
     ends = (0, 3)
-    in_pair = [w_in, swap_row(w_in, 1)]
-    out_pair = [w_out, swap_row(after(w_out, in_pair[1]), 1)]
     both = line_gather(jnp.stack([tokens, upstream]))
+    in_pair = [w_in, swap_row(after(w_in, both), 1)]
     token_even = across(jnp.stack([block[0] for block in both]))
-    up_mine = after(jnp.stack([block[1] for block in both]), token_even[1:])
-    up_even = across(up_mine)
+    up_even = across(after(jnp.stack([block[1] for block in both]), token_even[1:]))
     all_tokens = with_odd(token_even)
+    out_pair = [w_out, swap_row(after(w_out, in_pair[1], all_tokens), 1)]
     own, far = to_hidden(info_in, all_tokens, in_pair, cols, False, ends)
-    far = swap_row(far, 3)
-    hidden = add(own, far)
+    hidden = add(own, swap_row(far, 3))
     activ = silu(hidden)
+    activ_far = swap_row(activ, 3)
     all_up = with_odd(after(up_even, own))
-    activ_far = swap_row(activ, 3)
-    own, far = to_hidden(info_out, after(all_up, activ_far), out_pair, cols, True, ends)
+    own, far = to_hidden(info_out, after(all_up, activ), out_pair, cols, True, ends)
     far, activ_near = swap_row(far, 3), swap_row(after(activ, own), 1)
     ends_activ = after([activ, activ_far], own)
     layer_parts = from_hidden(info_out, ends_activ, out_pair, cols, False, ends, devices)
@@ -326,14 +321,17 @@
     layer_sums = finish_col(pair_sums(*after(layer_parts, grad_hidden)))
     ends_grad = after([grad_hidden, grad_far], all_activ[2], layer_sums)
     input_parts = from_hidden(info_in, ends_grad, in_pair, cols, True, ends, devices)
-    grad_near, grad_next = swap_row(grad_hidden, 1), swap_row(grad_far, 1)
-    all_grad = [grad_hidden, grad_near, grad_next, grad_far]
+    layer_far = swap_row(layer_sums[1], 3)
     input_pairs = pair_sums(*input_parts)
-    input_sums = finish_col(input_pairs)
-    all_activ, all_grad = after((all_activ, all_grad), input_pairs)
+    all_activ = after(all_activ, input_pairs)
     grad_w_out = slot_grads(info_out, all_up, all_activ, slots, cols, False)
+    near, far = swap_row(grad_hidden, 1), swap_row(grad_far, 1)
+    input_sums = finish_col(input_pairs, grad_w_out, near, far)
+    all_grad = after([grad_hidden, near, far, grad_far], input_sums)
     grad_w_in = slot_grads(info_in, all_tokens, all_grad, slots, cols, True)
-    layer_out, grad_tokens = finish_row(layer_sums), finish_row(input_sums)
+    input_far = after(swap_row(input_sums[1], 3), grad_w_in)
+    layer_out = rows_first(add(layer_sums[0], after(layer_far, input_sums)))
+    grad_tokens = rows_first(add(input_sums[0], input_far))
     return layer_out, grad_tokens, grad_w_in, grad_w_out
 
 

time: 302 us -> 253 us (0.84)
  waiting for transfers between devices: 196 us -> 150 us
  Pallas kernels: 49 us -> 45.8 us
    ppermute x15, waiting for transfers between devices: 146 us -> 103 us  [swap_row(): return lax.ppermute(x, 'row', [(s, s ^ t) for s in range(4)])]
    ppermute x22, waiting for transfers between devices: 50.3 us -> 47.1 us  [swap_col(): return lax.ppermute(x, 'col', [(s, s ^ m) for s in range(count)])]
    pallas_call x6, Pallas kernels: 49 us -> 45.8 us  [call(): pl.pallas_call(kernel, out_shape=out_shape, in_specs=[pl.BlockSpec(memory...]
  transfers between devices with their start and end apart: 37 -> 37, of which waited for: 17 -> 20; matrix products, arithmetic and copies ran while one was open for 4% -> 3% of each run, Pallas kernels for 10% -> 15%
where the time goes in v9:
time: 253 us; the launch traced here: 252 us
  waiting for transfers between devices  150 us (59%)
  Pallas kernels  45.8 us (18%)
  starting transfers between devices  41.3 us (16%)
  local copies, waits for them, and re-layouts  7.27 us (3%)
  other arithmetic  6.37 us (3%)
    ppermute x15, waiting for transfers between devices, swap_row(): return lax.ppermute(x, 'row', [(s, s ^ t) for s in range(4)])  103 us
    ppermute x22, waiting for transfers between devices, swap_col(): return lax.ppermute(x, 'col', [(s, s ^ m) for s in range(count)])  47.1 us
    pallas_call x6, Pallas kernels, call(): pl.pallas_call(kernel, out_shape=out_shape, in_specs=[pl.BlockSpec(memory...  45.8 us
    ppermute x15, starting transfers between devices, swap_row(): return lax.ppermute(x, 'row', [(s, s ^ t) for s in range(4)])  25.8 us
    ppermute x22, starting transfers between devices, swap_col(): return lax.ppermute(x, 'col', [(s, s ^ m) for s in range(count)])  15.5 us
    unnamed x70, local copies, waits for them, and re-layouts  5.81 us
  transfers between devices with their start and end apart: 37, of which 20 were waited for; matrix products, arithmetic and copies ran while one was open for 3% of the time, Pallas kernels for 15%

profile of v9, /device:TPU:0, one launch (start us, length us, event | category | flops | bytes accessed | tf_op | source)
XLA Modules:
  0.0 252.1 jit_solution(11922941171695528171)
XLA Ops:
  3.1 3.1 %collective-permute-start = (bf16[2,2,128,256]{3,2,1,0:T(8,128)(2,1)S(1)}, bf16[2,2,128,256]{3,2,1,0:T(8,128)(2,1)S(1)}, u32[]{:S(2)}, u32[]{:S(2)}) collective-permute-start(bf16[2,2,128,256]{3,2,1,0:T(8,128)(2,1)S(1)} %pad_maximum_fusion.2), channel_id=1, source_target_pairs={{0,8},{8,0},{16,24},{24,16},{1,9},{9,1},{17,25},{25,17},{2,10},{10... | collective-permute-start | bytes 786440 | tf_op jit(solution)/shard_map/ppermute | solution.py:226
  6.2 2.6 %collective-permute-start.1 = (bf16[2,2,128,256]{3,2,1,0:T(8,128)(2,1)S(1)}, bf16[2,2,128,256]{3,2,1,0:T(8,128)(2,1)S(1)}, u32[]{:S(2)}, u32[]{:S(2)}) collective-permute-start(bf16[2,2,128,256]{3,2,1,0:T(8,128)(2,1)S(1)} %pad_maximum_fusion.2), channel_id=1, source_target_pairs={{0,16},{8,24},{16,0},{24,8},{1,17},{9,25},{17,1},{25,9},{2,18},{10... | collective-permute-start | bytes 786440 | tf_op jit(solution)/shard_map/ppermute | solution.py:226
  8.8 8.6 %collective-permute-done = bf16[2,2,128,256]{3,2,1,0:T(8,128)(2,1)S(1)} collective-permute-done((bf16[2,2,128,256]{3,2,1,0:T(8,128)(2,1)S(1)}, bf16[2,2,128,256]{3,2,1,0:T(8,128)(2,1)S(1)}, u32[]{:S(2)}, u32[]{:S(2)}) %collective-permute-start) | collective-permute-done | bytes 262176 | tf_op jit(solution)/shard_map/ppermute | solution.py:226
  17.4 10.2 %collective-permute-done.1 = bf16[2,2,128,256]{3,2,1,0:T(8,128)(2,1)S(1)} collective-permute-done((bf16[2,2,128,256]{3,2,1,0:T(8,128)(2,1)S(1)}, bf16[2,2,128,256]{3,2,1,0:T(8,128)(2,1)S(1)}, u32[]{:S(2)}, u32[]{:S(2)}) %collective-permute-start.1) | collective-permute-done | bytes 262176 | tf_op jit(solution)/shard_map/ppermute | solution.py:226
  27.6 4.8 %collective-permute-start.3 = (bf16[16,256,256]{2,1,0:T(8,128)(2,1)}, bf16[16,256,256]{2,1,0:T(8,128)(2,1)S(1)}, u32[]{:S(2)}, u32[]{:S(2)}) collective-permute-start(bf16[16,256,256]{2,1,0:T(8,128)(2,1)} %bitcast.61), channel_id=1, source_target_pairs={{0,8},{8,0},{16,24},{24,16},{1,9},{9,1},{17,25},{25,17},{2,10},{10... | collective-permute-start | bytes 6291464 | tf_op jit(solution)/shard_map/ppermute | solution.py:226
  36.7 11.4 %collective-permute-done.5.refs_4_.refs_2_ = bf16[4,2,128,256]{3,2,1,0:T(8,128)(2,1)S(1)} collective-permute-done((bf16[4,2,128,256]{3,2,1,0:T(8,128)(2,1)S(1)}, bf16[4,2,128,256]{3,2,1,0:T(8,128)(2,1)S(1)}, u32[]{:S(2)}, u32[]{:S(2)}) %collective-permute-start.5) | collective-permute-done | bytes 524320 | tf_op jit(solution)/shard_map/ppermute | solution.py:222
  48.1 9.8 %collective-permute-done.7.refs_6_.refs_4_ = bf16[4,2,128,256]{3,2,1,0:T(8,128)(2,1)S(1)} collective-permute-done((bf16[4,2,128,256]{3,2,1,0:T(8,128)(2,1)S(1)}, bf16[4,2,128,256]{3,2,1,0:T(8,128)(2,1)S(1)}, u32[]{:S(2)}, u32[]{:S(2)}) %collective-permute-start.7) | collective-permute-done | bytes 524320 | tf_op jit(solution)/shard_map/ppermute | solution.py:222
  60.6 16.5 %collective-permute-done.3.refs_1_ = bf16[16,256,256]{2,1,0:T(8,128)(2,1)S(1)} collective-permute-done((bf16[16,256,256]{2,1,0:T(8,128)(2,1)}, bf16[16,256,256]{2,1,0:T(8,128)(2,1)S(1)}, u32[]{:S(2)}, u32[]{:S(2)}) %collective-permute-start.3) | collective-permute-done | bytes 2097184 | tf_op jit(solution)/shard_map/ppermute | solution.py:226
  84.1 7.6 %shard_map.93 = (bf16[8,128,256]{2,1,0:T(8,128)(2,1)}, bf16[8,128,256]{2,1,0:T(8,128)(2,1)}) custom-call(s32[34]{0:T(128)} %pad_add_fusion.2.info, bf16[16,256,256]{2,1,0:T(8,128)(2,1)} %bitcast.62, bf16[16,256,256]{2,1,0:T(8,128)(2,1)} %copy-done.1, bf16[4,2,128,256]{3,2,1,0:T(8,128)(2,1)} %copy-done.2, bf16[4,2,128,256]{3,2,1,0:T(8,128)(2,1)} %copy-done.9, ...), custom_call_target="tpu_custom_call" | custom-call | flops 1073741824 | bytes 8388608 | tf_op jit(solution)/shard_map/pallas_call | solution.py:146
  95.5 9.0 %collective-permute-done.15.refs_6_.refs_4_ = bf16[4,2,128,256]{3,2,1,0:T(8,128)(2,1)S(1)} collective-permute-done((bf16[4,2,128,256]{3,2,1,0:T(8,128)(2,1)S(1)}, bf16[4,2,128,256]{3,2,1,0:T(8,128)(2,1)S(1)}, u32[]{:S(2)}, u32[]{:S(2)}) %collective-permute-start.15) | collective-permute-done | bytes 524320 | tf_op jit(solution)/shard_map/ppermute | solution.py:222
  105.1 30.8 %collective-permute-done.12 = bf16[8,128,256]{2,1,0:T(8,128)(2,1)S(1)} collective-permute-done((bf16[8,128,256]{2,1,0:T(8,128)(2,1)}, bf16[8,128,256]{2,1,0:T(8,128)(2,1)S(1)}, u32[]{:S(2)}, u32[]{:S(2)}) %collective-permute-start.12) | collective-permute-done | bytes 524320 | tf_op jit(solution)/shard_map/ppermute | solution.py:226
  140.5 8.0 %shard_map.94 = (bf16[8,128,256]{2,1,0:T(8,128)(2,1)}, bf16[8,128,256]{2,1,0:T(8,128)(2,1)}) custom-call(s32[34]{0:T(128)} %pad_add_fusion.info, bf16[16,256,256]{2,1,0:T(8,128)(2,1)} %bitcast.58, bf16[16,256,256]{2,1,0:T(8,128)(2,1)} %collective-permute-done.11.refs_1_, bf16[4,2,128,256]{3,2,1,0:T(8,128)(2,1)} %copy-done.3, ...), custom_call_target="tpu_custom_call" | custom-call | flops 1073741824 | bytes 8388608 | tf_op jit(solution)/shard_map/pallas_call | solution.py:146
  151.0 3.6 %collective-permute-done.13.refs_3_.refs_11_ = bf16[8,128,256]{2,1,0:T(8,128)(2,1)S(1)} collective-permute-done((bf16[8,128,256]{2,1,0:T(8,128)(2,1)S(1)}, bf16[8,128,256]{2,1,0:T(8,128)(2,1)S(1)}, u32[]{:S(2)}, u32[]{:S(2)}) %collective-permute-start.13) | collective-permute-done | bytes 524320 | tf_op jit(solution)/shard_map/ppermute | solution.py:226
  155.5 7.6 %shard_map.95 = (bf16[4,2,2,128,256]{4,3,2,1,0:T(8,128)(2,1)}, bf16[4,2,2,128,256]{4,3,2,1,0:T(8,128)(2,1)}) custom-call(s32[34]{0:T(128)} %pad_add_fusion.info, bf16[16,256,256]{2,1,0:T(8,128)(2,1)} %bitcast.59, bf16[16,256,256]{2,1,0:T(8,128)(2,1)} %collective-permute-done.11.refs_1_, bf16[8,128,256]{2,1,0:T(8,128)(2,1)} %copy-done.5, ...), custom_call_target="tpu_custom_call" | custom-call | flops 1073741824 | bytes 8388608 | tf_op jit(solution)/shard_map/pallas_call | solution.py:146
  163.1 2.7 %collective-permute-done.21 = bf16[8,128,256]{2,1,0:T(8,128)(2,1)S(1)} collective-permute-done((bf16[8,128,256]{2,1,0:T(8,128)(2,1)}, bf16[8,128,256]{2,1,0:T(8,128)(2,1)S(1)}, u32[]{:S(2)}, u32[]{:S(2)}) %collective-permute-start.21) | collective-permute-done | bytes 524320 | tf_op jit(solution)/shard_map/ppermute | solution.py:226
  165.8 10.9 %collective-permute-done.22.refs_9_ = bf16[8,128,256]{2,1,0:T(8,128)(2,1)S(1)} collective-permute-done((bf16[8,128,256]{2,1,0:T(8,128)(2,1)S(1)}, bf16[8,128,256]{2,1,0:T(8,128)(2,1)S(1)}, u32[]{:S(2)}, u32[]{:S(2)}) %collective-permute-start.22) | collective-permute-done | bytes 524320 | tf_op jit(solution)/shard_map/ppermute | solution.py:226
  184.0 5.7 %collective-permute-done.24 = bf16[2,2,128,256]{3,2,1,0:T(8,128)(2,1)S(1)} collective-permute-done((bf16[2,2,128,256]{3,2,1,0:T(8,128)(2,1)S(1)}, bf16[2,2,128,256]{3,2,1,0:T(8,128)(2,1)S(1)}, u32[]{:S(2)}, u32[]{:S(2)}) %collective-permute-start.24) | collective-permute-done | bytes 262176 | tf_op jit(solution)/shard_map/ppermute | solution.py:222
  189.6 6.0 %collective-permute-done.25 = bf16[2,2,128,256]{3,2,1,0:T(8,128)(2,1)S(1)} collective-permute-done((bf16[2,2,128,256]{3,2,1,0:T(8,128)(2,1)S(1)}, bf16[2,2,128,256]{3,2,1,0:T(8,128)(2,1)S(1)}, u32[]{:S(2)}, u32[]{:S(2)}) %collective-permute-start.25) | collective-permute-done | bytes 262176 | tf_op jit(solution)/shard_map/ppermute | solution.py:222
  195.8 8.1 %collective-permute-done.29.refs_10_ = bf16[8,128,256]{2,1,0:T(8,128)(2,1)S(1)} collective-permute-done((bf16[8,128,256]{2,1,0:T(8,128)(2,1)S(1)}, bf16[8,128,256]{2,1,0:T(8,128)(2,1)S(1)}, u32[]{:S(2)}, u32[]{:S(2)}) %collective-permute-start.29) | collective-permute-done | bytes 524320 | tf_op jit(solution)/shard_map/ppermute | solution.py:226
  204.0 8.0 %shard_map.96 = (bf16[4,2,2,128,256]{4,3,2,1,0:T(8,128)(2,1)}, bf16[4,2,2,128,256]{4,3,2,1,0:T(8,128)(2,1)}) custom-call(s32[34]{0:T(128)} %pad_add_fusion.2.info, bf16[16,256,256]{2,1,0:T(8,128)(2,1)} %bitcast.63, bf16[16,256,256]{2,1,0:T(8,128)(2,1)} %copy-done.1, bf16[8,128,256]{2,1,0:T(8,128)(2,1)} %copy-done.4, bf16[8,128,256]{2,1,0:T(8,128)(2,1)} %copy-done.21), custom_call_target="tpu_custom_call" | custom-call | flops 1073741824 | bytes 8388608 | tf_op jit(solution)/shard_map/pallas_call | solution.py:146
  220.1 7.3 %shard_map.97 = bf16[16,256,256]{2,1,0:T(8,128)(2,1)} custom-call(s32[34]{0:T(128)} %pad_add_fusion.info, bf16[4,2,128,256]{3,2,1,0:T(8,128)(2,1)} %copy-done.3, bf16[4,2,128,256]{3,2,1,0:T(8,128)(2,1)} %copy-done.16, bf16[4,2,128,256]{3,2,1,0:T(8,128)(2,1)} %copy-done.13, bf16[4,2,128,256]{3,2,1,0:T(8,128)(2,1)} %copy-done.17, ...), custom_call_target="tpu_custom_call" | custom-call | flops 1073741824 | bytes 8388608 | tf_op jit(solution)/shard_map/pallas_call | solution.py:146
  229.7 8.1 %collective-permute-done.35.refs_10_ = bf16[8,128,256]{2,1,0:T(8,128)(2,1)S(1)} collective-permute-done((bf16[8,128,256]{2,1,0:T(8,128)(2,1)}, bf16[8,128,256]{2,1,0:T(8,128)(2,1)S(1)}, u32[]{:S(2)}, u32[]{:S(2)}) %collective-permute-start.35) | collective-permute-done | bytes 524320 | tf_op jit(solution)/shard_map/ppermute | solution.py:226
  238.0 3.5 %collective-permute-done.27 = bf16[2,128,256]{2,1,0:T(8,128)(2,1)S(1)} collective-permute-done((bf16[2,128,256]{2,1,0:T(8,128)(2,1)S(1)}, bf16[2,128,256]{2,1,0:T(8,128)(2,1)S(1)}, u32[]{:S(2)}, u32[]{:S(2)}) %collective-permute-start.27) | collective-permute-done | bytes 131104 | tf_op jit(solution)/shard_map/ppermute | solution.py:226
  243.8 7.3 %shard_map.98 = bf16[16,256,256]{2,1,0:T(8,128)(2,1)} custom-call(s32[34]{0:T(128)} %pad_add_fusion.2.info, bf16[4,2,128,256]{3,2,1,0:T(8,128)(2,1)} %copy-done.2, bf16[4,2,128,256]{3,2,1,0:T(8,128)(2,1)} %copy-done.9, bf16[4,2,128,256]{3,2,1,0:T(8,128)(2,1)} %copy-done.6, bf16[4,2,128,256]{3,2,1,0:T(8,128)(2,1)} %copy-done.10, ...), custom_call_target="tpu_custom_call" | custom-call | flops 1073741824 | bytes 8388608 | tf_op jit(solution)/shard_map/pallas_call | solution.py:146
  (151 shorter events, 49.8 us)
Async XLA Ops:
  6.2 21.4 %collective-permute-start.1 = (bf16[2,2,128,256]{3,2,1,0:T(8,128)(2,1)S(1)}, bf16[2,2,128,256]{3,2,1,0:T(8,128)(2,1)S(1)}, u32[]{:S(2)}, u32[]{:S(2)}) collective-permute-start(bf16[2,2,128,256]{3,2,1,0:T(8,128)(2,1)S(1)} %pad_maximum_fusion.2), channel_id=1, source_target_pairs={{0,16},{8,24},{16,0},{24,8},{1,17},{9,25},{17,1},{25,9},{2,18},{10... | collective-permute-start | bytes 786440 | tf_op jit(solution)/shard_map/ppermute | solution.py:226
  8.8 18.8 %collective-permute-start.2 = (bf16[2,2,128,256]{3,2,1,0:T(8,128)(2,1)S(1)}, bf16[2,2,128,256]{3,2,1,0:T(8,128)(2,1)S(1)}, u32[]{:S(2)}, u32[]{:S(2)}) collective-permute-start(bf16[2,2,128,256]{3,2,1,0:T(8,128)(2,1)S(1)} %pad_maximum_fusion.2), channel_id=1, source_target_pairs={{0,24},{8,16},{16,8},{24,0},{1,25},{9,17},{17,9},{25,1},{2,26},{10... | collective-permute-start | bytes 786440 | tf_op jit(solution)/shard_map/ppermute | solution.py:226
  27.6 49.4 %collective-permute-start.3 = (bf16[16,256,256]{2,1,0:T(8,128)(2,1)}, bf16[16,256,256]{2,1,0:T(8,128)(2,1)S(1)}, u32[]{:S(2)}, u32[]{:S(2)}) collective-permute-start(bf16[16,256,256]{2,1,0:T(8,128)(2,1)} %bitcast.61), channel_id=1, source_target_pairs={{0,8},{8,0},{16,24},{24,16},{1,9},{9,1},{17,25},{25,17},{2,10},{10... | collective-permute-start | bytes 6291464 | tf_op jit(solution)/shard_map/ppermute | solution.py:226
  34.7 23.2 %collective-permute-start.7 = (bf16[4,2,128,256]{3,2,1,0:T(8,128)(2,1)S(1)}, bf16[4,2,128,256]{3,2,1,0:T(8,128)(2,1)S(1)}, u32[]{:S(2)}, u32[]{:S(2)}) collective-permute-start(bf16[4,2,128,256]{3,2,1,0:T(8,128)(2,1)S(1)} %pad_maximum_fusion.refs_2_.refs_0_), channel_id=1, source_target_pairs={{0,4},{1,5},{2,6},{3,7},{4,0},{5,1},{6,2},{7,3},{8,12},{9,13},{10,... | collective-permute-start | bytes 1572872 | tf_op jit(solution)/shard_map/ppermute | solution.py:222
  36.2 21.7 %collective-permute-start.9 = (bf16[4,2,128,256]{3,2,1,0:T(8,128)(2,1)S(1)}, bf16[4,2,128,256]{3,2,1,0:T(8,128)(2,1)S(1)}, u32[]{:S(2)}, u32[]{:S(2)}) collective-permute-start(bf16[4,2,128,256]{3,2,1,0:T(8,128)(2,1)S(1)} %pad_maximum_fusion.refs_2_.refs_0_), channel_id=1, source_target_pairs={{0,6},{1,7},{2,4},{3,5},{4,2},{5,3},{6,0},{7,1},{8,14},{9,15},{10,... | collective-permute-start | bytes 1572872 | tf_op jit(solution)/shard_map/ppermute | solution.py:222
  36.7 21.7 %collective-permute-start.4 = (bf16[4,2,128,256]{3,2,1,0:T(8,128)(2,1)S(1)}, bf16[4,2,128,256]{3,2,1,0:T(8,128)(2,1)S(1)}, u32[]{:S(2)}, u32[]{:S(2)}) collective-permute-start(bf16[4,2,128,256]{3,2,1,0:T(8,128)(2,1)S(1)} %pad_maximum_fusion.refs_2_.refs_0_), channel_id=1, source_target_pairs={{0,1},{1,0},{2,3},{3,2},{4,5},{5,4},{6,7},{7,6},{8,9},{9,8},{10,11... | collective-permute-start | bytes 1572872 | tf_op jit(solution)/shard_map/ppermute | solution.py:222
  77.1 62.3 %collective-permute-start.11 = (bf16[16,256,256]{2,1,0:T(8,128)(2,1)S(1)}, bf16[16,256,256]{2,1,0:T(8,128)(2,1)}, u32[]{:S(2)}, u32[]{:S(2)}) collective-permute-start(bf16[16,256,256]{2,1,0:T(8,128)(2,1)S(1)} %bitcast.60), channel_id=1, source_target_pairs={{0,8},{8,0},{16,24},{24,16},{1,9},{9,1},{17,25},{25,17},{2,10},{10... | collective-permute-start | bytes 6291464 | tf_op jit(solution)/shard_map/ppermute | solution.py:226
  80.5 14.9 %collective-permute-start.14 = (bf16[4,2,128,256]{3,2,1,0:T(8,128)(2,1)S(1)}, bf16[4,2,128,256]{3,2,1,0:T(8,128)(2,1)S(1)}, u32[]{:S(2)}, u32[]{:S(2)}) collective-permute-start(bf16[4,2,128,256]{3,2,1,0:T(8,128)(2,1)S(1)} %pad_maximum_fusion.1.refs_2_.refs_0_), channel_id=1, source_target_pairs={{0,2},{1,3},{2,0},{3,1},{4,6},{5,7},{6,4},{7,5},{8,10},{9,11},{10,... | collective-permute-start | bytes 1572872 | tf_op jit(solution)/shard_map/ppermute | solution.py:222
  82.1 22.3 %collective-permute-start.15 = (bf16[4,2,128,256]{3,2,1,0:T(8,128)(2,1)S(1)}, bf16[4,2,128,256]{3,2,1,0:T(8,128)(2,1)S(1)}, u32[]{:S(2)}, u32[]{:S(2)}) collective-permute-start(bf16[4,2,128,256]{3,2,1,0:T(8,128)(2,1)S(1)} %pad_maximum_fusion.1.refs_2_.refs_0_), channel_id=1, source_target_pairs={{0,4},{1,5},{2,6},{3,7},{4,0},{5,1},{6,2},{7,3},{8,12},{9,13},{10,... | collective-permute-start | bytes 1572872 | tf_op jit(solution)/shard_map/ppermute | solution.py:222
  83.6 20.8 %collective-permute-start.16 = (bf16[4,2,128,256]{3,2,1,0:T(8,128)(2,1)S(1)}, bf16[4,2,128,256]{3,2,1,0:T(8,128)(2,1)S(1)}, u32[]{:S(2)}, u32[]{:S(2)}) collective-permute-start(bf16[4,2,128,256]{3,2,1,0:T(8,128)(2,1)S(1)} %pad_maximum_fusion.1.refs_2_.refs_0_), channel_id=1, source_target_pairs={{0,6},{1,7},{2,4},{3,5},{4,2},{5,3},{6,0},{7,1},{8,14},{9,15},{10,... | collective-permute-start | bytes 1572872 | tf_op jit(solution)/shard_map/ppermute | solution.py:222
  91.8 44.1 %collective-permute-start.12 = (bf16[8,128,256]{2,1,0:T(8,128)(2,1)}, bf16[8,128,256]{2,1,0:T(8,128)(2,1)S(1)}, u32[]{:S(2)}, u32[]{:S(2)}) collective-permute-start(bf16[8,128,256]{2,1,0:T(8,128)(2,1)} %get-tuple-element.57), channel_id=1, source_target_pairs={{0,24},{8,16},{16,8},{24,0},{1,25},{9,17},{17,9},{25,1},{2,26},{10... | collective-permute-start | bytes 1572872 | tf_op jit(solution)/shard_map/ppermute | solution.py:226
  104.4 33.4 %collective-permute-start.17 = (bf16[4,2,128,256]{3,2,1,0:T(8,128)(2,1)S(1)}, bf16[4,2,128,256]{3,2,1,0:T(8,128)(2,1)S(1)}, u32[]{:S(2)}, u32[]{:S(2)}) collective-permute-start(bf16[4,2,128,256]{3,2,1,0:T(8,128)(2,1)S(1)} %pad_maximum_fusion.1.refs_2_.refs_0_), channel_id=1, source_target_pairs={{0,1},{1,0},{2,3},{3,2},{4,5},{5,4},{6,7},{7,6},{8,9},{9,8},{10,11... | collective-permute-start | bytes 1572872 | tf_op jit(solution)/shard_map/ppermute | solution.py:222
  104.5 34.8 %collective-permute-start.18 = (bf16[4,2,128,256]{3,2,1,0:T(8,128)(2,1)S(1)}, bf16[4,2,128,256]{3,2,1,0:T(8,128)(2,1)S(1)}, u32[]{:S(2)}, u32[]{:S(2)}) collective-permute-start(bf16[4,2,128,256]{3,2,1,0:T(8,128)(2,1)S(1)} %collective-permute-done.14.refs_4_.refs_2_), channel_id=1, source_target_pairs={{0,1},{1,0},{2,3},{3,2},{4,5},{5,4},{6,7},{7,6},{8,9},{9,8},{10,11... | collective-permute-start | bytes 1572872 | tf_op jit(solution)/shard_map/ppermute | solution.py:222
  105.0 34.3 %collective-permute-start.19 = (bf16[4,2,128,256]{3,2,1,0:T(8,128)(2,1)S(1)}, bf16[4,2,128,256]{3,2,1,0:T(8,128)(2,1)S(1)}, u32[]{:S(2)}, u32[]{:S(2)}) collective-permute-start(bf16[4,2,128,256]{3,2,1,0:T(8,128)(2,1)S(1)} %collective-permute-done.15.refs_6_.refs_4_), channel_id=1, source_target_pairs={{0,1},{1,0},{2,3},{3,2},{4,5},{5,4},{6,7},{7,6},{8,9},{9,8},{10,11... | collective-permute-start | bytes 1572872 | tf_op jit(solution)/shard_map/ppermute | solution.py:222
  137.9 16.8 %collective-permute-start.13 = (bf16[8,128,256]{2,1,0:T(8,128)(2,1)S(1)}, bf16[8,128,256]{2,1,0:T(8,128)(2,1)S(1)}, u32[]{:S(2)}, u32[]{:S(2)}) collective-permute-start(bf16[8,128,256]{2,1,0:T(8,128)(2,1)S(1)} %multiply_convert_fusion.1.refs_2_.refs_8_), channel_id=1, source_target_pairs={{0,24},{8,16},{16,8},{24,0},{1,25},{9,17},{17,9},{25,1},{2,26},{10... | collective-permute-start | bytes 1572872 | tf_op jit(solution)/shard_map/ppermute | solution.py:226
  148.5 17.3 %collective-permute-start.21 = (bf16[8,128,256]{2,1,0:T(8,128)(2,1)}, bf16[8,128,256]{2,1,0:T(8,128)(2,1)S(1)}, u32[]{:S(2)}, u32[]{:S(2)}) collective-permute-start(bf16[8,128,256]{2,1,0:T(8,128)(2,1)} %get-tuple-element.76), channel_id=1, source_target_pairs={{0,24},{8,16},{16,8},{24,0},{1,25},{9,17},{17,9},{25,1},{2,26},{10... | collective-permute-start | bytes 1572872 | tf_op jit(solution)/shard_map/ppermute | solution.py:226
  151.0 25.6 %collective-permute-start.22 = (bf16[8,128,256]{2,1,0:T(8,128)(2,1)S(1)}, bf16[8,128,256]{2,1,0:T(8,128)(2,1)S(1)}, u32[]{:S(2)}, u32[]{:S(2)}) collective-permute-start(bf16[8,128,256]{2,1,0:T(8,128)(2,1)S(1)} %multiply_convert_fusion.1.refs_2_.refs_8_), channel_id=1, source_target_pairs={{0,8},{8,0},{16,24},{24,16},{1,9},{9,1},{17,25},{25,17},{2,10},{10... | collective-permute-start | bytes 1572872 | tf_op jit(solution)/shard_map/ppermute | solution.py:226
  177.3 18.5 %collective-permute-start.28 = (bf16[8,128,256]{2,1,0:T(8,128)(2,1)S(1)}, bf16[8,128,256]{2,1,0:T(8,128)(2,1)S(1)}, u32[]{:S(2)}, u32[]{:S(2)}) collective-permute-start(bf16[8,128,256]{2,1,0:T(8,128)(2,1)S(1)} %multiply_convert_fusion.refs_2_.refs_8_), channel_id=1, source_target_pairs={{0,24},{8,16},{16,8},{24,0},{1,25},{9,17},{17,9},{25,1},{2,26},{10... | collective-permute-start | bytes 1572872 | tf_op jit(solution)/shard_map/ppermute | solution.py:226
  178.7 25.2 %collective-permute-start.29 = (bf16[8,128,256]{2,1,0:T(8,128)(2,1)S(1)}, bf16[8,128,256]{2,1,0:T(8,128)(2,1)S(1)}, u32[]{:S(2)}, u32[]{:S(2)}) collective-permute-start(bf16[8,128,256]{2,1,0:T(8,128)(2,1)S(1)} %copy-done.23), channel_id=1, source_target_pairs={{0,8},{8,0},{16,24},{24,16},{1,9},{9,1},{17,25},{25,17},{2,10},{10... | collective-permute-start | bytes 1572872 | tf_op jit(solution)/shard_map/ppermute | solution.py:226
  212.1 15.4 %collective-permute-start.34 = (bf16[8,128,256]{2,1,0:T(8,128)(2,1)}, bf16[8,128,256]{2,1,0:T(8,128)(2,1)S(1)}, u32[]{:S(2)}, u32[]{:S(2)}) collective-permute-start(bf16[8,128,256]{2,1,0:T(8,128)(2,1)} %copy-done.4), channel_id=1, source_target_pairs={{0,8},{8,0},{16,24},{24,16},{1,9},{9,1},{17,25},{25,17},{2,10},{10... | collective-permute-start | bytes 1572872 | tf_op jit(solution)/shard_map/ppermute | solution.py:226
  212.5 25.4 %collective-permute-start.35 = (bf16[8,128,256]{2,1,0:T(8,128)(2,1)}, bf16[8,128,256]{2,1,0:T(8,128)(2,1)S(1)}, u32[]{:S(2)}, u32[]{:S(2)}) collective-permute-start(bf16[8,128,256]{2,1,0:T(8,128)(2,1)} %copy-done.21), channel_id=1, source_target_pairs={{0,8},{8,0},{16,24},{24,16},{1,9},{9,1},{17,25},{25,17},{2,10},{10... | collective-permute-start | bytes 1572872 | tf_op jit(solution)/shard_map/ppermute | solution.py:226
  216.6 21.3 %collective-permute-start.31 = (bf16[2,2,128,256]{3,2,1,0:T(8,128)(2,1)S(1)}, bf16[2,2,128,256]{3,2,1,0:T(8,128)(2,1)S(1)}, u32[]{:S(2)}, u32[]{:S(2)}) collective-permute-start(bf16[2,2,128,256]{3,2,1,0:T(8,128)(2,1)S(1)} %get-tuple-element.110), channel_id=1, source_target_pairs={{0,2},{1,3},{2,0},{3,1},{4,6},{5,7},{6,4},{7,5},{8,10},{9,11},{10,... | collective-permute-start | bytes 786440 | tf_op jit(solution)/shard_map/ppermute | solution.py:222
  218.1 19.7 %collective-permute-start.32 = (bf16[2,2,128,256]{3,2,1,0:T(8,128)(2,1)S(1)}, bf16[2,2,128,256]{3,2,1,0:T(8,128)(2,1)S(1)}, u32[]{:S(2)}, u32[]{:S(2)}) collective-permute-start(bf16[2,2,128,256]{3,2,1,0:T(8,128)(2,1)S(1)} %get-tuple-element.109), channel_id=1, source_target_pairs={{0,4},{1,5},{2,6},{3,7},{4,0},{5,1},{6,2},{7,3},{8,12},{9,13},{10,... | collective-permute-start | bytes 786440 | tf_op jit(solution)/shard_map/ppermute | solution.py:222
  219.6 18.2 %collective-permute-start.33 = (bf16[2,2,128,256]{3,2,1,0:T(8,128)(2,1)S(1)}, bf16[2,2,128,256]{3,2,1,0:T(8,128)(2,1)S(1)}, u32[]{:S(2)}, u32[]{:S(2)}) collective-permute-start(bf16[2,2,128,256]{3,2,1,0:T(8,128)(2,1)S(1)} %get-tuple-element.108), channel_id=1, source_target_pairs={{0,6},{1,7},{2,4},{3,5},{4,2},{5,3},{6,0},{7,1},{8,14},{9,15},{10,... | collective-permute-start | bytes 786440 | tf_op jit(solution)/shard_map/ppermute | solution.py:222
  (46 other events, 876.1 us)

commit v10 on v9

--- a/solution.py
+++ b/solution.py
@@ -300,33 +300,35 @@
 def on_line(info_in, info_out, tokens, upstream, w_in, w_out, cols, devices):
     slots = w_in.shape[0]
     ends = (0, 3)
-    both = line_gather(jnp.stack([tokens, upstream]))
-    in_pair = [w_in, swap_row(after(w_in, both), 1)]
+    mine = jnp.stack([tokens, upstream])
+    both = line_gather(mine)
+    in_pair = [w_in, swap_row(after(w_in, mine), 1)]
     token_even = across(jnp.stack([block[0] for block in both]))
     up_even = across(after(jnp.stack([block[1] for block in both]), token_even[1:]))
     all_tokens = with_odd(token_even)
-    out_pair = [w_out, swap_row(after(w_out, in_pair[1], all_tokens), 1)]
+    out_pair = [w_out, swap_row(after(w_out, all_tokens), 1)]
     own, far = to_hidden(info_in, all_tokens, in_pair, cols, False, ends)
     hidden = add(own, swap_row(far, 3))
     activ = silu(hidden)
     activ_far = swap_row(activ, 3)
     all_up = with_odd(after(up_even, own))
     own, far = to_hidden(info_out, after(all_up, activ), out_pair, cols, True, ends)
-    far, activ_near = swap_row(far, 3), swap_row(after(activ, own), 1)
+    far = swap_row(far, 3)
     ends_activ = after([activ, activ_far], own)
     layer_parts = from_hidden(info_out, ends_activ, out_pair, cols, False, ends, devices)
-    grad_hidden = activations(hidden, add(own, after(far, layer_parts, activ_near)))
+    grad_hidden = activations(hidden, add(own, after(far, layer_parts)))
     grad_far = swap_row(grad_hidden, 3)
-    all_activ = [activ, activ_near, swap_row(after(activ_far, grad_hidden), 1), activ_far]
+    activ, activ_far = after((activ, activ_far), grad_hidden)
+    all_activ = [activ, swap_row(activ, 1), swap_row(activ_far, 1), activ_far]
     layer_sums = finish_col(pair_sums(*after(layer_parts, grad_hidden)))
-    ends_grad = after([grad_hidden, grad_far], all_activ[2], layer_sums)
+    ends_grad = after([grad_hidden, grad_far], layer_sums)
     input_parts = from_hidden(info_in, ends_grad, in_pair, cols, True, ends, devices)
     layer_far = swap_row(layer_sums[1], 3)
     input_pairs = pair_sums(*input_parts)
     all_activ = after(all_activ, input_pairs)
     grad_w_out = slot_grads(info_out, all_up, all_activ, slots, cols, False)
     near, far = swap_row(grad_hidden, 1), swap_row(grad_far, 1)
-    input_sums = finish_col(input_pairs, grad_w_out, near, far)
+    input_sums = finish_col(input_pairs, grad_w_out)
     all_grad = after([grad_hidden, near, far, grad_far], input_sums)
     grad_w_in = slot_grads(info_in, all_tokens, all_grad, slots, cols, True)
     input_far = after(swap_row(input_sums[1], 3), grad_w_in)

time: 253 us -> 255 us (level)
  starting transfers between devices: 41.3 us -> 55.5 us
  waiting for transfers between devices: 150 us -> 137 us
    ppermute x15, starting transfers between devices: 25.8 us -> 40.1 us  [swap_row(): return lax.ppermute(x, 'row', [(s, s ^ t) for s in range(4)])]
    ppermute x15, waiting for transfers between devices: 103 us -> 95.4 us  [swap_row(): return lax.ppermute(x, 'row', [(s, s ^ t) for s in range(4)])]
    ppermute x22, waiting for transfers between devices: 47.1 us -> 42 us  [swap_col(): return lax.ppermute(x, 'col', [(s, s ^ m) for s in range(count)])]
    unnamed x70 -> x74, local copies, waits for them, and re-layouts: 5.81 us -> 6.63 us
  transfers between devices with their start and end apart: 37 -> 37, of which waited for: 20 -> 18; matrix products, arithmetic and copies ran while one was open for 3% -> 3% of each run, Pallas kernels for 15% -> 15%
where the time goes in v10:
time: 255 us; the launch traced here: 254 us
  waiting for transfers between devices  137 us (54%)
  starting transfers between devices  55.5 us (22%)
  Pallas kernels  45.7 us (18%)
  local copies, waits for them, and re-layouts  8.06 us (3%)
  other arithmetic  6.48 us (3%)
    ppermute x15, waiting for transfers between devices, swap_row(): return lax.ppermute(x, 'row', [(s, s ^ t) for s in range(4)])  95.4 us
    pallas_call x6, Pallas kernels, call(): pl.pallas_call(kernel, out_shape=out_shape, in_specs=[pl.BlockSpec(memory...  45.7 us
    ppermute x22, waiting for transfers between devices, swap_col(): return lax.ppermute(x, 'col', [(s, s ^ m) for s in range(count)])  42 us
    ppermute x15, starting transfers between devices, swap_row(): return lax.ppermute(x, 'row', [(s, s ^ t) for s in range(4)])  40.1 us
    ppermute x22, starting transfers between devices, swap_col(): return lax.ppermute(x, 'col', [(s, s ^ m) for s in range(count)])  15.4 us
    unnamed x74, local copies, waits for them, and re-layouts  6.63 us
  transfers between devices with their start and end apart: 37, of which 18 were waited for; matrix products, arithmetic and copies ran while one was open for 3% of the time, Pallas kernels for 15%

profile of v10, /device:TPU:0, one launch (start us, length us, event | category | flops | bytes accessed | tf_op | source)
XLA Modules:
  0.0 254.4 jit_solution(9760670543544586839)
XLA Ops:
  3.1 3.1 %collective-permute-start = (bf16[2,2,128,256]{3,2,1,0:T(8,128)(2,1)S(1)}, bf16[2,2,128,256]{3,2,1,0:T(8,128)(2,1)S(1)}, u32[]{:S(2)}, u32[]{:S(2)}) collective-permute-start(bf16[2,2,128,256]{3,2,1,0:T(8,128)(2,1)S(1)} %pad_maximum_fusion.2), channel_id=1, source_target_pairs={{0,8},{8,0},{16,24},{24,16},{1,9},{9,1},{17,25},{25,17},{2,10},{10... | collective-permute-start | bytes 786440 | tf_op jit(solution)/shard_map/ppermute | solution.py:226
  6.2 2.6 %collective-permute-start.1 = (bf16[2,2,128,256]{3,2,1,0:T(8,128)(2,1)S(1)}, bf16[2,2,128,256]{3,2,1,0:T(8,128)(2,1)S(1)}, u32[]{:S(2)}, u32[]{:S(2)}) collective-permute-start(bf16[2,2,128,256]{3,2,1,0:T(8,128)(2,1)S(1)} %pad_maximum_fusion.2), channel_id=1, source_target_pairs={{0,16},{8,24},{16,0},{24,8},{1,17},{9,25},{17,1},{25,9},{2,18},{10... | collective-permute-start | bytes 786440 | tf_op jit(solution)/shard_map/ppermute | solution.py:226
  9.7 8.5 %collective-permute-done = bf16[2,2,128,256]{3,2,1,0:T(8,128)(2,1)S(1)} collective-permute-done((bf16[2,2,128,256]{3,2,1,0:T(8,128)(2,1)S(1)}, bf16[2,2,128,256]{3,2,1,0:T(8,128)(2,1)S(1)}, u32[]{:S(2)}, u32[]{:S(2)}) %collective-permute-start) | collective-permute-done | bytes 262176 | tf_op jit(solution)/shard_map/ppermute | solution.py:226
  18.2 9.4 %collective-permute-done.1 = bf16[2,2,128,256]{3,2,1,0:T(8,128)(2,1)S(1)} collective-permute-done((bf16[2,2,128,256]{3,2,1,0:T(8,128)(2,1)S(1)}, bf16[2,2,128,256]{3,2,1,0:T(8,128)(2,1)S(1)}, u32[]{:S(2)}, u32[]{:S(2)}) %collective-permute-start.1) | collective-permute-done | bytes 262176 | tf_op jit(solution)/shard_map/ppermute | solution.py:226
  32.0 11.4 %collective-permute-done.4.refs_4_.refs_2_ = bf16[4,2,128,256]{3,2,1,0:T(8,128)(2,1)S(1)} collective-permute-done((bf16[4,2,128,256]{3,2,1,0:T(8,128)(2,1)S(1)}, bf16[4,2,128,256]{3,2,1,0:T(8,128)(2,1)S(1)}, u32[]{:S(2)}, u32[]{:S(2)}) %collective-permute-start.4) | collective-permute-done | bytes 524320 | tf_op jit(solution)/shard_map/ppermute | solution.py:222
  43.4 8.7 %collective-permute-done.6.refs_6_.refs_4_ = bf16[4,2,128,256]{3,2,1,0:T(8,128)(2,1)S(1)} collective-permute-done((bf16[4,2,128,256]{3,2,1,0:T(8,128)(2,1)S(1)}, bf16[4,2,128,256]{3,2,1,0:T(8,128)(2,1)S(1)}, u32[]{:S(2)}, u32[]{:S(2)}) %collective-permute-start.6) | collective-permute-done | bytes 524320 | tf_op jit(solution)/shard_map/ppermute | solution.py:222
  54.8 6.2 %collective-permute-start.10 = (bf16[16,256,256]{2,1,0:T(8,128)(2,1)S(1)}, bf16[16,256,256]{2,1,0:T(8,128)(2,1)}, u32[]{:S(2)}, u32[]{:S(2)}) collective-permute-start(bf16[16,256,256]{2,1,0:T(8,128)(2,1)S(1)} %bitcast.60), channel_id=1, source_target_pairs={{0,8},{8,0},{16,24},{24,16},{1,9},{9,1},{17,25},{25,17},{2,10},{10... | collective-permute-start | bytes 6291464 | tf_op jit(solution)/shard_map/ppermute | solution.py:226
  66.3 3.4 %collective-permute-done.11.refs_1_ = bf16[16,256,256]{2,1,0:T(8,128)(2,1)} collective-permute-done((bf16[16,256,256]{2,1,0:T(8,128)(2,1)}, bf16[16,256,256]{2,1,0:T(8,128)(2,1)}, u32[]{:S(2)}, u32[]{:S(2)}) %collective-permute-start.11) | collective-permute-done | bytes 2097184 | tf_op jit(solution)/shard_map/ppermute | solution.py:226
  69.7 7.6 %shard_map.93 = (bf16[8,128,256]{2,1,0:T(8,128)(2,1)}, bf16[8,128,256]{2,1,0:T(8,128)(2,1)}) custom-call(s32[34]{0:T(128)} %pad_add_fusion.2.info, bf16[16,256,256]{2,1,0:T(8,128)(2,1)} %bitcast.62, bf16[16,256,256]{2,1,0:T(8,128)(2,1)} %collective-permute-done.11.refs_1_, bf16[4,2,128,256]{3,2,1,0:T(8,128)(2,1)} %copy-done.1, ...), custom_call_target="tpu_custom_call" | custom-call | flops 1073741824 | bytes 8388608 | tf_op jit(solution)/shard_map/pallas_call | solution.py:146
  77.3 4.2 %collective-permute-start.12 = (bf16[8,128,256]{2,1,0:T(8,128)(2,1)}, bf16[8,128,256]{2,1,0:T(8,128)(2,1)S(1)}, u32[]{:S(2)}, u32[]{:S(2)}) collective-permute-start(bf16[8,128,256]{2,1,0:T(8,128)(2,1)} %get-tuple-element.57), channel_id=1, source_target_pairs={{0,24},{8,16},{16,8},{24,0},{1,25},{9,17},{17,9},{25,1},{2,26},{10... | collective-permute-start | bytes 1572872 | tf_op jit(solution)/shard_map/ppermute | solution.py:226
  81.5 5.6 %collective-permute-done.15.refs_6_.refs_4_ = bf16[4,2,128,256]{3,2,1,0:T(8,128)(2,1)S(1)} collective-permute-done((bf16[4,2,128,256]{3,2,1,0:T(8,128)(2,1)S(1)}, bf16[4,2,128,256]{3,2,1,0:T(8,128)(2,1)S(1)}, u32[]{:S(2)}, u32[]{:S(2)}) %collective-permute-start.15) | collective-permute-done | bytes 524320 | tf_op jit(solution)/shard_map/ppermute | solution.py:222
  89.3 38.0 %collective-permute-done.12 = bf16[8,128,256]{2,1,0:T(8,128)(2,1)S(1)} collective-permute-done((bf16[8,128,256]{2,1,0:T(8,128)(2,1)}, bf16[8,128,256]{2,1,0:T(8,128)(2,1)S(1)}, u32[]{:S(2)}, u32[]{:S(2)}) %collective-permute-start.12) | collective-permute-done | bytes 524320 | tf_op jit(solution)/shard_map/ppermute | solution.py:226
  131.9 8.0 %shard_map.94 = (bf16[8,128,256]{2,1,0:T(8,128)(2,1)}, bf16[8,128,256]{2,1,0:T(8,128)(2,1)}) custom-call(s32[34]{0:T(128)} %pad_add_fusion.info, bf16[16,256,256]{2,1,0:T(8,128)(2,1)} %bitcast.58, bf16[16,256,256]{2,1,0:T(8,128)(2,1)} %collective-permute-done.10.refs_1_, bf16[4,2,128,256]{3,2,1,0:T(8,128)(2,1)} %copy-done.2, ...), custom_call_target="tpu_custom_call" | custom-call | flops 1073741824 | bytes 8388608 | tf_op jit(solution)/shard_map/pallas_call | solution.py:146
  142.4 3.6 %collective-permute-done.13.refs_3_.refs_11_ = bf16[8,128,256]{2,1,0:T(8,128)(2,1)S(1)} collective-permute-done((bf16[8,128,256]{2,1,0:T(8,128)(2,1)S(1)}, bf16[8,128,256]{2,1,0:T(8,128)(2,1)S(1)}, u32[]{:S(2)}, u32[]{:S(2)}) %collective-permute-start.13) | collective-permute-done | bytes 524320 | tf_op jit(solution)/shard_map/ppermute | solution.py:226
  146.7 7.6 %shard_map.95 = (bf16[4,2,2,128,256]{4,3,2,1,0:T(8,128)(2,1)}, bf16[4,2,2,128,256]{4,3,2,1,0:T(8,128)(2,1)}) custom-call(s32[34]{0:T(128)} %pad_add_fusion.info, bf16[16,256,256]{2,1,0:T(8,128)(2,1)} %bitcast.59, bf16[16,256,256]{2,1,0:T(8,128)(2,1)} %collective-permute-done.10.refs_1_, bf16[8,128,256]{2,1,0:T(8,128)(2,1)} %copy-done.5, ...), custom_call_target="tpu_custom_call" | custom-call | flops 1073741824 | bytes 8388608 | tf_op jit(solution)/shard_map/pallas_call | solution.py:146
  164.1 5.7 %collective-permute-done.23 = bf16[2,2,128,256]{3,2,1,0:T(8,128)(2,1)S(1)} collective-permute-done((bf16[2,2,128,256]{3,2,1,0:T(8,128)(2,1)S(1)}, bf16[2,2,128,256]{3,2,1,0:T(8,128)(2,1)S(1)}, u32[]{:S(2)}, u32[]{:S(2)}) %collective-permute-start.23) | collective-permute-done | bytes 262176 | tf_op jit(solution)/shard_map/ppermute | solution.py:222
  169.7 6.0 %collective-permute-done.24 = bf16[2,2,128,256]{3,2,1,0:T(8,128)(2,1)S(1)} collective-permute-done((bf16[2,2,128,256]{3,2,1,0:T(8,128)(2,1)S(1)}, bf16[2,2,128,256]{3,2,1,0:T(8,128)(2,1)S(1)}, u32[]{:S(2)}, u32[]{:S(2)}) %collective-permute-start.24) | collective-permute-done | bytes 262176 | tf_op jit(solution)/shard_map/ppermute | solution.py:222
  176.7 7.8 %shard_map.96 = (bf16[4,2,2,128,256]{4,3,2,1,0:T(8,128)(2,1)}, bf16[4,2,2,128,256]{4,3,2,1,0:T(8,128)(2,1)}) custom-call(s32[34]{0:T(128)} %pad_add_fusion.2.info, bf16[16,256,256]{2,1,0:T(8,128)(2,1)} %bitcast.63, bf16[16,256,256]{2,1,0:T(8,128)(2,1)} %collective-permute-done.11.refs_1_, bf16[8,128,256]{2,1,0:T(8,128)(2,1)} %copy-done.3, ...), custom_call_target="tpu_custom_call" | custom-call | flops 1073741824 | bytes 8388608 | tf_op jit(solution)/shard_map/pallas_call | solution.py:146
  184.6 9.5 %collective-permute-start.32 = (bf16[8,128,256]{2,1,0:T(8,128)(2,1)S(1)}, bf16[8,128,256]{2,1,0:T(8,128)(2,1)S(1)}, u32[]{:S(2)}, u32[]{:S(2)}) collective-permute-start(bf16[8,128,256]{2,1,0:T(8,128)(2,1)S(1)} %copy-done.6), channel_id=1, source_target_pairs={{0,8},{8,0},{16,24},{24,16},{1,9},{9,1},{17,25},{25,17},{2,10},{10... | collective-permute-start | bytes 1572872 | tf_op jit(solution)/shard_map/ppermute | solution.py:226
  199.5 7.4 %collective-permute-done.32.refs_9_ = bf16[8,128,256]{2,1,0:T(8,128)(2,1)S(1)} collective-permute-done((bf16[8,128,256]{2,1,0:T(8,128)(2,1)S(1)}, bf16[8,128,256]{2,1,0:T(8,128)(2,1)S(1)}, u32[]{:S(2)}, u32[]{:S(2)}) %collective-permute-start.32) | collective-permute-done | bytes 524320 | tf_op jit(solution)/shard_map/ppermute | solution.py:226
  208.9 9.3 %collective-permute-done.33.refs_10_ = bf16[8,128,256]{2,1,0:T(8,128)(2,1)S(1)} collective-permute-done((bf16[8,128,256]{2,1,0:T(8,128)(2,1)S(1)}, bf16[8,128,256]{2,1,0:T(8,128)(2,1)S(1)}, u32[]{:S(2)}, u32[]{:S(2)}) %collective-permute-start.33) | collective-permute-done | bytes 524320 | tf_op jit(solution)/shard_map/ppermute | solution.py:226
  220.1 7.3 %shard_map.97 = bf16[16,256,256]{2,1,0:T(8,128)(2,1)} custom-call(s32[34]{0:T(128)} %pad_add_fusion.info, bf16[4,2,128,256]{3,2,1,0:T(8,128)(2,1)} %copy-done.2, bf16[4,2,128,256]{3,2,1,0:T(8,128)(2,1)} %copy-done.17, bf16[4,2,128,256]{3,2,1,0:T(8,128)(2,1)} %copy-done.14, bf16[4,2,128,256]{3,2,1,0:T(8,128)(2,1)} %copy-done.18, ...), custom_call_target="tpu_custom_call" | custom-call | flops 1073741824 | bytes 8388608 | tf_op jit(solution)/shard_map/pallas_call | solution.py:146
  231.6 13.5 %collective-permute-done.26 = bf16[2,128,256]{2,1,0:T(8,128)(2,1)S(1)} collective-permute-done((bf16[2,128,256]{2,1,0:T(8,128)(2,1)S(1)}, bf16[2,128,256]{2,1,0:T(8,128)(2,1)S(1)}, u32[]{:S(2)}, u32[]{:S(2)}) %collective-permute-start.26) | collective-permute-done | bytes 131104 | tf_op jit(solution)/shard_map/ppermute | solution.py:226
  246.1 7.3 %shard_map.98 = bf16[16,256,256]{2,1,0:T(8,128)(2,1)} custom-call(s32[34]{0:T(128)} %pad_add_fusion.2.info, bf16[4,2,128,256]{3,2,1,0:T(8,128)(2,1)} %copy-done.1, bf16[4,2,128,256]{3,2,1,0:T(8,128)(2,1)} %copy-done.10, bf16[4,2,128,256]{3,2,1,0:T(8,128)(2,1)} %copy-done.7, bf16[4,2,128,256]{3,2,1,0:T(8,128)(2,1)} %copy-done.11, ...), custom_call_target="tpu_custom_call" | custom-call | flops 1073741824 | bytes 8388608 | tf_op jit(solution)/shard_map/pallas_call | solution.py:146
  (155 shorter events, 51.6 us)
Async XLA Ops:
  6.2 21.4 %collective-permute-start.1 = (bf16[2,2,128,256]{3,2,1,0:T(8,128)(2,1)S(1)}, bf16[2,2,128,256]{3,2,1,0:T(8,128)(2,1)S(1)}, u32[]{:S(2)}, u32[]{:S(2)}) collective-permute-start(bf16[2,2,128,256]{3,2,1,0:T(8,128)(2,1)S(1)} %pad_maximum_fusion.2), channel_id=1, source_target_pairs={{0,16},{8,24},{16,0},{24,8},{1,17},{9,25},{17,1},{25,9},{2,18},{10... | collective-permute-start | bytes 786440 | tf_op jit(solution)/shard_map/ppermute | solution.py:226
  8.8 18.8 %collective-permute-start.2 = (bf16[2,2,128,256]{3,2,1,0:T(8,128)(2,1)S(1)}, bf16[2,2,128,256]{3,2,1,0:T(8,128)(2,1)S(1)}, u32[]{:S(2)}, u32[]{:S(2)}) collective-permute-start(bf16[2,2,128,256]{3,2,1,0:T(8,128)(2,1)S(1)} %pad_maximum_fusion.2), channel_id=1, source_target_pairs={{0,24},{8,16},{16,8},{24,0},{1,25},{9,17},{17,9},{25,1},{2,26},{10... | collective-permute-start | bytes 786440 | tf_op jit(solution)/shard_map/ppermute | solution.py:226
  8.8 60.8 %collective-permute-start.11 = (bf16[16,256,256]{2,1,0:T(8,128)(2,1)}, bf16[16,256,256]{2,1,0:T(8,128)(2,1)}, u32[]{:S(2)}, u32[]{:S(2)}) collective-permute-start(bf16[16,256,256]{2,1,0:T(8,128)(2,1)} %bitcast.61), channel_id=1, source_target_pairs={{0,8},{8,0},{16,24},{24,16},{1,9},{9,1},{17,25},{25,17},{2,10},{10... | collective-permute-start | bytes 6291464 | tf_op jit(solution)/shard_map/ppermute | solution.py:226
  30.0 22.1 %collective-permute-start.6 = (bf16[4,2,128,256]{3,2,1,0:T(8,128)(2,1)S(1)}, bf16[4,2,128,256]{3,2,1,0:T(8,128)(2,1)S(1)}, u32[]{:S(2)}, u32[]{:S(2)}) collective-permute-start(bf16[4,2,128,256]{3,2,1,0:T(8,128)(2,1)S(1)} %pad_maximum_fusion.refs_2_.refs_0_), channel_id=1, source_target_pairs={{0,4},{1,5},{2,6},{3,7},{4,0},{5,1},{6,2},{7,3},{8,12},{9,13},{10,... | collective-permute-start | bytes 1572872 | tf_op jit(solution)/shard_map/ppermute | solution.py:222
  31.5 20.6 %collective-permute-start.8 = (bf16[4,2,128,256]{3,2,1,0:T(8,128)(2,1)S(1)}, bf16[4,2,128,256]{3,2,1,0:T(8,128)(2,1)S(1)}, u32[]{:S(2)}, u32[]{:S(2)}) collective-permute-start(bf16[4,2,128,256]{3,2,1,0:T(8,128)(2,1)S(1)} %pad_maximum_fusion.refs_2_.refs_0_), channel_id=1, source_target_pairs={{0,6},{1,7},{2,4},{3,5},{4,2},{5,3},{6,0},{7,1},{8,14},{9,15},{10,... | collective-permute-start | bytes 1572872 | tf_op jit(solution)/shard_map/ppermute | solution.py:222
  32.0 20.7 %collective-permute-start.3 = (bf16[4,2,128,256]{3,2,1,0:T(8,128)(2,1)S(1)}, bf16[4,2,128,256]{3,2,1,0:T(8,128)(2,1)S(1)}, u32[]{:S(2)}, u32[]{:S(2)}) collective-permute-start(bf16[4,2,128,256]{3,2,1,0:T(8,128)(2,1)S(1)} %pad_maximum_fusion.refs_2_.refs_0_), channel_id=1, source_target_pairs={{0,1},{1,0},{2,3},{3,2},{4,5},{5,4},{6,7},{7,6},{8,9},{9,8},{10,11... | collective-permute-start | bytes 1572872 | tf_op jit(solution)/shard_map/ppermute | solution.py:222
  54.8 76.0 %collective-permute-start.10 = (bf16[16,256,256]{2,1,0:T(8,128)(2,1)S(1)}, bf16[16,256,256]{2,1,0:T(8,128)(2,1)}, u32[]{:S(2)}, u32[]{:S(2)}) collective-permute-start(bf16[16,256,256]{2,1,0:T(8,128)(2,1)S(1)} %bitcast.60), channel_id=1, source_target_pairs={{0,8},{8,0},{16,24},{24,16},{1,9},{9,1},{17,25},{25,17},{2,10},{10... | collective-permute-start | bytes 6291464 | tf_op jit(solution)/shard_map/ppermute | solution.py:226
  62.7 18.7 %collective-permute-start.14 = (bf16[4,2,128,256]{3,2,1,0:T(8,128)(2,1)S(1)}, bf16[4,2,128,256]{3,2,1,0:T(8,128)(2,1)S(1)}, u32[]{:S(2)}, u32[]{:S(2)}) collective-permute-start(bf16[4,2,128,256]{3,2,1,0:T(8,128)(2,1)S(1)} %pad_maximum_fusion.1.refs_2_.refs_0_), channel_id=1, source_target_pairs={{0,2},{1,3},{2,0},{3,1},{4,6},{5,7},{6,4},{7,5},{8,10},{9,11},{10,... | collective-permute-start | bytes 1572872 | tf_op jit(solution)/shard_map/ppermute | solution.py:222
  63.3 23.8 %collective-permute-start.15 = (bf16[4,2,128,256]{3,2,1,0:T(8,128)(2,1)S(1)}, bf16[4,2,128,256]{3,2,1,0:T(8,128)(2,1)S(1)}, u32[]{:S(2)}, u32[]{:S(2)}) collective-permute-start(bf16[4,2,128,256]{3,2,1,0:T(8,128)(2,1)S(1)} %pad_maximum_fusion.1.refs_2_.refs_0_), channel_id=1, source_target_pairs={{0,4},{1,5},{2,6},{3,7},{4,0},{5,1},{6,2},{7,3},{8,12},{9,13},{10,... | collective-permute-start | bytes 1572872 | tf_op jit(solution)/shard_map/ppermute | solution.py:222
  64.9 23.8 %collective-permute-start.16 = (bf16[4,2,128,256]{3,2,1,0:T(8,128)(2,1)S(1)}, bf16[4,2,128,256]{3,2,1,0:T(8,128)(2,1)S(1)}, u32[]{:S(2)}, u32[]{:S(2)}) collective-permute-start(bf16[4,2,128,256]{3,2,1,0:T(8,128)(2,1)S(1)} %pad_maximum_fusion.1.refs_2_.refs_0_), channel_id=1, source_target_pairs={{0,6},{1,7},{2,4},{3,5},{4,2},{5,3},{6,0},{7,1},{8,14},{9,15},{10,... | collective-permute-start | bytes 1572872 | tf_op jit(solution)/shard_map/ppermute | solution.py:222
  77.3 50.0 %collective-permute-start.12 = (bf16[8,128,256]{2,1,0:T(8,128)(2,1)}, bf16[8,128,256]{2,1,0:T(8,128)(2,1)S(1)}, u32[]{:S(2)}, u32[]{:S(2)}) collective-permute-start(bf16[8,128,256]{2,1,0:T(8,128)(2,1)} %get-tuple-element.57), channel_id=1, source_target_pairs={{0,24},{8,16},{16,8},{24,0},{1,25},{9,17},{17,9},{25,1},{2,26},{10... | collective-permute-start | bytes 1572872 | tf_op jit(solution)/shard_map/ppermute | solution.py:226
  88.7 40.6 %collective-permute-start.17 = (bf16[4,2,128,256]{3,2,1,0:T(8,128)(2,1)S(1)}, bf16[4,2,128,256]{3,2,1,0:T(8,128)(2,1)S(1)}, u32[]{:S(2)}, u32[]{:S(2)}) collective-permute-start(bf16[4,2,128,256]{3,2,1,0:T(8,128)(2,1)S(1)} %pad_maximum_fusion.1.refs_2_.refs_0_), channel_id=1, source_target_pairs={{0,1},{1,0},{2,3},{3,2},{4,5},{5,4},{6,7},{7,6},{8,9},{9,8},{10,11... | collective-permute-start | bytes 1572872 | tf_op jit(solution)/shard_map/ppermute | solution.py:222
  88.7 42.0 %collective-permute-start.18 = (bf16[4,2,128,256]{3,2,1,0:T(8,128)(2,1)S(1)}, bf16[4,2,128,256]{3,2,1,0:T(8,128)(2,1)S(1)}, u32[]{:S(2)}, u32[]{:S(2)}) collective-permute-start(bf16[4,2,128,256]{3,2,1,0:T(8,128)(2,1)S(1)} %collective-permute-done.14.refs_4_.refs_2_), channel_id=1, source_target_pairs={{0,1},{1,0},{2,3},{3,2},{4,5},{5,4},{6,7},{7,6},{8,9},{9,8},{10,11... | collective-permute-start | bytes 1572872 | tf_op jit(solution)/shard_map/ppermute | solution.py:222
  89.2 41.5 %collective-permute-start.19 = (bf16[4,2,128,256]{3,2,1,0:T(8,128)(2,1)S(1)}, bf16[4,2,128,256]{3,2,1,0:T(8,128)(2,1)S(1)}, u32[]{:S(2)}, u32[]{:S(2)}) collective-permute-start(bf16[4,2,128,256]{3,2,1,0:T(8,128)(2,1)S(1)} %collective-permute-done.15.refs_6_.refs_4_), channel_id=1, source_target_pairs={{0,1},{1,0},{2,3},{3,2},{4,5},{5,4},{6,7},{7,6},{8,9},{9,8},{10,11... | collective-permute-start | bytes 1572872 | tf_op jit(solution)/shard_map/ppermute | solution.py:222
  157.5 18.5 %collective-permute-start.27 = (bf16[8,128,256]{2,1,0:T(8,128)(2,1)S(1)}, bf16[8,128,256]{2,1,0:T(8,128)(2,1)S(1)}, u32[]{:S(2)}, u32[]{:S(2)}) collective-permute-start(bf16[8,128,256]{2,1,0:T(8,128)(2,1)S(1)} %multiply_convert_fusion.refs_2_.refs_8_), channel_id=1, source_target_pairs={{0,24},{8,16},{16,8},{24,0},{1,25},{9,17},{17,9},{25,1},{2,26},{10... | collective-permute-start | bytes 1572872 | tf_op jit(solution)/shard_map/ppermute | solution.py:226
  184.6 22.3 %collective-permute-start.32 = (bf16[8,128,256]{2,1,0:T(8,128)(2,1)S(1)}, bf16[8,128,256]{2,1,0:T(8,128)(2,1)S(1)}, u32[]{:S(2)}, u32[]{:S(2)}) collective-permute-start(bf16[8,128,256]{2,1,0:T(8,128)(2,1)S(1)} %copy-done.6), channel_id=1, source_target_pairs={{0,8},{8,0},{16,24},{24,16},{1,9},{9,1},{17,25},{25,17},{2,10},{10... | collective-permute-start | bytes 1572872 | tf_op jit(solution)/shard_map/ppermute | solution.py:226
  194.2 24.0 %collective-permute-start.33 = (bf16[8,128,256]{2,1,0:T(8,128)(2,1)S(1)}, bf16[8,128,256]{2,1,0:T(8,128)(2,1)S(1)}, u32[]{:S(2)}, u32[]{:S(2)}) collective-permute-start(bf16[8,128,256]{2,1,0:T(8,128)(2,1)S(1)} %copy-done.25), channel_id=1, source_target_pairs={{0,8},{8,0},{16,24},{24,16},{1,9},{9,1},{17,25},{25,17},{2,10},{10... | collective-permute-start | bytes 1572872 | tf_op jit(solution)/shard_map/ppermute | solution.py:226
  196.0 31.5 %collective-permute-start.29 = (bf16[2,2,128,256]{3,2,1,0:T(8,128)(2,1)S(1)}, bf16[2,2,128,256]{3,2,1,0:T(8,128)(2,1)S(1)}, u32[]{:S(2)}, u32[]{:S(2)}) collective-permute-start(bf16[2,2,128,256]{3,2,1,0:T(8,128)(2,1)S(1)} %get-tuple-element.110), channel_id=1, source_target_pairs={{0,2},{1,3},{2,0},{3,1},{4,6},{5,7},{6,4},{7,5},{8,10},{9,11},{10,... | collective-permute-start | bytes 786440 | tf_op jit(solution)/shard_map/ppermute | solution.py:222
  197.5 31.7 %collective-permute-start.30 = (bf16[2,2,128,256]{3,2,1,0:T(8,128)(2,1)S(1)}, bf16[2,2,128,256]{3,2,1,0:T(8,128)(2,1)S(1)}, u32[]{:S(2)}, u32[]{:S(2)}) collective-permute-start(bf16[2,2,128,256]{3,2,1,0:T(8,128)(2,1)S(1)} %get-tuple-element.109), channel_id=1, source_target_pairs={{0,4},{1,5},{2,6},{3,7},{4,0},{5,1},{6,2},{7,3},{8,12},{9,13},{10,... | collective-permute-start | bytes 786440 | tf_op jit(solution)/shard_map/ppermute | solution.py:222
  199.0 30.2 %collective-permute-start.31 = (bf16[2,2,128,256]{3,2,1,0:T(8,128)(2,1)S(1)}, bf16[2,2,128,256]{3,2,1,0:T(8,128)(2,1)S(1)}, u32[]{:S(2)}, u32[]{:S(2)}) collective-permute-start(bf16[2,2,128,256]{3,2,1,0:T(8,128)(2,1)S(1)} %get-tuple-element.108), channel_id=1, source_target_pairs={{0,6},{1,7},{2,4},{3,5},{4,2},{5,3},{6,0},{7,1},{8,14},{9,15},{10,... | collective-permute-start | bytes 786440 | tf_op jit(solution)/shard_map/ppermute | solution.py:222
  206.9 38.2 %collective-permute-start.35 = (bf16[8,128,256]{2,1,0:T(8,128)(2,1)S(1)}, bf16[8,128,256]{2,1,0:T(8,128)(2,1)S(1)}, u32[]{:S(2)}, u32[]{:S(2)}) collective-permute-start(bf16[8,128,256]{2,1,0:T(8,128)(2,1)S(1)} %copy-done.4), channel_id=1, source_target_pairs={{0,8},{8,0},{16,24},{24,16},{1,9},{9,1},{17,25},{25,17},{2,10},{10... | collective-permute-start | bytes 1572872 | tf_op jit(solution)/shard_map/ppermute | solution.py:226
  218.2 27.0 %collective-permute-start.36 = (bf16[8,128,256]{2,1,0:T(8,128)(2,1)S(1)}, bf16[8,128,256]{2,1,0:T(8,128)(2,1)S(1)}, u32[]{:S(2)}, u32[]{:S(2)}) collective-permute-start(bf16[8,128,256]{2,1,0:T(8,128)(2,1)S(1)} %copy-done.23), channel_id=1, source_target_pairs={{0,8},{8,0},{16,24},{24,16},{1,9},{9,1},{17,25},{25,17},{2,10},{10... | collective-permute-start | bytes 1572872 | tf_op jit(solution)/shard_map/ppermute | solution.py:226
  227.5 17.6 %collective-permute-start.26 = (bf16[2,128,256]{2,1,0:T(8,128)(2,1)S(1)}, bf16[2,128,256]{2,1,0:T(8,128)(2,1)S(1)}, u32[]{:S(2)}, u32[]{:S(2)}) collective-permute-start(bf16[2,128,256]{2,1,0:T(8,128)(2,1)S(1)} %slice_bitcast_fusion.10), channel_id=1, source_target_pairs={{0,24},{8,16},{16,8},{24,0},{1,25},{9,17},{17,9},{25,1},{2,26},{10... | collective-permute-start | bytes 393224 | tf_op jit(solution)/shard_map/ppermute | solution.py:226
  229.4 24.1 %collective-permute-start.34 = (bf16[2,128,256]{2,1,0:T(8,128)(2,1)S(1)}, bf16[2,128,256]{2,1,0:T(8,128)(2,1)S(1)}, u32[]{:S(2)}, u32[]{:S(2)}) collective-permute-start(bf16[2,128,256]{2,1,0:T(8,128)(2,1)S(1)} %slice_bitcast_fusion.8), channel_id=1, source_target_pairs={{0,24},{8,16},{16,8},{24,0},{1,25},{9,17},{17,9},{25,1},{2,26},{10... | collective-permute-start | bytes 393224 | tf_op jit(solution)/shard_map/ppermute | solution.py:226
  (48 other events, 708.9 us)

commit v11 on v10

--- a/solution.py
+++ b/solution.py
@@ -321,14 +321,14 @@
     activ, activ_far = after((activ, activ_far), grad_hidden)
     all_activ = [activ, swap_row(activ, 1), swap_row(activ_far, 1), activ_far]
     layer_sums = finish_col(pair_sums(*after(layer_parts, grad_hidden)))
-    ends_grad = after([grad_hidden, grad_far], layer_sums)
+    ends_grad = after([grad_hidden, grad_far], layer_sums, all_activ[1])
     input_parts = from_hidden(info_in, ends_grad, in_pair, cols, True, ends, devices)
     layer_far = swap_row(layer_sums[1], 3)
     input_pairs = pair_sums(*input_parts)
     all_activ = after(all_activ, input_pairs)
     grad_w_out = slot_grads(info_out, all_up, all_activ, slots, cols, False)
     near, far = swap_row(grad_hidden, 1), swap_row(grad_far, 1)
-    input_sums = finish_col(input_pairs, grad_w_out)
+    input_sums = finish_col(input_pairs, grad_w_out, near, far)
     all_grad = after([grad_hidden, near, far, grad_far], input_sums)
     grad_w_in = slot_grads(info_in, all_tokens, all_grad, slots, cols, True)
     input_far = after(swap_row(input_sums[1], 3), grad_w_in)

time: 255 us -> 249 us (0.976)
  starting transfers between devices: 55.5 us -> 50 us
    ppermute x15, starting transfers between devices: 40.1 us -> 32.6 us  [swap_row(): return lax.ppermute(x, 'row', [(s, s ^ t) for s in range(4)])]
    unnamed x74 -> x70, local copies, waits for them, and re-layouts: 6.63 us -> 6.55 us
where the time goes in v11:
time: 249 us; the launch traced here: 247 us
  waiting for transfers between devices  136 us (55%)
  starting transfers between devices  50 us (20%)
  Pallas kernels  45.7 us (18%)
  local copies, waits for them, and re-layouts  8 us (3%)
  other arithmetic  6.33 us (3%)
    ppermute x15, waiting for transfers between devices, swap_row(): return lax.ppermute(x, 'row', [(s, s ^ t) for s in range(4)])  94.6 us
    pallas_call x6, Pallas kernels, call(): pl.pallas_call(kernel, out_shape=out_shape, in_specs=[pl.BlockSpec(memory...  45.7 us
    ppermute x22, waiting for transfers between devices, swap_col(): return lax.ppermute(x, 'col', [(s, s ^ m) for s in range(count)])  41.1 us
    ppermute x15, starting transfers between devices, swap_row(): return lax.ppermute(x, 'row', [(s, s ^ t) for s in range(4)])  32.6 us
    ppermute x22, starting transfers between devices, swap_col(): return lax.ppermute(x, 'col', [(s, s ^ m) for s in range(count)])  17.5 us
    unnamed x70, local copies, waits for them, and re-layouts  6.55 us
  transfers between devices with their start and end apart: 37, of which 18 were waited for; matrix products, arithmetic and copies ran while one was open for 3% of the time, Pallas kernels for 15%

profile of v11, /device:TPU:0, one launch (start us, length us, event | category | flops | bytes accessed | tf_op | source)
XLA Modules:
  0.0 247.0 jit_solution(9092028530329155917)
XLA Ops:
  3.1 3.1 %collective-permute-start = (bf16[2,2,128,256]{3,2,1,0:T(8,128)(2,1)S(1)}, bf16[2,2,128,256]{3,2,1,0:T(8,128)(2,1)S(1)}, u32[]{:S(2)}, u32[]{:S(2)}) collective-permute-start(bf16[2,2,128,256]{3,2,1,0:T(8,128)(2,1)S(1)} %pad_maximum_fusion.2), channel_id=1, source_target_pairs={{0,8},{8,0},{16,24},{24,16},{1,9},{9,1},{17,25},{25,17},{2,10},{10... | collective-permute-start | bytes 786440 | tf_op jit(solution)/shard_map/ppermute | solution.py:226
  6.2 2.6 %collective-permute-start.1 = (bf16[2,2,128,256]{3,2,1,0:T(8,128)(2,1)S(1)}, bf16[2,2,128,256]{3,2,1,0:T(8,128)(2,1)S(1)}, u32[]{:S(2)}, u32[]{:S(2)}) collective-permute-start(bf16[2,2,128,256]{3,2,1,0:T(8,128)(2,1)S(1)} %pad_maximum_fusion.2), channel_id=1, source_target_pairs={{0,16},{8,24},{16,0},{24,8},{1,17},{9,25},{17,1},{25,9},{2,18},{10... | collective-permute-start | bytes 786440 | tf_op jit(solution)/shard_map/ppermute | solution.py:226
  9.7 8.5 %collective-permute-done = bf16[2,2,128,256]{3,2,1,0:T(8,128)(2,1)S(1)} collective-permute-done((bf16[2,2,128,256]{3,2,1,0:T(8,128)(2,1)S(1)}, bf16[2,2,128,256]{3,2,1,0:T(8,128)(2,1)S(1)}, u32[]{:S(2)}, u32[]{:S(2)}) %collective-permute-start) | collective-permute-done | bytes 262176 | tf_op jit(solution)/shard_map/ppermute | solution.py:226
  18.2 9.4 %collective-permute-done.1 = bf16[2,2,128,256]{3,2,1,0:T(8,128)(2,1)S(1)} collective-permute-done((bf16[2,2,128,256]{3,2,1,0:T(8,128)(2,1)S(1)}, bf16[2,2,128,256]{3,2,1,0:T(8,128)(2,1)S(1)}, u32[]{:S(2)}, u32[]{:S(2)}) %collective-permute-start.1) | collective-permute-done | bytes 262176 | tf_op jit(solution)/shard_map/ppermute | solution.py:226
  32.0 11.4 %collective-permute-done.4.refs_4_.refs_2_ = bf16[4,2,128,256]{3,2,1,0:T(8,128)(2,1)S(1)} collective-permute-done((bf16[4,2,128,256]{3,2,1,0:T(8,128)(2,1)S(1)}, bf16[4,2,128,256]{3,2,1,0:T(8,128)(2,1)S(1)}, u32[]{:S(2)}, u32[]{:S(2)}) %collective-permute-start.4) | collective-permute-done | bytes 524320 | tf_op jit(solution)/shard_map/ppermute | solution.py:222
  43.4 8.7 %collective-permute-done.6.refs_6_.refs_4_ = bf16[4,2,128,256]{3,2,1,0:T(8,128)(2,1)S(1)} collective-permute-done((bf16[4,2,128,256]{3,2,1,0:T(8,128)(2,1)S(1)}, bf16[4,2,128,256]{3,2,1,0:T(8,128)(2,1)S(1)}, u32[]{:S(2)}, u32[]{:S(2)}) %collective-permute-start.6) | collective-permute-done | bytes 524320 | tf_op jit(solution)/shard_map/ppermute | solution.py:222
  54.8 6.2 %collective-permute-start.10 = (bf16[16,256,256]{2,1,0:T(8,128)(2,1)S(1)}, bf16[16,256,256]{2,1,0:T(8,128)(2,1)}, u32[]{:S(2)}, u32[]{:S(2)}) collective-permute-start(bf16[16,256,256]{2,1,0:T(8,128)(2,1)S(1)} %bitcast.60), channel_id=1, source_target_pairs={{0,8},{8,0},{16,24},{24,16},{1,9},{9,1},{17,25},{25,17},{2,10},{10... | collective-permute-start | bytes 6291464 | tf_op jit(solution)/shard_map/ppermute | solution.py:226
  66.2 3.4 %collective-permute-done.11.refs_1_ = bf16[16,256,256]{2,1,0:T(8,128)(2,1)} collective-permute-done((bf16[16,256,256]{2,1,0:T(8,128)(2,1)}, bf16[16,256,256]{2,1,0:T(8,128)(2,1)}, u32[]{:S(2)}, u32[]{:S(2)}) %collective-permute-start.11) | collective-permute-done | bytes 2097184 | tf_op jit(solution)/shard_map/ppermute | solution.py:226
  69.7 7.6 %shard_map.93 = (bf16[8,128,256]{2,1,0:T(8,128)(2,1)}, bf16[8,128,256]{2,1,0:T(8,128)(2,1)}) custom-call(s32[34]{0:T(128)} %pad_add_fusion.2.info, bf16[16,256,256]{2,1,0:T(8,128)(2,1)} %bitcast.62, bf16[16,256,256]{2,1,0:T(8,128)(2,1)} %collective-permute-done.11.refs_1_, bf16[4,2,128,256]{3,2,1,0:T(8,128)(2,1)} %copy-done.1, ...), custom_call_target="tpu_custom_call" | custom-call | flops 1073741824 | bytes 8388608 | tf_op jit(solution)/shard_map/pallas_call | solution.py:146
  77.3 4.2 %collective-permute-start.12 = (bf16[8,128,256]{2,1,0:T(8,128)(2,1)}, bf16[8,128,256]{2,1,0:T(8,128)(2,1)S(1)}, u32[]{:S(2)}, u32[]{:S(2)}) collective-permute-start(bf16[8,128,256]{2,1,0:T(8,128)(2,1)} %get-tuple-element.57), channel_id=1, source_target_pairs={{0,24},{8,16},{16,8},{24,0},{1,25},{9,17},{17,9},{25,1},{2,26},{10... | collective-permute-start | bytes 1572872 | tf_op jit(solution)/shard_map/ppermute | solution.py:226
  81.5 5.5 %collective-permute-done.15.refs_6_.refs_4_ = bf16[4,2,128,256]{3,2,1,0:T(8,128)(2,1)S(1)} collective-permute-done((bf16[4,2,128,256]{3,2,1,0:T(8,128)(2,1)S(1)}, bf16[4,2,128,256]{3,2,1,0:T(8,128)(2,1)S(1)}, u32[]{:S(2)}, u32[]{:S(2)}) %collective-permute-start.15) | collective-permute-done | bytes 524320 | tf_op jit(solution)/shard_map/ppermute | solution.py:222
  89.2 38.1 %collective-permute-done.12 = bf16[8,128,256]{2,1,0:T(8,128)(2,1)S(1)} collective-permute-done((bf16[8,128,256]{2,1,0:T(8,128)(2,1)}, bf16[8,128,256]{2,1,0:T(8,128)(2,1)S(1)}, u32[]{:S(2)}, u32[]{:S(2)}) %collective-permute-start.12) | collective-permute-done | bytes 524320 | tf_op jit(solution)/shard_map/ppermute | solution.py:226
  131.9 8.0 %shard_map.94 = (bf16[8,128,256]{2,1,0:T(8,128)(2,1)}, bf16[8,128,256]{2,1,0:T(8,128)(2,1)}) custom-call(s32[34]{0:T(128)} %pad_add_fusion.info, bf16[16,256,256]{2,1,0:T(8,128)(2,1)} %bitcast.58, bf16[16,256,256]{2,1,0:T(8,128)(2,1)} %collective-permute-done.10.refs_1_, bf16[4,2,128,256]{3,2,1,0:T(8,128)(2,1)} %copy-done.2, ...), custom_call_target="tpu_custom_call" | custom-call | flops 1073741824 | bytes 8388608 | tf_op jit(solution)/shard_map/pallas_call | solution.py:146
  142.3 3.6 %collective-permute-done.13.refs_3_.refs_11_ = bf16[8,128,256]{2,1,0:T(8,128)(2,1)S(1)} collective-permute-done((bf16[8,128,256]{2,1,0:T(8,128)(2,1)S(1)}, bf16[8,128,256]{2,1,0:T(8,128)(2,1)S(1)}, u32[]{:S(2)}, u32[]{:S(2)}) %collective-permute-start.13) | collective-permute-done | bytes 524320 | tf_op jit(solution)/shard_map/ppermute | solution.py:226
  146.7 7.6 %shard_map.95 = (bf16[4,2,2,128,256]{4,3,2,1,0:T(8,128)(2,1)}, bf16[4,2,2,128,256]{4,3,2,1,0:T(8,128)(2,1)}) custom-call(s32[34]{0:T(128)} %pad_add_fusion.info, bf16[16,256,256]{2,1,0:T(8,128)(2,1)} %bitcast.59, bf16[16,256,256]{2,1,0:T(8,128)(2,1)} %collective-permute-done.10.refs_1_, bf16[8,128,256]{2,1,0:T(8,128)(2,1)} %copy-done.4, ...), custom_call_target="tpu_custom_call" | custom-call | flops 1073741824 | bytes 8388608 | tf_op jit(solution)/shard_map/pallas_call | solution.py:146
  159.2 3.5 %collective-permute-start.28 = (bf16[8,128,256]{2,1,0:T(8,128)(2,1)S(1)}, bf16[8,128,256]{2,1,0:T(8,128)(2,1)S(1)}, u32[]{:S(2)}, u32[]{:S(2)}) collective-permute-start(bf16[8,128,256]{2,1,0:T(8,128)(2,1)S(1)} %copy-done.5), channel_id=1, source_target_pairs={{0,8},{8,0},{16,24},{24,16},{1,9},{9,1},{17,25},{25,17},{2,10},{10... | collective-permute-start | bytes 1572872 | tf_op jit(solution)/shard_map/ppermute | solution.py:226
  166.7 5.7 %collective-permute-done.23 = bf16[2,2,128,256]{3,2,1,0:T(8,128)(2,1)S(1)} collective-permute-done((bf16[2,2,128,256]{3,2,1,0:T(8,128)(2,1)S(1)}, bf16[2,2,128,256]{3,2,1,0:T(8,128)(2,1)S(1)}, u32[]{:S(2)}, u32[]{:S(2)}) %collective-permute-start.23) | collective-permute-done | bytes 262176 | tf_op jit(solution)/shard_map/ppermute | solution.py:222
  172.4 5.7 %collective-permute-done.24 = bf16[2,2,128,256]{3,2,1,0:T(8,128)(2,1)S(1)} collective-permute-done((bf16[2,2,128,256]{3,2,1,0:T(8,128)(2,1)S(1)}, bf16[2,2,128,256]{3,2,1,0:T(8,128)(2,1)S(1)}, u32[]{:S(2)}, u32[]{:S(2)}) %collective-permute-start.24) | collective-permute-done | bytes 262176 | tf_op jit(solution)/shard_map/ppermute | solution.py:222
  178.3 6.6 %collective-permute-done.28.refs_9_ = bf16[8,128,256]{2,1,0:T(8,128)(2,1)S(1)} collective-permute-done((bf16[8,128,256]{2,1,0:T(8,128)(2,1)S(1)}, bf16[8,128,256]{2,1,0:T(8,128)(2,1)S(1)}, u32[]{:S(2)}, u32[]{:S(2)}) %collective-permute-start.28) | collective-permute-done | bytes 524320 | tf_op jit(solution)/shard_map/ppermute | solution.py:226
  185.7 7.8 %shard_map.96 = (bf16[4,2,2,128,256]{4,3,2,1,0:T(8,128)(2,1)}, bf16[4,2,2,128,256]{4,3,2,1,0:T(8,128)(2,1)}) custom-call(s32[34]{0:T(128)} %pad_add_fusion.2.info, bf16[16,256,256]{2,1,0:T(8,128)(2,1)} %bitcast.63, bf16[16,256,256]{2,1,0:T(8,128)(2,1)} %collective-permute-done.11.refs_1_, bf16[8,128,256]{2,1,0:T(8,128)(2,1)} %copy-done.3, ...), custom_call_target="tpu_custom_call" | custom-call | flops 1073741824 | bytes 8388608 | tf_op jit(solution)/shard_map/pallas_call | solution.py:146
  201.1 18.7 %collective-permute-done.33.refs_10_ = bf16[8,128,256]{2,1,0:T(8,128)(2,1)S(1)} collective-permute-done((bf16[8,128,256]{2,1,0:T(8,128)(2,1)S(1)}, bf16[8,128,256]{2,1,0:T(8,128)(2,1)S(1)}, u32[]{:S(2)}, u32[]{:S(2)}) %collective-permute-start.33) | collective-permute-done | bytes 524320 | tf_op jit(solution)/shard_map/ppermute | solution.py:226
  222.3 7.3 %shard_map.97 = bf16[16,256,256]{2,1,0:T(8,128)(2,1)} custom-call(s32[34]{0:T(128)} %pad_add_fusion.info, bf16[4,2,128,256]{3,2,1,0:T(8,128)(2,1)} %copy-done.2, bf16[4,2,128,256]{3,2,1,0:T(8,128)(2,1)} %copy-done.16, bf16[4,2,128,256]{3,2,1,0:T(8,128)(2,1)} %copy-done.13, bf16[4,2,128,256]{3,2,1,0:T(8,128)(2,1)} %copy-done.17, ...), custom_call_target="tpu_custom_call" | custom-call | flops 1073741824 | bytes 8388608 | tf_op jit(solution)/shard_map/pallas_call | solution.py:146
  233.8 4.0 %collective-permute-done.26 = bf16[2,128,256]{2,1,0:T(8,128)(2,1)S(1)} collective-permute-done((bf16[2,128,256]{2,1,0:T(8,128)(2,1)S(1)}, bf16[2,128,256]{2,1,0:T(8,128)(2,1)S(1)}, u32[]{:S(2)}, u32[]{:S(2)}) %collective-permute-start.26) | collective-permute-done | bytes 131104 | tf_op jit(solution)/shard_map/ppermute | solution.py:226
  238.7 7.3 %shard_map.98 = bf16[16,256,256]{2,1,0:T(8,128)(2,1)} custom-call(s32[34]{0:T(128)} %pad_add_fusion.2.info, bf16[4,2,128,256]{3,2,1,0:T(8,128)(2,1)} %copy-done.1, bf16[4,2,128,256]{3,2,1,0:T(8,128)(2,1)} %copy-done.9, bf16[4,2,128,256]{3,2,1,0:T(8,128)(2,1)} %copy-done.6, bf16[4,2,128,256]{3,2,1,0:T(8,128)(2,1)} %copy-done.10, ...), custom_call_target="tpu_custom_call" | custom-call | flops 1073741824 | bytes 8388608 | tf_op jit(solution)/shard_map/pallas_call | solution.py:146
  (151 shorter events, 51.3 us)
Async XLA Ops:
  3.1 15.1 %collective-permute-start = (bf16[2,2,128,256]{3,2,1,0:T(8,128)(2,1)S(1)}, bf16[2,2,128,256]{3,2,1,0:T(8,128)(2,1)S(1)}, u32[]{:S(2)}, u32[]{:S(2)}) collective-permute-start(bf16[2,2,128,256]{3,2,1,0:T(8,128)(2,1)S(1)} %pad_maximum_fusion.2), channel_id=1, source_target_pairs={{0,8},{8,0},{16,24},{24,16},{1,9},{9,1},{17,25},{25,17},{2,10},{10... | collective-permute-start | bytes 786440 | tf_op jit(solution)/shard_map/ppermute | solution.py:226
  6.2 21.4 %collective-permute-start.1 = (bf16[2,2,128,256]{3,2,1,0:T(8,128)(2,1)S(1)}, bf16[2,2,128,256]{3,2,1,0:T(8,128)(2,1)S(1)}, u32[]{:S(2)}, u32[]{:S(2)}) collective-permute-start(bf16[2,2,128,256]{3,2,1,0:T(8,128)(2,1)S(1)} %pad_maximum_fusion.2), channel_id=1, source_target_pairs={{0,16},{8,24},{16,0},{24,8},{1,17},{9,25},{17,1},{25,9},{2,18},{10... | collective-permute-start | bytes 786440 | tf_op jit(solution)/shard_map/ppermute | solution.py:226
  8.8 18.8 %collective-permute-start.2 = (bf16[2,2,128,256]{3,2,1,0:T(8,128)(2,1)S(1)}, bf16[2,2,128,256]{3,2,1,0:T(8,128)(2,1)S(1)}, u32[]{:S(2)}, u32[]{:S(2)}) collective-permute-start(bf16[2,2,128,256]{3,2,1,0:T(8,128)(2,1)S(1)} %pad_maximum_fusion.2), channel_id=1, source_target_pairs={{0,24},{8,16},{16,8},{24,0},{1,25},{9,17},{17,9},{25,1},{2,26},{10... | collective-permute-start | bytes 786440 | tf_op jit(solution)/shard_map/ppermute | solution.py:226
  8.8 60.8 %collective-permute-start.11 = (bf16[16,256,256]{2,1,0:T(8,128)(2,1)}, bf16[16,256,256]{2,1,0:T(8,128)(2,1)}, u32[]{:S(2)}, u32[]{:S(2)}) collective-permute-start(bf16[16,256,256]{2,1,0:T(8,128)(2,1)} %bitcast.61), channel_id=1, source_target_pairs={{0,8},{8,0},{16,24},{24,16},{1,9},{9,1},{17,25},{25,17},{2,10},{10... | collective-permute-start | bytes 6291464 | tf_op jit(solution)/shard_map/ppermute | solution.py:226
  30.0 22.1 %collective-permute-start.6 = (bf16[4,2,128,256]{3,2,1,0:T(8,128)(2,1)S(1)}, bf16[4,2,128,256]{3,2,1,0:T(8,128)(2,1)S(1)}, u32[]{:S(2)}, u32[]{:S(2)}) collective-permute-start(bf16[4,2,128,256]{3,2,1,0:T(8,128)(2,1)S(1)} %pad_maximum_fusion.refs_2_.refs_0_), channel_id=1, source_target_pairs={{0,4},{1,5},{2,6},{3,7},{4,0},{5,1},{6,2},{7,3},{8,12},{9,13},{10,... | collective-permute-start | bytes 1572872 | tf_op jit(solution)/shard_map/ppermute | solution.py:222
  31.5 20.6 %collective-permute-start.8 = (bf16[4,2,128,256]{3,2,1,0:T(8,128)(2,1)S(1)}, bf16[4,2,128,256]{3,2,1,0:T(8,128)(2,1)S(1)}, u32[]{:S(2)}, u32[]{:S(2)}) collective-permute-start(bf16[4,2,128,256]{3,2,1,0:T(8,128)(2,1)S(1)} %pad_maximum_fusion.refs_2_.refs_0_), channel_id=1, source_target_pairs={{0,6},{1,7},{2,4},{3,5},{4,2},{5,3},{6,0},{7,1},{8,14},{9,15},{10,... | collective-permute-start | bytes 1572872 | tf_op jit(solution)/shard_map/ppermute | solution.py:222
  32.0 20.7 %collective-permute-start.3 = (bf16[4,2,128,256]{3,2,1,0:T(8,128)(2,1)S(1)}, bf16[4,2,128,256]{3,2,1,0:T(8,128)(2,1)S(1)}, u32[]{:S(2)}, u32[]{:S(2)}) collective-permute-start(bf16[4,2,128,256]{3,2,1,0:T(8,128)(2,1)S(1)} %pad_maximum_fusion.refs_2_.refs_0_), channel_id=1, source_target_pairs={{0,1},{1,0},{2,3},{3,2},{4,5},{5,4},{6,7},{7,6},{8,9},{9,8},{10,11... | collective-permute-start | bytes 1572872 | tf_op jit(solution)/shard_map/ppermute | solution.py:222
  54.8 76.0 %collective-permute-start.10 = (bf16[16,256,256]{2,1,0:T(8,128)(2,1)S(1)}, bf16[16,256,256]{2,1,0:T(8,128)(2,1)}, u32[]{:S(2)}, u32[]{:S(2)}) collective-permute-start(bf16[16,256,256]{2,1,0:T(8,128)(2,1)S(1)} %bitcast.60), channel_id=1, source_target_pairs={{0,8},{8,0},{16,24},{24,16},{1,9},{9,1},{17,25},{25,17},{2,10},{10... | collective-permute-start | bytes 6291464 | tf_op jit(solution)/shard_map/ppermute | solution.py:226
  62.7 18.8 %collective-permute-start.14 = (bf16[4,2,128,256]{3,2,1,0:T(8,128)(2,1)S(1)}, bf16[4,2,128,256]{3,2,1,0:T(8,128)(2,1)S(1)}, u32[]{:S(2)}, u32[]{:S(2)}) collective-permute-start(bf16[4,2,128,256]{3,2,1,0:T(8,128)(2,1)S(1)} %pad_maximum_fusion.1.refs_2_.refs_0_), channel_id=1, source_target_pairs={{0,2},{1,3},{2,0},{3,1},{4,6},{5,7},{6,4},{7,5},{8,10},{9,11},{10,... | collective-permute-start | bytes 1572872 | tf_op jit(solution)/shard_map/ppermute | solution.py:222
  63.2 23.8 %collective-permute-start.15 = (bf16[4,2,128,256]{3,2,1,0:T(8,128)(2,1)S(1)}, bf16[4,2,128,256]{3,2,1,0:T(8,128)(2,1)S(1)}, u32[]{:S(2)}, u32[]{:S(2)}) collective-permute-start(bf16[4,2,128,256]{3,2,1,0:T(8,128)(2,1)S(1)} %pad_maximum_fusion.1.refs_2_.refs_0_), channel_id=1, source_target_pairs={{0,4},{1,5},{2,6},{3,7},{4,0},{5,1},{6,2},{7,3},{8,12},{9,13},{10,... | collective-permute-start | bytes 1572872 | tf_op jit(solution)/shard_map/ppermute | solution.py:222
  64.8 23.8 %collective-permute-start.16 = (bf16[4,2,128,256]{3,2,1,0:T(8,128)(2,1)S(1)}, bf16[4,2,128,256]{3,2,1,0:T(8,128)(2,1)S(1)}, u32[]{:S(2)}, u32[]{:S(2)}) collective-permute-start(bf16[4,2,128,256]{3,2,1,0:T(8,128)(2,1)S(1)} %pad_maximum_fusion.1.refs_2_.refs_0_), channel_id=1, source_target_pairs={{0,6},{1,7},{2,4},{3,5},{4,2},{5,3},{6,0},{7,1},{8,14},{9,15},{10,... | collective-permute-start | bytes 1572872 | tf_op jit(solution)/shard_map/ppermute | solution.py:222
  77.3 50.0 %collective-permute-start.12 = (bf16[8,128,256]{2,1,0:T(8,128)(2,1)}, bf16[8,128,256]{2,1,0:T(8,128)(2,1)S(1)}, u32[]{:S(2)}, u32[]{:S(2)}) collective-permute-start(bf16[8,128,256]{2,1,0:T(8,128)(2,1)} %get-tuple-element.57), channel_id=1, source_target_pairs={{0,24},{8,16},{16,8},{24,0},{1,25},{9,17},{17,9},{25,1},{2,26},{10... | collective-permute-start | bytes 1572872 | tf_op jit(solution)/shard_map/ppermute | solution.py:226
  88.6 40.6 %collective-permute-start.17 = (bf16[4,2,128,256]{3,2,1,0:T(8,128)(2,1)S(1)}, bf16[4,2,128,256]{3,2,1,0:T(8,128)(2,1)S(1)}, u32[]{:S(2)}, u32[]{:S(2)}) collective-permute-start(bf16[4,2,128,256]{3,2,1,0:T(8,128)(2,1)S(1)} %pad_maximum_fusion.1.refs_2_.refs_0_), channel_id=1, source_target_pairs={{0,1},{1,0},{2,3},{3,2},{4,5},{5,4},{6,7},{7,6},{8,9},{9,8},{10,11... | collective-permute-start | bytes 1572872 | tf_op jit(solution)/shard_map/ppermute | solution.py:222
  88.6 42.1 %collective-permute-start.18 = (bf16[4,2,128,256]{3,2,1,0:T(8,128)(2,1)S(1)}, bf16[4,2,128,256]{3,2,1,0:T(8,128)(2,1)S(1)}, u32[]{:S(2)}, u32[]{:S(2)}) collective-permute-start(bf16[4,2,128,256]{3,2,1,0:T(8,128)(2,1)S(1)} %collective-permute-done.14.refs_4_.refs_2_), channel_id=1, source_target_pairs={{0,1},{1,0},{2,3},{3,2},{4,5},{5,4},{6,7},{7,6},{8,9},{9,8},{10,11... | collective-permute-start | bytes 1572872 | tf_op jit(solution)/shard_map/ppermute | solution.py:222
  89.1 41.6 %collective-permute-start.19 = (bf16[4,2,128,256]{3,2,1,0:T(8,128)(2,1)S(1)}, bf16[4,2,128,256]{3,2,1,0:T(8,128)(2,1)S(1)}, u32[]{:S(2)}, u32[]{:S(2)}) collective-permute-start(bf16[4,2,128,256]{3,2,1,0:T(8,128)(2,1)S(1)} %collective-permute-done.15.refs_6_.refs_4_), channel_id=1, source_target_pairs={{0,1},{1,0},{2,3},{3,2},{4,5},{5,4},{6,7},{7,6},{8,9},{9,8},{10,11... | collective-permute-start | bytes 1572872 | tf_op jit(solution)/shard_map/ppermute | solution.py:222
  129.3 16.7 %collective-permute-start.13 = (bf16[8,128,256]{2,1,0:T(8,128)(2,1)S(1)}, bf16[8,128,256]{2,1,0:T(8,128)(2,1)S(1)}, u32[]{:S(2)}, u32[]{:S(2)}) collective-permute-start(bf16[8,128,256]{2,1,0:T(8,128)(2,1)S(1)} %multiply_convert_fusion.1.refs_2_.refs_8_), channel_id=1, source_target_pairs={{0,24},{8,16},{16,8},{24,0},{1,25},{9,17},{17,9},{25,1},{2,26},{10... | collective-permute-start | bytes 1572872 | tf_op jit(solution)/shard_map/ppermute | solution.py:226
  139.9 16.9 %collective-permute-start.21 = (bf16[8,128,256]{2,1,0:T(8,128)(2,1)}, bf16[8,128,256]{2,1,0:T(8,128)(2,1)S(1)}, u32[]{:S(2)}, u32[]{:S(2)}) collective-permute-start(bf16[8,128,256]{2,1,0:T(8,128)(2,1)} %get-tuple-element.76), channel_id=1, source_target_pairs={{0,24},{8,16},{16,8},{24,0},{1,25},{9,17},{17,9},{25,1},{2,26},{10... | collective-permute-start | bytes 1572872 | tf_op jit(solution)/shard_map/ppermute | solution.py:226
  157.5 27.4 %collective-permute-start.27 = (bf16[8,128,256]{2,1,0:T(8,128)(2,1)S(1)}, bf16[8,128,256]{2,1,0:T(8,128)(2,1)S(1)}, u32[]{:S(2)}, u32[]{:S(2)}) collective-permute-start(bf16[8,128,256]{2,1,0:T(8,128)(2,1)S(1)} %multiply_convert_fusion.refs_2_.refs_8_), channel_id=1, source_target_pairs={{0,24},{8,16},{16,8},{24,0},{1,25},{9,17},{17,9},{25,1},{2,26},{10... | collective-permute-start | bytes 1572872 | tf_op jit(solution)/shard_map/ppermute | solution.py:226
  159.2 25.6 %collective-permute-start.28 = (bf16[8,128,256]{2,1,0:T(8,128)(2,1)S(1)}, bf16[8,128,256]{2,1,0:T(8,128)(2,1)S(1)}, u32[]{:S(2)}, u32[]{:S(2)}) collective-permute-start(bf16[8,128,256]{2,1,0:T(8,128)(2,1)S(1)} %copy-done.5), channel_id=1, source_target_pairs={{0,8},{8,0},{16,24},{24,16},{1,9},{9,1},{17,25},{25,17},{2,10},{10... | collective-permute-start | bytes 1572872 | tf_op jit(solution)/shard_map/ppermute | solution.py:226
  193.6 36.0 %collective-permute-start.34 = (bf16[8,128,256]{2,1,0:T(8,128)(2,1)}, bf16[8,128,256]{2,1,0:T(8,128)(2,1)S(1)}, u32[]{:S(2)}, u32[]{:S(2)}) collective-permute-start(bf16[8,128,256]{2,1,0:T(8,128)(2,1)} %copy-done.3), channel_id=1, source_target_pairs={{0,8},{8,0},{16,24},{24,16},{1,9},{9,1},{17,25},{25,17},{2,10},{10... | collective-permute-start | bytes 1572872 | tf_op jit(solution)/shard_map/ppermute | solution.py:226
  194.1 25.7 %collective-permute-start.33 = (bf16[8,128,256]{2,1,0:T(8,128)(2,1)S(1)}, bf16[8,128,256]{2,1,0:T(8,128)(2,1)S(1)}, u32[]{:S(2)}, u32[]{:S(2)}) collective-permute-start(bf16[8,128,256]{2,1,0:T(8,128)(2,1)S(1)} %copy-done.23), channel_id=1, source_target_pairs={{0,8},{8,0},{16,24},{24,16},{1,9},{9,1},{17,25},{25,17},{2,10},{10... | collective-permute-start | bytes 1572872 | tf_op jit(solution)/shard_map/ppermute | solution.py:226
  195.6 35.7 %collective-permute-start.35 = (bf16[8,128,256]{2,1,0:T(8,128)(2,1)}, bf16[8,128,256]{2,1,0:T(8,128)(2,1)S(1)}, u32[]{:S(2)}, u32[]{:S(2)}) collective-permute-start(bf16[8,128,256]{2,1,0:T(8,128)(2,1)} %copy-done.21), channel_id=1, source_target_pairs={{0,8},{8,0},{16,24},{24,16},{1,9},{9,1},{17,25},{25,17},{2,10},{10... | collective-permute-start | bytes 1572872 | tf_op jit(solution)/shard_map/ppermute | solution.py:226
  198.1 33.3 %collective-permute-start.30 = (bf16[2,2,128,256]{3,2,1,0:T(8,128)(2,1)S(1)}, bf16[2,2,128,256]{3,2,1,0:T(8,128)(2,1)S(1)}, u32[]{:S(2)}, u32[]{:S(2)}) collective-permute-start(bf16[2,2,128,256]{3,2,1,0:T(8,128)(2,1)S(1)} %get-tuple-element.110), channel_id=1, source_target_pairs={{0,2},{1,3},{2,0},{3,1},{4,6},{5,7},{6,4},{7,5},{8,10},{9,11},{10,... | collective-permute-start | bytes 786440 | tf_op jit(solution)/shard_map/ppermute | solution.py:222
  199.6 31.8 %collective-permute-start.31 = (bf16[2,2,128,256]{3,2,1,0:T(8,128)(2,1)S(1)}, bf16[2,2,128,256]{3,2,1,0:T(8,128)(2,1)S(1)}, u32[]{:S(2)}, u32[]{:S(2)}) collective-permute-start(bf16[2,2,128,256]{3,2,1,0:T(8,128)(2,1)S(1)} %get-tuple-element.109), channel_id=1, source_target_pairs={{0,4},{1,5},{2,6},{3,7},{4,0},{5,1},{6,2},{7,3},{8,12},{9,13},{10,... | collective-permute-start | bytes 786440 | tf_op jit(solution)/shard_map/ppermute | solution.py:222
  (46 other events, 713.0 us)

commit v12 on v11

--- a/solution.py
+++ b/solution.py
@@ -256,9 +256,8 @@
     return add(even, swap_col(odd, 1)).astype(jnp.bfloat16)
 
 
-def finish_col(pairs, *wait):
-    sums = [pairs[0]] + [swap_col(pairs[m], 2 * m) for m in range(1, pairs.shape[0])]
-    return add(*after(sums, *wait)).astype(jnp.bfloat16)
+def col_terms(pairs):
+    return [pairs[0]] + [swap_col(pairs[m], 2 * m) for m in range(1, pairs.shape[0])]
 
 
 def rows_first(total):
@@ -320,19 +319,22 @@
     grad_far = swap_row(grad_hidden, 3)
     activ, activ_far = after((activ, activ_far), grad_hidden)
     all_activ = [activ, swap_row(activ, 1), swap_row(activ_far, 1), activ_far]
-    layer_sums = finish_col(pair_sums(*after(layer_parts, grad_hidden)))
+    layer_terms = col_terms(pair_sums(*after(layer_parts, grad_hidden)))
+    layer_sums = add(*layer_terms).astype(jnp.bfloat16)
     ends_grad = after([grad_hidden, grad_far], layer_sums, all_activ[1])
     input_parts = from_hidden(info_in, ends_grad, in_pair, cols, True, ends, devices)
     layer_far = swap_row(layer_sums[1], 3)
     input_pairs = pair_sums(*input_parts)
-    all_activ = after(all_activ, input_pairs)
+    input_terms = col_terms(input_pairs)
+    all_activ = after(all_activ, input_terms)
     grad_w_out = slot_grads(info_out, all_up, all_activ, slots, cols, False)
+    grad_hidden, grad_far = after((grad_hidden, grad_far), input_pairs)
     near, far = swap_row(grad_hidden, 1), swap_row(grad_far, 1)
-    input_sums = finish_col(input_pairs, grad_w_out, near, far)
+    input_sums = add(*after(input_terms, grad_w_out, near, far)).astype(jnp.bfloat16)
     all_grad = after([grad_hidden, near, far, grad_far], input_sums)
     grad_w_in = slot_grads(info_in, all_tokens, all_grad, slots, cols, True)
     input_far = after(swap_row(input_sums[1], 3), grad_w_in)
-    layer_out = rows_first(add(layer_sums[0], after(layer_far, input_sums)))
+    layer_out = rows_first(add(layer_sums[0], after(layer_far, grad_w_in)))
     grad_tokens = rows_first(add(input_sums[0], input_far))
     return layer_out, grad_tokens, grad_w_in, grad_w_out
 

time: 249 us -> 248 us (level)
  starting transfers between devices: 50 us -> 43.9 us
  waiting for transfers between devices: 136 us -> 141 us
    ppermute x22, waiting for transfers between devices: 41.1 us -> 48.1 us  [swap_col(): return lax.ppermute(x, 'col', [(s, s ^ m) for s in range(count)])]
    ppermute x15, starting transfers between devices: 32.6 us -> 27.4 us  [swap_row(): return lax.ppermute(x, 'row', [(s, s ^ t) for s in range(4)])]
    unnamed x70 -> x74, local copies, waits for them, and re-layouts: 6.55 us -> 7.96 us
  transfers between devices with their start and end apart: 37 -> 37, of which waited for: 18 -> 22; matrix products, arithmetic and copies ran while one was open for 3% -> 3% of each run, Pallas kernels for 15% -> 15%
where the time goes in v12:
time: 248 us
  waiting for transfers between devices  141 us (57%)
  Pallas kernels  45.7 us (18%)
  starting transfers between devices  43.9 us (18%)
  local copies, waits for them, and re-layouts  9.37 us (4%)
  other arithmetic  6.4 us (3%)
    ppermute x15, waiting for transfers between devices, swap_row(): return lax.ppermute(x, 'row', [(s, s ^ t) for s in range(4)])  93.2 us
    ppermute x22, waiting for transfers between devices, swap_col(): return lax.ppermute(x, 'col', [(s, s ^ m) for s in range(count)])  48.1 us
    pallas_call x6, Pallas kernels, call(): pl.pallas_call(kernel, out_shape=out_shape, in_specs=[pl.BlockSpec(memory...  45.7 us
    ppermute x15, starting transfers between devices, swap_row(): return lax.ppermute(x, 'row', [(s, s ^ t) for s in range(4)])  27.4 us
    ppermute x22, starting transfers between devices, swap_col(): return lax.ppermute(x, 'col', [(s, s ^ m) for s in range(count)])  16.5 us
    unnamed x74, local copies, waits for them, and re-layouts  7.96 us
  transfers between devices with their start and end apart: 37, of which 22 were waited for; matrix products, arithmetic and copies ran while one was open for 3% of the time, Pallas kernels for 15%

profile of v12, /device:TPU:0, one launch (start us, length us, event | category | flops | bytes accessed | tf_op | source)
XLA Modules:
  0.0 247.8 jit_solution(13655683108066654284)
XLA Ops:
  3.1 5.1 %collective-permute-start.2 = (bf16[2,2,128,256]{3,2,1,0:T(8,128)(2,1)S(1)}, bf16[2,2,128,256]{3,2,1,0:T(8,128)(2,1)S(1)}, u32[]{:S(2)}, u32[]{:S(2)}) collective-permute-start(bf16[2,2,128,256]{3,2,1,0:T(8,128)(2,1)S(1)} %pad_maximum_fusion.2), channel_id=1, source_target_pairs={{0,24},{8,16},{16,8},{24,0},{1,25},{9,17},{17,9},{25,1},{2,26},{10... | collective-permute-start | bytes 786440 | tf_op jit(solution)/shard_map/ppermute | solution.py:226
  10.3 5.2 %collective-permute-done.2 = bf16[2,2,128,256]{3,2,1,0:T(8,128)(2,1)S(1)} collective-permute-done((bf16[2,2,128,256]{3,2,1,0:T(8,128)(2,1)S(1)}, bf16[2,2,128,256]{3,2,1,0:T(8,128)(2,1)S(1)}, u32[]{:S(2)}, u32[]{:S(2)}) %collective-permute-start.2) | collective-permute-done | bytes 262176 | tf_op jit(solution)/shard_map/ppermute | solution.py:226
  15.6 15.1 %collective-permute-done.1 = bf16[2,2,128,256]{3,2,1,0:T(8,128)(2,1)S(1)} collective-permute-done((bf16[2,2,128,256]{3,2,1,0:T(8,128)(2,1)S(1)}, bf16[2,2,128,256]{3,2,1,0:T(8,128)(2,1)S(1)}, u32[]{:S(2)}, u32[]{:S(2)}) %collective-permute-start.1) | collective-permute-done | bytes 262176 | tf_op jit(solution)/shard_map/ppermute | solution.py:226
  35.0 12.3 %collective-permute-done.8.refs_8_.refs_6_ = bf16[4,2,128,256]{3,2,1,0:T(8,128)(2,1)S(1)} collective-permute-done((bf16[4,2,128,256]{3,2,1,0:T(8,128)(2,1)S(1)}, bf16[4,2,128,256]{3,2,1,0:T(8,128)(2,1)S(1)}, u32[]{:S(2)}, u32[]{:S(2)}) %collective-permute-start.8) | collective-permute-done | bytes 524320 | tf_op jit(solution)/shard_map/ppermute | solution.py:222
  47.3 9.2 %collective-permute-done.6.refs_6_.refs_4_ = bf16[4,2,128,256]{3,2,1,0:T(8,128)(2,1)S(1)} collective-permute-done((bf16[4,2,128,256]{3,2,1,0:T(8,128)(2,1)S(1)}, bf16[4,2,128,256]{3,2,1,0:T(8,128)(2,1)S(1)}, u32[]{:S(2)}, u32[]{:S(2)}) %collective-permute-start.6) | collective-permute-done | bytes 524320 | tf_op jit(solution)/shard_map/ppermute | solution.py:222
  65.3 6.0 %collective-permute-done.11.refs_1_ = bf16[16,256,256]{2,1,0:T(8,128)(2,1)} collective-permute-done((bf16[16,256,256]{2,1,0:T(8,128)(2,1)}, bf16[16,256,256]{2,1,0:T(8,128)(2,1)}, u32[]{:S(2)}, u32[]{:S(2)}) %collective-permute-start.11) | collective-permute-done | bytes 2097184 | tf_op jit(solution)/shard_map/ppermute | solution.py:226
  71.3 7.7 %shard_map.93 = (bf16[8,128,256]{2,1,0:T(8,128)(2,1)}, bf16[8,128,256]{2,1,0:T(8,128)(2,1)}) custom-call(s32[34]{0:T(128)} %pad_add_fusion.2.info, bf16[16,256,256]{2,1,0:T(8,128)(2,1)} %bitcast.65, bf16[16,256,256]{2,1,0:T(8,128)(2,1)} %collective-permute-done.11.refs_1_, bf16[4,2,128,256]{3,2,1,0:T(8,128)(2,1)} %copy-done.1, ...), custom_call_target="tpu_custom_call" | custom-call | flops 1073741824 | bytes 8388608 | tf_op jit(solution)/shard_map/pallas_call | solution.py:146
  79.0 3.3 %collective-permute-start.12 = (bf16[8,128,256]{2,1,0:T(8,128)(2,1)}, bf16[8,128,256]{2,1,0:T(8,128)(2,1)S(1)}, u32[]{:S(2)}, u32[]{:S(2)}) collective-permute-start(bf16[8,128,256]{2,1,0:T(8,128)(2,1)} %get-tuple-element.55), channel_id=1, source_target_pairs={{0,24},{8,16},{16,8},{24,0},{1,25},{9,17},{17,9},{25,1},{2,26},{10... | collective-permute-start | bytes 1572872 | tf_op jit(solution)/shard_map/ppermute | solution.py:226
  82.3 5.6 %collective-permute-done.15.refs_6_.refs_4_ = bf16[4,2,128,256]{3,2,1,0:T(8,128)(2,1)S(1)} collective-permute-done((bf16[4,2,128,256]{3,2,1,0:T(8,128)(2,1)S(1)}, bf16[4,2,128,256]{3,2,1,0:T(8,128)(2,1)S(1)}, u32[]{:S(2)}, u32[]{:S(2)}) %collective-permute-start.15) | collective-permute-done | bytes 524320 | tf_op jit(solution)/shard_map/ppermute | solution.py:222
  88.6 38.4 %collective-permute-done.12 = bf16[8,128,256]{2,1,0:T(8,128)(2,1)S(1)} collective-permute-done((bf16[8,128,256]{2,1,0:T(8,128)(2,1)}, bf16[8,128,256]{2,1,0:T(8,128)(2,1)S(1)}, u32[]{:S(2)}, u32[]{:S(2)}) %collective-permute-start.12) | collective-permute-done | bytes 524320 | tf_op jit(solution)/shard_map/ppermute | solution.py:226
  129.0 3.7 %collective-permute-start.13 = (bf16[8,128,256]{2,1,0:T(8,128)(2,1)S(1)}, bf16[8,128,256]{2,1,0:T(8,128)(2,1)S(1)}, u32[]{:S(2)}, u32[]{:S(2)}) collective-permute-start(bf16[8,128,256]{2,1,0:T(8,128)(2,1)S(1)} %multiply_convert_fusion.1.refs_2_.refs_8_), channel_id=1, source_target_pairs={{0,24},{8,16},{16,8},{24,0},{1,25},{9,17},{17,9},{25,1},{2,26},{10... | collective-permute-start | bytes 1572872 | tf_op jit(solution)/shard_map/ppermute | solution.py:226
  133.9 8.0 %shard_map.94 = (bf16[8,128,256]{2,1,0:T(8,128)(2,1)}, bf16[8,128,256]{2,1,0:T(8,128)(2,1)}) custom-call(s32[34]{0:T(128)} %pad_add_fusion.info, bf16[16,256,256]{2,1,0:T(8,128)(2,1)} %bitcast.61, bf16[16,256,256]{2,1,0:T(8,128)(2,1)} %collective-permute-done.10.refs_1_, bf16[4,2,128,256]{3,2,1,0:T(8,128)(2,1)} %copy-done.2, ...), custom_call_target="tpu_custom_call" | custom-call | flops 1073741824 | bytes 8388608 | tf_op jit(solution)/shard_map/pallas_call | solution.py:146
  146.2 7.6 %shard_map.95 = (bf16[4,2,2,128,256]{4,3,2,1,0:T(8,128)(2,1)}, bf16[4,2,2,128,256]{4,3,2,1,0:T(8,128)(2,1)}) custom-call(s32[34]{0:T(128)} %pad_add_fusion.info, bf16[16,256,256]{2,1,0:T(8,128)(2,1)} %bitcast.62, bf16[16,256,256]{2,1,0:T(8,128)(2,1)} %collective-permute-done.10.refs_1_, bf16[8,128,256]{2,1,0:T(8,128)(2,1)} %copy-done.3, ...), custom_call_target="tpu_custom_call" | custom-call | flops 1073741824 | bytes 8388608 | tf_op jit(solution)/shard_map/pallas_call | solution.py:146
  153.8 4.2 %collective-permute-done.21 = bf16[8,128,256]{2,1,0:T(8,128)(2,1)S(1)} collective-permute-done((bf16[8,128,256]{2,1,0:T(8,128)(2,1)}, bf16[8,128,256]{2,1,0:T(8,128)(2,1)S(1)}, u32[]{:S(2)}, u32[]{:S(2)}) %collective-permute-start.21) | collective-permute-done | bytes 524320 | tf_op jit(solution)/shard_map/ppermute | solution.py:226
  160.9 3.8 %collective-permute-start.28 = (bf16[8,128,256]{2,1,0:T(8,128)(2,1)S(1)}, bf16[8,128,256]{2,1,0:T(8,128)(2,1)S(1)}, u32[]{:S(2)}, u32[]{:S(2)}) collective-permute-start(bf16[8,128,256]{2,1,0:T(8,128)(2,1)S(1)} %copy-done.4), channel_id=1, source_target_pairs={{0,8},{8,0},{16,24},{24,16},{1,9},{9,1},{17,25},{25,17},{2,10},{10... | collective-permute-start | bytes 1572872 | tf_op jit(solution)/shard_map/ppermute | solution.py:226
  168.6 5.7 %collective-permute-done.23 = bf16[2,2,128,256]{3,2,1,0:T(8,128)(2,1)S(1)} collective-permute-done((bf16[2,2,128,256]{3,2,1,0:T(8,128)(2,1)S(1)}, bf16[2,2,128,256]{3,2,1,0:T(8,128)(2,1)S(1)}, u32[]{:S(2)}, u32[]{:S(2)}) %collective-permute-start.23) | collective-permute-done | bytes 262176 | tf_op jit(solution)/shard_map/ppermute | solution.py:222
  174.3 5.6 %collective-permute-done.25 = bf16[2,2,128,256]{3,2,1,0:T(8,128)(2,1)S(1)} collective-permute-done((bf16[2,2,128,256]{3,2,1,0:T(8,128)(2,1)S(1)}, bf16[2,2,128,256]{3,2,1,0:T(8,128)(2,1)S(1)}, u32[]{:S(2)}, u32[]{:S(2)}) %collective-permute-start.25) | collective-permute-done | bytes 262176 | tf_op jit(solution)/shard_map/ppermute | solution.py:222
  181.4 4.7 %collective-permute-done.28.refs_9_ = bf16[8,128,256]{2,1,0:T(8,128)(2,1)S(1)} collective-permute-done((bf16[8,128,256]{2,1,0:T(8,128)(2,1)S(1)}, bf16[8,128,256]{2,1,0:T(8,128)(2,1)S(1)}, u32[]{:S(2)}, u32[]{:S(2)}) %collective-permute-start.28) | collective-permute-done | bytes 524320 | tf_op jit(solution)/shard_map/ppermute | solution.py:226
  187.0 7.8 %shard_map.96 = (bf16[4,2,2,128,256]{4,3,2,1,0:T(8,128)(2,1)}, bf16[4,2,2,128,256]{4,3,2,1,0:T(8,128)(2,1)}) custom-call(s32[34]{0:T(128)} %pad_add_fusion.2.info, bf16[16,256,256]{2,1,0:T(8,128)(2,1)} %bitcast.66, bf16[16,256,256]{2,1,0:T(8,128)(2,1)} %collective-permute-done.11.refs_1_, bf16[8,128,256]{2,1,0:T(8,128)(2,1)} %copy-done.5, ...), custom_call_target="tpu_custom_call" | custom-call | flops 1073741824 | bytes 8388608 | tf_op jit(solution)/shard_map/pallas_call | solution.py:146
  204.5 5.2 %collective-permute-done.35.refs_10_ = bf16[8,128,256]{2,1,0:T(8,128)(2,1)S(1)} collective-permute-done((bf16[8,128,256]{2,1,0:T(8,128)(2,1)S(1)}, bf16[8,128,256]{2,1,0:T(8,128)(2,1)S(1)}, u32[]{:S(2)}, u32[]{:S(2)}) %collective-permute-start.35) | collective-permute-done | bytes 524320 | tf_op jit(solution)/shard_map/ppermute | solution.py:226
  217.1 7.3 %shard_map.97 = bf16[16,256,256]{2,1,0:T(8,128)(2,1)} custom-call(s32[34]{0:T(128)} %pad_add_fusion.info, bf16[4,2,128,256]{3,2,1,0:T(8,128)(2,1)} %copy-done.2, bf16[4,2,128,256]{3,2,1,0:T(8,128)(2,1)} %copy-done.17, bf16[4,2,128,256]{3,2,1,0:T(8,128)(2,1)} %copy-done.16, bf16[4,2,128,256]{3,2,1,0:T(8,128)(2,1)} %copy-done.18, ...), custom_call_target="tpu_custom_call" | custom-call | flops 1073741824 | bytes 8388608 | tf_op jit(solution)/shard_map/pallas_call | solution.py:146
  224.4 7.2 %collective-permute-done.31.refs_10_ = bf16[8,128,256]{2,1,0:T(8,128)(2,1)S(1)} collective-permute-done((bf16[8,128,256]{2,1,0:T(8,128)(2,1)S(1)}, bf16[8,128,256]{2,1,0:T(8,128)(2,1)S(1)}, u32[]{:S(2)}, u32[]{:S(2)}) %collective-permute-start.31) | collective-permute-done | bytes 524320 | tf_op jit(solution)/shard_map/ppermute | solution.py:226
  232.5 7.3 %shard_map.98 = bf16[16,256,256]{2,1,0:T(8,128)(2,1)} custom-call(s32[34]{0:T(128)} %pad_add_fusion.2.info, bf16[4,2,128,256]{3,2,1,0:T(8,128)(2,1)} %copy-done.1, bf16[4,2,128,256]{3,2,1,0:T(8,128)(2,1)} %copy-done.10, bf16[4,2,128,256]{3,2,1,0:T(8,128)(2,1)} %copy-done.9, bf16[4,2,128,256]{3,2,1,0:T(8,128)(2,1)} %copy-done.13, ...), custom_call_target="tpu_custom_call" | custom-call | flops 1073741824 | bytes 8388608 | tf_op jit(solution)/shard_map/pallas_call | solution.py:146
  243.1 3.8 %collective-permute-done.36 = bf16[2,128,256]{2,1,0:T(8,128)(2,1)S(1)} collective-permute-done((bf16[2,128,256]{2,1,0:T(8,128)(2,1)S(1)}, bf16[2,128,256]{2,1,0:T(8,128)(2,1)S(1)}, u32[]{:S(2)}, u32[]{:S(2)}) %collective-permute-start.36) | collective-permute-done | bytes 131104 | tf_op jit(solution)/shard_map/ppermute | solution.py:226
  (155 shorter events, 56.7 us)
Async XLA Ops:
  8.3 22.4 %collective-permute-start.1 = (bf16[2,2,128,256]{3,2,1,0:T(8,128)(2,1)S(1)}, bf16[2,2,128,256]{3,2,1,0:T(8,128)(2,1)S(1)}, u32[]{:S(2)}, u32[]{:S(2)}) collective-permute-start(bf16[2,2,128,256]{3,2,1,0:T(8,128)(2,1)S(1)} %pad_maximum_fusion.2), channel_id=1, source_target_pairs={{0,16},{8,24},{16,0},{24,8},{1,17},{9,25},{17,1},{25,9},{2,18},{10... | collective-permute-start | bytes 786440 | tf_op jit(solution)/shard_map/ppermute | solution.py:226
  8.3 22.4 %collective-permute-start = (bf16[2,2,128,256]{3,2,1,0:T(8,128)(2,1)S(1)}, bf16[2,2,128,256]{3,2,1,0:T(8,128)(2,1)S(1)}, u32[]{:S(2)}, u32[]{:S(2)}) collective-permute-start(bf16[2,2,128,256]{3,2,1,0:T(8,128)(2,1)S(1)} %pad_maximum_fusion.2), channel_id=1, source_target_pairs={{0,8},{8,0},{16,24},{24,16},{1,9},{9,1},{17,25},{25,17},{2,10},{10... | collective-permute-start | bytes 786440 | tf_op jit(solution)/shard_map/ppermute | solution.py:226
  8.9 62.4 %collective-permute-start.11 = (bf16[16,256,256]{2,1,0:T(8,128)(2,1)}, bf16[16,256,256]{2,1,0:T(8,128)(2,1)}, u32[]{:S(2)}, u32[]{:S(2)}) collective-permute-start(bf16[16,256,256]{2,1,0:T(8,128)(2,1)} %bitcast.64), channel_id=1, source_target_pairs={{0,8},{8,0},{16,24},{24,16},{1,9},{9,1},{17,25},{25,17},{2,10},{10... | collective-permute-start | bytes 6291464 | tf_op jit(solution)/shard_map/ppermute | solution.py:226
  31.5 15.9 %collective-permute-start.8 = (bf16[4,2,128,256]{3,2,1,0:T(8,128)(2,1)S(1)}, bf16[4,2,128,256]{3,2,1,0:T(8,128)(2,1)S(1)}, u32[]{:S(2)}, u32[]{:S(2)}) collective-permute-start(bf16[4,2,128,256]{3,2,1,0:T(8,128)(2,1)S(1)} %pad_maximum_fusion.refs_2_.refs_0_), channel_id=1, source_target_pairs={{0,6},{1,7},{2,4},{3,5},{4,2},{5,3},{6,0},{7,1},{8,14},{9,15},{10,... | collective-permute-start | bytes 1572872 | tf_op jit(solution)/shard_map/ppermute | solution.py:222
  34.0 22.6 %collective-permute-start.6 = (bf16[4,2,128,256]{3,2,1,0:T(8,128)(2,1)S(1)}, bf16[4,2,128,256]{3,2,1,0:T(8,128)(2,1)S(1)}, u32[]{:S(2)}, u32[]{:S(2)}) collective-permute-start(bf16[4,2,128,256]{3,2,1,0:T(8,128)(2,1)S(1)} %pad_maximum_fusion.refs_2_.refs_0_), channel_id=1, source_target_pairs={{0,4},{1,5},{2,6},{3,7},{4,0},{5,1},{6,2},{7,3},{8,12},{9,13},{10,... | collective-permute-start | bytes 1572872 | tf_op jit(solution)/shard_map/ppermute | solution.py:222
  34.5 22.2 %collective-permute-start.4 = (bf16[4,2,128,256]{3,2,1,0:T(8,128)(2,1)S(1)}, bf16[4,2,128,256]{3,2,1,0:T(8,128)(2,1)S(1)}, u32[]{:S(2)}, u32[]{:S(2)}) collective-permute-start(bf16[4,2,128,256]{3,2,1,0:T(8,128)(2,1)S(1)} %pad_maximum_fusion.refs_2_.refs_0_), channel_id=1, source_target_pairs={{0,2},{1,3},{2,0},{3,1},{4,6},{5,7},{6,4},{7,5},{8,10},{9,11},{10,... | collective-permute-start | bytes 1572872 | tf_op jit(solution)/shard_map/ppermute | solution.py:222
  35.0 22.1 %collective-permute-start.3 = (bf16[4,2,128,256]{3,2,1,0:T(8,128)(2,1)S(1)}, bf16[4,2,128,256]{3,2,1,0:T(8,128)(2,1)S(1)}, u32[]{:S(2)}, u32[]{:S(2)}) collective-permute-start(bf16[4,2,128,256]{3,2,1,0:T(8,128)(2,1)S(1)} %pad_maximum_fusion.refs_2_.refs_0_), channel_id=1, source_target_pairs={{0,1},{1,0},{2,3},{3,2},{4,5},{5,4},{6,7},{7,6},{8,9},{9,8},{10,11... | collective-permute-start | bytes 1572872 | tf_op jit(solution)/shard_map/ppermute | solution.py:222
  59.3 73.5 %collective-permute-start.10 = (bf16[16,256,256]{2,1,0:T(8,128)(2,1)S(1)}, bf16[16,256,256]{2,1,0:T(8,128)(2,1)}, u32[]{:S(2)}, u32[]{:S(2)}) collective-permute-start(bf16[16,256,256]{2,1,0:T(8,128)(2,1)S(1)} %bitcast.63), channel_id=1, source_target_pairs={{0,8},{8,0},{16,24},{24,16},{1,9},{9,1},{17,25},{25,17},{2,10},{10... | collective-permute-start | bytes 6291464 | tf_op jit(solution)/shard_map/ppermute | solution.py:226
  61.7 20.6 %collective-permute-start.16 = (bf16[4,2,128,256]{3,2,1,0:T(8,128)(2,1)S(1)}, bf16[4,2,128,256]{3,2,1,0:T(8,128)(2,1)S(1)}, u32[]{:S(2)}, u32[]{:S(2)}) collective-permute-start(bf16[4,2,128,256]{3,2,1,0:T(8,128)(2,1)S(1)} %pad_maximum_fusion.1.refs_2_.refs_0_), channel_id=1, source_target_pairs={{0,6},{1,7},{2,4},{3,5},{4,2},{5,3},{6,0},{7,1},{8,14},{9,15},{10,... | collective-permute-start | bytes 1572872 | tf_op jit(solution)/shard_map/ppermute | solution.py:222
  63.5 24.4 %collective-permute-start.15 = (bf16[4,2,128,256]{3,2,1,0:T(8,128)(2,1)S(1)}, bf16[4,2,128,256]{3,2,1,0:T(8,128)(2,1)S(1)}, u32[]{:S(2)}, u32[]{:S(2)}) collective-permute-start(bf16[4,2,128,256]{3,2,1,0:T(8,128)(2,1)S(1)} %pad_maximum_fusion.1.refs_2_.refs_0_), channel_id=1, source_target_pairs={{0,4},{1,5},{2,6},{3,7},{4,0},{5,1},{6,2},{7,3},{8,12},{9,13},{10,... | collective-permute-start | bytes 1572872 | tf_op jit(solution)/shard_map/ppermute | solution.py:222
  64.8 23.2 %collective-permute-start.14 = (bf16[4,2,128,256]{3,2,1,0:T(8,128)(2,1)S(1)}, bf16[4,2,128,256]{3,2,1,0:T(8,128)(2,1)S(1)}, u32[]{:S(2)}, u32[]{:S(2)}) collective-permute-start(bf16[4,2,128,256]{3,2,1,0:T(8,128)(2,1)S(1)} %pad_maximum_fusion.1.refs_2_.refs_0_), channel_id=1, source_target_pairs={{0,2},{1,3},{2,0},{3,1},{4,6},{5,7},{6,4},{7,5},{8,10},{9,11},{10,... | collective-permute-start | bytes 1572872 | tf_op jit(solution)/shard_map/ppermute | solution.py:222
  79.0 48.0 %collective-permute-start.12 = (bf16[8,128,256]{2,1,0:T(8,128)(2,1)}, bf16[8,128,256]{2,1,0:T(8,128)(2,1)S(1)}, u32[]{:S(2)}, u32[]{:S(2)}) collective-permute-start(bf16[8,128,256]{2,1,0:T(8,128)(2,1)} %get-tuple-element.55), channel_id=1, source_target_pairs={{0,24},{8,16},{16,8},{24,0},{1,25},{9,17},{17,9},{25,1},{2,26},{10... | collective-permute-start | bytes 1572872 | tf_op jit(solution)/shard_map/ppermute | solution.py:226
  88.0 41.0 %collective-permute-start.17 = (bf16[4,2,128,256]{3,2,1,0:T(8,128)(2,1)S(1)}, bf16[4,2,128,256]{3,2,1,0:T(8,128)(2,1)S(1)}, u32[]{:S(2)}, u32[]{:S(2)}) collective-permute-start(bf16[4,2,128,256]{3,2,1,0:T(8,128)(2,1)S(1)} %pad_maximum_fusion.1.refs_2_.refs_0_), channel_id=1, source_target_pairs={{0,1},{1,0},{2,3},{3,2},{4,5},{5,4},{6,7},{7,6},{8,9},{9,8},{10,11... | collective-permute-start | bytes 1572872 | tf_op jit(solution)/shard_map/ppermute | solution.py:222
  88.1 44.6 %collective-permute-start.18 = (bf16[4,2,128,256]{3,2,1,0:T(8,128)(2,1)S(1)}, bf16[4,2,128,256]{3,2,1,0:T(8,128)(2,1)S(1)}, u32[]{:S(2)}, u32[]{:S(2)}) collective-permute-start(bf16[4,2,128,256]{3,2,1,0:T(8,128)(2,1)S(1)} %collective-permute-done.14.refs_4_.refs_2_), channel_id=1, source_target_pairs={{0,1},{1,0},{2,3},{3,2},{4,5},{5,4},{6,7},{7,6},{8,9},{9,8},{10,11... | collective-permute-start | bytes 1572872 | tf_op jit(solution)/shard_map/ppermute | solution.py:222
  88.5 44.2 %collective-permute-start.19 = (bf16[4,2,128,256]{3,2,1,0:T(8,128)(2,1)S(1)}, bf16[4,2,128,256]{3,2,1,0:T(8,128)(2,1)S(1)}, u32[]{:S(2)}, u32[]{:S(2)}) collective-permute-start(bf16[4,2,128,256]{3,2,1,0:T(8,128)(2,1)S(1)} %collective-permute-done.15.refs_6_.refs_4_), channel_id=1, source_target_pairs={{0,1},{1,0},{2,3},{3,2},{4,5},{5,4},{6,7},{7,6},{8,9},{9,8},{10,11... | collective-permute-start | bytes 1572872 | tf_op jit(solution)/shard_map/ppermute | solution.py:222
  129.0 16.4 %collective-permute-start.13 = (bf16[8,128,256]{2,1,0:T(8,128)(2,1)S(1)}, bf16[8,128,256]{2,1,0:T(8,128)(2,1)S(1)}, u32[]{:S(2)}, u32[]{:S(2)}) collective-permute-start(bf16[8,128,256]{2,1,0:T(8,128)(2,1)S(1)} %multiply_convert_fusion.1.refs_2_.refs_8_), channel_id=1, source_target_pairs={{0,24},{8,16},{16,8},{24,0},{1,25},{9,17},{17,9},{25,1},{2,26},{10... | collective-permute-start | bytes 1572872 | tf_op jit(solution)/shard_map/ppermute | solution.py:226
  141.9 16.2 %collective-permute-start.21 = (bf16[8,128,256]{2,1,0:T(8,128)(2,1)}, bf16[8,128,256]{2,1,0:T(8,128)(2,1)S(1)}, u32[]{:S(2)}, u32[]{:S(2)}) collective-permute-start(bf16[8,128,256]{2,1,0:T(8,128)(2,1)} %get-tuple-element.74), channel_id=1, source_target_pairs={{0,24},{8,16},{16,8},{24,0},{1,25},{9,17},{17,9},{25,1},{2,26},{10... | collective-permute-start | bytes 1572872 | tf_op jit(solution)/shard_map/ppermute | solution.py:226
  158.7 27.4 %collective-permute-start.27 = (bf16[8,128,256]{2,1,0:T(8,128)(2,1)S(1)}, bf16[8,128,256]{2,1,0:T(8,128)(2,1)S(1)}, u32[]{:S(2)}, u32[]{:S(2)}) collective-permute-start(bf16[8,128,256]{2,1,0:T(8,128)(2,1)S(1)} %multiply_convert_fusion.refs_2_.refs_8_), channel_id=1, source_target_pairs={{0,24},{8,16},{16,8},{24,0},{1,25},{9,17},{17,9},{25,1},{2,26},{10... | collective-permute-start | bytes 1572872 | tf_op jit(solution)/shard_map/ppermute | solution.py:226
  160.9 25.3 %collective-permute-start.28 = (bf16[8,128,256]{2,1,0:T(8,128)(2,1)S(1)}, bf16[8,128,256]{2,1,0:T(8,128)(2,1)S(1)}, u32[]{:S(2)}, u32[]{:S(2)}) collective-permute-start(bf16[8,128,256]{2,1,0:T(8,128)(2,1)S(1)} %copy-done.4), channel_id=1, source_target_pairs={{0,8},{8,0},{16,24},{24,16},{1,9},{9,1},{17,25},{25,17},{2,10},{10... | collective-permute-start | bytes 1572872 | tf_op jit(solution)/shard_map/ppermute | solution.py:226
  166.6 13.3 %collective-permute-start.25 = (bf16[2,2,128,256]{3,2,1,0:T(8,128)(2,1)S(1)}, bf16[2,2,128,256]{3,2,1,0:T(8,128)(2,1)S(1)}, u32[]{:S(2)}, u32[]{:S(2)}) collective-permute-start(bf16[2,2,128,256]{3,2,1,0:T(8,128)(2,1)S(1)} %get-tuple-element.109), channel_id=1, source_target_pairs={{0,6},{1,7},{2,4},{3,5},{4,2},{5,3},{6,0},{7,1},{8,14},{9,15},{10,... | collective-permute-start | bytes 786440 | tf_op jit(solution)/shard_map/ppermute | solution.py:222
  194.9 14.8 %collective-permute-start.35 = (bf16[8,128,256]{2,1,0:T(8,128)(2,1)S(1)}, bf16[8,128,256]{2,1,0:T(8,128)(2,1)S(1)}, u32[]{:S(2)}, u32[]{:S(2)}) collective-permute-start(bf16[8,128,256]{2,1,0:T(8,128)(2,1)S(1)} %copy-done.23), channel_id=1, source_target_pairs={{0,8},{8,0},{16,24},{24,16},{1,9},{9,1},{17,25},{25,17},{2,10},{10... | collective-permute-start | bytes 1572872 | tf_op jit(solution)/shard_map/ppermute | solution.py:226
  199.3 25.1 %collective-permute-start.30 = (bf16[8,128,256]{2,1,0:T(8,128)(2,1)S(1)}, bf16[8,128,256]{2,1,0:T(8,128)(2,1)S(1)}, u32[]{:S(2)}, u32[]{:S(2)}) collective-permute-start(bf16[8,128,256]{2,1,0:T(8,128)(2,1)S(1)} %copy-done.6), channel_id=1, source_target_pairs={{0,8},{8,0},{16,24},{24,16},{1,9},{9,1},{17,25},{25,17},{2,10},{10... | collective-permute-start | bytes 1572872 | tf_op jit(solution)/shard_map/ppermute | solution.py:226
  199.9 31.8 %collective-permute-start.31 = (bf16[8,128,256]{2,1,0:T(8,128)(2,1)S(1)}, bf16[8,128,256]{2,1,0:T(8,128)(2,1)S(1)}, u32[]{:S(2)}, u32[]{:S(2)}) collective-permute-start(bf16[8,128,256]{2,1,0:T(8,128)(2,1)S(1)} %copy-done.25), channel_id=1, source_target_pairs={{0,8},{8,0},{16,24},{24,16},{1,9},{9,1},{17,25},{25,17},{2,10},{10... | collective-permute-start | bytes 1572872 | tf_op jit(solution)/shard_map/ppermute | solution.py:226
  211.2 28.6 %collective-permute-start.26 = (bf16[2,128,256]{2,1,0:T(8,128)(2,1)S(1)}, bf16[2,128,256]{2,1,0:T(8,128)(2,1)S(1)}, u32[]{:S(2)}, u32[]{:S(2)}) collective-permute-start(bf16[2,128,256]{2,1,0:T(8,128)(2,1)S(1)} %slice_bitcast_fusion.10), channel_id=1, source_target_pairs={{0,24},{8,16},{16,8},{24,0},{1,25},{9,17},{17,9},{25,1},{2,26},{10... | collective-permute-start | bytes 393224 | tf_op jit(solution)/shard_map/ppermute | solution.py:226
  (48 other events, 662.2 us)

commit v13 on v12

--- a/solution.py
+++ b/solution.py
@@ -334,7 +334,7 @@
     all_grad = after([grad_hidden, near, far, grad_far], input_sums)
     grad_w_in = slot_grads(info_in, all_tokens, all_grad, slots, cols, True)
     input_far = after(swap_row(input_sums[1], 3), grad_w_in)
-    layer_out = rows_first(add(layer_sums[0], after(layer_far, grad_w_in)))
+    layer_out = rows_first(add(layer_sums[0], after(layer_far, input_sums)))
     grad_tokens = rows_first(add(input_sums[0], input_far))
     return layer_out, grad_tokens, grad_w_in, grad_w_out
 

time: 248 us -> 247 us (level)
  no operation moved by 1% of the time
where the time goes in v13:
time: 247 us; the launch traced here: 246 us
  waiting for transfers between devices  141 us (57%)
  Pallas kernels  45.7 us (19%)
  starting transfers between devices  43.3 us (18%)
  local copies, waits for them, and re-layouts  8.74 us (4%)
  other arithmetic  6.42 us (3%)
    ppermute x15, waiting for transfers between devices, swap_row(): return lax.ppermute(x, 'row', [(s, s ^ t) for s in range(4)])  92.7 us
    ppermute x22, waiting for transfers between devices, swap_col(): return lax.ppermute(x, 'col', [(s, s ^ m) for s in range(count)])  48.1 us
    pallas_call x6, Pallas kernels, call(): pl.pallas_call(kernel, out_shape=out_shape, in_specs=[pl.BlockSpec(memory...  45.7 us
    ppermute x15, starting transfers between devices, swap_row(): return lax.ppermute(x, 'row', [(s, s ^ t) for s in range(4)])  26.8 us
    ppermute x22, starting transfers between devices, swap_col(): return lax.ppermute(x, 'col', [(s, s ^ m) for s in range(count)])  16.5 us
    unnamed x74, local copies, waits for them, and re-layouts  7.32 us
  transfers between devices with their start and end apart: 37, of which 22 were waited for; matrix products, arithmetic and copies ran while one was open for 3% of the time, Pallas kernels for 15%

profile of v13, /device:TPU:0, one launch (start us, length us, event | category | flops | bytes accessed | tf_op | source)
XLA Modules:
  0.0 246.1 jit_solution(10594357341982214823)
XLA Ops:
  3.1 5.1 %collective-permute-start.2 = (bf16[2,2,128,256]{3,2,1,0:T(8,128)(2,1)S(1)}, bf16[2,2,128,256]{3,2,1,0:T(8,128)(2,1)S(1)}, u32[]{:S(2)}, u32[]{:S(2)}) collective-permute-start(bf16[2,2,128,256]{3,2,1,0:T(8,128)(2,1)S(1)} %pad_maximum_fusion.2), channel_id=1, source_target_pairs={{0,24},{8,16},{16,8},{24,0},{1,25},{9,17},{17,9},{25,1},{2,26},{10... | collective-permute-start | bytes 786440 | tf_op jit(solution)/shard_map/ppermute | solution.py:226
  10.3 5.2 %collective-permute-done.2 = bf16[2,2,128,256]{3,2,1,0:T(8,128)(2,1)S(1)} collective-permute-done((bf16[2,2,128,256]{3,2,1,0:T(8,128)(2,1)S(1)}, bf16[2,2,128,256]{3,2,1,0:T(8,128)(2,1)S(1)}, u32[]{:S(2)}, u32[]{:S(2)}) %collective-permute-start.2) | collective-permute-done | bytes 262176 | tf_op jit(solution)/shard_map/ppermute | solution.py:226
  15.6 15.1 %collective-permute-done.1 = bf16[2,2,128,256]{3,2,1,0:T(8,128)(2,1)S(1)} collective-permute-done((bf16[2,2,128,256]{3,2,1,0:T(8,128)(2,1)S(1)}, bf16[2,2,128,256]{3,2,1,0:T(8,128)(2,1)S(1)}, u32[]{:S(2)}, u32[]{:S(2)}) %collective-permute-start.1) | collective-permute-done | bytes 262176 | tf_op jit(solution)/shard_map/ppermute | solution.py:226
  35.0 12.3 %collective-permute-done.8.refs_8_.refs_6_ = bf16[4,2,128,256]{3,2,1,0:T(8,128)(2,1)S(1)} collective-permute-done((bf16[4,2,128,256]{3,2,1,0:T(8,128)(2,1)S(1)}, bf16[4,2,128,256]{3,2,1,0:T(8,128)(2,1)S(1)}, u32[]{:S(2)}, u32[]{:S(2)}) %collective-permute-start.8) | collective-permute-done | bytes 524320 | tf_op jit(solution)/shard_map/ppermute | solution.py:222
  47.3 9.2 %collective-permute-done.6.refs_6_.refs_4_ = bf16[4,2,128,256]{3,2,1,0:T(8,128)(2,1)S(1)} collective-permute-done((bf16[4,2,128,256]{3,2,1,0:T(8,128)(2,1)S(1)}, bf16[4,2,128,256]{3,2,1,0:T(8,128)(2,1)S(1)}, u32[]{:S(2)}, u32[]{:S(2)}) %collective-permute-start.6) | collective-permute-done | bytes 524320 | tf_op jit(solution)/shard_map/ppermute | solution.py:222
  65.3 6.0 %collective-permute-done.11.refs_1_ = bf16[16,256,256]{2,1,0:T(8,128)(2,1)} collective-permute-done((bf16[16,256,256]{2,1,0:T(8,128)(2,1)}, bf16[16,256,256]{2,1,0:T(8,128)(2,1)}, u32[]{:S(2)}, u32[]{:S(2)}) %collective-permute-start.11) | collective-permute-done | bytes 2097184 | tf_op jit(solution)/shard_map/ppermute | solution.py:226
  71.3 7.7 %shard_map.93 = (bf16[8,128,256]{2,1,0:T(8,128)(2,1)}, bf16[8,128,256]{2,1,0:T(8,128)(2,1)}) custom-call(s32[34]{0:T(128)} %pad_add_fusion.2.info, bf16[16,256,256]{2,1,0:T(8,128)(2,1)} %bitcast.65, bf16[16,256,256]{2,1,0:T(8,128)(2,1)} %collective-permute-done.11.refs_1_, bf16[4,2,128,256]{3,2,1,0:T(8,128)(2,1)} %copy-done.1, ...), custom_call_target="tpu_custom_call" | custom-call | flops 1073741824 | bytes 8388608 | tf_op jit(solution)/shard_map/pallas_call | solution.py:146
  79.0 3.3 %collective-permute-start.12 = (bf16[8,128,256]{2,1,0:T(8,128)(2,1)}, bf16[8,128,256]{2,1,0:T(8,128)(2,1)S(1)}, u32[]{:S(2)}, u32[]{:S(2)}) collective-permute-start(bf16[8,128,256]{2,1,0:T(8,128)(2,1)} %get-tuple-element.55), channel_id=1, source_target_pairs={{0,24},{8,16},{16,8},{24,0},{1,25},{9,17},{17,9},{25,1},{2,26},{10... | collective-permute-start | bytes 1572872 | tf_op jit(solution)/shard_map/ppermute | solution.py:226
  82.3 5.6 %collective-permute-done.15.refs_6_.refs_4_ = bf16[4,2,128,256]{3,2,1,0:T(8,128)(2,1)S(1)} collective-permute-done((bf16[4,2,128,256]{3,2,1,0:T(8,128)(2,1)S(1)}, bf16[4,2,128,256]{3,2,1,0:T(8,128)(2,1)S(1)}, u32[]{:S(2)}, u32[]{:S(2)}) %collective-permute-start.15) | collective-permute-done | bytes 524320 | tf_op jit(solution)/shard_map/ppermute | solution.py:222
  88.6 38.4 %collective-permute-done.12 = bf16[8,128,256]{2,1,0:T(8,128)(2,1)S(1)} collective-permute-done((bf16[8,128,256]{2,1,0:T(8,128)(2,1)}, bf16[8,128,256]{2,1,0:T(8,128)(2,1)S(1)}, u32[]{:S(2)}, u32[]{:S(2)}) %collective-permute-start.12) | collective-permute-done | bytes 524320 | tf_op jit(solution)/shard_map/ppermute | solution.py:226
  129.0 3.7 %collective-permute-start.13 = (bf16[8,128,256]{2,1,0:T(8,128)(2,1)S(1)}, bf16[8,128,256]{2,1,0:T(8,128)(2,1)S(1)}, u32[]{:S(2)}, u32[]{:S(2)}) collective-permute-start(bf16[8,128,256]{2,1,0:T(8,128)(2,1)S(1)} %multiply_convert_fusion.1.refs_2_.refs_8_), channel_id=1, source_target_pairs={{0,24},{8,16},{16,8},{24,0},{1,25},{9,17},{17,9},{25,1},{2,26},{10... | collective-permute-start | bytes 1572872 | tf_op jit(solution)/shard_map/ppermute | solution.py:226
  133.9 8.0 %shard_map.94 = (bf16[8,128,256]{2,1,0:T(8,128)(2,1)}, bf16[8,128,256]{2,1,0:T(8,128)(2,1)}) custom-call(s32[34]{0:T(128)} %pad_add_fusion.info, bf16[16,256,256]{2,1,0:T(8,128)(2,1)} %bitcast.61, bf16[16,256,256]{2,1,0:T(8,128)(2,1)} %collective-permute-done.10.refs_1_, bf16[4,2,128,256]{3,2,1,0:T(8,128)(2,1)} %copy-done.2, ...), custom_call_target="tpu_custom_call" | custom-call | flops 1073741824 | bytes 8388608 | tf_op jit(solution)/shard_map/pallas_call | solution.py:146
  146.2 7.6 %shard_map.95 = (bf16[4,2,2,128,256]{4,3,2,1,0:T(8,128)(2,1)}, bf16[4,2,2,128,256]{4,3,2,1,0:T(8,128)(2,1)}) custom-call(s32[34]{0:T(128)} %pad_add_fusion.info, bf16[16,256,256]{2,1,0:T(8,128)(2,1)} %bitcast.62, bf16[16,256,256]{2,1,0:T(8,128)(2,1)} %collective-permute-done.10.refs_1_, bf16[8,128,256]{2,1,0:T(8,128)(2,1)} %copy-done.5, ...), custom_call_target="tpu_custom_call" | custom-call | flops 1073741824 | bytes 8388608 | tf_op jit(solution)/shard_map/pallas_call | solution.py:146
  153.8 4.2 %collective-permute-done.21 = bf16[8,128,256]{2,1,0:T(8,128)(2,1)S(1)} collective-permute-done((bf16[8,128,256]{2,1,0:T(8,128)(2,1)}, bf16[8,128,256]{2,1,0:T(8,128)(2,1)S(1)}, u32[]{:S(2)}, u32[]{:S(2)}) %collective-permute-start.21) | collective-permute-done | bytes 524320 | tf_op jit(solution)/shard_map/ppermute | solution.py:226
  160.9 3.8 %collective-permute-start.28 = (bf16[8,128,256]{2,1,0:T(8,128)(2,1)S(1)}, bf16[8,128,256]{2,1,0:T(8,128)(2,1)S(1)}, u32[]{:S(2)}, u32[]{:S(2)}) collective-permute-start(bf16[8,128,256]{2,1,0:T(8,128)(2,1)S(1)} %copy-done.6), channel_id=1, source_target_pairs={{0,8},{8,0},{16,24},{24,16},{1,9},{9,1},{17,25},{25,17},{2,10},{10... | collective-permute-start | bytes 1572872 | tf_op jit(solution)/shard_map/ppermute | solution.py:226
  168.6 5.7 %collective-permute-done.23 = bf16[2,2,128,256]{3,2,1,0:T(8,128)(2,1)S(1)} collective-permute-done((bf16[2,2,128,256]{3,2,1,0:T(8,128)(2,1)S(1)}, bf16[2,2,128,256]{3,2,1,0:T(8,128)(2,1)S(1)}, u32[]{:S(2)}, u32[]{:S(2)}) %collective-permute-start.23) | collective-permute-done | bytes 262176 | tf_op jit(solution)/shard_map/ppermute | solution.py:222
  174.3 5.6 %collective-permute-done.25 = bf16[2,2,128,256]{3,2,1,0:T(8,128)(2,1)S(1)} collective-permute-done((bf16[2,2,128,256]{3,2,1,0:T(8,128)(2,1)S(1)}, bf16[2,2,128,256]{3,2,1,0:T(8,128)(2,1)S(1)}, u32[]{:S(2)}, u32[]{:S(2)}) %collective-permute-start.25) | collective-permute-done | bytes 262176 | tf_op jit(solution)/shard_map/ppermute | solution.py:222
  181.4 4.7 %collective-permute-done.28.refs_9_ = bf16[8,128,256]{2,1,0:T(8,128)(2,1)S(1)} collective-permute-done((bf16[8,128,256]{2,1,0:T(8,128)(2,1)S(1)}, bf16[8,128,256]{2,1,0:T(8,128)(2,1)S(1)}, u32[]{:S(2)}, u32[]{:S(2)}) %collective-permute-start.28) | collective-permute-done | bytes 524320 | tf_op jit(solution)/shard_map/ppermute | solution.py:226
  187.0 7.8 %shard_map.96 = (bf16[4,2,2,128,256]{4,3,2,1,0:T(8,128)(2,1)}, bf16[4,2,2,128,256]{4,3,2,1,0:T(8,128)(2,1)}) custom-call(s32[34]{0:T(128)} %pad_add_fusion.2.info, bf16[16,256,256]{2,1,0:T(8,128)(2,1)} %bitcast.66, bf16[16,256,256]{2,1,0:T(8,128)(2,1)} %collective-permute-done.11.refs_1_, bf16[8,128,256]{2,1,0:T(8,128)(2,1)} %copy-done.3, ...), custom_call_target="tpu_custom_call" | custom-call | flops 1073741824 | bytes 8388608 | tf_op jit(solution)/shard_map/pallas_call | solution.py:146
  204.5 5.2 %collective-permute-done.33.refs_10_ = bf16[8,128,256]{2,1,0:T(8,128)(2,1)S(1)} collective-permute-done((bf16[8,128,256]{2,1,0:T(8,128)(2,1)S(1)}, bf16[8,128,256]{2,1,0:T(8,128)(2,1)S(1)}, u32[]{:S(2)}, u32[]{:S(2)}) %collective-permute-start.33) | collective-permute-done | bytes 524320 | tf_op jit(solution)/shard_map/ppermute | solution.py:226
  217.1 7.3 %shard_map.97 = bf16[16,256,256]{2,1,0:T(8,128)(2,1)} custom-call(s32[34]{0:T(128)} %pad_add_fusion.info, bf16[4,2,128,256]{3,2,1,0:T(8,128)(2,1)} %copy-done.2, bf16[4,2,128,256]{3,2,1,0:T(8,128)(2,1)} %copy-done.17, bf16[4,2,128,256]{3,2,1,0:T(8,128)(2,1)} %copy-done.16, bf16[4,2,128,256]{3,2,1,0:T(8,128)(2,1)} %copy-done.18, ...), custom_call_target="tpu_custom_call" | custom-call | flops 1073741824 | bytes 8388608 | tf_op jit(solution)/shard_map/pallas_call | solution.py:146
  224.4 7.2 %collective-permute-done.35.refs_10_ = bf16[8,128,256]{2,1,0:T(8,128)(2,1)S(1)} collective-permute-done((bf16[8,128,256]{2,1,0:T(8,128)(2,1)S(1)}, bf16[8,128,256]{2,1,0:T(8,128)(2,1)S(1)}, u32[]{:S(2)}, u32[]{:S(2)}) %collective-permute-start.35) | collective-permute-done | bytes 524320 | tf_op jit(solution)/shard_map/ppermute | solution.py:226
  231.8 3.3 %collective-permute-done.26 = bf16[2,128,256]{2,1,0:T(8,128)(2,1)S(1)} collective-permute-done((bf16[2,128,256]{2,1,0:T(8,128)(2,1)S(1)}, bf16[2,128,256]{2,1,0:T(8,128)(2,1)S(1)}, u32[]{:S(2)}, u32[]{:S(2)}) %collective-permute-start.26) | collective-permute-done | bytes 131104 | tf_op jit(solution)/shard_map/ppermute | solution.py:226
  237.8 7.3 %shard_map.98 = bf16[16,256,256]{2,1,0:T(8,128)(2,1)} custom-call(s32[34]{0:T(128)} %pad_add_fusion.2.info, bf16[4,2,128,256]{3,2,1,0:T(8,128)(2,1)} %copy-done.1, bf16[4,2,128,256]{3,2,1,0:T(8,128)(2,1)} %copy-done.10, bf16[4,2,128,256]{3,2,1,0:T(8,128)(2,1)} %copy-done.9, bf16[4,2,128,256]{3,2,1,0:T(8,128)(2,1)} %copy-done.13, ...), custom_call_target="tpu_custom_call" | custom-call | flops 1073741824 | bytes 8388608 | tf_op jit(solution)/shard_map/pallas_call | solution.py:146
  (155 shorter events, 55.5 us)
Async XLA Ops:
  8.3 22.4 %collective-permute-start.1 = (bf16[2,2,128,256]{3,2,1,0:T(8,128)(2,1)S(1)}, bf16[2,2,128,256]{3,2,1,0:T(8,128)(2,1)S(1)}, u32[]{:S(2)}, u32[]{:S(2)}) collective-permute-start(bf16[2,2,128,256]{3,2,1,0:T(8,128)(2,1)S(1)} %pad_maximum_fusion.2), channel_id=1, source_target_pairs={{0,16},{8,24},{16,0},{24,8},{1,17},{9,25},{17,1},{25,9},{2,18},{10... | collective-permute-start | bytes 786440 | tf_op jit(solution)/shard_map/ppermute | solution.py:226
  8.3 22.4 %collective-permute-start = (bf16[2,2,128,256]{3,2,1,0:T(8,128)(2,1)S(1)}, bf16[2,2,128,256]{3,2,1,0:T(8,128)(2,1)S(1)}, u32[]{:S(2)}, u32[]{:S(2)}) collective-permute-start(bf16[2,2,128,256]{3,2,1,0:T(8,128)(2,1)S(1)} %pad_maximum_fusion.2), channel_id=1, source_target_pairs={{0,8},{8,0},{16,24},{24,16},{1,9},{9,1},{17,25},{25,17},{2,10},{10... | collective-permute-start | bytes 786440 | tf_op jit(solution)/shard_map/ppermute | solution.py:226
  8.9 62.4 %collective-permute-start.11 = (bf16[16,256,256]{2,1,0:T(8,128)(2,1)}, bf16[16,256,256]{2,1,0:T(8,128)(2,1)}, u32[]{:S(2)}, u32[]{:S(2)}) collective-permute-start(bf16[16,256,256]{2,1,0:T(8,128)(2,1)} %bitcast.64), channel_id=1, source_target_pairs={{0,8},{8,0},{16,24},{24,16},{1,9},{9,1},{17,25},{25,17},{2,10},{10... | collective-permute-start | bytes 6291464 | tf_op jit(solution)/shard_map/ppermute | solution.py:226
  31.5 15.9 %collective-permute-start.8 = (bf16[4,2,128,256]{3,2,1,0:T(8,128)(2,1)S(1)}, bf16[4,2,128,256]{3,2,1,0:T(8,128)(2,1)S(1)}, u32[]{:S(2)}, u32[]{:S(2)}) collective-permute-start(bf16[4,2,128,256]{3,2,1,0:T(8,128)(2,1)S(1)} %pad_maximum_fusion.refs_2_.refs_0_), channel_id=1, source_target_pairs={{0,6},{1,7},{2,4},{3,5},{4,2},{5,3},{6,0},{7,1},{8,14},{9,15},{10,... | collective-permute-start | bytes 1572872 | tf_op jit(solution)/shard_map/ppermute | solution.py:222
  34.0 22.6 %collective-permute-start.6 = (bf16[4,2,128,256]{3,2,1,0:T(8,128)(2,1)S(1)}, bf16[4,2,128,256]{3,2,1,0:T(8,128)(2,1)S(1)}, u32[]{:S(2)}, u32[]{:S(2)}) collective-permute-start(bf16[4,2,128,256]{3,2,1,0:T(8,128)(2,1)S(1)} %pad_maximum_fusion.refs_2_.refs_0_), channel_id=1, source_target_pairs={{0,4},{1,5},{2,6},{3,7},{4,0},{5,1},{6,2},{7,3},{8,12},{9,13},{10,... | collective-permute-start | bytes 1572872 | tf_op jit(solution)/shard_map/ppermute | solution.py:222
  34.5 22.2 %collective-permute-start.4 = (bf16[4,2,128,256]{3,2,1,0:T(8,128)(2,1)S(1)}, bf16[4,2,128,256]{3,2,1,0:T(8,128)(2,1)S(1)}, u32[]{:S(2)}, u32[]{:S(2)}) collective-permute-start(bf16[4,2,128,256]{3,2,1,0:T(8,128)(2,1)S(1)} %pad_maximum_fusion.refs_2_.refs_0_), channel_id=1, source_target_pairs={{0,2},{1,3},{2,0},{3,1},{4,6},{5,7},{6,4},{7,5},{8,10},{9,11},{10,... | collective-permute-start | bytes 1572872 | tf_op jit(solution)/shard_map/ppermute | solution.py:222
  35.0 22.1 %collective-permute-start.3 = (bf16[4,2,128,256]{3,2,1,0:T(8,128)(2,1)S(1)}, bf16[4,2,128,256]{3,2,1,0:T(8,128)(2,1)S(1)}, u32[]{:S(2)}, u32[]{:S(2)}) collective-permute-start(bf16[4,2,128,256]{3,2,1,0:T(8,128)(2,1)S(1)} %pad_maximum_fusion.refs_2_.refs_0_), channel_id=1, source_target_pairs={{0,1},{1,0},{2,3},{3,2},{4,5},{5,4},{6,7},{7,6},{8,9},{9,8},{10,11... | collective-permute-start | bytes 1572872 | tf_op jit(solution)/shard_map/ppermute | solution.py:222
  59.3 73.5 %collective-permute-start.10 = (bf16[16,256,256]{2,1,0:T(8,128)(2,1)S(1)}, bf16[16,256,256]{2,1,0:T(8,128)(2,1)}, u32[]{:S(2)}, u32[]{:S(2)}) collective-permute-start(bf16[16,256,256]{2,1,0:T(8,128)(2,1)S(1)} %bitcast.63), channel_id=1, source_target_pairs={{0,8},{8,0},{16,24},{24,16},{1,9},{9,1},{17,25},{25,17},{2,10},{10... | collective-permute-start | bytes 6291464 | tf_op jit(solution)/shard_map/ppermute | solution.py:226
  61.7 20.6 %collective-permute-start.16 = (bf16[4,2,128,256]{3,2,1,0:T(8,128)(2,1)S(1)}, bf16[4,2,128,256]{3,2,1,0:T(8,128)(2,1)S(1)}, u32[]{:S(2)}, u32[]{:S(2)}) collective-permute-start(bf16[4,2,128,256]{3,2,1,0:T(8,128)(2,1)S(1)} %pad_maximum_fusion.1.refs_2_.refs_0_), channel_id=1, source_target_pairs={{0,6},{1,7},{2,4},{3,5},{4,2},{5,3},{6,0},{7,1},{8,14},{9,15},{10,... | collective-permute-start | bytes 1572872 | tf_op jit(solution)/shard_map/ppermute | solution.py:222
  63.5 24.4 %collective-permute-start.15 = (bf16[4,2,128,256]{3,2,1,0:T(8,128)(2,1)S(1)}, bf16[4,2,128,256]{3,2,1,0:T(8,128)(2,1)S(1)}, u32[]{:S(2)}, u32[]{:S(2)}) collective-permute-start(bf16[4,2,128,256]{3,2,1,0:T(8,128)(2,1)S(1)} %pad_maximum_fusion.1.refs_2_.refs_0_), channel_id=1, source_target_pairs={{0,4},{1,5},{2,6},{3,7},{4,0},{5,1},{6,2},{7,3},{8,12},{9,13},{10,... | collective-permute-start | bytes 1572872 | tf_op jit(solution)/shard_map/ppermute | solution.py:222
  64.8 23.2 %collective-permute-start.14 = (bf16[4,2,128,256]{3,2,1,0:T(8,128)(2,1)S(1)}, bf16[4,2,128,256]{3,2,1,0:T(8,128)(2,1)S(1)}, u32[]{:S(2)}, u32[]{:S(2)}) collective-permute-start(bf16[4,2,128,256]{3,2,1,0:T(8,128)(2,1)S(1)} %pad_maximum_fusion.1.refs_2_.refs_0_), channel_id=1, source_target_pairs={{0,2},{1,3},{2,0},{3,1},{4,6},{5,7},{6,4},{7,5},{8,10},{9,11},{10,... | collective-permute-start | bytes 1572872 | tf_op jit(solution)/shard_map/ppermute | solution.py:222
  79.0 48.0 %collective-permute-start.12 = (bf16[8,128,256]{2,1,0:T(8,128)(2,1)}, bf16[8,128,256]{2,1,0:T(8,128)(2,1)S(1)}, u32[]{:S(2)}, u32[]{:S(2)}) collective-permute-start(bf16[8,128,256]{2,1,0:T(8,128)(2,1)} %get-tuple-element.55), channel_id=1, source_target_pairs={{0,24},{8,16},{16,8},{24,0},{1,25},{9,17},{17,9},{25,1},{2,26},{10... | collective-permute-start | bytes 1572872 | tf_op jit(solution)/shard_map/ppermute | solution.py:226
  88.0 41.0 %collective-permute-start.17 = (bf16[4,2,128,256]{3,2,1,0:T(8,128)(2,1)S(1)}, bf16[4,2,128,256]{3,2,1,0:T(8,128)(2,1)S(1)}, u32[]{:S(2)}, u32[]{:S(2)}) collective-permute-start(bf16[4,2,128,256]{3,2,1,0:T(8,128)(2,1)S(1)} %pad_maximum_fusion.1.refs_2_.refs_0_), channel_id=1, source_target_pairs={{0,1},{1,0},{2,3},{3,2},{4,5},{5,4},{6,7},{7,6},{8,9},{9,8},{10,11... | collective-permute-start | bytes 1572872 | tf_op jit(solution)/shard_map/ppermute | solution.py:222
  88.1 44.6 %collective-permute-start.18 = (bf16[4,2,128,256]{3,2,1,0:T(8,128)(2,1)S(1)}, bf16[4,2,128,256]{3,2,1,0:T(8,128)(2,1)S(1)}, u32[]{:S(2)}, u32[]{:S(2)}) collective-permute-start(bf16[4,2,128,256]{3,2,1,0:T(8,128)(2,1)S(1)} %collective-permute-done.14.refs_4_.refs_2_), channel_id=1, source_target_pairs={{0,1},{1,0},{2,3},{3,2},{4,5},{5,4},{6,7},{7,6},{8,9},{9,8},{10,11... | collective-permute-start | bytes 1572872 | tf_op jit(solution)/shard_map/ppermute | solution.py:222
  88.5 44.2 %collective-permute-start.19 = (bf16[4,2,128,256]{3,2,1,0:T(8,128)(2,1)S(1)}, bf16[4,2,128,256]{3,2,1,0:T(8,128)(2,1)S(1)}, u32[]{:S(2)}, u32[]{:S(2)}) collective-permute-start(bf16[4,2,128,256]{3,2,1,0:T(8,128)(2,1)S(1)} %collective-permute-done.15.refs_6_.refs_4_), channel_id=1, source_target_pairs={{0,1},{1,0},{2,3},{3,2},{4,5},{5,4},{6,7},{7,6},{8,9},{9,8},{10,11... | collective-permute-start | bytes 1572872 | tf_op jit(solution)/shard_map/ppermute | solution.py:222
  129.0 16.4 %collective-permute-start.13 = (bf16[8,128,256]{2,1,0:T(8,128)(2,1)S(1)}, bf16[8,128,256]{2,1,0:T(8,128)(2,1)S(1)}, u32[]{:S(2)}, u32[]{:S(2)}) collective-permute-start(bf16[8,128,256]{2,1,0:T(8,128)(2,1)S(1)} %multiply_convert_fusion.1.refs_2_.refs_8_), channel_id=1, source_target_pairs={{0,24},{8,16},{16,8},{24,0},{1,25},{9,17},{17,9},{25,1},{2,26},{10... | collective-permute-start | bytes 1572872 | tf_op jit(solution)/shard_map/ppermute | solution.py:226
  141.9 16.2 %collective-permute-start.21 = (bf16[8,128,256]{2,1,0:T(8,128)(2,1)}, bf16[8,128,256]{2,1,0:T(8,128)(2,1)S(1)}, u32[]{:S(2)}, u32[]{:S(2)}) collective-permute-start(bf16[8,128,256]{2,1,0:T(8,128)(2,1)} %get-tuple-element.74), channel_id=1, source_target_pairs={{0,24},{8,16},{16,8},{24,0},{1,25},{9,17},{17,9},{25,1},{2,26},{10... | collective-permute-start | bytes 1572872 | tf_op jit(solution)/shard_map/ppermute | solution.py:226
  158.7 27.4 %collective-permute-start.27 = (bf16[8,128,256]{2,1,0:T(8,128)(2,1)S(1)}, bf16[8,128,256]{2,1,0:T(8,128)(2,1)S(1)}, u32[]{:S(2)}, u32[]{:S(2)}) collective-permute-start(bf16[8,128,256]{2,1,0:T(8,128)(2,1)S(1)} %multiply_convert_fusion.refs_2_.refs_8_), channel_id=1, source_target_pairs={{0,24},{8,16},{16,8},{24,0},{1,25},{9,17},{17,9},{25,1},{2,26},{10... | collective-permute-start | bytes 1572872 | tf_op jit(solution)/shard_map/ppermute | solution.py:226
  160.9 25.3 %collective-permute-start.28 = (bf16[8,128,256]{2,1,0:T(8,128)(2,1)S(1)}, bf16[8,128,256]{2,1,0:T(8,128)(2,1)S(1)}, u32[]{:S(2)}, u32[]{:S(2)}) collective-permute-start(bf16[8,128,256]{2,1,0:T(8,128)(2,1)S(1)} %copy-done.6), channel_id=1, source_target_pairs={{0,8},{8,0},{16,24},{24,16},{1,9},{9,1},{17,25},{25,17},{2,10},{10... | collective-permute-start | bytes 1572872 | tf_op jit(solution)/shard_map/ppermute | solution.py:226
  166.6 13.3 %collective-permute-start.25 = (bf16[2,2,128,256]{3,2,1,0:T(8,128)(2,1)S(1)}, bf16[2,2,128,256]{3,2,1,0:T(8,128)(2,1)S(1)}, u32[]{:S(2)}, u32[]{:S(2)}) collective-permute-start(bf16[2,2,128,256]{3,2,1,0:T(8,128)(2,1)S(1)} %get-tuple-element.109), channel_id=1, source_target_pairs={{0,6},{1,7},{2,4},{3,5},{4,2},{5,3},{6,0},{7,1},{8,14},{9,15},{10,... | collective-permute-start | bytes 786440 | tf_op jit(solution)/shard_map/ppermute | solution.py:222
  194.9 14.8 %collective-permute-start.33 = (bf16[8,128,256]{2,1,0:T(8,128)(2,1)S(1)}, bf16[8,128,256]{2,1,0:T(8,128)(2,1)S(1)}, u32[]{:S(2)}, u32[]{:S(2)}) collective-permute-start(bf16[8,128,256]{2,1,0:T(8,128)(2,1)S(1)} %copy-done.23), channel_id=1, source_target_pairs={{0,8},{8,0},{16,24},{24,16},{1,9},{9,1},{17,25},{25,17},{2,10},{10... | collective-permute-start | bytes 1572872 | tf_op jit(solution)/shard_map/ppermute | solution.py:226
  199.3 25.1 %collective-permute-start.34 = (bf16[8,128,256]{2,1,0:T(8,128)(2,1)S(1)}, bf16[8,128,256]{2,1,0:T(8,128)(2,1)S(1)}, u32[]{:S(2)}, u32[]{:S(2)}) collective-permute-start(bf16[8,128,256]{2,1,0:T(8,128)(2,1)S(1)} %copy-done.4), channel_id=1, source_target_pairs={{0,8},{8,0},{16,24},{24,16},{1,9},{9,1},{17,25},{25,17},{2,10},{10... | collective-permute-start | bytes 1572872 | tf_op jit(solution)/shard_map/ppermute | solution.py:226
  199.9 31.8 %collective-permute-start.35 = (bf16[8,128,256]{2,1,0:T(8,128)(2,1)S(1)}, bf16[8,128,256]{2,1,0:T(8,128)(2,1)S(1)}, u32[]{:S(2)}, u32[]{:S(2)}) collective-permute-start(bf16[8,128,256]{2,1,0:T(8,128)(2,1)S(1)} %copy-done.25), channel_id=1, source_target_pairs={{0,8},{8,0},{16,24},{24,16},{1,9},{9,1},{17,25},{25,17},{2,10},{10... | collective-permute-start | bytes 1572872 | tf_op jit(solution)/shard_map/ppermute | solution.py:226
  211.2 23.9 %collective-permute-start.26 = (bf16[2,128,256]{2,1,0:T(8,128)(2,1)S(1)}, bf16[2,128,256]{2,1,0:T(8,128)(2,1)S(1)}, u32[]{:S(2)}, u32[]{:S(2)}) collective-permute-start(bf16[2,128,256]{2,1,0:T(8,128)(2,1)S(1)} %slice_bitcast_fusion.10), channel_id=1, source_target_pairs={{0,24},{8,16},{16,8},{24,0},{1,25},{9,17},{17,9},{25,1},{2,26},{10... | collective-permute-start | bytes 393224 | tf_op jit(solution)/shard_map/ppermute | solution.py:226
  (48 other events, 676.4 us)
